TPU v7x, 256 devices: a whole 4x4x8 slice. The times are simulated.
256 devices in a mesh: grp: 16 (over x, y), seq: 16 (over z, core).
Axes of the slice: x: 4, y: 4, z: 8, core: 2. Of those that a mesh axis runs over, the one named last changes fastest.
Arguments:
- q_spatial: bfloat16 [256, 256, 1536], P(('grp', 'seq')), may hold values from -5 to 5
- k_spatial: bfloat16 [256, 256, 1536], P(('grp', 'seq')), may hold values from -5 to 5
- v_spatial: bfloat16 [256, 256, 1536], P(('grp', 'seq')), may hold values from -6 to 6
- q_temporal: bfloat16 [256, 256, 1536], P(('grp', 'seq')), may hold values from -5 to 5
- k_temporal: bfloat16 [256, 256, 1536], P(('grp', 'seq')), may hold values from -5 to 5
- rel_bias: float32 [12, 31], replicated, may hold values from -4 to 4
- clip_ids: int32 [16, 16], P('grp', 'seq'), may hold values from 0 to 15, as said below
- cotangent: bfloat16 [256, 256, 1536], P(('grp', 'seq')), may hold values from -6 to 6
Outputs:
- result: bfloat16 [256, 256, 1536], P(('grp', 'seq'))
- grad_q_spatial: bfloat16 [256, 256, 1536], P(('grp', 'seq'))
- grad_k_spatial: bfloat16 [256, 256, 1536], P(('grp', 'seq'))
- grad_v_spatial: bfloat16 [256, 256, 1536], P(('grp', 'seq'))
- grad_q_temporal: bfloat16 [256, 256, 1536], P(('grp', 'seq'))
- grad_k_temporal: bfloat16 [256, 256, 1536], P(('grp', 'seq'))
- grad_rel_bias: float32 [12, 31], replicated
Inputs may be any that keep to these rules, and one draw needn't show every extreme that they name: `clip_ids`: within a group, clips are numbered from 0 in frame order and a clip's frames are consecutive; some group is a single clip of all 16 frames and some group has only one-frame clips.
All inputs are finite; a program needn't handle non-finite values.
Results may differ from a plain program's by a relative error of at most 0.027.
Values may be sent and summed in bfloat16 or wider, within the bound.
No kernel may reach another device: no remote copies, remote signals or barrier semaphores. Data moves between devices by JAX's collectives and lax.ppermute only.
A program may use at most 64 MiB of HBM per device.

v0:
```python
import jax
import jax.numpy as jnp
from jax import lax
from jax.sharding import PartitionSpec as P

HEADS = 12


SPATIAL = ("bihd,bjhd->bhij", "bhij,bjhd->bihd", "bhij,bihd->bjhd")
TEMPORAL = ("ibhd,jbhd->bhij", "bhij,jbhd->ibhd", "bhij,ibhd->jbhd")
NEG_FILL = -1e30


def product(pattern, left, right):
    return jnp.einsum(pattern, left, right, preferred_element_type=jnp.float32)


def attend(queries, key_heads, values, bias_term, same_clip, patterns):
    factor = queries.shape[-1] ** (-0.5)
    scores = product(patterns[0], queries, key_heads) * factor + bias_term
    scores = jnp.where(same_clip, scores, NEG_FILL)
    row_max = jnp.max(scores, axis=-1, keepdims=True)
    raw_weights = jnp.where(same_clip, jnp.exp(scores - row_max), 0.0)
    attn_prob = raw_weights / jnp.sum(raw_weights, axis=-1, keepdims=True)
    attn_low = attn_prob.astype(jnp.bfloat16)
    mixed = product(patterns[1], attn_low, values).astype(jnp.bfloat16)
    return (mixed, attn_prob, attn_low)


def attend_back(queries, key_heads, values, attn_prob, attn_low, upstream, patterns):
    factor = queries.shape[-1] ** (-0.5)
    grad_prob = product(patterns[0], upstream, values)
    grad_values = product(patterns[2], attn_low, upstream).astype(jnp.bfloat16)
    row_dot = jnp.sum(attn_prob * grad_prob, axis=-1, keepdims=True)
    grad_score = attn_prob * (grad_prob - row_dot)
    grad_low = (grad_score * factor).astype(jnp.bfloat16)
    grad_q = product(patterns[1], grad_low, key_heads).astype(jnp.bfloat16)
    grad_k = product(patterns[2], grad_low, queries).astype(jnp.bfloat16)
    return (grad_q, grad_k, grad_values, grad_score)


def offsets_table(frames):
    rows = jnp.arange(frames, dtype=jnp.int32)
    offset = rows[:, None] - rows[None, :] + (frames - 1)
    slots = jnp.arange(2 * frames - 1, dtype=jnp.int32)
    return (offset[:, :, None] == slots[None, None, :]).astype(jnp.float32)


def per_device(
    q_spatial, k_spatial, v_spatial, q_temporal, k_temporal, rel_bias, clip_ids, cotangent
):
    frames_dev, patches, width = q_spatial.shape
    head_shape = (frames_dev, patches, HEADS, width // HEADS)
    q_sp = q_spatial.reshape(head_shape)
    k_sp = k_spatial.reshape(head_shape)
    v_sp = v_spatial.reshape(head_shape)
    q_tm = q_temporal.reshape(head_shape)
    k_tm = k_temporal.reshape(head_shape)
    upstream = cotangent.reshape(head_shape)
    every = jnp.ones((patches, patches), dtype=bool)
    spatial_out, sp_prob, sp_low = attend(q_sp, k_sp, v_sp, 0.0, every, SPATIAL)
    clip_row = lax.all_gather(clip_ids, "seq", axis=1, tiled=True)[0]
    q_tile, k_tile, v_tile = (
        lax.all_to_all(q_tm, "seq", split_axis=1, concat_axis=0, tiled=True),
        lax.all_to_all(k_tm, "seq", split_axis=1, concat_axis=0, tiled=True),
        lax.all_to_all(spatial_out, "seq", split_axis=1, concat_axis=0, tiled=True),
    )
    table = offsets_table(clip_row.shape[0])
    bias_grid = jnp.einsum("hr,ijr->hij", rel_bias, table, precision=lax.Precision.HIGHEST)
    same_clip = clip_row[:, None] == clip_row[None, :]
    result_tile, tm_prob, tm_low = attend(q_tile, k_tile, v_tile, bias_grid, same_clip, TEMPORAL)
    up_tile = lax.all_to_all(upstream, "seq", split_axis=1, concat_axis=0, tiled=True)
    grad_qt_tile, grad_kt_tile, grad_mid_tile, grad_score = attend_back(
        q_tile, k_tile, v_tile, tm_prob, tm_low, up_tile, TEMPORAL
    )
    bias_terms = jnp.einsum(
        "hij,ijr->hr", jnp.sum(grad_score, axis=0), table, precision=lax.Precision.HIGHEST
    )
    total_bias = lax.psum(bias_terms, ("grp", "seq"))
    result, grad_qt, grad_kt, grad_mid = (
        lax.all_to_all(result_tile, "seq", split_axis=0, concat_axis=1, tiled=True),
        lax.all_to_all(grad_qt_tile, "seq", split_axis=0, concat_axis=1, tiled=True),
        lax.all_to_all(grad_kt_tile, "seq", split_axis=0, concat_axis=1, tiled=True),
        lax.all_to_all(grad_mid_tile, "seq", split_axis=0, concat_axis=1, tiled=True),
    )
    grad_qs, grad_ks, grad_vs, spatial_score = attend_back(
        q_sp, k_sp, v_sp, sp_prob, sp_low, grad_mid, SPATIAL
    )
    flat = (frames_dev, patches, width)
    return (
        result.reshape(flat),
        grad_qs.reshape(flat),
        grad_ks.reshape(flat),
        grad_vs.reshape(flat),
        grad_qt.reshape(flat),
        grad_kt.reshape(flat),
        total_bias,
    )


def solution(mesh):
    placed = (
        P(("grp", "seq"), None, None),
        P(("grp", "seq"), None, None),
        P(("grp", "seq"), None, None),
        P(("grp", "seq"), None, None),
        P(("grp", "seq"), None, None),
        P(),
        P("grp", "seq"),
        P(("grp", "seq"), None, None),
    )
    return jax.shard_map(
        per_device,
        mesh=mesh,
        in_specs=placed,
        out_specs=(
            P(("grp", "seq"), None, None),
            P(("grp", "seq"), None, None),
            P(("grp", "seq"), None, None),
            P(("grp", "seq"), None, None),
            P(("grp", "seq"), None, None),
            P(("grp", "seq"), None, None),
            P(),
        ),
        check_vma=False,
    )
```

profile of v0, /device:TPU:1, one launch (start us, length us, event | category | flops | bytes accessed | tf_op | source)
XLA Modules:
  0.0 354.5 jit_solution(16727430808362648515)
XLA Ops:
  3.1 2.9 fusion.58
  6.0 2.6 fusion.31
  10.1 10.0 %all-to-all-start = ((bf16[1,256,12,128]{3,2,0,1:T(8,128)(2,1)}), bf16[1,256,12,128]{3,2,0,1:T(8,128)(2,1)S(1)}, u32[]{:S(2)}, u32[]{:S(2)}) async-start(bf16[1,256,12,128]{3,2,0,1:T(8,128)(2,1)} %copy.160), calls=%async_computation | async-start | bytes 2097152 | tf_op jit(solution)/shard_map/all_to_all | solution.py:66
  22.1 25.9 %all-to-all-done = bf16[1,256,12,128]{3,2,0,1:T(8,128)(2,1)S(1)} async-done(((bf16[1,256,12,128]{3,2,0,1:T(8,128)(2,1)}), bf16[1,256,12,128]{3,2,0,1:T(8,128)(2,1)S(1)}, u32[]{:S(2)}, u32[]{:S(2)}) %all-to-all-start) | async-done | bytes 786464 | tf_op jit(solution)/shard_map/all_to_all | solution.py:66
  48.0 3.6 %all-to-all-start.4 = ((bf16[1,256,12,128]{3,2,0,1:T(8,128)(2,1)}), bf16[1,256,12,128]{3,2,0,1:T(8,128)(2,1)S(1)}, u32[]{:S(2)}, u32[]{:S(2)}) async-start(bf16[1,256,12,128]{3,2,0,1:T(8,128)(2,1)} %copy.176), calls=%async_computation.4 | async-start | bytes 2097152 | tf_op jit(solution)/shard_map/all_to_all | solution.py:72
  51.5 2.3 copy.162
  53.8 2.6 copy.163
  56.4 23.0 %all-to-all-done.4 = bf16[1,256,12,128]{3,2,0,1:T(8,128)(2,1)S(1)} async-done(((bf16[1,256,12,128]{3,2,0,1:T(8,128)(2,1)}), bf16[1,256,12,128]{3,2,0,1:T(8,128)(2,1)S(1)}, u32[]{:S(2)}, u32[]{:S(2)}) %all-to-all-start.4) | async-done | bytes 786464 | tf_op jit(solution)/shard_map/all_to_all | solution.py:72
  79.4 4.2 %all-to-all-start.1 = ((bf16[1,256,12,128]{3,2,0,1:T(8,128)(2,1)}), bf16[1,256,12,128]{3,2,0,1:T(8,128)(2,1)}, u32[]{:S(2)}, u32[]{:S(2)}) async-start(bf16[1,256,12,128]{3,2,0,1:T(8,128)(2,1)} %copy.163), calls=%async_computation.1 | async-start | bytes 2097152 | tf_op jit(solution)/shard_map/all_to_all | solution.py:64
  86.0 2.6 copy.166
  88.6 22.4 %all-to-all-done.1 = bf16[1,256,12,128]{3,2,0,1:T(8,128)(2,1)} async-done(((bf16[1,256,12,128]{3,2,0,1:T(8,128)(2,1)}), bf16[1,256,12,128]{3,2,0,1:T(8,128)(2,1)}, u32[]{:S(2)}, u32[]{:S(2)}) %all-to-all-start.1) | async-done | bytes 786464 | tf_op jit(solution)/shard_map/all_to_all | solution.py:64
  111.0 4.2 %all-to-all-start.2 = ((bf16[1,256,12,128]{3,2,0,1:T(8,128)(2,1)}), bf16[1,256,12,128]{3,2,0,1:T(8,128)(2,1)}, u32[]{:S(2)}, u32[]{:S(2)}) async-start(bf16[1,256,12,128]{3,2,0,1:T(8,128)(2,1)} %copy.166), calls=%async_computation.2 | async-start | bytes 2097152 | tf_op jit(solution)/shard_map/all_to_all | solution.py:65
  117.7 28.8 %all-reduce = s32[16]{0:T(128)S(1)} all-reduce(s32[16]{0:T(128)S(1)} %bitcast_dynamic-update-slice_fusion), channel_id=1, replica_groups=mesh['grp'=16,'seq'=16] {'seq'}, use_global_device_ids=true, to_apply=%add | all-reduce | flops 16 | bytes 128 | tf_op jit(solution)/shard_map/eq | solution.py:70
  148.8 4.4 %fusion.59 = (f32[16,12,16]{2,1,0:T(8,128)S(1)}, f32[16,12,16,16]{2,3,1,0:T(8,128)}) fusion(pred[16,16]{0,1:T(8,128)(4,1)S(1)} %broadcast_compare_fusion, f32[12,16,16]{1,2,0:T(8,128)S(1)} %copy.170, bf16[16,16,12,128]{3,2,1,0:T(8,128)(2,1)} %bitcast.15, bf16[16,16,12,128]{3,2,1,0:T(8,128)(2,1)} %bitcast.12), kind=kOutput, calls=%fused_computation.69 | convolution fusion | flops 12877839 | bytes 1794304 | tf_op jit(solution)/shard_map/sub | solution.py:23
  153.1 5.4 %fusion.29 = bf16[16,16,12,128]{3,0,2,1:T(8,128)(2,1)} fusion(bf16[16,16,12,128]{3,2,1,0:T(8,128)(2,1)} %bitcast.15, f32[16,12,16,16]{3,2,1,0:T(8,128)} %fusion.35, f32[16,12,16,16]{2,3,1,0:T(8,128)} %get-tuple-element.45, f32[16,12,16]{2,1,0:T(8,128)S(1)} %get-tuple-element.44), kind=kOutput, calls=%fused_computation.33 | convolution fusion | flops 13323279 | bytes 1978368 | tf_op jit(solution)/shard_map/bhij,jbhd->ibhd/dot_general | solution.py:15
  158.5 2.5 copy.190
  161.1 6.7 %all-to-all-start.6 = ((bf16[16,16,12,128]{3,1,2,0:T(8,128)(2,1)}), bf16[16,16,12,128]{3,1,2,0:T(8,128)(2,1)}, u32[]{:S(2)}, u32[]{:S(2)}) async-start(bf16[16,16,12,128]{3,1,2,0:T(8,128)(2,1)} %copy.190), calls=%async_computation.6 | async-start | bytes 1572864 | tf_op jit(solution)/shard_map/all_to_all | solution.py:82
  167.7 5.4 %fusion.30 = bf16[16,16,12,128]{3,0,2,1:T(8,128)(2,1)} fusion(bf16[16,16,12,128]{3,2,1,0:T(8,128)(2,1)} %bitcast.12, f32[16,12,16,16]{3,2,1,0:T(8,128)} %fusion.35, f32[16,12,16,16]{2,3,1,0:T(8,128)} %get-tuple-element.45, f32[16,12,16]{2,1,0:T(8,128)S(1)} %get-tuple-element.44), kind=kOutput, calls=%fused_computation.34 | convolution fusion | flops 13323279 | bytes 1978368 | tf_op jit(solution)/shard_map/bhij,ibhd->jbhd/dot_general | solution.py:15
  173.1 2.5 copy.193
  175.6 14.9 %all-to-all-done.6 = bf16[16,16,12,128]{3,1,2,0:T(8,128)(2,1)} async-done(((bf16[16,16,12,128]{3,1,2,0:T(8,128)(2,1)}), bf16[16,16,12,128]{3,1,2,0:T(8,128)(2,1)}, u32[]{:S(2)}, u32[]{:S(2)}) %all-to-all-start.6) | async-done | bytes 786464 | tf_op jit(solution)/shard_map/all_to_all | solution.py:82
  190.5 4.2 %all-to-all-start.7 = ((bf16[16,16,12,128]{3,1,2,0:T(8,128)(2,1)}), bf16[16,16,12,128]{3,1,2,0:T(8,128)(2,1)}, u32[]{:S(2)}, u32[]{:S(2)}) async-start(bf16[16,16,12,128]{3,1,2,0:T(8,128)(2,1)} %copy.193), calls=%async_computation.7 | async-start | bytes 1572864 | tf_op jit(solution)/shard_map/all_to_all | solution.py:83
  198.2 18.2 %all-to-all-done.7 = bf16[16,16,12,128]{3,1,2,0:T(8,128)(2,1)} async-done(((bf16[16,16,12,128]{3,1,2,0:T(8,128)(2,1)}), bf16[16,16,12,128]{3,1,2,0:T(8,128)(2,1)}, u32[]{:S(2)}, u32[]{:S(2)}) %all-to-all-start.7) | async-done | bytes 786464 | tf_op jit(solution)/shard_map/all_to_all | solution.py:83
  216.5 3.5 all-to-all-start.5
  220.0 3.6 %fusion.60 = f32[12,16,16]{1,2,0:T(8,128)S(1)} fusion(f32[16,12,16,16]{3,2,1,0:T(8,128)} %fusion.35, f32[16,12,16,16]{2,3,1,0:T(8,128)} %get-tuple-element.45, f32[16,12,16]{2,1,0:T(8,128)S(1)} %get-tuple-element.44), kind=kOutput, calls=%fused_computation.70 | output fusion | flops 294927 | bytes 417792 | tf_op jit(solution)/shard_map/sub | solution.py:35
  227.3 15.1 %all-to-all-done.5 = bf16[16,16,12,128]{3,1,2,0:T(8,128)(2,1)S(1)} async-done(((bf16[16,16,12,128]{3,1,2,0:T(8,128)(2,1)}), bf16[16,16,12,128]{3,1,2,0:T(8,128)(2,1)S(1)}, u32[]{:S(2)}, u32[]{:S(2)}) %all-to-all-start.5) | async-done | bytes 786464 | tf_op jit(solution)/shard_map/all_to_all | solution.py:84
  242.3 3.5 all-to-all-start.3
  246.1 77.7 %psum.7 = f32[12,31]{1,0:T(8,128)} all-reduce(f32[12,31]{1,0:T(8,128)S(1)} %convolution_bitcast_fusion.1), channel_id=1, replica_groups=mesh['grp'=16,'seq'=16] {'grp','seq'}, use_global_device_ids=true, to_apply=%region_7.8 | all-reduce | flops 372 | bytes 2976 | tf_op jit(solution)/shard_map/psum | solution.py:79
  330.7 2.3 fusion.65
  333.0 6.7 %fusion.24 = bf16[12,256,128]{1,2,0:T(8,128)(2,1)} fusion(bf16[256,12,128]{0,2,1:T(8,128)(2,1)S(1)} %bitcast.113, f32[12,256,256]{1,2,0:T(8,128)} %fusion.65, f32[12,256,256]{1,2,0:T(8,128)} %get-tuple-element.43, f32[12,256]{1,0:T(8,128)S(1)} %get-tuple-element.42), kind=kOutput, calls=%fused_computation.30 | convolution fusion | flops 207228160 | bytes 7876608 | tf_op jit(solution)/shard_map/bhij,bihd->bjhd/dot_general | solution.py:15
  339.7 2.4 copy.197
  342.1 5.8 %fusion.21 = bf16[12,256,128]{1,2,0:T(8,128)(2,1)S(1)} fusion(bf16[256,12,128]{0,2,1:T(8,128)(2,1)S(1)} %bitcast.111, f32[12,256,256]{1,2,0:T(8,128)} %fusion.65, f32[12,256,256]{1,2,0:T(8,128)} %get-tuple-element.43, f32[12,256]{1,0:T(8,128)S(1)} %get-tuple-element.42), kind=kOutput, calls=%fused_computation.29 | convolution fusion | flops 207228160 | bytes 7876608 | tf_op jit(solution)/shard_map/bhij,bjhd->bihd/dot_general | solution.py:15
  349.0 2.6 convolution_convert_fusion.2
  (52 shorter events, 30.5 us)
Async XLA Ops:
  0.6 114.6 %copy-start = (f32[12,31]{1,0:T(8,128)S(1)}, f32[12,31]{1,0:T(8,128)}, u32[]{:S(2)}) copy-start(f32[12,31]{1,0:T(8,128)} %param.13) | copy-start | bytes 4468
  0.6 1.5 copy-start.2
  0.7 1.8 copy-start.3
  2.2 0.9 copy-start.7
  2.5 3.5 copy-start.5
  8.5 11.5 %copy-start.4 = (bf16[1,256,1536]{2,1,0:T(8,128)(2,1)S(1)}, bf16[1,256,1536]{2,1,0:T(8,128)(2,1)}, u32[]{:S(2)}) copy-start(bf16[1,256,1536]{2,1,0:T(8,128)(2,1)} %param.15) | copy-start | bytes 2359300
  10.1 37.9 %all-to-all-start = ((bf16[1,256,12,128]{3,2,0,1:T(8,128)(2,1)}), bf16[1,256,12,128]{3,2,0,1:T(8,128)(2,1)S(1)}, u32[]{:S(2)}, u32[]{:S(2)}) async-start(bf16[1,256,12,128]{3,2,0,1:T(8,128)(2,1)} %copy.160), calls=%async_computation | async-start | bytes 2097152 | tf_op jit(solution)/shard_map/all_to_all | solution.py:66
  48.0 31.5 %all-to-all-start.4 = ((bf16[1,256,12,128]{3,2,0,1:T(8,128)(2,1)}), bf16[1,256,12,128]{3,2,0,1:T(8,128)(2,1)S(1)}, u32[]{:S(2)}, u32[]{:S(2)}) async-start(bf16[1,256,12,128]{3,2,0,1:T(8,128)(2,1)} %copy.176), calls=%async_computation.4 | async-start | bytes 2097152 | tf_op jit(solution)/shard_map/all_to_all | solution.py:72
  79.4 31.6 %all-to-all-start.1 = ((bf16[1,256,12,128]{3,2,0,1:T(8,128)(2,1)}), bf16[1,256,12,128]{3,2,0,1:T(8,128)(2,1)}, u32[]{:S(2)}, u32[]{:S(2)}) async-start(bf16[1,256,12,128]{3,2,0,1:T(8,128)(2,1)} %copy.163), calls=%async_computation.1 | async-start | bytes 2097152 | tf_op jit(solution)/shard_map/all_to_all | solution.py:64
  88.6 27.8 %copy-start.9 = (u32[256]{0:T(256)S(1)}, u32[256]{0:T(256)}, u32[]{:S(2)}) copy-start(u32[256]{0:T(256)} %constant.21) | copy-start | bytes 3076
  111.0 37.8 %all-to-all-start.2 = ((bf16[1,256,12,128]{3,2,0,1:T(8,128)(2,1)}), bf16[1,256,12,128]{3,2,0,1:T(8,128)(2,1)}, u32[]{:S(2)}, u32[]{:S(2)}) async-start(bf16[1,256,12,128]{3,2,0,1:T(8,128)(2,1)} %copy.166), calls=%async_computation.2 | async-start | bytes 2097152 | tf_op jit(solution)/shard_map/all_to_all | solution.py:65
  161.1 29.5 %all-to-all-start.6 = ((bf16[16,16,12,128]{3,1,2,0:T(8,128)(2,1)}), bf16[16,16,12,128]{3,1,2,0:T(8,128)(2,1)}, u32[]{:S(2)}, u32[]{:S(2)}) async-start(bf16[16,16,12,128]{3,1,2,0:T(8,128)(2,1)} %copy.190), calls=%async_computation.6 | async-start | bytes 1572864 | tf_op jit(solution)/shard_map/all_to_all | solution.py:82
  190.5 25.9 %all-to-all-start.7 = ((bf16[16,16,12,128]{3,1,2,0:T(8,128)(2,1)}), bf16[16,16,12,128]{3,1,2,0:T(8,128)(2,1)}, u32[]{:S(2)}, u32[]{:S(2)}) async-start(bf16[16,16,12,128]{3,1,2,0:T(8,128)(2,1)} %copy.193), calls=%async_computation.7 | async-start | bytes 1572864 | tf_op jit(solution)/shard_map/all_to_all | solution.py:83
  216.5 25.8 %all-to-all-start.5 = ((bf16[16,16,12,128]{3,1,2,0:T(8,128)(2,1)}), bf16[16,16,12,128]{3,1,2,0:T(8,128)(2,1)S(1)}, u32[]{:S(2)}, u32[]{:S(2)}) async-start(bf16[16,16,12,128]{3,1,2,0:T(8,128)(2,1)} %copy.179), calls=%async_computation.5 | async-start | bytes 1572864 | tf_op jit(solution)/shard_map/all_to_all | solution.py:84
  242.3 3.8 %copy-start.1 = (bf16[16,16,12,128]{3,1,2,0:T(8,128)(2,1)}, bf16[16,16,12,128]{3,1,2,0:T(8,128)(2,1)S(1)}, u32[]{:S(2)}) copy-start(bf16[16,16,12,128]{3,1,2,0:T(8,128)(2,1)S(1)} %all-to-all-done.5) | copy-start | bytes 2359300
  242.3 110.5 %all-to-all-start.3 = ((bf16[16,16,12,128]{3,1,2,0:T(8,128)(2,1)}), bf16[16,16,12,128]{3,1,2,0:T(8,128)(2,1)S(1)}, u32[]{:S(2)}, u32[]{:S(2)}) async-start(bf16[16,16,12,128]{3,1,2,0:T(8,128)(2,1)} %copy.173), calls=%async_computation.3 | async-start | bytes 1572864 | tf_op jit(solution)/shard_map/all_to_all | solution.py:81
  330.7 2.3 copy-start.8
  339.7 2.4 copy-start.6
where the time goes:
time: 356 us; the launch traced here: 354 us
  waiting for transfers between devices  119 us (33%)
  blocking collectives  107 us (30%)
  matrix products  44.9 us (13%)
  starting transfers between devices  39.9 us (11%)
  local copies, waits for them, and re-layouts  38.4 us (11%)
  other arithmetic  3.71 us (1%)
    psum x1, blocking collectives, per_device(): total_bias = lax.psum(bias_terms, ('grp', 'seq'))  77.7 us
    dot_general x10, matrix products, product(): return jnp.einsum(pattern, left, right, preferred_element_type=jnp.float32)  37.1 us
    eq x1, blocking collectives, per_device(): same_clip = clip_row[:, None] == clip_row[None, :]  28.8 us
    all_to_all x1, waiting for transfers between devices, per_device(): lax.all_to_all(spatial_out, 'seq', split_axis=1, concat_axis=0, tiled=True)  25.9 us
    all_to_all x1, waiting for transfers between devices, per_device(): lax.all_to_all(upstream, 'seq', split_axis=1, concat_axis=0, tiled=True)  23 us
    all_to_all x1, waiting for transfers between devices, per_device(): lax.all_to_all(q_tm, 'seq', split_axis=1, concat_axis=0, tiled=True)  22.4 us
    all_to_all x1, waiting for transfers between devices, per_device(): lax.all_to_all(grad_kt_tile, 'seq', split_axis=0, concat_axis=1, tiled=True)  18.2 us
    all_to_all x1, waiting for transfers between devices, per_device(): lax.all_to_all(grad_mid_tile, 'seq', split_axis=0, concat_axis=1, tiled=T...  15.1 us
  transfers between devices with their start and end apart: 8, of which 6 were waited for; matrix products, arithmetic and copies ran while one was open for 18% of the time, Pallas kernels for 0%

commit v1 on v0

v1 whole, which is shorter than its diff:
```python
import functools

import jax
import jax.numpy as jnp
from jax import lax
from jax.experimental import pallas as pl
from jax.experimental.pallas import tpu as pltpu
from jax.sharding import PartitionSpec as P

HEADS = 12
DIM = 128
SEQ = 16
TOK = 16
ROWS = SEQ * TOK
WIDTH = HEADS * DIM
SCALE = DIM ** (-0.5)
NEG = -1e30
BF = jnp.bfloat16
F32 = jnp.float32
PARAMS = pltpu.CompilerParams(vmem_limit_bytes=40 * 1024 * 1024)


def mm(left, right):
    return lax.dot_general(left, right, (((1,), (0,)), ((), ())), preferred_element_type=F32)


def mm_nt(left, right):
    return lax.dot_general(left, right, (((1,), (1,)), ((), ())), preferred_element_type=F32)


def mm_tn(left, right):
    return lax.dot_general(left, right, (((0,), (0,)), ((), ())), preferred_element_type=F32)


def softmax(scores):
    raw = jnp.exp(scores - jnp.max(scores, axis=-1, keepdims=True))
    return raw / jnp.sum(raw, axis=-1, keepdims=True)


def cost(products, rw):
    return pl.CostEstimate(
        flops=2 * products * HEADS * ROWS * ROWS * DIM,
        bytes_accessed=rw * ROWS * WIDTH * 2,
        transcendentals=HEADS * ROWS * ROWS,
    )


FRAME = pl.BlockSpec((1, ROWS, DIM), lambda h: (0, 0, h))
PROB = pl.BlockSpec((1, ROWS, ROWS), lambda h: (h, 0, 0))


def frame_shape():
    return jax.ShapeDtypeStruct((1, ROWS, WIDTH), BF)


def tile_spec(first):
    return pl.BlockSpec((SEQ, 1, TOK, DIM), lambda h: (0, first + h, 0, 0))


def spatial_fwd_kernel(q_ref, k_ref, v_ref, out_ref):
    prob = softmax(mm_nt(q_ref[0], k_ref[0]) * SCALE)
    out = mm(prob.astype(BF), v_ref[0]).astype(BF)
    out_ref[:, 0] = out.reshape(SEQ, TOK, DIM)


def spatial_bwd_kernel(q_ref, k_ref, v_ref, up_ref, gq_ref, gk_ref, gv_ref):
    q, k, v = q_ref[0], k_ref[0], v_ref[0]
    up = up_ref[:, 0].reshape(ROWS, DIM)
    prob = softmax(mm_nt(q, k) * SCALE)
    grad_prob = mm_nt(up, v)
    gv_ref[0] = mm_tn(prob.astype(BF), up).astype(BF)
    row_dot = jnp.sum(prob * grad_prob, axis=-1, keepdims=True)
    low = (prob * (grad_prob - row_dot) * SCALE).astype(BF)
    gq_ref[0] = mm(low, k).astype(BF)
    gk_ref[0] = mm_tn(low, q).astype(BF)


def temporal_a_kernel(q_ref, k_ref, up_ref, bias_ref, ccol_ref, crow_ref, prob_ref, mid_ref):
    q = q_ref[:, 0].reshape(ROWS, DIM)
    k = k_ref[:, 0].reshape(ROWS, DIM)
    up = up_ref[:, 0].reshape(ROWS, DIM)
    row = lax.broadcasted_iota(jnp.int32, (ROWS, ROWS), 0)
    col = lax.broadcasted_iota(jnp.int32, (ROWS, ROWS), 1)
    same = ((row & (TOK - 1)) == (col & (TOK - 1))) & (ccol_ref[...] == crow_ref[...])
    bias = jnp.broadcast_to(bias_ref[0][:, None, :], (SEQ, TOK, ROWS)).reshape(ROWS, ROWS)
    scores = jnp.where(same, mm_nt(q, k) * SCALE + bias, NEG)
    raw = jnp.where(same, jnp.exp(scores - jnp.max(scores, axis=-1, keepdims=True)), 0.0)
    prob = raw / jnp.sum(raw, axis=-1, keepdims=True)
    prob_ref[0] = prob
    mid_ref[:, 0] = mm_tn(prob.astype(BF), up).astype(BF).reshape(SEQ, TOK, DIM)


def temporal_b_kernel(q_ref, k_ref, up_ref, so_ref, prob_ref, out_ref, bias_ref):
    q = q_ref[:, 0].reshape(ROWS, DIM)
    k = k_ref[:, 0].reshape(ROWS, DIM)
    up = up_ref[:, 0].reshape(ROWS, DIM)
    so = so_ref[:, 0].reshape(ROWS, DIM)
    prob = prob_ref[0]
    out_ref[:, 0] = mm(prob.astype(BF), so).astype(BF).reshape(SEQ, TOK, DIM)
    grad_prob = mm_nt(up, so)
    row_dot = jnp.sum(prob * grad_prob, axis=-1, keepdims=True)
    score = prob * (grad_prob - row_dot)
    bias_ref[0] = jnp.sum(score.reshape(SEQ, TOK, ROWS), axis=1)
    low = (score * SCALE).astype(BF)
    out_ref[:, 1] = mm(low, k).astype(BF).reshape(SEQ, TOK, DIM)
    out_ref[:, 2] = mm_tn(low, q).astype(BF).reshape(SEQ, TOK, DIM)


def pack_kernel(clip_ref, q_ref, k_ref, up_ref, out_ref):
    for i, ref in enumerate((q_ref, k_ref, up_ref)):
        for h in range(HEADS):
            block = ref[0, :, h * DIM:(h + 1) * DIM]
            out_ref[:, i * HEADS + h] = block.reshape(SEQ, TOK, DIM)
    clip = jnp.full((SEQ, TOK, DIM), clip_ref[0, 0], jnp.int32)
    out_ref[:, 3 * HEADS] = clip.astype(F32).astype(BF)


def unpack_kernel(in_ref, res_ref, gq_ref, gk_ref):
    for h in range(HEADS):
        for i, ref in enumerate((res_ref, gq_ref, gk_ref)):
            ref[0, :, h * DIM:(h + 1) * DIM] = in_ref[:, 3 * h + i].reshape(ROWS, DIM)


def exchange(packed):
    return lax.all_to_all(packed, "seq", split_axis=0, concat_axis=0, tiled=True)


def sum_of_four(terms, axis, step):
    size = lax.axis_size(axis)

    def partner(mask):
        return lax.ppermute(terms, axis, [(i, i ^ (mask * step)) for i in range(size)])

    return (terms + partner(1)) + (partner(2) + partner(3))


def bias_sum(terms):
    for axis, step in (("grp", 1), ("grp", 4), ("seq", 1), ("seq", 4)):
        terms = sum_of_four(terms, axis, step)
    return terms


def offsets_table():
    rows = jnp.arange(SEQ, dtype=jnp.int32)
    offset = rows[:, None] - rows[None, :] + (SEQ - 1)
    slots = jnp.arange(2 * SEQ - 1, dtype=jnp.int32)
    return (offset[:, :, None] == slots[None, None, :]).astype(F32)


def per_device(
    q_spatial, k_spatial, v_spatial, q_temporal, k_temporal, rel_bias, clip_ids, cotangent
):
    vmem = pl.BlockSpec(memory_space=pltpu.VMEM)
    packed = pl.pallas_call(
        pack_kernel,
        out_shape=jax.ShapeDtypeStruct((SEQ, 3 * HEADS + 1, TOK, DIM), BF),
        in_specs=[pl.BlockSpec(memory_space=pltpu.SMEM), vmem, vmem, vmem],
        out_specs=vmem,
        compiler_params=PARAMS,
        name="pack",
    )(clip_ids, q_temporal, k_temporal, cotangent)
    there = exchange(packed)

    spatial_out = pl.pallas_call(
        spatial_fwd_kernel,
        grid=(HEADS,),
        out_shape=jax.ShapeDtypeStruct((SEQ, HEADS, TOK, DIM), BF),
        in_specs=[FRAME] * 3,
        out_specs=tile_spec(0),
        compiler_params=PARAMS,
        cost_estimate=cost(2, 4),
        name="spatial_fwd",
    )(q_spatial, k_spatial, v_spatial)
    there, spatial_out = lax.optimization_barrier((there, spatial_out))
    so = exchange(spatial_out)

    table = offsets_table()
    wide = jnp.repeat(table, TOK, axis=1)
    bias = jnp.einsum("hr,icr->hic", rel_bias, wide, precision=lax.Precision.HIGHEST)
    clips = there[:, 3 * HEADS, :, 0].astype(F32).reshape(ROWS)
    prob, mid = pl.pallas_call(
        temporal_a_kernel,
        grid=(HEADS,),
        out_shape=(
            jax.ShapeDtypeStruct((HEADS, ROWS, ROWS), F32),
            jax.ShapeDtypeStruct((SEQ, HEADS, TOK, DIM), BF),
        ),
        in_specs=[
            tile_spec(0),
            tile_spec(HEADS),
            tile_spec(2 * HEADS),
            pl.BlockSpec((1, SEQ, ROWS), lambda h: (h, 0, 0)),
            pl.BlockSpec((ROWS, 1), lambda h: (0, 0)),
            pl.BlockSpec((1, ROWS), lambda h: (0, 0)),
        ],
        out_specs=(PROB, tile_spec(0)),
        compiler_params=PARAMS,
        cost_estimate=cost(2, 12),
        name="temporal_a",
    )(there, there, there, bias, clips[:, None], clips[None, :])
    so, mid = lax.optimization_barrier((so, mid))
    grad_mid = exchange(mid)

    back, score_rows = pl.pallas_call(
        temporal_b_kernel,
        grid=(HEADS,),
        out_shape=(
            jax.ShapeDtypeStruct((SEQ, 3 * HEADS, TOK, DIM), BF),
            jax.ShapeDtypeStruct((HEADS, SEQ, ROWS), F32),
        ),
        in_specs=[tile_spec(0), tile_spec(HEADS), tile_spec(2 * HEADS), tile_spec(0), PROB],
        out_specs=(
            pl.BlockSpec((SEQ, 3, TOK, DIM), lambda h: (0, h, 0, 0)),
            pl.BlockSpec((1, SEQ, ROWS), lambda h: (h, 0, 0)),
        ),
        compiler_params=PARAMS,
        cost_estimate=cost(4, 12),
        name="temporal_b",
    )(there, there, there, so, prob)
    grad_mid, back = lax.optimization_barrier((grad_mid, back))
    returned = exchange(back)

    terms = jnp.einsum("hic,icr->hr", score_rows, wide, precision=lax.Precision.HIGHEST)
    total_bias = bias_sum(terms)

    grad_qs, grad_ks, grad_vs = pl.pallas_call(
        spatial_bwd_kernel,
        grid=(HEADS,),
        out_shape=(frame_shape(),) * 3,
        in_specs=[FRAME] * 3 + [tile_spec(0)],
        out_specs=(FRAME,) * 3,
        compiler_params=PARAMS,
        cost_estimate=cost(5, 7),
        name="spatial_bwd",
    )(q_spatial, k_spatial, v_spatial, grad_mid)

    result, grad_qt, grad_kt = pl.pallas_call(
        unpack_kernel,
        out_shape=(frame_shape(),) * 3,
        in_specs=[vmem],
        out_specs=(vmem,) * 3,
        compiler_params=PARAMS,
        name="unpack",
    )(returned)
    return result, grad_qs, grad_ks, grad_vs, grad_qt, grad_kt, total_bias


def solution(mesh):
    frames = P(("grp", "seq"), None, None)
    return jax.shard_map(
        per_device,
        mesh=mesh,
        in_specs=(frames,) * 5 + (P(), P("grp", "seq"), frames),
        out_specs=(frames,) * 6 + (P(),),
        check_vma=False,
    )
```

time: 356 us -> 208 us (0.58)
  blocking collectives: 107 us -> 0 us
  matrix products: 44.9 us -> 4.91 us
  Pallas kernels: 0 us -> 36.2 us
  local copies, waits for them, and re-layouts: 38.4 us -> 13.3 us
  waiting for transfers between devices: 119 us -> 109 us
    psum x1 -> x0, blocking collectives: 77.7 us -> none  [per_device(): total_bias = lax.psum(bias_terms, ('grp', 'seq'))]
    all_to_all x8 -> x4, waiting for transfers between devices: 119 us -> 66.5 us  [exchange(): lax.all_to_all(packed, 'seq', split_axis=0, concat_axis=0, tiled=True)]
    ppermute x0 -> x12, waiting for transfers between devices: none -> 42.1 us  [partner(): lax.ppermute(terms, axis, [(i, i ^ mask * step) for i in range(size)])]
    pallas_call x0 -> x6, Pallas kernels: none -> 36.2 us  [the longest x1 11.2 us: per_device(): pl.pallas_call(spatial_bwd_kernel, grid=(HEADS,), out_shape=(frame_shape(...]
    dot_general x12 -> x2, matrix products: 37.6 us -> 4.91 us  [the longest x1 2.97 us: per_device(): jnp.einsum('hic,icr->hr', score_rows, wide, precision=lax.Precision.HIGHEST)]
    eq x1 -> x0, blocking collectives: 28.8 us -> none  [per_device(): same_clip = clip_row[:, None] == clip_row[None, :]]
    ppermute x0 -> x12, starting transfers between devices: none -> 17.1 us  [partner(): lax.ppermute(terms, axis, [(i, i ^ mask * step) for i in range(size)])]
    all_to_all x8 -> x4, starting transfers between devices: 39.9 us -> 23.3 us  [exchange(): lax.all_to_all(packed, 'seq', split_axis=0, concat_axis=0, tiled=True)]
  transfers between devices with their start and end apart: 8 -> 16, of which waited for: 6 -> 12; matrix products, arithmetic and copies ran while one was open for 18% -> 3% of each run, Pallas kernels for 0% -> 17%
where the time goes in v1:
time: 208 us; the launch traced here: 206 us
  waiting for transfers between devices  109 us (52%)
  starting transfers between devices  40.5 us (19%)
  Pallas kernels  36.2 us (17%)
  local copies, waits for them, and re-layouts  13.3 us (6%)
  matrix products  4.91 us (2%)
    all_to_all x4, waiting for transfers between devices, exchange(): lax.all_to_all(packed, 'seq', split_axis=0, concat_axis=0, tiled=True)  66.5 us
    ppermute x12, waiting for transfers between devices, partner(): lax.ppermute(terms, axis, [(i, i ^ mask * step) for i in range(size)])  42.1 us
    all_to_all x4, starting transfers between devices, exchange(): lax.all_to_all(packed, 'seq', split_axis=0, concat_axis=0, tiled=True)  23.3 us
    ppermute x12, starting transfers between devices, partner(): lax.ppermute(terms, axis, [(i, i ^ mask * step) for i in range(size)])  17.1 us
    unnamed x32, local copies, waits for them, and re-layouts  12.9 us
    pallas_call x1, Pallas kernels, per_device(): pl.pallas_call(spatial_bwd_kernel, grid=(HEADS,), out_shape=(frame_shape(...  11.2 us
    pallas_call x1, Pallas kernels, per_device(): pl.pallas_call(temporal_a_kernel, grid=(HEADS,), out_shape=(jax.ShapeDtyp...  8.02 us
    pallas_call x1, Pallas kernels, per_device(): pl.pallas_call(spatial_fwd_kernel, grid=(HEADS,), out_shape=jax.ShapeDtyp...  7.84 us
  transfers between devices with their start and end apart: 16, of which 12 were waited for; matrix products, arithmetic and copies ran while one was open for 3% of the time, Pallas kernels for 17%

profile of v1, /device:TPU:1, one launch (start us, length us, event | category | flops | bytes accessed | tf_op | source)
XLA Modules:
  0.0 205.9 jit_solution(10091734564775062583)
XLA Ops:
  1.3 1.1 copy-done.5
  2.4 1.1 copy-done.6
  3.6 1.1 copy-done.7
  5.1 1.4 copy-done.1
  6.6 10.1 %all-to-all-start = ((bf16[16,37,16,128]{3,2,1,0:T(8,128)(2,1)}), bf16[16,37,16,128]{3,2,1,0:T(8,128)(2,1)S(1)}, u32[]{:S(2)}, u32[]{:S(2)}) async-start(bf16[16,37,16,128]{3,2,1,0:T(8,128)(2,1)} %copy-done.1), calls=%async_computation | async-start | bytes 4849664 | tf_op jit(solution)/shard_map/all_to_all | solution.py:125
  16.7 1.1 copy-done.11
  17.8 1.1 copy-done.13
  19.0 7.8 %spatial_fwd.1 = bf16[16,12,16,128]{3,2,1,0:T(8,128)(2,1)} custom-call(bf16[1,256,1536]{2,1,0:T(8,128)(2,1)S(1)} %copy-done.9, bf16[1,256,1536]{2,1,0:T(8,128)(2,1)S(1)} %copy-done.11, bf16[1,256,1536]{2,1,0:T(8,128)(2,1)S(1)} %copy-done.13), custom_call_target="tpu_custom_call" | custom-call | flops 402653184 | bytes 3145728 | tf_op jit(solution)/shard_map/spatial_fwd/pallas_call | solution.py:164
  26.8 45.5 %all-to-all-done.q_ref.k_ref.up_ref = bf16[16,37,16,128]{3,2,1,0:T(8,128)(2,1)S(1)} async-done(((bf16[16,37,16,128]{3,2,1,0:T(8,128)(2,1)}), bf16[16,37,16,128]{3,2,1,0:T(8,128)(2,1)S(1)}, u32[]{:S(2)}, u32[]{:S(2)}) %all-to-all-start) | async-done | bytes 2424864 | tf_op jit(solution)/shard_map/all_to_all | solution.py:125
  72.2 5.4 %all-to-all-start.1 = ((bf16[16,12,16,128]{3,2,1,0:T(8,128)(2,1)}), bf16[16,12,16,128]{3,2,1,0:T(8,128)(2,1)S(1)}, u32[]{:S(2)}, u32[]{:S(2)}) async-start(bf16[16,12,16,128]{3,2,1,0:T(8,128)(2,1)} %spatial_fwd.1), calls=%async_computation.1 | async-start | bytes 1572864 | tf_op jit(solution)/shard_map/all_to_all | solution.py:125
  78.0 1.9 fusion.3
  80.2 8.0 %temporal_a.1 = (f32[12,256,256]{2,1,0:T(8,128)S(1)}, bf16[16,12,16,128]{3,2,1,0:T(8,128)(2,1)S(1)}) custom-call(bf16[16,37,16,128]{3,2,1,0:T(8,128)(2,1)S(1)} %all-to-all-done.q_ref.k_ref.up_ref, bf16[16,37,16,128]{3,2,1,0:T(8,128)(2,1)S(1)} %all-to-all-done.q_ref.k_ref.up_ref, bf16[16,37,16,128]{3,2,1,0:T(8,128)(2,1)S(1)} %all-to-all-done.q_ref.k_ref.up_ref, ...), custom_call_target="tpu_custom_call" | custom-call | flops 402653184 | bytes 9437184 | tf_op jit(solution)/shard_map/temporal_a/pallas_call | solution.py:181
  88.3 1.6 copy-done.2
  90.8 9.5 %all-to-all-done.1.so_ref = bf16[16,12,16,128]{3,2,1,0:T(8,128)(2,1)S(1)} async-done(((bf16[16,12,16,128]{3,2,1,0:T(8,128)(2,1)}), bf16[16,12,16,128]{3,2,1,0:T(8,128)(2,1)S(1)}, u32[]{:S(2)}, u32[]{:S(2)}) %all-to-all-start.1) | async-done | bytes 786464 | tf_op jit(solution)/shard_map/all_to_all | solution.py:125
  100.3 4.2 %all-to-all-start.2 = ((bf16[16,12,16,128]{3,2,1,0:T(8,128)(2,1)}), bf16[16,12,16,128]{3,2,1,0:T(8,128)(2,1)}, u32[]{:S(2)}, u32[]{:S(2)}) async-start(bf16[16,12,16,128]{3,2,1,0:T(8,128)(2,1)} %copy-done.8), calls=%async_computation.2 | async-start | bytes 1572864 | tf_op jit(solution)/shard_map/all_to_all | solution.py:125
  104.5 1.9 copy-done.3
  106.4 6.9 %temporal_b.1 = (bf16[16,36,16,128]{3,2,1,0:T(8,128)(2,1)S(1)}, f32[12,16,256]{2,1,0:T(8,128)S(1)}) custom-call(bf16[16,37,16,128]{3,2,1,0:T(8,128)(2,1)S(1)} %all-to-all-done.q_ref.k_ref.up_ref, bf16[16,37,16,128]{3,2,1,0:T(8,128)(2,1)S(1)} %all-to-all-done.q_ref.k_ref.up_ref, bf16[16,37,16,128]{3,2,1,0:T(8,128)(2,1)S(1)} %all-to-all-done.q_ref.k_ref.up_ref, ...), custom_call_target="tpu_custom_call" | custom-call | flops 805306368 | bytes 9437184 | tf_op jit(solution)/shard_map/temporal_b/pallas_call | solution.py:204
  113.3 1.4 copy-done.4
  114.7 11.5 %all-to-all-done.2.up_ref = bf16[16,12,16,128]{3,2,1,0:T(8,128)(2,1)} async-done(((bf16[16,12,16,128]{3,2,1,0:T(8,128)(2,1)}), bf16[16,12,16,128]{3,2,1,0:T(8,128)(2,1)}, u32[]{:S(2)}, u32[]{:S(2)}) %all-to-all-start.2) | async-done | bytes 786464 | tf_op jit(solution)/shard_map/all_to_all | solution.py:125
  126.3 3.6 %all-to-all-start.3 = ((bf16[16,36,16,128]{3,2,1,0:T(8,128)(2,1)}), bf16[16,36,16,128]{3,2,1,0:T(8,128)(2,1)S(1)}, u32[]{:S(2)}, u32[]{:S(2)}) async-start(bf16[16,36,16,128]{3,2,1,0:T(8,128)(2,1)} %copy-done.4), calls=%async_computation.3 | async-start | bytes 4718592 | tf_op jit(solution)/shard_map/all_to_all | solution.py:125
  129.9 3.0 %convolution_bitcast_fusion = f32[12,31]{1,0:T(8,128)S(1)} fusion(f32[16,256,31]{2,1,0:T(8,128)} %bitcast.15, f32[12,16,256]{2,1,0:T(8,128)S(1)} %get-tuple-element.38), kind=kOutput, calls=%fused_computation | convolution fusion | flops 18284544 | bytes 706000 | tf_op jit(solution)/shard_map/hic,icr->hr/dot_general | solution.py:223
  132.9 3.0 %collective-permute-start.1 = (f32[12,31]{1,0:T(8,128)S(1)}, f32[12,31]{1,0:T(8,128)S(1)}, u32[]{:S(2)}, u32[]{:S(2)}) collective-permute-start(f32[12,31]{1,0:T(8,128)S(1)} %convolution_bitcast_fusion), channel_id=1, source_target_pairs={{0,32},{16,48},{32,0},{48,16},{64,96},{80,112},{96,64},{112,80},{1... | collective-permute-start | bytes 4472 | tf_op jit(solution)/shard_map/ppermute | solution.py:132
  137.3 2.6 %collective-permute-done.2 = f32[12,31]{1,0:T(8,128)S(1)} collective-permute-done((f32[12,31]{1,0:T(8,128)S(1)}, f32[12,31]{1,0:T(8,128)S(1)}, u32[]{:S(2)}, u32[]{:S(2)}) %collective-permute-start.2) | collective-permute-done | bytes 1520 | tf_op jit(solution)/shard_map/ppermute | solution.py:132
  139.9 2.8 %collective-permute-start.4 = (f32[12,31]{1,0:T(8,128)S(1)}, f32[12,31]{1,0:T(8,128)S(1)}, u32[]{:S(2)}, u32[]{:S(2)}) collective-permute-start(f32[12,31]{1,0:T(8,128)S(1)} %add_add_fusion.3), channel_id=1, source_target_pairs={{0,128},{16,144},{32,160},{48,176},{64,192},{80,208},{96,224},{112... | collective-permute-start | bytes 4472 | tf_op jit(solution)/shard_map/ppermute | solution.py:132
  144.3 2.5 %collective-permute-done.5 = f32[12,31]{1,0:T(8,128)S(1)} collective-permute-done((f32[12,31]{1,0:T(8,128)S(1)}, f32[12,31]{1,0:T(8,128)S(1)}, u32[]{:S(2)}, u32[]{:S(2)}) %collective-permute-start.5) | collective-permute-done | bytes 1520 | tf_op jit(solution)/shard_map/ppermute | solution.py:132
  147.8 2.6 %collective-permute-start.8 = (f32[12,31]{1,0:T(8,128)S(1)}, f32[12,31]{1,0:T(8,128)S(1)}, u32[]{:S(2)}, u32[]{:S(2)}) collective-permute-start(f32[12,31]{1,0:T(8,128)S(1)} %add_add_fusion.2), channel_id=1, source_target_pairs={{0,3},{1,2},{2,1},{3,0},{4,7},{5,6},{6,5},{7,4},{8,11},{9,10},{10,... | collective-permute-start | bytes 4472 | tf_op jit(solution)/shard_map/ppermute | solution.py:132
  150.7 32.0 %collective-permute-done.7 = f32[12,31]{1,0:T(8,128)S(1)} collective-permute-done((f32[12,31]{1,0:T(8,128)S(1)}, f32[12,31]{1,0:T(8,128)S(1)}, u32[]{:S(2)}, u32[]{:S(2)}) %collective-permute-start.7) | collective-permute-done | bytes 1520 | tf_op jit(solution)/shard_map/ppermute | solution.py:132
  183.4 4.1 %collective-permute-start.10 = (f32[12,31]{1,0:T(8,128)S(1)}, f32[12,31]{1,0:T(8,128)S(1)}, u32[]{:S(2)}, u32[]{:S(2)}) collective-permute-start(f32[12,31]{1,0:T(8,128)S(1)} %add_add_fusion.1), channel_id=1, source_target_pairs={{0,8},{1,9},{2,10},{3,11},{4,12},{5,13},{6,14},{7,15},{8,0},{9,1},... | collective-permute-start | bytes 4472 | tf_op jit(solution)/shard_map/ppermute | solution.py:132
  187.4 1.4 collective-permute-start.11
  189.9 2.1 %collective-permute-done.11 = f32[12,31]{1,0:T(8,128)S(1)} collective-permute-done((f32[12,31]{1,0:T(8,128)S(1)}, f32[12,31]{1,0:T(8,128)S(1)}, u32[]{:S(2)}, u32[]{:S(2)}) %collective-permute-start.11) | collective-permute-done | bytes 1520 | tf_op jit(solution)/shard_map/ppermute | solution.py:132
  192.8 11.2 %spatial_bwd.1 = (bf16[1,256,1536]{2,1,0:T(8,128)(2,1)}, bf16[1,256,1536]{2,1,0:T(8,128)(2,1)}, bf16[1,256,1536]{2,1,0:T(8,128)(2,1)}) custom-call(bf16[1,256,1536]{2,1,0:T(8,128)(2,1)S(1)} %copy-done.10, bf16[1,256,1536]{2,1,0:T(8,128)(2,1)S(1)} %copy-done.12, bf16[1,256,1536]{2,1,0:T(8,128)(2,1)S(1)} %copy-done.14, ...), custom_call_target="tpu_custom_call" | custom-call | flops 1006632960 | bytes 5505024 | tf_op jit(solution)/shard_map/spatial_bwd/pallas_call | solution.py:226
  204.1 1.8 unpack.1
  (51 shorter events, 8.7 us)
Async XLA Ops:
  0.6 77.3 %copy-start = (f32[12,31]{1,0:T(8,128)S(1)}, f32[12,31]{1,0:T(8,128)}, u32[]{:S(2)}) copy-start(f32[12,31]{1,0:T(8,128)} %param.13) | copy-start | bytes 4468
  1.3 1.1 copy-start.5
  2.4 1.1 copy-start.6
  3.6 1.1 copy-start.7
  5.1 1.4 copy-start.1
  6.6 10.1 %copy-start.9 = (bf16[1,256,1536]{2,1,0:T(8,128)(2,1)S(1)}, bf16[1,256,1536]{2,1,0:T(8,128)(2,1)}, u32[]{:S(2)}) copy-start(bf16[1,256,1536]{2,1,0:T(8,128)(2,1)} %q_ref.5) | copy-start | bytes 2359300
  6.6 65.7 %all-to-all-start = ((bf16[16,37,16,128]{3,2,1,0:T(8,128)(2,1)}), bf16[16,37,16,128]{3,2,1,0:T(8,128)(2,1)S(1)}, u32[]{:S(2)}, u32[]{:S(2)}) async-start(bf16[16,37,16,128]{3,2,1,0:T(8,128)(2,1)} %copy-done.1), calls=%async_computation | async-start | bytes 4849664 | tf_op jit(solution)/shard_map/all_to_all | solution.py:125
  16.7 1.1 copy-start.11
  17.8 1.1 copy-start.13
  72.2 28.1 %all-to-all-start.1 = ((bf16[16,12,16,128]{3,2,1,0:T(8,128)(2,1)}), bf16[16,12,16,128]{3,2,1,0:T(8,128)(2,1)S(1)}, u32[]{:S(2)}, u32[]{:S(2)}) async-start(bf16[16,12,16,128]{3,2,1,0:T(8,128)(2,1)} %spatial_fwd.1), calls=%async_computation.1 | async-start | bytes 1572864 | tf_op jit(solution)/shard_map/all_to_all | solution.py:125
  77.9 2.1 %copy-start.15 = (f32[16,16,16,31]{3,2,1,0:T(8,128)}, f32[16,16,16,31]{3,2,1,0:T(8,128)S(1)}, u32[]{:S(2)}) copy-start(f32[16,16,16,31]{3,2,1,0:T(8,128)S(1)} %broadcast_in_dim.4) | copy-start | bytes 1523716
  88.3 1.6 copy-start.2
  89.9 0.9 copy-start.8
  100.3 25.9 %all-to-all-start.2 = ((bf16[16,12,16,128]{3,2,1,0:T(8,128)(2,1)}), bf16[16,12,16,128]{3,2,1,0:T(8,128)(2,1)}, u32[]{:S(2)}, u32[]{:S(2)}) async-start(bf16[16,12,16,128]{3,2,1,0:T(8,128)(2,1)} %copy-done.8), calls=%async_computation.2 | async-start | bytes 1572864 | tf_op jit(solution)/shard_map/all_to_all | solution.py:125
  104.5 1.9 copy-start.3
  113.3 1.4 copy-start.4
  126.3 77.8 %all-to-all-start.3 = ((bf16[16,36,16,128]{3,2,1,0:T(8,128)(2,1)}), bf16[16,36,16,128]{3,2,1,0:T(8,128)(2,1)S(1)}, u32[]{:S(2)}, u32[]{:S(2)}) async-start(bf16[16,36,16,128]{3,2,1,0:T(8,128)(2,1)} %copy-done.4), calls=%async_computation.3 | async-start | bytes 4718592 | tf_op jit(solution)/shard_map/all_to_all | solution.py:125
  129.9 62.9 %copy-start.10 = (bf16[1,256,1536]{2,1,0:T(8,128)(2,1)S(1)}, bf16[1,256,1536]{2,1,0:T(8,128)(2,1)}, u32[]{:S(2)}) copy-start(bf16[1,256,1536]{2,1,0:T(8,128)(2,1)} %q_ref.5) | copy-start | bytes 2359300
  129.9 62.9 %copy-start.12 = (bf16[1,256,1536]{2,1,0:T(8,128)(2,1)S(1)}, bf16[1,256,1536]{2,1,0:T(8,128)(2,1)}, u32[]{:S(2)}) copy-start(bf16[1,256,1536]{2,1,0:T(8,128)(2,1)} %k_ref.5) | copy-start | bytes 2359300
  129.9 62.9 %copy-start.14 = (bf16[1,256,1536]{2,1,0:T(8,128)(2,1)S(1)}, bf16[1,256,1536]{2,1,0:T(8,128)(2,1)}, u32[]{:S(2)}) copy-start(bf16[1,256,1536]{2,1,0:T(8,128)(2,1)} %v_ref.3) | copy-start | bytes 2359300
  132.9 4.4 %collective-permute-start.1 = (f32[12,31]{1,0:T(8,128)S(1)}, f32[12,31]{1,0:T(8,128)S(1)}, u32[]{:S(2)}, u32[]{:S(2)}) collective-permute-start(f32[12,31]{1,0:T(8,128)S(1)} %convolution_bitcast_fusion), channel_id=1, source_target_pairs={{0,32},{16,48},{32,0},{48,16},{64,96},{80,112},{96,64},{112,80},{1... | collective-permute-start | bytes 4472 | tf_op jit(solution)/shard_map/ppermute | solution.py:132
  135.9 4.0 %collective-permute-start.2 = (f32[12,31]{1,0:T(8,128)S(1)}, f32[12,31]{1,0:T(8,128)S(1)}, u32[]{:S(2)}, u32[]{:S(2)}) collective-permute-start(f32[12,31]{1,0:T(8,128)S(1)} %convolution_bitcast_fusion), channel_id=1, source_target_pairs={{0,48},{16,32},{32,16},{48,0},{64,112},{80,96},{96,80},{112,64},{1... | collective-permute-start | bytes 4472 | tf_op jit(solution)/shard_map/ppermute | solution.py:132
  136.7 3.2 %collective-permute-start = (f32[12,31]{1,0:T(8,128)S(1)}, f32[12,31]{1,0:T(8,128)S(1)}, u32[]{:S(2)}, u32[]{:S(2)}) collective-permute-start(f32[12,31]{1,0:T(8,128)S(1)} %convolution_bitcast_fusion), channel_id=1, source_target_pairs={{0,16},{16,0},{32,48},{48,32},{64,80},{80,64},{96,112},{112,96},{1... | collective-permute-start | bytes 4472 | tf_op jit(solution)/shard_map/ppermute | solution.py:132
  139.9 4.4 %collective-permute-start.4 = (f32[12,31]{1,0:T(8,128)S(1)}, f32[12,31]{1,0:T(8,128)S(1)}, u32[]{:S(2)}, u32[]{:S(2)}) collective-permute-start(f32[12,31]{1,0:T(8,128)S(1)} %add_add_fusion.3), channel_id=1, source_target_pairs={{0,128},{16,144},{32,160},{48,176},{64,192},{80,208},{96,224},{112... | collective-permute-start | bytes 4472 | tf_op jit(solution)/shard_map/ppermute | solution.py:132
  142.8 4.0 %collective-permute-start.5 = (f32[12,31]{1,0:T(8,128)S(1)}, f32[12,31]{1,0:T(8,128)S(1)}, u32[]{:S(2)}, u32[]{:S(2)}) collective-permute-start(f32[12,31]{1,0:T(8,128)S(1)} %add_add_fusion.3), channel_id=1, source_target_pairs={{0,192},{16,208},{32,224},{48,240},{64,128},{80,144},{96,160},{112... | collective-permute-start | bytes 4472 | tf_op jit(solution)/shard_map/ppermute | solution.py:132
  143.6 3.1 %collective-permute-start.3 = (f32[12,31]{1,0:T(8,128)S(1)}, f32[12,31]{1,0:T(8,128)S(1)}, u32[]{:S(2)}, u32[]{:S(2)}) collective-permute-start(f32[12,31]{1,0:T(8,128)S(1)} %add_add_fusion.3), channel_id=1, source_target_pairs={{0,64},{16,80},{32,96},{48,112},{64,0},{80,16},{96,32},{112,48},{1... | collective-permute-start | bytes 4472 | tf_op jit(solution)/shard_map/ppermute | solution.py:132
  146.8 35.9 %collective-permute-start.7 = (f32[12,31]{1,0:T(8,128)S(1)}, f32[12,31]{1,0:T(8,128)S(1)}, u32[]{:S(2)}, u32[]{:S(2)}) collective-permute-start(f32[12,31]{1,0:T(8,128)S(1)} %add_add_fusion.2), channel_id=1, source_target_pairs={{0,2},{1,3},{2,0},{3,1},{4,6},{5,7},{6,4},{7,5},{8,10},{9,11},{10,... | collective-permute-start | bytes 4472 | tf_op jit(solution)/shard_map/ppermute | solution.py:132
  147.8 35.5 %collective-permute-start.8 = (f32[12,31]{1,0:T(8,128)S(1)}, f32[12,31]{1,0:T(8,128)S(1)}, u32[]{:S(2)}, u32[]{:S(2)}) collective-permute-start(f32[12,31]{1,0:T(8,128)S(1)} %add_add_fusion.2), channel_id=1, source_target_pairs={{0,3},{1,2},{2,1},{3,0},{4,7},{5,6},{6,5},{7,4},{8,11},{9,10},{10,... | collective-permute-start | bytes 4472 | tf_op jit(solution)/shard_map/ppermute | solution.py:132
  150.4 32.9 %collective-permute-start.6 = (f32[12,31]{1,0:T(8,128)S(1)}, f32[12,31]{1,0:T(8,128)S(1)}, u32[]{:S(2)}, u32[]{:S(2)}) collective-permute-start(f32[12,31]{1,0:T(8,128)S(1)} %add_add_fusion.2), channel_id=1, source_target_pairs={{0,1},{1,0},{2,3},{3,2},{4,5},{5,4},{6,7},{7,6},{8,9},{9,8},{10,11... | collective-permute-start | bytes 4472 | tf_op jit(solution)/shard_map/ppermute | solution.py:132
  183.4 6.6 %collective-permute-start.10 = (f32[12,31]{1,0:T(8,128)S(1)}, f32[12,31]{1,0:T(8,128)S(1)}, u32[]{:S(2)}, u32[]{:S(2)}) collective-permute-start(f32[12,31]{1,0:T(8,128)S(1)} %add_add_fusion.1), channel_id=1, source_target_pairs={{0,8},{1,9},{2,10},{3,11},{4,12},{5,13},{6,14},{7,15},{8,0},{9,1},... | collective-permute-start | bytes 4472 | tf_op jit(solution)/shard_map/ppermute | solution.py:132
  187.4 4.6 %collective-permute-start.11 = (f32[12,31]{1,0:T(8,128)S(1)}, f32[12,31]{1,0:T(8,128)S(1)}, u32[]{:S(2)}, u32[]{:S(2)}) collective-permute-start(f32[12,31]{1,0:T(8,128)S(1)} %add_add_fusion.1), channel_id=1, source_target_pairs={{0,12},{1,13},{2,14},{3,15},{4,8},{5,9},{6,10},{7,11},{8,4},{9,5},... | collective-permute-start | bytes 4472 | tf_op jit(solution)/shard_map/ppermute | solution.py:132
  188.8 3.4 %collective-permute-start.9 = (f32[12,31]{1,0:T(8,128)S(1)}, f32[12,31]{1,0:T(8,128)S(1)}, u32[]{:S(2)}, u32[]{:S(2)}) collective-permute-start(f32[12,31]{1,0:T(8,128)S(1)} %add_add_fusion.1), channel_id=1, source_target_pairs={{0,4},{1,5},{2,6},{3,7},{4,0},{5,1},{6,2},{7,3},{8,12},{9,13},{10,... | collective-permute-start | bytes 4472 | tf_op jit(solution)/shard_map/ppermute | solution.py:132

commit v2 on v0

v2 whole, which is shorter than its diff:
```python
import jax
import jax.numpy as jnp
from jax import lax
from jax.experimental import pallas as pl
from jax.experimental.pallas import tpu as pltpu
from jax.sharding import PartitionSpec as P

HEADS = 12
DIM = 128
SEQ = 16
CHIPS = 8
TOK = 16
ROWS = SEQ * TOK
WIDTH = HEADS * DIM
SCALE = DIM ** (-0.5)
NEG = -1e30
BF = jnp.bfloat16
F32 = jnp.float32
PARAMS = pltpu.CompilerParams(vmem_limit_bytes=48 * 1024 * 1024)
PARTS = 4
LONG = 10**12
VMEM = pl.BlockSpec(memory_space=pltpu.VMEM)
SMEM = pl.BlockSpec(memory_space=pltpu.SMEM)
HBM = pl.BlockSpec(memory_space=pltpu.HBM)


def mm(left, right):
    return lax.dot_general(left, right, (((1,), (0,)), ((), ())), preferred_element_type=F32)


def mm_nt(left, right):
    return lax.dot_general(left, right, (((1,), (1,)), ((), ())), preferred_element_type=F32)


def mm_tn(left, right):
    return lax.dot_general(left, right, (((0,), (0,)), ((), ())), preferred_element_type=F32)


def softmax(scores):
    raw = jnp.exp(scores - jnp.max(scores, axis=-1, keepdims=True))
    return raw / jnp.sum(raw, axis=-1, keepdims=True)


def units(n, tiles):
    return jax.ShapeDtypeStruct((n, tiles, TOK, DIM), BF)


def frame():
    return jax.ShapeDtypeStruct((1, ROWS, WIDTH), BF)


def probs():
    return jax.ShapeDtypeStruct((HEADS, ROWS, ROWS), F32)


def head(h):
    return slice(h * DIM, (h + 1) * DIM)


def rows_of(ref, tile):
    return ref[:, tile].reshape(ROWS, DIM)


SHIFTS = (1, -1, 3, -3, 2, -2, 4)
SLOTS = tuple((d, x) for x in range(2) for d in range(CHIPS))


def slot_rows(frames_ref, ref, tile):
    return jnp.concatenate([ref[frames_ref[s], tile] for s in range(SEQ)], axis=0)


def put_slots(frames_ref, ref, tile, value):
    low = value.astype(BF)
    for s in range(SEQ):
        ref[frames_ref[s], tile] = low[s * TOK:(s + 1) * TOK]


def pack_kernel(clip_ref, q_ref, k_ref, up_ref, out_ref, held, sems):
    copies = []
    size = ROWS // PARTS
    for i, ref in enumerate((q_ref, k_ref, up_ref)):
        for part in range(PARTS):
            rows = pl.ds(part * size, size)
            copies.append(
                pltpu.make_async_copy(ref.at[0, rows], held.at[i, rows], sems.at[i, part])
            )
            copies[-1].start()
    clip = jnp.full((SEQ, TOK, DIM), clip_ref[0, 0], jnp.int32).astype(F32).astype(BF)
    out_ref[:, 3 * HEADS] = clip
    units_of = SEQ // PARTS
    for i in range(3):
        for part in range(PARTS):
            copies[i * PARTS + part].wait()
            for h in range(HEADS):
                block = held[i, part * size:(part + 1) * size, head(h)]
                out_ref[part * units_of:(part + 1) * units_of, i * HEADS + h] = block.reshape(
                    units_of, TOK, DIM
                )


def spatial_fwd_kernel(pos_ref, q_ref, k_ref, v_ref, keep_ref, give_ref, prob_ref):
    z, first = pos_ref[0], pos_ref[1] == 0
    for h in range(HEADS):
        prob = softmax(mm_nt(q_ref[0, :, head(h)], k_ref[0, :, head(h)]) * SCALE)
        prob_ref[h] = prob
        out = mm(prob.astype(BF), v_ref[0, :, head(h)])
        for chip in range(CHIPS):
            even = out[2 * chip * TOK:(2 * chip + 1) * TOK]
            odd = out[(2 * chip + 1) * TOK:(2 * chip + 2) * TOK]
            shift = (chip - z) & (CHIPS - 1)
            keep_ref[shift, h] = jnp.where(first, even, odd).astype(BF)
            give_ref[shift, h] = jnp.where(first, odd, even).astype(BF)


def merge_kernel(keep_ref, got_ref, *outs):
    for out, shift in zip(outs, (0,) + SHIFTS):
        out[0] = keep_ref[shift % CHIPS]
        out[1] = got_ref[shift % CHIPS]


def spatial_bwd_kernel(q_ref, k_ref, v_ref, prob_ref, mid_ref, gq_ref, gk_ref, gv_ref):
    for h in range(HEADS):
        q, k, v = q_ref[0, :, head(h)], k_ref[0, :, head(h)], v_ref[0, :, head(h)]
        up = rows_of(mid_ref, h)
        prob = prob_ref[h]
        grad_prob = mm_nt(up, v)
        gv_ref[0, :, head(h)] = mm_tn(prob.astype(BF), up).astype(BF)
        row_dot = jnp.sum(prob * grad_prob, axis=-1, keepdims=True)
        low = (prob * (grad_prob - row_dot) * SCALE).astype(BF)
        gq_ref[0, :, head(h)] = mm(low, k).astype(BF)
        gk_ref[0, :, head(h)] = mm_tn(low, q).astype(BF)


def temporal_a_kernel(frames_ref, in_ref, bias_ref, prob_ref, mid_ref):
    row = lax.broadcasted_iota(jnp.int32, (ROWS, ROWS), 0)
    col = lax.broadcasted_iota(jnp.int32, (ROWS, ROWS), 1)
    clip = slot_rows(frames_ref, in_ref, 3 * HEADS).astype(F32)
    other = clip.T
    same = (row & (TOK - 1)) == (col & (TOK - 1))
    same &= jnp.concatenate([clip] * 2, axis=1) == jnp.concatenate([other] * 2, axis=0)
    mask = jnp.where(same, 0.0, NEG)
    for h in range(HEADS):
        q, k, up = (slot_rows(frames_ref, in_ref, i * HEADS + h) for i in range(3))
        bias = jnp.broadcast_to(bias_ref[h][:, None, :], (SEQ, TOK, ROWS)).reshape(ROWS, ROWS)
        prob = softmax((mm_nt(q, k) * SCALE + bias) + mask)
        prob_ref[h] = prob
        put_slots(frames_ref, mid_ref, h, mm_tn(prob.astype(BF), up))


def temporal_b_kernel(frames_ref, in_ref, prob_ref, *refs):
    so_refs, (out_ref, bias_ref) = dict(zip((0,) + SHIFTS, refs)), refs[-2:]
    so_at = [(so_refs[d if d <= CHIPS // 2 else d - CHIPS], x) for d, x in SLOTS]
    for h in range(HEADS):
        q, k, up = (slot_rows(frames_ref, in_ref, i * HEADS + h) for i in range(3))
        so = jnp.concatenate([ref[x, h] for ref, x in so_at], axis=0)
        prob = prob_ref[h]
        grad_prob = mm_nt(up, so)
        put_slots(frames_ref, out_ref, h, mm(prob.astype(BF), so))
        score = prob * (grad_prob - jnp.sum(prob * grad_prob, axis=-1, keepdims=True))
        bias_ref[h] = jnp.sum(score.reshape(SEQ, TOK, ROWS), axis=1)
        low = (score * SCALE).astype(BF)
        put_slots(frames_ref, out_ref, HEADS + h, mm(low, k))
        put_slots(frames_ref, out_ref, 2 * HEADS + h, mm_tn(low, q))


def add_tile_kernel(tile_ref, in_ref, out_ref, sem):
    copies = [
        pltpu.make_async_copy(tile_ref, out_ref.at[u, 3 * HEADS], sem.at[u]) for u in range(SEQ)
    ]
    for copy in copies:
        copy.start()
    for copy in copies:
        copy.wait()


def unpack_kernel(in_ref, *outs):
    for tile in range(3 * HEADS):
        outs[tile // HEADS][0, :, head(tile % HEADS)] = rows_of(in_ref, tile)
    outs[3][...] = jnp.sum(in_ref[:, 3 * HEADS].astype(F32), axis=0)


def call(kernel, name, specs, inputs, outputs, scratch=(), estimate=1000, params=PARAMS, **more):
    return pl.pallas_call(
        kernel,
        out_shape=tuple(outputs),
        in_specs=specs,
        out_specs=(VMEM,) * len(outputs),
        scratch_shapes=scratch,
        compiler_params=params,
        cost_estimate=pl.CostEstimate(flops=estimate, bytes_accessed=1000, transcendentals=0),
        name=name,
        **more,
    )(*inputs)


def exchange(packed):
    return lax.all_to_all(packed, "seq", split_axis=0, concat_axis=0, tiled=True)


def pair(terms, axis, mask):
    size = lax.axis_size(axis)
    return lax.ppermute(terms, axis, [(i, i ^ mask) for i in range(size)])


def sum_of_four(terms, axis, step):
    one, two, three = (pair(terms, axis, step * mask) for mask in (1, 2, 3))
    return (terms + one) + (two + three)


def move(message, s, x):
    perm = [(2 * z + c, 2 * ((z + s) % CHIPS) + (c ^ x)) for z in range(CHIPS) for c in range(2)]
    return lax.ppermute(message, "seq", perm)


def bfloat_parts(terms):
    parts = []
    for _ in range(3):
        part = lax.reduce_precision(terms, 8, 7)
        parts.append(jnp.pad(part, ((0, TOK - HEADS), (0, 1))))
        terms = terms - part
    return jnp.pad(jnp.concatenate(parts, axis=1), ((0, 0), (0, DIM - 96))).astype(BF)


def offsets_table(frames):
    offset = frames[:, None] - frames[None, :] + (SEQ - 1)
    slots = jnp.arange(2 * SEQ - 1, dtype=jnp.int32)
    return (offset[:, :, None] == slots[None, None, :]).astype(F32)


def per_device(
    q_spatial, k_spatial, v_spatial, q_temporal, k_temporal, rel_bias, clip_ids, cotangent
):
    index = lax.axis_index("seq").astype(jnp.int32)
    z, c = index >> 1, index & 1
    pos = jnp.stack([z, c])
    away = jnp.array([d for d, x in SLOTS], jnp.int32)
    swapped = jnp.array([x for d, x in SLOTS], jnp.int32)
    frames = 2 * ((z - away) & (CHIPS - 1)) + (c ^ swapped)

    tiles = 3 * HEADS + 1
    (packed,) = call(
        pack_kernel,
        "pack",
        [SMEM] + [HBM] * 3,
        [clip_ids, q_temporal, k_temporal, cotangent],
        [units(SEQ, tiles)],
        [pltpu.VMEM((3, ROWS, WIDTH), BF), pltpu.SemaphoreType.DMA((3, PARTS))],
        params=pltpu.CompilerParams(vmem_limit_bytes=56 * 1024 * 1024),
    )
    there = exchange(packed)

    spatial = [q_spatial, k_spatial, v_spatial]
    spatial, rel_bias, frames, _ = lax.optimization_barrier((spatial, rel_bias, frames, packed))
    wide = jnp.repeat(offsets_table(frames), TOK, axis=1)
    bias = jnp.einsum("hr,icr->hic", rel_bias, wide, precision=lax.Precision.HIGHEST)
    keep_so, give_so, sp_prob = call(
        spatial_fwd_kernel,
        "spatial_fwd",
        [SMEM] + [VMEM] * 3,
        [pos, *spatial],
        [units(CHIPS, HEADS)] * 2 + [probs()],
    )
    got_so = move(give_so, 0, 1)
    stay, *messages = call(
        merge_kernel, "merge", [VMEM] * 2, [keep_so, got_so], [units(2, HEADS)] * CHIPS
    )
    so = [stay, *(move(m, s, 0) for m, s in zip(messages, SHIFTS))]

    there, _, bias = lax.optimization_barrier((there, messages, bias))
    prob, mid = call(
        temporal_a_kernel,
        "temporal_a",
        [SMEM] + [VMEM] * 2,
        [frames, there, bias],
        [probs(), units(SEQ, HEADS)],
    )
    grad_mid = exchange(mid)

    back, score_rows = call(
        temporal_b_kernel,
        "temporal_b",
        [SMEM] + [VMEM] * (2 + CHIPS),
        [frames, there, prob, *so],
        [units(SEQ, tiles), jax.ShapeDtypeStruct((HEADS, SEQ, ROWS), F32)],
        estimate=LONG,
    )
    terms = jnp.einsum("hic,icr->hr", score_rows, wide, precision=lax.Precision.HIGHEST)
    terms = sum_of_four(sum_of_four(terms, "grp", 1), "grp", 4)
    (back,) = call(
        add_tile_kernel,
        "add_tile",
        [VMEM] * 2,
        [bfloat_parts(terms), back],
        [units(SEQ, tiles)],
        [pltpu.SemaphoreType.DMA((SEQ,))],
        input_output_aliases={1: 0},
    )
    grad_mid, back = lax.optimization_barrier((grad_mid, back))
    returned = exchange(back)

    grad_qs, grad_ks, grad_vs = call(
        spatial_bwd_kernel, "spatial_bwd", [VMEM] * 5, [*spatial, sp_prob, grad_mid], [frame()] * 3
    )
    result, grad_qt, grad_kt, total = call(
        unpack_kernel,
        "unpack",
        [VMEM],
        [returned],
        [frame()] * 3 + [jax.ShapeDtypeStruct((TOK, DIM), F32)],
    )
    total = total[:HEADS]
    total_bias = total[:, :31] + total[:, 32:63] + total[:, 64:95]
    return result, grad_qs, grad_ks, grad_vs, grad_qt, grad_kt, total_bias


def solution(mesh):
    frames = P(("grp", "seq"), None, None)
    return jax.shard_map(
        per_device,
        mesh=mesh,
        in_specs=(frames,) * 5 + (P(), P("grp", "seq"), frames),
        out_specs=(frames,) * 6 + (P(),),
        check_vma=False,
    )
```

time: 356 us -> 187 us (0.53)
  blocking collectives: 107 us -> 0 us
  matrix products: 44.9 us -> 3.71 us
  local copies, waits for them, and re-layouts: 38.4 us -> 9.5 us
  Pallas kernels: 0 us -> 28.3 us
  waiting for transfers between devices: 119 us -> 94.9 us
  starting transfers between devices: 39.9 us -> 47.5 us
    psum x1 -> x0, blocking collectives: 77.7 us -> none  [per_device(): total_bias = lax.psum(bias_terms, ('grp', 'seq'))]
    all_to_all x8 -> x3, waiting for transfers between devices: 119 us -> 46.1 us  [exchange(): lax.all_to_all(packed, 'seq', split_axis=0, concat_axis=0, tiled=True)]
    ppermute x0 -> x14, waiting for transfers between devices: none -> 48.7 us  [the longest x8 41.8 us: move(): return lax.ppermute(message, 'seq', perm)]
    dot_general x12 -> x2, matrix products: 37.6 us -> 3.71 us  [the longest x1 2.5 us: per_device(): jnp.einsum('hr,icr->hic', rel_bias, wide, precision=lax.Precision.HIGHEST)]
    eq x1 -> x0, blocking collectives: 28.8 us -> none  [per_device(): same_clip = clip_row[:, None] == clip_row[None, :]]
    pallas_call x0 -> x8, Pallas kernels: none -> 28.3 us  [call(): pl.pallas_call(kernel, out_shape=tuple(outputs), in_specs=specs, out_spec...]
    ppermute x0 -> x14, starting transfers between devices: none -> 19 us  [the longest x8 12.1 us: move(): return lax.ppermute(message, 'seq', perm)]
    all_to_all x8 -> x3, starting transfers between devices: 39.9 us -> 28.5 us  [exchange(): lax.all_to_all(packed, 'seq', split_axis=0, concat_axis=0, tiled=True)]
  transfers between devices with their start and end apart: 8 -> 17, of which waited for: 6 -> 7; matrix products, arithmetic and copies ran while one was open for 18% -> 3% of each run, Pallas kernels for 0% -> 12%
where the time goes in v2:
time: 187 us; the launch traced here: 186 us
  waiting for transfers between devices  94.9 us (51%)
  starting transfers between devices  47.5 us (25%)
  Pallas kernels  28.3 us (15%)
  local copies, waits for them, and re-layouts  9.5 us (5%)
  matrix products  3.71 us (2%)
    all_to_all x3, waiting for transfers between devices, exchange(): lax.all_to_all(packed, 'seq', split_axis=0, concat_axis=0, tiled=True)  46.1 us
    ppermute x8, waiting for transfers between devices, move(): return lax.ppermute(message, 'seq', perm)  41.8 us
    all_to_all x3, starting transfers between devices, exchange(): lax.all_to_all(packed, 'seq', split_axis=0, concat_axis=0, tiled=True)  28.5 us
    pallas_call x8, Pallas kernels, call(): pl.pallas_call(kernel, out_shape=tuple(outputs), in_specs=specs, out_spec...  28.3 us
    ppermute x8, starting transfers between devices, move(): return lax.ppermute(message, 'seq', perm)  12.1 us
    unnamed x24, local copies, waits for them, and re-layouts  8.27 us
    ppermute x6, waiting for transfers between devices, pair(): return lax.ppermute(terms, axis, [(i, i ^ mask) for i in range(size)])  6.95 us
    ppermute x6, starting transfers between devices, pair(): return lax.ppermute(terms, axis, [(i, i ^ mask) for i in range(size)])  6.84 us
  transfers between devices with their start and end apart: 17, of which 7 were waited for; matrix products, arithmetic and copies ran while one was open for 3% of the time, Pallas kernels for 12%

profile of v2, /device:TPU:1, one launch (start us, length us, event | category | flops | bytes accessed | tf_op | source)
XLA Modules:
  0.0 186.4 jit_solution(9087504017881675012)
XLA Ops:
  1.3 3.3 %pack.1 = bf16[16,37,16,128]{3,2,1,0:T(8,128)(2,1)} custom-call(s32[1,1]{1,0:T(1,128)S(6)} %copy.29.clip_ref, bf16[1,256,1536]{2,1,0:T(8,128)(2,1)} %q_ref.1, bf16[1,256,1536]{2,1,0:T(8,128)(2,1)} %k_ref.1, bf16[1,256,1536]{2,1,0:T(8,128)(2,1)} %up_ref.1), custom_call_target="tpu_custom_call" | custom-call | flops 1000 | bytes 1000 | tf_op jit(solution)/shard_map/pack/pallas_call | solution.py:183
  4.6 10.1 %all-to-all-start = ((bf16[16,37,16,128]{3,2,1,0:T(8,128)(2,1)}), bf16[16,37,16,128]{3,2,1,0:T(8,128)(2,1)S(1)}, u32[]{:S(2)}, u32[]{:S(2)}) async-start(bf16[16,37,16,128]{3,2,1,0:T(8,128)(2,1)} %pack.1), calls=%async_computation | async-start | bytes 4849664 | tf_op jit(solution)/shard_map/all_to_all | solution.py:197
  14.9 1.1 copy-done.3
  16.0 1.1 copy-done.5
  17.1 4.1 %spatial_fwd.1 = (bf16[8,12,16,128]{3,2,1,0:T(8,128)(2,1)S(1)}, bf16[8,12,16,128]{3,2,1,0:T(8,128)(2,1)S(1)}, f32[12,256,256]{2,1,0:T(8,128)}) custom-call(s32[2]{0:T(128)S(1)} %pad_add_fusion.pos_ref, bf16[1,256,1536]{2,1,0:T(8,128)(2,1)S(1)} %copy-done.2, bf16[1,256,1536]{2,1,0:T(8,128)(2,1)S(1)} %copy-done.3, bf16[1,256,1536]{2,1,0:T(8,128)(2,1)S(1)} %copy-done.5), custom_call_target="tpu_custom_call" | custom-call | flops 1000 | bytes 1000 | tf_op jit(solution)/shard_map/spatial_fwd/pallas_call | solution.py:183
  21.4 1.5 collective-permute-done.got_ref
  23.8 1.4 collective-permute-start.1
  25.2 1.3 collective-permute-start.2
  26.6 3.0 %collective-permute-start.3 = (bf16[2,12,16,128]{3,2,1,0:T(8,128)(2,1)}, bf16[2,12,16,128]{3,2,1,0:T(8,128)(2,1)}, u32[]{:S(2)}, u32[]{:S(2)}) collective-permute-start(bf16[2,12,16,128]{3,2,1,0:T(8,128)(2,1)} %get-tuple-element.46), channel_id=1, source_target_pairs={{0,6},{1,7},{2,8},{3,9},{4,10},{5,11},{6,12},{7,13},{8,14},{9,15},... | collective-permute-start | bytes 294920 | tf_op jit(solution)/shard_map/ppermute | solution.py:212
  29.6 1.6 collective-permute-start.4
  31.1 1.1 collective-permute-start.5
  32.2 40.2 %collective-permute-done.1.refs_1_ = bf16[2,12,16,128]{3,2,1,0:T(8,128)(2,1)S(1)} collective-permute-done((bf16[2,12,16,128]{3,2,1,0:T(8,128)(2,1)S(1)}, bf16[2,12,16,128]{3,2,1,0:T(8,128)(2,1)S(1)}, u32[]{:S(2)}, u32[]{:S(2)}) %collective-permute-start.1) | collective-permute-done | bytes 98336 | tf_op jit(solution)/shard_map/ppermute | solution.py:212
  72.4 2.1 %collective-permute-start.6 = (bf16[2,12,16,128]{3,2,1,0:T(8,128)(2,1)}, bf16[2,12,16,128]{3,2,1,0:T(8,128)(2,1)}, u32[]{:S(2)}, u32[]{:S(2)}) collective-permute-start(bf16[2,12,16,128]{3,2,1,0:T(8,128)(2,1)} %get-tuple-element.49), channel_id=1, source_target_pairs={{0,12},{1,13},{2,14},{3,15},{4,0},{5,1},{6,2},{7,3},{8,4},{9,5},{1... | collective-permute-start | bytes 294920 | tf_op jit(solution)/shard_map/ppermute | solution.py:212
  74.5 1.7 collective-permute-start.7
  76.3 1.4 copy-done.8
  77.7 2.5 %fusion.4 = f32[12,16,256]{2,0,1:T(8,128)} fusion(f32[16,256,31]{2,1,0:T(8,128)S(1)} %bitcast.10, f32[12,31]{1,0:T(8,128)S(1)} %copy-done), kind=kOutput, calls=%fused_computation.14 | convolution fusion | flops 18284544 | bytes 706000 | tf_op jit(solution)/shard_map/hr,icr->hic/dot_general | solution.py:255
  80.2 1.1 copy.21.bias_ref
  81.3 4.8 %temporal_a.1 = (f32[12,256,256]{2,1,0:T(8,128)}, bf16[16,12,16,128]{3,2,1,0:T(8,128)(2,1)S(1)}) custom-call(s32[16]{0:T(128)S(1)} %fusion.13.frames_ref, bf16[16,37,16,128]{3,2,1,0:T(8,128)(2,1)S(1)} %all-to-all-done.in_ref, f32[12,16,256]{2,1,0:T(8,128)S(1)} %copy.21.bias_ref), custom_call_target="tpu_custom_call" | custom-call | flops 1000 | bytes 1000 | tf_op jit(solution)/shard_map/temporal_a/pallas_call | solution.py:183
  87.0 8.7 %all-to-all-start.1 = ((bf16[16,12,16,128]{3,2,1,0:T(8,128)(2,1)}), bf16[16,12,16,128]{3,2,1,0:T(8,128)(2,1)}, u32[]{:S(2)}, u32[]{:S(2)}) async-start(bf16[16,12,16,128]{3,2,1,0:T(8,128)(2,1)} %copy-done.7), calls=%async_computation.1 | async-start | bytes 1572864 | tf_op jit(solution)/shard_map/all_to_all | solution.py:197
  95.7 6.0 %temporal_b.1 = (bf16[16,37,16,128]{3,2,1,0:T(8,128)(2,1)S(1)}, f32[12,16,256]{2,1,0:T(8,128)S(1)}) custom-call(s32[16]{0:T(128)S(1)} %fusion.13.frames_ref, bf16[16,37,16,128]{3,2,1,0:T(8,128)(2,1)S(1)} %all-to-all-done.in_ref, f32[12,256,256]{2,1,0:T(8,128)} %get-tuple-element.55.prob_ref, bf16[2,12,16,128]{3,2,1,0:T(8,128)(2,1)S(1)} %get-tuple-element.56.refs_0_, ...), custom_call_target="tpu_custom_call" | custom-call | flops 999999995904 | bytes 1000 | tf_op jit(solution)/shard_map/temporal_b/pallas_call | solution.py:183
  101.8 1.2 convolution_bitcast_fusion
  103.0 2.8 %collective-permute-start.10 = (f32[12,31]{1,0:T(8,128)S(1)}, f32[12,31]{1,0:T(8,128)S(1)}, u32[]{:S(2)}, u32[]{:S(2)}) collective-permute-start(f32[12,31]{1,0:T(8,128)S(1)} %convolution_bitcast_fusion), channel_id=1, source_target_pairs={{0,48},{16,32},{32,16},{48,0},{64,112},{80,96},{96,80},{112,64},{1... | collective-permute-start | bytes 4472 | tf_op jit(solution)/shard_map/ppermute | solution.py:202
  107.3 3.0 %collective-permute-done.9 = f32[12,31]{1,0:T(8,128)S(1)} collective-permute-done((f32[12,31]{1,0:T(8,128)S(1)}, f32[12,31]{1,0:T(8,128)S(1)}, u32[]{:S(2)}, u32[]{:S(2)}) %collective-permute-start.9) | collective-permute-done | bytes 1520 | tf_op jit(solution)/shard_map/ppermute | solution.py:202
  110.3 2.6 %collective-permute-start.13 = (f32[12,31]{1,0:T(8,128)S(1)}, f32[12,31]{1,0:T(8,128)S(1)}, u32[]{:S(2)}, u32[]{:S(2)}) collective-permute-start(f32[12,31]{1,0:T(8,128)S(1)} %add_add_fusion.1), channel_id=1, source_target_pairs={{0,192},{16,208},{32,224},{48,240},{64,128},{80,144},{96,160},{112... | collective-permute-start | bytes 4472 | tf_op jit(solution)/shard_map/ppermute | solution.py:202
  114.1 2.8 %collective-permute-done.12 = f32[12,31]{1,0:T(8,128)S(1)} collective-permute-done((f32[12,31]{1,0:T(8,128)S(1)}, f32[12,31]{1,0:T(8,128)S(1)}, u32[]{:S(2)}, u32[]{:S(2)}) %collective-permute-start.12) | collective-permute-done | bytes 1520 | tf_op jit(solution)/shard_map/ppermute | solution.py:202
  117.2 1.4 copy-done.1
  118.6 9.7 %all-to-all-start.2 = ((bf16[16,37,16,128]{3,2,1,0:T(8,128)(2,1)}), bf16[16,37,16,128]{3,2,1,0:T(8,128)(2,1)S(1)}, u32[]{:S(2)}, u32[]{:S(2)}) async-start(bf16[16,37,16,128]{3,2,1,0:T(8,128)(2,1)} %copy-done.1), calls=%async_computation.2 | async-start | bytes 4849664 | tf_op jit(solution)/shard_map/all_to_all | solution.py:197
  128.3 1.1 copy-done.4
  129.5 1.1 copy-done.6
  130.6 7.2 %spatial_bwd.1 = (bf16[1,256,1536]{2,1,0:T(8,128)(2,1)}, bf16[1,256,1536]{2,1,0:T(8,128)(2,1)}, bf16[1,256,1536]{2,1,0:T(8,128)(2,1)}) custom-call(bf16[1,256,1536]{2,1,0:T(8,128)(2,1)S(1)} %copy-done.2, bf16[1,256,1536]{2,1,0:T(8,128)(2,1)S(1)} %copy-done.4, bf16[1,256,1536]{2,1,0:T(8,128)(2,1)S(1)} %copy-done.6, ...), custom_call_target="tpu_custom_call" | custom-call | flops 1000 | bytes 1000 | tf_op jit(solution)/shard_map/spatial_bwd/pallas_call | solution.py:183
  137.8 46.1 %all-to-all-done.2.in_ref = bf16[16,37,16,128]{3,2,1,0:T(8,128)(2,1)S(1)} async-done(((bf16[16,37,16,128]{3,2,1,0:T(8,128)(2,1)}), bf16[16,37,16,128]{3,2,1,0:T(8,128)(2,1)S(1)}, u32[]{:S(2)}, u32[]{:S(2)}) %all-to-all-start.2) | async-done | bytes 2424864 | tf_op jit(solution)/shard_map/all_to_all | solution.py:197
  183.9 1.8 unpack.1
  (48 shorter events, 6.0 us)
Async XLA Ops:
  0.6 77.1 %copy-start = (f32[12,31]{1,0:T(8,128)S(1)}, f32[12,31]{1,0:T(8,128)}, u32[]{:S(2)}) copy-start(f32[12,31]{1,0:T(8,128)} %param.15) | copy-start | bytes 4468
  4.6 10.2 %copy-start.10 = (s32[16]{0:T(128)S(1)}, s32[16]{0:T(128)}, u32[]{:S(2)}) copy-start(s32[16]{0:T(128)} %constant.37) | copy-start | bytes 196
  4.6 10.2 %copy-start.11 = (s32[16]{0:T(128)S(1)}, s32[16]{0:T(128)}, u32[]{:S(2)}) copy-start(s32[16]{0:T(128)} %constant.21.clone) | copy-start | bytes 196
  4.6 10.3 %copy-start.2 = (bf16[1,256,1536]{2,1,0:T(8,128)(2,1)S(1)}, bf16[1,256,1536]{2,1,0:T(8,128)(2,1)}, u32[]{:S(2)}) copy-start(bf16[1,256,1536]{2,1,0:T(8,128)(2,1)} %q_ref.3) | copy-start | bytes 2359300
  4.6 75.6 %all-to-all-start = ((bf16[16,37,16,128]{3,2,1,0:T(8,128)(2,1)}), bf16[16,37,16,128]{3,2,1,0:T(8,128)(2,1)S(1)}, u32[]{:S(2)}, u32[]{:S(2)}) async-start(bf16[16,37,16,128]{3,2,1,0:T(8,128)(2,1)} %pack.1), calls=%async_computation | async-start | bytes 4849664 | tf_op jit(solution)/shard_map/all_to_all | solution.py:197
  14.9 1.1 copy-start.3
  16.0 1.1 copy-start.5
  21.3 1.7 collective-permute-start
  23.8 48.6 %collective-permute-start.1 = (bf16[2,12,16,128]{3,2,1,0:T(8,128)(2,1)S(1)}, bf16[2,12,16,128]{3,2,1,0:T(8,128)(2,1)S(1)}, u32[]{:S(2)}, u32[]{:S(2)}) collective-permute-start(bf16[2,12,16,128]{3,2,1,0:T(8,128)(2,1)S(1)} %get-tuple-element.44), channel_id=1, source_target_pairs={{0,2},{1,3},{2,4},{3,5},{4,6},{5,7},{6,8},{7,9},{8,10},{9,11},{10,... | collective-permute-start | bytes 294920 | tf_op jit(solution)/shard_map/ppermute | solution.py:212
  25.2 49.3 %collective-permute-start.2 = (bf16[2,12,16,128]{3,2,1,0:T(8,128)(2,1)S(1)}, bf16[2,12,16,128]{3,2,1,0:T(8,128)(2,1)S(1)}, u32[]{:S(2)}, u32[]{:S(2)}) collective-permute-start(bf16[2,12,16,128]{3,2,1,0:T(8,128)(2,1)S(1)} %get-tuple-element.45), channel_id=1, source_target_pairs={{0,14},{1,15},{2,0},{3,1},{4,2},{5,3},{6,4},{7,5},{8,6},{9,7},{10,... | collective-permute-start | bytes 294920 | tf_op jit(solution)/shard_map/ppermute | solution.py:212
  26.6 69.1 %collective-permute-start.3 = (bf16[2,12,16,128]{3,2,1,0:T(8,128)(2,1)}, bf16[2,12,16,128]{3,2,1,0:T(8,128)(2,1)}, u32[]{:S(2)}, u32[]{:S(2)}) collective-permute-start(bf16[2,12,16,128]{3,2,1,0:T(8,128)(2,1)} %get-tuple-element.46), channel_id=1, source_target_pairs={{0,6},{1,7},{2,8},{3,9},{4,10},{5,11},{6,12},{7,13},{8,14},{9,15},... | collective-permute-start | bytes 294920 | tf_op jit(solution)/shard_map/ppermute | solution.py:212
  29.6 66.1 %collective-permute-start.4 = (bf16[2,12,16,128]{3,2,1,0:T(8,128)(2,1)}, bf16[2,12,16,128]{3,2,1,0:T(8,128)(2,1)}, u32[]{:S(2)}, u32[]{:S(2)}) collective-permute-start(bf16[2,12,16,128]{3,2,1,0:T(8,128)(2,1)} %get-tuple-element.47), channel_id=1, source_target_pairs={{0,10},{1,11},{2,12},{3,13},{4,14},{5,15},{6,0},{7,1},{8,2},{9,3},... | collective-permute-start | bytes 294920 | tf_op jit(solution)/shard_map/ppermute | solution.py:212
  31.1 64.6 %collective-permute-start.5 = (bf16[2,12,16,128]{3,2,1,0:T(8,128)(2,1)}, bf16[2,12,16,128]{3,2,1,0:T(8,128)(2,1)}, u32[]{:S(2)}, u32[]{:S(2)}) collective-permute-start(bf16[2,12,16,128]{3,2,1,0:T(8,128)(2,1)} %get-tuple-element.48), channel_id=1, source_target_pairs={{0,4},{1,5},{2,6},{3,7},{4,8},{5,9},{6,10},{7,11},{8,12},{9,13},{1... | collective-permute-start | bytes 294920 | tf_op jit(solution)/shard_map/ppermute | solution.py:212
  72.4 23.3 %collective-permute-start.6 = (bf16[2,12,16,128]{3,2,1,0:T(8,128)(2,1)}, bf16[2,12,16,128]{3,2,1,0:T(8,128)(2,1)}, u32[]{:S(2)}, u32[]{:S(2)}) collective-permute-start(bf16[2,12,16,128]{3,2,1,0:T(8,128)(2,1)} %get-tuple-element.49), channel_id=1, source_target_pairs={{0,12},{1,13},{2,14},{3,15},{4,0},{5,1},{6,2},{7,3},{8,4},{9,5},{1... | collective-permute-start | bytes 294920 | tf_op jit(solution)/shard_map/ppermute | solution.py:212
  74.5 21.2 %collective-permute-start.7 = (bf16[2,12,16,128]{3,2,1,0:T(8,128)(2,1)}, bf16[2,12,16,128]{3,2,1,0:T(8,128)(2,1)}, u32[]{:S(2)}, u32[]{:S(2)}) collective-permute-start(bf16[2,12,16,128]{3,2,1,0:T(8,128)(2,1)} %get-tuple-element.50), channel_id=1, source_target_pairs={{0,8},{1,9},{2,10},{3,11},{4,12},{5,13},{6,14},{7,15},{8,0},{9,1},... | collective-permute-start | bytes 294920 | tf_op jit(solution)/shard_map/ppermute | solution.py:212
  76.3 1.4 copy-start.8
  86.1 0.9 copy-start.7
  87.0 31.6 %all-to-all-start.1 = ((bf16[16,12,16,128]{3,2,1,0:T(8,128)(2,1)}), bf16[16,12,16,128]{3,2,1,0:T(8,128)(2,1)}, u32[]{:S(2)}, u32[]{:S(2)}) async-start(bf16[16,12,16,128]{3,2,1,0:T(8,128)(2,1)} %copy-done.7), calls=%async_computation.1 | async-start | bytes 1572864 | tf_op jit(solution)/shard_map/all_to_all | solution.py:197
  95.7 6.1 %copy-start.9 = (f32[16,16,16,31]{3,2,1,0:T(8,128)S(1)}, f32[16,16,16,31]{3,2,1,0:T(8,128)}, u32[]{:S(2)}) copy-start(f32[16,16,16,31]{3,2,1,0:T(8,128)} %copy-done.8) | copy-start | bytes 1523716
  103.0 4.3 %collective-permute-start.10 = (f32[12,31]{1,0:T(8,128)S(1)}, f32[12,31]{1,0:T(8,128)S(1)}, u32[]{:S(2)}, u32[]{:S(2)}) collective-permute-start(f32[12,31]{1,0:T(8,128)S(1)} %convolution_bitcast_fusion), channel_id=1, source_target_pairs={{0,48},{16,32},{32,16},{48,0},{64,112},{80,96},{96,80},{112,64},{1... | collective-permute-start | bytes 4472 | tf_op jit(solution)/shard_map/ppermute | solution.py:202
  105.8 4.4 %collective-permute-start.9 = (f32[12,31]{1,0:T(8,128)S(1)}, f32[12,31]{1,0:T(8,128)S(1)}, u32[]{:S(2)}, u32[]{:S(2)}) collective-permute-start(f32[12,31]{1,0:T(8,128)S(1)} %convolution_bitcast_fusion), channel_id=1, source_target_pairs={{0,32},{16,48},{32,0},{48,16},{64,96},{80,112},{96,64},{112,80},{1... | collective-permute-start | bytes 4472 | tf_op jit(solution)/shard_map/ppermute | solution.py:202
  106.2 4.1 %collective-permute-start.8 = (f32[12,31]{1,0:T(8,128)S(1)}, f32[12,31]{1,0:T(8,128)S(1)}, u32[]{:S(2)}, u32[]{:S(2)}) collective-permute-start(f32[12,31]{1,0:T(8,128)S(1)} %convolution_bitcast_fusion), channel_id=1, source_target_pairs={{0,16},{16,0},{32,48},{48,32},{64,80},{80,64},{96,112},{112,96},{1... | collective-permute-start | bytes 4472 | tf_op jit(solution)/shard_map/ppermute | solution.py:202
  110.3 3.8 %collective-permute-start.13 = (f32[12,31]{1,0:T(8,128)S(1)}, f32[12,31]{1,0:T(8,128)S(1)}, u32[]{:S(2)}, u32[]{:S(2)}) collective-permute-start(f32[12,31]{1,0:T(8,128)S(1)} %add_add_fusion.1), channel_id=1, source_target_pairs={{0,192},{16,208},{32,224},{48,240},{64,128},{80,144},{96,160},{112... | collective-permute-start | bytes 4472 | tf_op jit(solution)/shard_map/ppermute | solution.py:202
  112.8 4.0 %collective-permute-start.12 = (f32[12,31]{1,0:T(8,128)S(1)}, f32[12,31]{1,0:T(8,128)S(1)}, u32[]{:S(2)}, u32[]{:S(2)}) collective-permute-start(f32[12,31]{1,0:T(8,128)S(1)} %add_add_fusion.1), channel_id=1, source_target_pairs={{0,128},{16,144},{32,160},{48,176},{64,192},{80,208},{96,224},{112... | collective-permute-start | bytes 4472 | tf_op jit(solution)/shard_map/ppermute | solution.py:202
  113.3 3.5 %collective-permute-start.11 = (f32[12,31]{1,0:T(8,128)S(1)}, f32[12,31]{1,0:T(8,128)S(1)}, u32[]{:S(2)}, u32[]{:S(2)}) collective-permute-start(f32[12,31]{1,0:T(8,128)S(1)} %add_add_fusion.1), channel_id=1, source_target_pairs={{0,64},{16,80},{32,96},{48,112},{64,0},{80,16},{96,32},{112,48},{1... | collective-permute-start | bytes 4472 | tf_op jit(solution)/shard_map/ppermute | solution.py:202
  117.2 1.4 copy-start.1
  118.6 65.2 %all-to-all-start.2 = ((bf16[16,37,16,128]{3,2,1,0:T(8,128)(2,1)}), bf16[16,37,16,128]{3,2,1,0:T(8,128)(2,1)S(1)}, u32[]{:S(2)}, u32[]{:S(2)}) async-start(bf16[16,37,16,128]{3,2,1,0:T(8,128)(2,1)} %copy-done.1), calls=%async_computation.2 | async-start | bytes 4849664 | tf_op jit(solution)/shard_map/all_to_all | solution.py:197
  128.3 1.1 copy-start.4
  129.4 1.1 copy-start.6

commit v3 on v2

--- a/solution.py
+++ b/solution.py
@@ -53,6 +53,10 @@
     return jax.ShapeDtypeStruct((HEADS, ROWS, ROWS), F32)
 
 
+def range_row(chip, core):
+    return pl.multiple_of((2 * (chip & (CHIPS - 1)) + core) * TOK, TOK)
+
+
 def head(h):
     return slice(h * DIM, (h + 1) * DIM)
 
@@ -67,6 +71,13 @@
 
 def slot_rows(frames_ref, ref, tile):
     return jnp.concatenate([ref[frames_ref[s], tile] for s in range(SEQ)], axis=0)
+
+
+def put_pairs(keep_ref, give_ref, tile, value):
+    low = value.astype(BF)
+    for d in range(CHIPS):
+        keep_ref[d, tile] = low[d * TOK:(d + 1) * TOK]
+        give_ref[d, tile] = low[(CHIPS + d) * TOK:(CHIPS + d + 1) * TOK]
 
 
 def put_slots(frames_ref, ref, tile, value):
@@ -118,6 +129,18 @@
         out[1] = got_ref[shift % CHIPS]
 
 
+def merge_last_kernel(tile_ref, keep_ref, got_ref, *outs):
+    for out, shift in zip(outs, (0,) + SHIFTS):
+        out[:HEADS] = keep_ref[-shift % CHIPS]
+        out[HEADS:2 * HEADS] = got_ref[-shift % CHIPS]
+        out[2 * HEADS] = tile_ref[...]
+
+
+def pair_rows(pos_ref, shift):
+    z, c = pos_ref[0], pos_ref[1]
+    return range_row(z - shift, c), range_row(z - shift, 1 - c)
+
+
 def spatial_bwd_kernel(q_ref, k_ref, v_ref, prob_ref, mid_ref, gq_ref, gk_ref, gv_ref):
     for h in range(HEADS):
         q, k, v = q_ref[0, :, head(h)], k_ref[0, :, head(h)], v_ref[0, :, head(h)]
@@ -148,7 +171,7 @@
 
 
 def temporal_b_kernel(frames_ref, in_ref, prob_ref, *refs):
-    so_refs, (out_ref, bias_ref) = dict(zip((0,) + SHIFTS, refs)), refs[-2:]
+    so_refs, (out_ref, keep_ref, give_ref, bias_ref) = dict(zip((0,) + SHIFTS, refs)), refs[-4:]
     so_at = [(so_refs[d if d <= CHIPS // 2 else d - CHIPS], x) for d, x in SLOTS]
     for h in range(HEADS):
         q, k, up = (slot_rows(frames_ref, in_ref, i * HEADS + h) for i in range(3))
@@ -160,23 +183,28 @@
         bias_ref[h] = jnp.sum(score.reshape(SEQ, TOK, ROWS), axis=1)
         low = (score * SCALE).astype(BF)
         put_slots(frames_ref, out_ref, HEADS + h, mm(low, k))
-        put_slots(frames_ref, out_ref, 2 * HEADS + h, mm_tn(low, q))
-
-
-def add_tile_kernel(tile_ref, in_ref, out_ref, sem):
-    copies = [
-        pltpu.make_async_copy(tile_ref, out_ref.at[u, 3 * HEADS], sem.at[u]) for u in range(SEQ)
-    ]
-    for copy in copies:
-        copy.start()
-    for copy in copies:
-        copy.wait()
+        put_pairs(keep_ref, give_ref, h, mm_tn(low, q))
 
 
 def unpack_kernel(in_ref, *outs):
-    for tile in range(3 * HEADS):
+    for tile in range(2 * HEADS):
         outs[tile // HEADS][0, :, head(tile % HEADS)] = rows_of(in_ref, tile)
-    outs[3][...] = jnp.sum(in_ref[:, 3 * HEADS].astype(F32), axis=0)
+
+
+def finish_kernel(pos_ref, *refs):
+    messages, (gk_ref, bias_ref) = refs[:CHIPS], refs[CHIPS:]
+    for ref, shift in zip(messages, (0,) + SHIFTS):
+        for x, row in enumerate(pair_rows(pos_ref, shift)):
+            for h in range(HEADS):
+                gk_ref[0, pl.ds(row, TOK), head(h)] = ref[x * HEADS + h]
+    z = pos_ref[0]
+    total = jnp.zeros((TOK, DIM), F32)
+    for chip in range(CHIPS):
+        for ref, shift in zip(messages, (0,) + SHIFTS):
+            mine = ((z - shift) & (CHIPS - 1)) == chip
+            total += jnp.where(mine, ref[2 * HEADS].astype(F32), 0.0)
+    total = total + pltpu.roll(total, DIM - 32, 1) + pltpu.roll(total, DIM - 64, 1)
+    bias_ref[...] = total[:HEADS, :2 * SEQ - 1]
 
 
 def call(kernel, name, specs, inputs, outputs, scratch=(), estimate=1000, params=PARAMS, **more):
@@ -212,6 +240,10 @@
     return lax.ppermute(message, "seq", perm)
 
 
+def sent(messages):
+    return [messages[0], *(move(m, s, 0) for m, s in zip(messages[1:], SHIFTS))]
+
+
 def bfloat_parts(terms):
     parts = []
     for _ in range(3):
@@ -260,13 +292,14 @@
         [pos, *spatial],
         [units(CHIPS, HEADS)] * 2 + [probs()],
     )
+    give_so, bias = lax.optimization_barrier((give_so, bias))
     got_so = move(give_so, 0, 1)
-    stay, *messages = call(
+    so_messages = call(
         merge_kernel, "merge", [VMEM] * 2, [keep_so, got_so], [units(2, HEADS)] * CHIPS
     )
-    so = [stay, *(move(m, s, 0) for m, s in zip(messages, SHIFTS))]
-
-    there, _, bias = lax.optimization_barrier((there, messages, bias))
+    so = sent(so_messages)
+
+    there, _, bias = lax.optimization_barrier((there, so_messages, bias))
     prob, mid = call(
         temporal_a_kernel,
         "temporal_a",
@@ -276,40 +309,49 @@
     )
     grad_mid = exchange(mid)
 
-    back, score_rows = call(
+    back, keep_back, give_back, score_rows = call(
         temporal_b_kernel,
         "temporal_b",
         [SMEM] + [VMEM] * (2 + CHIPS),
         [frames, there, prob, *so],
-        [units(SEQ, tiles), jax.ShapeDtypeStruct((HEADS, SEQ, ROWS), F32)],
+        [units(SEQ, 2 * HEADS)]
+        + [units(CHIPS, HEADS)] * 2
+        + [jax.ShapeDtypeStruct((HEADS, SEQ, ROWS), F32)],
         estimate=LONG,
     )
+    back, _ = lax.optimization_barrier((back, grad_mid))
+    returned = exchange(back)
+
+    grad_qs, grad_ks, grad_vs = call(
+        spatial_bwd_kernel,
+        "spatial_bwd",
+        [VMEM] * 5,
+        [*spatial, sp_prob, grad_mid],
+        [frame()] * 3,
+        estimate=LONG,
+    )
+    score_rows, give_back, _ = lax.optimization_barrier((score_rows, give_back, grad_vs))
     terms = jnp.einsum("hic,icr->hr", score_rows, wide, precision=lax.Precision.HIGHEST)
+    terms = terms + move(terms, 0, 1)
     terms = sum_of_four(sum_of_four(terms, "grp", 1), "grp", 4)
-    (back,) = call(
-        add_tile_kernel,
-        "add_tile",
-        [VMEM] * 2,
-        [bfloat_parts(terms), back],
-        [units(SEQ, tiles)],
-        [pltpu.SemaphoreType.DMA((SEQ,))],
-        input_output_aliases={1: 0},
-    )
-    grad_mid, back = lax.optimization_barrier((grad_mid, back))
-    returned = exchange(back)
-
-    grad_qs, grad_ks, grad_vs = call(
-        spatial_bwd_kernel, "spatial_bwd", [VMEM] * 5, [*spatial, sp_prob, grad_mid], [frame()] * 3
-    )
-    result, grad_qt, grad_kt, total = call(
-        unpack_kernel,
-        "unpack",
-        [VMEM],
-        [returned],
-        [frame()] * 3 + [jax.ShapeDtypeStruct((TOK, DIM), F32)],
-    )
-    total = total[:HEADS]
-    total_bias = total[:, :31] + total[:, 32:63] + total[:, 64:95]
+    got_back = move(give_back, 0, 1)
+    tile = bfloat_parts(terms)
+    last = call(
+        merge_last_kernel,
+        "merge_last",
+        [VMEM] * 3,
+        [tile, keep_back, got_back],
+        [jax.ShapeDtypeStruct((2 * HEADS + 1, TOK, DIM), BF)] * CHIPS,
+    )
+    last = sent(last)
+    result, grad_qt = call(unpack_kernel, "unpack", [VMEM], [returned], [frame()] * 2)
+    grad_kt, total_bias = call(
+        finish_kernel,
+        "finish",
+        [SMEM] + [VMEM] * CHIPS,
+        [pos, *last],
+        [frame(), jax.ShapeDtypeStruct((HEADS, 2 * SEQ - 1), F32)],
+    )
     return result, grad_qs, grad_ks, grad_vs, grad_qt, grad_kt, total_bias
 
 

time: 187 us -> 178 us (0.952)
  waiting for transfers between devices: 94.9 us -> 75.7 us
  starting transfers between devices: 47.5 us -> 56.8 us
  Pallas kernels: 28.3 us -> 30.7 us
    all_to_all x3, waiting for transfers between devices: 46.1 us -> 12.3 us  [exchange(): lax.all_to_all(packed, 'seq', split_axis=0, concat_axis=0, tiled=True)]
    ppermute x8 -> x17, waiting for transfers between devices: 41.8 us -> 58.2 us  [move(): return lax.ppermute(message, 'seq', perm)]
    ppermute x8 -> x17, starting transfers between devices: 12.1 us -> 26.1 us  [move(): return lax.ppermute(message, 'seq', perm)]
    all_to_all x3, starting transfers between devices: 28.5 us -> 23.1 us  [exchange(): lax.all_to_all(packed, 'seq', split_axis=0, concat_axis=0, tiled=True)]
    pallas_call x8 -> x9, Pallas kernels: 28.3 us -> 30.7 us  [call(): pl.pallas_call(kernel, out_shape=tuple(outputs), in_specs=specs, out_spec...]
    unnamed x24 -> x44, local copies, waits for them, and re-layouts: 8.27 us -> 7.66 us
  transfers between devices with their start and end apart: 17 -> 26, of which waited for: 7 -> 12; matrix products, arithmetic and copies ran while one was open for 3% -> 3% of each run, Pallas kernels for 12% -> 14%
where the time goes in v3:
time: 178 us
  waiting for transfers between devices  75.7 us (43%)
  starting transfers between devices  56.8 us (32%)
  Pallas kernels  30.7 us (17%)
  local copies, waits for them, and re-layouts  8.9 us (5%)
  matrix products  3.71 us (2%)
    ppermute x17, waiting for transfers between devices, move(): return lax.ppermute(message, 'seq', perm)  58.2 us
    pallas_call x9, Pallas kernels, call(): pl.pallas_call(kernel, out_shape=tuple(outputs), in_specs=specs, out_spec...  30.7 us
    ppermute x17, starting transfers between devices, move(): return lax.ppermute(message, 'seq', perm)  26.1 us
    all_to_all x3, starting transfers between devices, exchange(): lax.all_to_all(packed, 'seq', split_axis=0, concat_axis=0, tiled=True)  23.1 us
    all_to_all x3, waiting for transfers between devices, exchange(): lax.all_to_all(packed, 'seq', split_axis=0, concat_axis=0, tiled=True)  12.3 us
    unnamed x44, local copies, waits for them, and re-layouts  7.66 us
    ppermute x6, starting transfers between devices, pair(): return lax.ppermute(terms, axis, [(i, i ^ mask) for i in range(size)])  7.64 us
    ppermute x6, waiting for transfers between devices, pair(): return lax.ppermute(terms, axis, [(i, i ^ mask) for i in range(size)])  5.21 us
  transfers between devices with their start and end apart: 26, of which 12 were waited for; matrix products, arithmetic and copies ran while one was open for 3% of the time, Pallas kernels for 14%

profile of v3, /device:TPU:1, one launch (start us, length us, event | category | flops | bytes accessed | tf_op | source)
XLA Modules:
  0.0 177.8 jit_solution(14321243106366499867)
XLA Ops:
  1.3 3.3 %pack.1 = bf16[16,37,16,128]{3,2,1,0:T(8,128)(2,1)} custom-call(s32[1,1]{1,0:T(1,128)S(6)} %copy.27.clip_ref, bf16[1,256,1536]{2,1,0:T(8,128)(2,1)} %q_ref.1, bf16[1,256,1536]{2,1,0:T(8,128)(2,1)} %k_ref.1, bf16[1,256,1536]{2,1,0:T(8,128)(2,1)} %up_ref.1), custom_call_target="tpu_custom_call" | custom-call | flops 1000 | bytes 1000 | tf_op jit(solution)/shard_map/pack/pallas_call | solution.py:211
  4.6 10.1 %all-to-all-start = ((bf16[16,37,16,128]{3,2,1,0:T(8,128)(2,1)}), bf16[16,37,16,128]{3,2,1,0:T(8,128)(2,1)S(1)}, u32[]{:S(2)}, u32[]{:S(2)}) async-start(bf16[16,37,16,128]{3,2,1,0:T(8,128)(2,1)} %pack.1), calls=%async_computation | async-start | bytes 4849664 | tf_op jit(solution)/shard_map/all_to_all | solution.py:225
  17.1 4.1 %spatial_fwd.1 = (bf16[8,12,16,128]{3,2,1,0:T(8,128)(2,1)S(1)}, bf16[8,12,16,128]{3,2,1,0:T(8,128)(2,1)S(1)}, f32[12,256,256]{2,1,0:T(8,128)}) custom-call(s32[2]{0:T(128)S(1)} %pad_add_fusion.pos_ref, bf16[1,256,1536]{2,1,0:T(8,128)(2,1)S(1)} %copy-done.2, bf16[1,256,1536]{2,1,0:T(8,128)(2,1)S(1)} %copy-done.3, bf16[1,256,1536]{2,1,0:T(8,128)(2,1)S(1)} %copy-done.5), custom_call_target="tpu_custom_call" | custom-call | flops 1000 | bytes 1000 | tf_op jit(solution)/shard_map/spatial_fwd/pallas_call | solution.py:211
  21.6 2.5 %fusion.4 = f32[12,16,256]{2,0,1:T(8,128)} fusion(f32[16,256,31]{2,1,0:T(8,128)S(1)} %bitcast.10, f32[12,31]{1,0:T(8,128)S(1)} %copy-done), kind=kOutput, calls=%fused_computation.14 | convolution fusion | flops 18284544 | bytes 706000 | tf_op jit(solution)/shard_map/hr,icr->hic/dot_general | solution.py:287
  24.3 1.6 collective-permute-done.got_ref
  29.4 2.9 %collective-permute-start.3 = (bf16[2,12,16,128]{3,2,1,0:T(8,128)(2,1)}, bf16[2,12,16,128]{3,2,1,0:T(8,128)(2,1)}, u32[]{:S(2)}, u32[]{:S(2)}) collective-permute-start(bf16[2,12,16,128]{3,2,1,0:T(8,128)(2,1)} %get-tuple-element.62), channel_id=1, source_target_pairs={{0,6},{1,7},{2,8},{3,9},{4,10},{5,11},{6,12},{7,13},{8,14},{9,15},... | collective-permute-start | bytes 294920 | tf_op jit(solution)/shard_map/ppermute | solution.py:240
  32.3 1.6 collective-permute-start.4
  34.9 37.5 %collective-permute-done.1.refs_1_ = bf16[2,12,16,128]{3,2,1,0:T(8,128)(2,1)S(1)} collective-permute-done((bf16[2,12,16,128]{3,2,1,0:T(8,128)(2,1)S(1)}, bf16[2,12,16,128]{3,2,1,0:T(8,128)(2,1)S(1)}, u32[]{:S(2)}, u32[]{:S(2)}) %collective-permute-start.1) | collective-permute-done | bytes 98336 | tf_op jit(solution)/shard_map/ppermute | solution.py:240
  72.4 2.1 %collective-permute-start.6 = (bf16[2,12,16,128]{3,2,1,0:T(8,128)(2,1)}, bf16[2,12,16,128]{3,2,1,0:T(8,128)(2,1)}, u32[]{:S(2)}, u32[]{:S(2)}) collective-permute-start(bf16[2,12,16,128]{3,2,1,0:T(8,128)(2,1)} %get-tuple-element.65), channel_id=1, source_target_pairs={{0,12},{1,13},{2,14},{3,15},{4,0},{5,1},{6,2},{7,3},{8,4},{9,5},{1... | collective-permute-start | bytes 294920 | tf_op jit(solution)/shard_map/ppermute | solution.py:240
  74.5 1.9 %collective-permute-start.7 = (bf16[2,12,16,128]{3,2,1,0:T(8,128)(2,1)}, bf16[2,12,16,128]{3,2,1,0:T(8,128)(2,1)}, u32[]{:S(2)}, u32[]{:S(2)}) collective-permute-start(bf16[2,12,16,128]{3,2,1,0:T(8,128)(2,1)} %get-tuple-element.66), channel_id=1, source_target_pairs={{0,8},{1,9},{2,10},{3,11},{4,12},{5,13},{6,14},{7,15},{8,0},{9,1},... | collective-permute-start | bytes 294920 | tf_op jit(solution)/shard_map/ppermute | solution.py:240
  77.5 4.8 %temporal_a.1 = (f32[12,256,256]{2,1,0:T(8,128)}, bf16[16,12,16,128]{3,2,1,0:T(8,128)(2,1)S(1)}) custom-call(s32[16]{0:T(128)S(1)} %fusion.13.frames_ref, bf16[16,37,16,128]{3,2,1,0:T(8,128)(2,1)S(1)} %all-to-all-done.in_ref, f32[12,16,256]{2,1,0:T(8,128)S(1)} %copy.20.bias_ref), custom_call_target="tpu_custom_call" | custom-call | flops 1000 | bytes 1000 | tf_op jit(solution)/shard_map/temporal_a/pallas_call | solution.py:211
  83.2 8.6 %all-to-all-start.1 = ((bf16[16,12,16,128]{3,2,1,0:T(8,128)(2,1)}), bf16[16,12,16,128]{3,2,1,0:T(8,128)(2,1)}, u32[]{:S(2)}, u32[]{:S(2)}) async-start(bf16[16,12,16,128]{3,2,1,0:T(8,128)(2,1)} %copy-done.7), calls=%async_computation.1 | async-start | bytes 1572864 | tf_op jit(solution)/shard_map/all_to_all | solution.py:225
  93.7 5.9 %temporal_b.1 = (bf16[16,24,16,128]{3,2,1,0:T(8,128)(2,1)S(1)}, bf16[8,12,16,128]{3,2,1,0:T(8,128)(2,1)S(1)}, bf16[8,12,16,128]{3,2,1,0:T(8,128)(2,1)S(1)}, f32[12,16,256]{2,1,0:T(8,128)S(1)}) custom-call(s32[16]{0:T(128)S(1)} %fusion.13.frames_ref, bf16[16,37,16,128]{3,2,1,0:T(8,128)(2,1)S(1)} %all-to-all-done.in_ref, ...), custom_call_target="tpu_custom_call" | custom-call | flops 999999995904 | bytes 1000 | tf_op jit(solution)/shard_map/temporal_b/pallas_call | solution.py:211
  102.3 12.3 %all-to-all-done.1.mid_ref = bf16[16,12,16,128]{3,2,1,0:T(8,128)(2,1)} async-done(((bf16[16,12,16,128]{3,2,1,0:T(8,128)(2,1)}), bf16[16,12,16,128]{3,2,1,0:T(8,128)(2,1)}, u32[]{:S(2)}, u32[]{:S(2)}) %all-to-all-start.1) | async-done | bytes 786464 | tf_op jit(solution)/shard_map/all_to_all | solution.py:225
  114.6 4.3 %all-to-all-start.2 = ((bf16[16,24,16,128]{3,2,1,0:T(8,128)(2,1)}), bf16[16,24,16,128]{3,2,1,0:T(8,128)(2,1)}, u32[]{:S(2)}, u32[]{:S(2)}) async-start(bf16[16,24,16,128]{3,2,1,0:T(8,128)(2,1)} %copy-done.1), calls=%async_computation.2 | async-start | bytes 3145728 | tf_op jit(solution)/shard_map/all_to_all | solution.py:225
  119.0 7.3 %spatial_bwd.1 = (bf16[1,256,1536]{2,1,0:T(8,128)(2,1)}, bf16[1,256,1536]{2,1,0:T(8,128)(2,1)}, bf16[1,256,1536]{2,1,0:T(8,128)(2,1)}) custom-call(bf16[1,256,1536]{2,1,0:T(8,128)(2,1)S(1)} %copy-done.2, bf16[1,256,1536]{2,1,0:T(8,128)(2,1)S(1)} %copy-done.4, bf16[1,256,1536]{2,1,0:T(8,128)(2,1)S(1)} %copy-done.6, ...), custom_call_target="tpu_custom_call" | custom-call | flops 999999995904 | bytes 1000 | tf_op jit(solution)/shard_map/spatial_bwd/pallas_call | solution.py:211
  128.8 2.9 %collective-permute-start.10 = (f32[12,31]{1,0:T(8,128)S(1)}, f32[12,31]{1,0:T(8,128)S(1)}, u32[]{:S(2)}, u32[]{:S(2)}) collective-permute-start(f32[12,31]{1,0:T(8,128)S(1)} %add.45), channel_id=1, source_target_pairs={{0,32},{16,48},{32,0},{48,16},{64,96},{80,112},{96,64},{112,80},{1... | collective-permute-start | bytes 4472 | tf_op jit(solution)/shard_map/ppermute | solution.py:230
  133.2 2.6 %collective-permute-done.11 = f32[12,31]{1,0:T(8,128)S(1)} collective-permute-done((f32[12,31]{1,0:T(8,128)S(1)}, f32[12,31]{1,0:T(8,128)S(1)}, u32[]{:S(2)}, u32[]{:S(2)}) %collective-permute-start.11) | collective-permute-done | bytes 1520 | tf_op jit(solution)/shard_map/ppermute | solution.py:230
  137.1 2.5 %collective-permute-start.13 = (f32[12,31]{1,0:T(8,128)S(1)}, f32[12,31]{1,0:T(8,128)S(1)}, u32[]{:S(2)}, u32[]{:S(2)}) collective-permute-start(f32[12,31]{1,0:T(8,128)S(1)} %add_add_fusion.1), channel_id=1, source_target_pairs={{0,128},{16,144},{32,160},{48,176},{64,192},{80,208},{96,224},{112... | collective-permute-start | bytes 4472 | tf_op jit(solution)/shard_map/ppermute | solution.py:230
  139.8 2.0 %collective-permute-start.15 = (bf16[8,12,16,128]{3,2,1,0:T(8,128)(2,1)S(1)}, bf16[8,12,16,128]{3,2,1,0:T(8,128)(2,1)S(1)}, u32[]{:S(2)}, u32[]{:S(2)}) collective-permute-start(bf16[8,12,16,128]{3,2,1,0:T(8,128)(2,1)S(1)} %copy-done.13), channel_id=1, source_target_pairs={{0,1},{1,0},{2,3},{3,2},{4,5},{5,4},{6,7},{7,6},{8,9},{9,8},{10,11... | collective-permute-start | bytes 1179656 | tf_op jit(solution)/shard_map/ppermute | solution.py:240
  141.8 1.9 %collective-permute-done.14 = f32[12,31]{1,0:T(8,128)S(1)} collective-permute-done((f32[12,31]{1,0:T(8,128)S(1)}, f32[12,31]{1,0:T(8,128)S(1)}, u32[]{:S(2)}, u32[]{:S(2)}) %collective-permute-start.14) | collective-permute-done | bytes 1520 | tf_op jit(solution)/shard_map/ppermute | solution.py:230
  144.1 2.6 %collective-permute-start.17 = (bf16[25,16,128]{2,1,0:T(8,128)(2,1)S(1)}, bf16[25,16,128]{2,1,0:T(8,128)(2,1)S(1)}, u32[]{:S(2)}, u32[]{:S(2)}) collective-permute-start(bf16[25,16,128]{2,1,0:T(8,128)(2,1)S(1)} %get-tuple-element.87), channel_id=1, source_target_pairs={{0,14},{1,15},{2,0},{3,1},{4,2},{5,3},{6,4},{7,5},{8,6},{9,7},{10,... | collective-permute-start | bytes 307208 | tf_op jit(solution)/shard_map/ppermute | solution.py:240
  146.6 1.8 %collective-permute-start.18 = (bf16[25,16,128]{2,1,0:T(8,128)(2,1)S(1)}, bf16[25,16,128]{2,1,0:T(8,128)(2,1)S(1)}, u32[]{:S(2)}, u32[]{:S(2)}) collective-permute-start(bf16[25,16,128]{2,1,0:T(8,128)(2,1)S(1)} %get-tuple-element.88), channel_id=1, source_target_pairs={{0,6},{1,7},{2,8},{3,9},{4,10},{5,11},{6,12},{7,13},{8,14},{9,15},... | collective-permute-start | bytes 307208 | tf_op jit(solution)/shard_map/ppermute | solution.py:240
  148.5 2.6 %collective-permute-start.19 = (bf16[25,16,128]{2,1,0:T(8,128)(2,1)S(1)}, bf16[25,16,128]{2,1,0:T(8,128)(2,1)S(1)}, u32[]{:S(2)}, u32[]{:S(2)}) collective-permute-start(bf16[25,16,128]{2,1,0:T(8,128)(2,1)S(1)} %get-tuple-element.89), channel_id=1, source_target_pairs={{0,10},{1,11},{2,12},{3,13},{4,14},{5,15},{6,0},{7,1},{8,2},{9,3},... | collective-permute-start | bytes 307208 | tf_op jit(solution)/shard_map/ppermute | solution.py:240
  151.1 6.2 %collective-permute-done.16.refs_1_ = bf16[25,16,128]{2,1,0:T(8,128)(2,1)S(1)} collective-permute-done((bf16[25,16,128]{2,1,0:T(8,128)(2,1)S(1)}, bf16[25,16,128]{2,1,0:T(8,128)(2,1)S(1)}, u32[]{:S(2)}, u32[]{:S(2)}) %collective-permute-start.16) | collective-permute-done | bytes 102432 | tf_op jit(solution)/shard_map/ppermute | solution.py:240
  157.3 2.1 %collective-permute-start.21 = (bf16[25,16,128]{2,1,0:T(8,128)(2,1)S(1)}, bf16[25,16,128]{2,1,0:T(8,128)(2,1)S(1)}, u32[]{:S(2)}, u32[]{:S(2)}) collective-permute-start(bf16[25,16,128]{2,1,0:T(8,128)(2,1)S(1)} %get-tuple-element.91), channel_id=1, source_target_pairs={{0,12},{1,13},{2,14},{3,15},{4,0},{5,1},{6,2},{7,3},{8,4},{9,5},{1... | collective-permute-start | bytes 307208 | tf_op jit(solution)/shard_map/ppermute | solution.py:240
  159.4 2.3 %collective-permute-start.22 = (bf16[25,16,128]{2,1,0:T(8,128)(2,1)S(1)}, bf16[25,16,128]{2,1,0:T(8,128)(2,1)S(1)}, u32[]{:S(2)}, u32[]{:S(2)}) collective-permute-start(bf16[25,16,128]{2,1,0:T(8,128)(2,1)S(1)} %get-tuple-element.92), channel_id=1, source_target_pairs={{0,8},{1,9},{2,10},{3,11},{4,12},{5,13},{6,14},{7,15},{8,0},{9,1},... | collective-permute-start | bytes 307208 | tf_op jit(solution)/shard_map/ppermute | solution.py:240
  161.7 1.7 collective-permute-done.18.refs_3_
  163.4 4.6 %collective-permute-done.20.refs_5_ = bf16[25,16,128]{2,1,0:T(8,128)(2,1)S(1)} collective-permute-done((bf16[25,16,128]{2,1,0:T(8,128)(2,1)S(1)}, bf16[25,16,128]{2,1,0:T(8,128)(2,1)S(1)}, u32[]{:S(2)}, u32[]{:S(2)}) %collective-permute-start.20) | collective-permute-done | bytes 102432 | tf_op jit(solution)/shard_map/ppermute | solution.py:240
  168.7 4.6 %collective-permute-done.22.refs_7_ = bf16[25,16,128]{2,1,0:T(8,128)(2,1)S(1)} collective-permute-done((bf16[25,16,128]{2,1,0:T(8,128)(2,1)S(1)}, bf16[25,16,128]{2,1,0:T(8,128)(2,1)S(1)}, u32[]{:S(2)}, u32[]{:S(2)}) %collective-permute-start.22) | collective-permute-done | bytes 102432 | tf_op jit(solution)/shard_map/ppermute | solution.py:240
  173.4 1.6 finish.1
  175.0 2.8 %unpack.1 = (bf16[1,256,1536]{2,1,0:T(8,128)(2,1)}, bf16[1,256,1536]{2,1,0:T(8,128)(2,1)}) custom-call(bf16[16,24,16,128]{3,2,1,0:T(8,128)(2,1)} %all-to-all-done.2.in_ref), custom_call_target="tpu_custom_call" | custom-call | flops 1000 | bytes 1000 | tf_op jit(solution)/shard_map/unpack/pallas_call | solution.py:211
  (87 shorter events, 20.5 us)
Async XLA Ops:
  0.6 21.0 %copy-start = (f32[12,31]{1,0:T(8,128)S(1)}, f32[12,31]{1,0:T(8,128)}, u32[]{:S(2)}) copy-start(f32[12,31]{1,0:T(8,128)} %param.15) | copy-start | bytes 4468
  4.6 71.8 %all-to-all-start = ((bf16[16,37,16,128]{3,2,1,0:T(8,128)(2,1)}), bf16[16,37,16,128]{3,2,1,0:T(8,128)(2,1)S(1)}, u32[]{:S(2)}, u32[]{:S(2)}) async-start(bf16[16,37,16,128]{3,2,1,0:T(8,128)(2,1)} %pack.1), calls=%async_computation | async-start | bytes 4849664 | tf_op jit(solution)/shard_map/all_to_all | solution.py:225
  21.6 52.9 %copy-start.18 = (f32[16,16,16,31]{3,2,1,0:T(8,128)}, f32[16,16,16,31]{3,2,1,0:T(8,128)S(1)}, u32[]{:S(2)}) copy-start(f32[16,16,16,31]{3,2,1,0:T(8,128)S(1)} %broadcast_in_dim.2) | copy-start | bytes 1523716
  24.2 1.7 collective-permute-start
  26.7 45.8 %collective-permute-start.1 = (bf16[2,12,16,128]{3,2,1,0:T(8,128)(2,1)S(1)}, bf16[2,12,16,128]{3,2,1,0:T(8,128)(2,1)S(1)}, u32[]{:S(2)}, u32[]{:S(2)}) collective-permute-start(bf16[2,12,16,128]{3,2,1,0:T(8,128)(2,1)S(1)} %get-tuple-element.60), channel_id=1, source_target_pairs={{0,2},{1,3},{2,4},{3,5},{4,6},{5,7},{6,8},{7,9},{8,10},{9,11},{10,... | collective-permute-start | bytes 294920 | tf_op jit(solution)/shard_map/ppermute | solution.py:240
  28.1 46.5 %collective-permute-start.2 = (bf16[2,12,16,128]{3,2,1,0:T(8,128)(2,1)S(1)}, bf16[2,12,16,128]{3,2,1,0:T(8,128)(2,1)S(1)}, u32[]{:S(2)}, u32[]{:S(2)}) collective-permute-start(bf16[2,12,16,128]{3,2,1,0:T(8,128)(2,1)S(1)} %get-tuple-element.61), channel_id=1, source_target_pairs={{0,14},{1,15},{2,0},{3,1},{4,2},{5,3},{6,4},{7,5},{8,6},{9,7},{10,... | collective-permute-start | bytes 294920 | tf_op jit(solution)/shard_map/ppermute | solution.py:240
  29.4 62.5 %collective-permute-start.3 = (bf16[2,12,16,128]{3,2,1,0:T(8,128)(2,1)}, bf16[2,12,16,128]{3,2,1,0:T(8,128)(2,1)}, u32[]{:S(2)}, u32[]{:S(2)}) collective-permute-start(bf16[2,12,16,128]{3,2,1,0:T(8,128)(2,1)} %get-tuple-element.62), channel_id=1, source_target_pairs={{0,6},{1,7},{2,8},{3,9},{4,10},{5,11},{6,12},{7,13},{8,14},{9,15},... | collective-permute-start | bytes 294920 | tf_op jit(solution)/shard_map/ppermute | solution.py:240
  32.3 59.6 %collective-permute-start.4 = (bf16[2,12,16,128]{3,2,1,0:T(8,128)(2,1)}, bf16[2,12,16,128]{3,2,1,0:T(8,128)(2,1)}, u32[]{:S(2)}, u32[]{:S(2)}) collective-permute-start(bf16[2,12,16,128]{3,2,1,0:T(8,128)(2,1)} %get-tuple-element.63), channel_id=1, source_target_pairs={{0,10},{1,11},{2,12},{3,13},{4,14},{5,15},{6,0},{7,1},{8,2},{9,3},... | collective-permute-start | bytes 294920 | tf_op jit(solution)/shard_map/ppermute | solution.py:240
  33.8 58.1 %collective-permute-start.5 = (bf16[2,12,16,128]{3,2,1,0:T(8,128)(2,1)}, bf16[2,12,16,128]{3,2,1,0:T(8,128)(2,1)}, u32[]{:S(2)}, u32[]{:S(2)}) collective-permute-start(bf16[2,12,16,128]{3,2,1,0:T(8,128)(2,1)} %get-tuple-element.64), channel_id=1, source_target_pairs={{0,4},{1,5},{2,6},{3,7},{4,8},{5,9},{6,10},{7,11},{8,12},{9,13},{1... | collective-permute-start | bytes 294920 | tf_op jit(solution)/shard_map/ppermute | solution.py:240
  72.4 19.5 %collective-permute-start.6 = (bf16[2,12,16,128]{3,2,1,0:T(8,128)(2,1)}, bf16[2,12,16,128]{3,2,1,0:T(8,128)(2,1)}, u32[]{:S(2)}, u32[]{:S(2)}) collective-permute-start(bf16[2,12,16,128]{3,2,1,0:T(8,128)(2,1)} %get-tuple-element.65), channel_id=1, source_target_pairs={{0,12},{1,13},{2,14},{3,15},{4,0},{5,1},{6,2},{7,3},{8,4},{9,5},{1... | collective-permute-start | bytes 294920 | tf_op jit(solution)/shard_map/ppermute | solution.py:240
  74.5 17.4 %collective-permute-start.7 = (bf16[2,12,16,128]{3,2,1,0:T(8,128)(2,1)}, bf16[2,12,16,128]{3,2,1,0:T(8,128)(2,1)}, u32[]{:S(2)}, u32[]{:S(2)}) collective-permute-start(bf16[2,12,16,128]{3,2,1,0:T(8,128)(2,1)} %get-tuple-element.66), channel_id=1, source_target_pairs={{0,8},{1,9},{2,10},{3,11},{4,12},{5,13},{6,14},{7,15},{8,0},{9,1},... | collective-permute-start | bytes 294920 | tf_op jit(solution)/shard_map/ppermute | solution.py:240
  83.2 31.4 %all-to-all-start.1 = ((bf16[16,12,16,128]{3,2,1,0:T(8,128)(2,1)}), bf16[16,12,16,128]{3,2,1,0:T(8,128)(2,1)}, u32[]{:S(2)}, u32[]{:S(2)}) async-start(bf16[16,12,16,128]{3,2,1,0:T(8,128)(2,1)} %copy-done.7), calls=%async_computation.1 | async-start | bytes 1572864 | tf_op jit(solution)/shard_map/all_to_all | solution.py:225
  102.3 16.6 %copy-start.4 = (bf16[1,256,1536]{2,1,0:T(8,128)(2,1)S(1)}, bf16[1,256,1536]{2,1,0:T(8,128)(2,1)}, u32[]{:S(2)}) copy-start(bf16[1,256,1536]{2,1,0:T(8,128)(2,1)} %k_ref.3) | copy-start | bytes 2359300
  102.3 16.7 %copy-start.6 = (bf16[1,256,1536]{2,1,0:T(8,128)(2,1)S(1)}, bf16[1,256,1536]{2,1,0:T(8,128)(2,1)}, u32[]{:S(2)}) copy-start(bf16[1,256,1536]{2,1,0:T(8,128)(2,1)} %v_ref.1) | copy-start | bytes 2359300
  114.6 60.3 %all-to-all-start.2 = ((bf16[16,24,16,128]{3,2,1,0:T(8,128)(2,1)}), bf16[16,24,16,128]{3,2,1,0:T(8,128)(2,1)}, u32[]{:S(2)}, u32[]{:S(2)}) async-start(bf16[16,24,16,128]{3,2,1,0:T(8,128)(2,1)} %copy-done.1), calls=%async_computation.2 | async-start | bytes 3145728 | tf_op jit(solution)/shard_map/all_to_all | solution.py:225
  126.3 17.5 %copy-start.9 = (bf16[8,12,16,128]{3,2,1,0:T(8,128)(2,1)S(1)}, bf16[8,12,16,128]{3,2,1,0:T(8,128)(2,1)}, u32[]{:S(2)}) copy-start(bf16[8,12,16,128]{3,2,1,0:T(8,128)(2,1)} %copy-done.8) | copy-start | bytes 1179652
  126.3 47.1 %copy-start.11 = (s32[2]{0:T(128)S(1)}, s32[2]{0:T(128)}, u32[]{:S(2)}) copy-start(s32[2]{0:T(128)} %copy-done.10) | copy-start | bytes 28
  127.5 1.3 collective-permute-start.8
  128.8 4.4 %collective-permute-start.10 = (f32[12,31]{1,0:T(8,128)S(1)}, f32[12,31]{1,0:T(8,128)S(1)}, u32[]{:S(2)}, u32[]{:S(2)}) collective-permute-start(f32[12,31]{1,0:T(8,128)S(1)} %add.45), channel_id=1, source_target_pairs={{0,32},{16,48},{32,0},{48,16},{64,96},{80,112},{96,64},{112,80},{1... | collective-permute-start | bytes 4472 | tf_op jit(solution)/shard_map/ppermute | solution.py:230
  131.7 4.1 %collective-permute-start.11 = (f32[12,31]{1,0:T(8,128)S(1)}, f32[12,31]{1,0:T(8,128)S(1)}, u32[]{:S(2)}, u32[]{:S(2)}) collective-permute-start(f32[12,31]{1,0:T(8,128)S(1)} %add.45), channel_id=1, source_target_pairs={{0,48},{16,32},{32,16},{48,0},{64,112},{80,96},{96,80},{112,64},{1... | collective-permute-start | bytes 4472 | tf_op jit(solution)/shard_map/ppermute | solution.py:230
  132.5 3.3 %collective-permute-start.9 = (f32[12,31]{1,0:T(8,128)S(1)}, f32[12,31]{1,0:T(8,128)S(1)}, u32[]{:S(2)}, u32[]{:S(2)}) collective-permute-start(f32[12,31]{1,0:T(8,128)S(1)} %add.45), channel_id=1, source_target_pairs={{0,16},{16,0},{32,48},{48,32},{64,80},{80,64},{96,112},{112,96},{1... | collective-permute-start | bytes 4472 | tf_op jit(solution)/shard_map/ppermute | solution.py:230
  135.8 6.0 %collective-permute-start.12 = (f32[12,31]{1,0:T(8,128)S(1)}, f32[12,31]{1,0:T(8,128)S(1)}, u32[]{:S(2)}, u32[]{:S(2)}) collective-permute-start(f32[12,31]{1,0:T(8,128)S(1)} %add_add_fusion.1), channel_id=1, source_target_pairs={{0,64},{16,80},{32,96},{48,112},{64,0},{80,16},{96,32},{112,48},{1... | collective-permute-start | bytes 4472 | tf_op jit(solution)/shard_map/ppermute | solution.py:230
  137.1 4.7 %collective-permute-start.13 = (f32[12,31]{1,0:T(8,128)S(1)}, f32[12,31]{1,0:T(8,128)S(1)}, u32[]{:S(2)}, u32[]{:S(2)}) collective-permute-start(f32[12,31]{1,0:T(8,128)S(1)} %add_add_fusion.1), channel_id=1, source_target_pairs={{0,128},{16,144},{32,160},{48,176},{64,192},{80,208},{96,224},{112... | collective-permute-start | bytes 4472 | tf_op jit(solution)/shard_map/ppermute | solution.py:230
  139.6 4.1 %collective-permute-start.14 = (f32[12,31]{1,0:T(8,128)S(1)}, f32[12,31]{1,0:T(8,128)S(1)}, u32[]{:S(2)}, u32[]{:S(2)}) collective-permute-start(f32[12,31]{1,0:T(8,128)S(1)} %add_add_fusion.1), channel_id=1, source_target_pairs={{0,192},{16,208},{32,224},{48,240},{64,128},{80,144},{96,160},{112... | collective-permute-start | bytes 4472 | tf_op jit(solution)/shard_map/ppermute | solution.py:230
  139.8 4.0 %collective-permute-start.15 = (bf16[8,12,16,128]{3,2,1,0:T(8,128)(2,1)S(1)}, bf16[8,12,16,128]{3,2,1,0:T(8,128)(2,1)S(1)}, u32[]{:S(2)}, u32[]{:S(2)}) collective-permute-start(bf16[8,12,16,128]{3,2,1,0:T(8,128)(2,1)S(1)} %copy-done.13), channel_id=1, source_target_pairs={{0,1},{1,0},{2,3},{3,2},{4,5},{5,4},{6,7},{7,6},{8,9},{9,8},{10,11... | collective-permute-start | bytes 1179656 | tf_op jit(solution)/shard_map/ppermute | solution.py:240
  143.9 13.4 %collective-permute-start.16 = (bf16[25,16,128]{2,1,0:T(8,128)(2,1)S(1)}, bf16[25,16,128]{2,1,0:T(8,128)(2,1)S(1)}, u32[]{:S(2)}, u32[]{:S(2)}) collective-permute-start(bf16[25,16,128]{2,1,0:T(8,128)(2,1)S(1)} %get-tuple-element.86), channel_id=1, source_target_pairs={{0,2},{1,3},{2,4},{3,5},{4,6},{5,7},{6,8},{7,9},{8,10},{9,11},{10,... | collective-permute-start | bytes 307208 | tf_op jit(solution)/shard_map/ppermute | solution.py:240
  144.1 15.3 %collective-permute-start.17 = (bf16[25,16,128]{2,1,0:T(8,128)(2,1)S(1)}, bf16[25,16,128]{2,1,0:T(8,128)(2,1)S(1)}, u32[]{:S(2)}, u32[]{:S(2)}) collective-permute-start(bf16[25,16,128]{2,1,0:T(8,128)(2,1)S(1)} %get-tuple-element.87), channel_id=1, source_target_pairs={{0,14},{1,15},{2,0},{3,1},{4,2},{5,3},{6,4},{7,5},{8,6},{9,7},{10,... | collective-permute-start | bytes 307208 | tf_op jit(solution)/shard_map/ppermute | solution.py:240
  146.6 16.7 %collective-permute-start.18 = (bf16[25,16,128]{2,1,0:T(8,128)(2,1)S(1)}, bf16[25,16,128]{2,1,0:T(8,128)(2,1)S(1)}, u32[]{:S(2)}, u32[]{:S(2)}) collective-permute-start(bf16[25,16,128]{2,1,0:T(8,128)(2,1)S(1)} %get-tuple-element.88), channel_id=1, source_target_pairs={{0,6},{1,7},{2,8},{3,9},{4,10},{5,11},{6,12},{7,13},{8,14},{9,15},... | collective-permute-start | bytes 307208 | tf_op jit(solution)/shard_map/ppermute | solution.py:240
  148.5 14.9 %collective-permute-start.19 = (bf16[25,16,128]{2,1,0:T(8,128)(2,1)S(1)}, bf16[25,16,128]{2,1,0:T(8,128)(2,1)S(1)}, u32[]{:S(2)}, u32[]{:S(2)}) collective-permute-start(bf16[25,16,128]{2,1,0:T(8,128)(2,1)S(1)} %get-tuple-element.89), channel_id=1, source_target_pairs={{0,10},{1,11},{2,12},{3,13},{4,14},{5,15},{6,0},{7,1},{8,2},{9,3},... | collective-permute-start | bytes 307208 | tf_op jit(solution)/shard_map/ppermute | solution.py:240
  151.1 16.8 %collective-permute-start.20 = (bf16[25,16,128]{2,1,0:T(8,128)(2,1)S(1)}, bf16[25,16,128]{2,1,0:T(8,128)(2,1)S(1)}, u32[]{:S(2)}, u32[]{:S(2)}) collective-permute-start(bf16[25,16,128]{2,1,0:T(8,128)(2,1)S(1)} %get-tuple-element.90), channel_id=1, source_target_pairs={{0,4},{1,5},{2,6},{3,7},{4,8},{5,9},{6,10},{7,11},{8,12},{9,13},{1... | collective-permute-start | bytes 307208 | tf_op jit(solution)/shard_map/ppermute | solution.py:240
  157.3 11.5 %collective-permute-start.21 = (bf16[25,16,128]{2,1,0:T(8,128)(2,1)S(1)}, bf16[25,16,128]{2,1,0:T(8,128)(2,1)S(1)}, u32[]{:S(2)}, u32[]{:S(2)}) collective-permute-start(bf16[25,16,128]{2,1,0:T(8,128)(2,1)S(1)} %get-tuple-element.91), channel_id=1, source_target_pairs={{0,12},{1,13},{2,14},{3,15},{4,0},{5,1},{6,2},{7,3},{8,4},{9,5},{1... | collective-permute-start | bytes 307208 | tf_op jit(solution)/shard_map/ppermute | solution.py:240
  159.4 14.0 %collective-permute-start.22 = (bf16[25,16,128]{2,1,0:T(8,128)(2,1)S(1)}, bf16[25,16,128]{2,1,0:T(8,128)(2,1)S(1)}, u32[]{:S(2)}, u32[]{:S(2)}) collective-permute-start(bf16[25,16,128]{2,1,0:T(8,128)(2,1)S(1)} %get-tuple-element.92), channel_id=1, source_target_pairs={{0,8},{1,9},{2,10},{3,11},{4,12},{5,13},{6,14},{7,15},{8,0},{9,1},... | collective-permute-start | bytes 307208 | tf_op jit(solution)/shard_map/ppermute | solution.py:240
  (16 other events, 83.0 us)

commit v4 on v3

--- a/solution.py
+++ b/solution.py
@@ -86,9 +86,9 @@
         ref[frames_ref[s], tile] = low[s * TOK:(s + 1) * TOK]
 
 
-def pack_kernel(clip_ref, q_ref, k_ref, up_ref, out_ref, held, sems):
+def pack_kernel(clip_ref, q_ref, k_ref, up_ref, out_ref, held, made, sems, out_sems):
     copies = []
-    size = ROWS // PARTS
+    size, units_of = ROWS // PARTS, SEQ // PARTS
     for i, ref in enumerate((q_ref, k_ref, up_ref)):
         for part in range(PARTS):
             rows = pl.ds(part * size, size)
@@ -96,17 +96,25 @@
                 pltpu.make_async_copy(ref.at[0, rows], held.at[i, rows], sems.at[i, part])
             )
             copies[-1].start()
+    last = pl.ds(3 * HEADS, 1)
     clip = jnp.full((SEQ, TOK, DIM), clip_ref[0, 0], jnp.int32).astype(F32).astype(BF)
-    out_ref[:, 3 * HEADS] = clip
-    units_of = SEQ // PARTS
+    made[:, 3 * HEADS] = clip
+    outs = [pltpu.make_async_copy(made.at[:, last], out_ref.at[:, last], out_sems.at[3 * PARTS])]
+    outs[-1].start()
     for i in range(3):
         for part in range(PARTS):
             copies[i * PARTS + part].wait()
+            units = pl.ds(part * units_of, units_of)
             for h in range(HEADS):
                 block = held[i, part * size:(part + 1) * size, head(h)]
-                out_ref[part * units_of:(part + 1) * units_of, i * HEADS + h] = block.reshape(
-                    units_of, TOK, DIM
-                )
+                made[units, i * HEADS + h] = block.reshape(units_of, TOK, DIM)
+            at = (units, pl.ds(i * HEADS, HEADS))
+            outs.append(
+                pltpu.make_async_copy(made.at[at], out_ref.at[at], out_sems.at[i * PARTS + part])
+            )
+            outs[-1].start()
+    for copy in outs:
+        copy.wait()
 
 
 def spatial_fwd_kernel(pos_ref, q_ref, k_ref, v_ref, keep_ref, give_ref, prob_ref):
@@ -207,17 +215,16 @@
     bias_ref[...] = total[:HEADS, :2 * SEQ - 1]
 
 
-def call(kernel, name, specs, inputs, outputs, scratch=(), estimate=1000, params=PARAMS, **more):
+def call(kernel, name, specs, inputs, outputs, scratch=(), estimate=1000, params=PARAMS, space=VMEM):
     return pl.pallas_call(
         kernel,
         out_shape=tuple(outputs),
         in_specs=specs,
-        out_specs=(VMEM,) * len(outputs),
+        out_specs=(space,) * len(outputs),
         scratch_shapes=scratch,
         compiler_params=params,
         cost_estimate=pl.CostEstimate(flops=estimate, bytes_accessed=1000, transcendentals=0),
         name=name,
-        **more,
     )(*inputs)
 
 
@@ -276,7 +283,13 @@
         [SMEM] + [HBM] * 3,
         [clip_ids, q_temporal, k_temporal, cotangent],
         [units(SEQ, tiles)],
-        [pltpu.VMEM((3, ROWS, WIDTH), BF), pltpu.SemaphoreType.DMA((3, PARTS))],
+        [
+            pltpu.VMEM((3, ROWS, WIDTH), BF),
+            pltpu.VMEM((SEQ, tiles, TOK, DIM), BF),
+            pltpu.SemaphoreType.DMA((3, PARTS)),
+            pltpu.SemaphoreType.DMA((3 * PARTS + 1,)),
+        ],
+        space=HBM,
         params=pltpu.CompilerParams(vmem_limit_bytes=56 * 1024 * 1024),
     )
     there = exchange(packed)
@@ -319,9 +332,21 @@
         + [jax.ShapeDtypeStruct((HEADS, SEQ, ROWS), F32)],
         estimate=LONG,
     )
-    back, _ = lax.optimization_barrier((back, grad_mid))
+    terms = jnp.einsum("hic,icr->hr", score_rows, wide, precision=lax.Precision.HIGHEST)
+    terms = terms + move(terms, 0, 1)
+    got_back = move(give_back, 0, 1)
+    last = sent(
+        call(
+            merge_last_kernel,
+            "merge_last",
+            [VMEM] * 3,
+            [bfloat_parts(terms), keep_back, got_back],
+            [jax.ShapeDtypeStruct((2 * HEADS + 1, TOK, DIM), BF)] * CHIPS,
+        )
+    )
     returned = exchange(back)
 
+    grad_mid, _ = lax.optimization_barrier((grad_mid, last))
     grad_qs, grad_ks, grad_vs = call(
         spatial_bwd_kernel,
         "spatial_bwd",
@@ -330,28 +355,16 @@
         [frame()] * 3,
         estimate=LONG,
     )
-    score_rows, give_back, _ = lax.optimization_barrier((score_rows, give_back, grad_vs))
-    terms = jnp.einsum("hic,icr->hr", score_rows, wide, precision=lax.Precision.HIGHEST)
-    terms = terms + move(terms, 0, 1)
-    terms = sum_of_four(sum_of_four(terms, "grp", 1), "grp", 4)
-    got_back = move(give_back, 0, 1)
-    tile = bfloat_parts(terms)
-    last = call(
-        merge_last_kernel,
-        "merge_last",
-        [VMEM] * 3,
-        [tile, keep_back, got_back],
-        [jax.ShapeDtypeStruct((2 * HEADS + 1, TOK, DIM), BF)] * CHIPS,
-    )
-    last = sent(last)
-    result, grad_qt = call(unpack_kernel, "unpack", [VMEM], [returned], [frame()] * 2)
-    grad_kt, total_bias = call(
+    last, _ = lax.optimization_barrier((last, grad_vs))
+    grad_kt, total = call(
         finish_kernel,
         "finish",
         [SMEM] + [VMEM] * CHIPS,
         [pos, *last],
         [frame(), jax.ShapeDtypeStruct((HEADS, 2 * SEQ - 1), F32)],
     )
+    total_bias = sum_of_four(sum_of_four(total, "grp", 1), "grp", 4)
+    result, grad_qt = call(unpack_kernel, "unpack", [VMEM], [returned], [frame()] * 2)
     return result, grad_qs, grad_ks, grad_vs, grad_qt, grad_kt, total_bias
 
 

time: 178 us -> 169 us (0.949)
  waiting for transfers between devices: 75.7 us -> 66.3 us
  local copies, waits for them, and re-layouts: 8.9 us -> 5.73 us
  starting transfers between devices: 56.8 us -> 59.4 us
    ppermute x17, waiting for transfers between devices: 58.2 us -> 46.5 us  [move(): return lax.ppermute(message, 'seq', perm)]
    all_to_all x3, starting transfers between devices: 23.1 us -> 27.5 us  [exchange(): lax.all_to_all(packed, 'seq', split_axis=0, concat_axis=0, tiled=True)]
    unnamed x44 -> x34, local copies, waits for them, and re-layouts: 7.66 us -> 4.5 us
    ppermute x6, waiting for transfers between devices: 5.21 us -> 7.3 us  [pair(): return lax.ppermute(terms, axis, [(i, i ^ mask) for i in range(size)])]
  transfers between devices with their start and end apart: 26 -> 26, of which waited for: 12 -> 10; matrix products, arithmetic and copies ran while one was open for 3% -> 3% of each run, Pallas kernels for 14% -> 15%
where the time goes in v4:
time: 169 us
  waiting for transfers between devices  66.3 us (39%)
  starting transfers between devices  59.4 us (35%)
  Pallas kernels  31.3 us (19%)
  local copies, waits for them, and re-layouts  5.73 us (3%)
  matrix products  3.71 us (2%)
    ppermute x17, waiting for transfers between devices, move(): return lax.ppermute(message, 'seq', perm)  46.5 us
    pallas_call x9, Pallas kernels, call(): pl.pallas_call(kernel, out_shape=tuple(outputs), in_specs=specs, out_spec...  31.3 us
    all_to_all x3, starting transfers between devices, exchange(): lax.all_to_all(packed, 'seq', split_axis=0, concat_axis=0, tiled=True)  27.5 us
    ppermute x17, starting transfers between devices, move(): return lax.ppermute(message, 'seq', perm)  25.2 us
    all_to_all x3, waiting for transfers between devices, exchange(): lax.all_to_all(packed, 'seq', split_axis=0, concat_axis=0, tiled=True)  12.5 us
    ppermute x6, waiting for transfers between devices, pair(): return lax.ppermute(terms, axis, [(i, i ^ mask) for i in range(size)])  7.3 us
    ppermute x6, starting transfers between devices, pair(): return lax.ppermute(terms, axis, [(i, i ^ mask) for i in range(size)])  6.66 us
    unnamed x34, local copies, waits for them, and re-layouts  4.5 us
  transfers between devices with their start and end apart: 26, of which 10 were waited for; matrix products, arithmetic and copies ran while one was open for 3% of the time, Pallas kernels for 15%

profile of v4, /device:TPU:1, one launch (start us, length us, event | category | flops | bytes accessed | tf_op | source)
XLA Modules:
  0.0 169.0 jit_solution(14876377161292487834)
XLA Ops:
  1.3 2.8 %pack.1 = bf16[16,37,16,128]{3,2,1,0:T(8,128)(2,1)} custom-call(s32[1,1]{1,0:T(1,128)S(6)} %copy.27.clip_ref, bf16[1,256,1536]{2,1,0:T(8,128)(2,1)} %q_ref.1, bf16[1,256,1536]{2,1,0:T(8,128)(2,1)} %k_ref.1, bf16[1,256,1536]{2,1,0:T(8,128)(2,1)} %up_ref.1), custom_call_target="tpu_custom_call" | custom-call | flops 1000 | bytes 1000 | tf_op jit(solution)/shard_map/pack/pallas_call | solution.py:219
  4.1 10.1 %all-to-all-start = ((bf16[16,37,16,128]{3,2,1,0:T(8,128)(2,1)}), bf16[16,37,16,128]{3,2,1,0:T(8,128)(2,1)S(1)}, u32[]{:S(2)}, u32[]{:S(2)}) async-start(bf16[16,37,16,128]{3,2,1,0:T(8,128)(2,1)} %pack.1), calls=%async_computation | async-start | bytes 4849664 | tf_op jit(solution)/shard_map/all_to_all | solution.py:232
  16.6 4.1 %spatial_fwd.1 = (bf16[8,12,16,128]{3,2,1,0:T(8,128)(2,1)S(1)}, bf16[8,12,16,128]{3,2,1,0:T(8,128)(2,1)S(1)}, f32[12,256,256]{2,1,0:T(8,128)}) custom-call(s32[2]{0:T(128)S(1)} %pad_add_fusion.pos_ref, bf16[1,256,1536]{2,1,0:T(8,128)(2,1)S(1)} %copy-done.1, bf16[1,256,1536]{2,1,0:T(8,128)(2,1)S(1)} %copy-done.2, bf16[1,256,1536]{2,1,0:T(8,128)(2,1)S(1)} %copy-done.4), custom_call_target="tpu_custom_call" | custom-call | flops 1000 | bytes 1000 | tf_op jit(solution)/shard_map/spatial_fwd/pallas_call | solution.py:219
  21.1 2.5 %fusion.4 = f32[12,16,256]{2,0,1:T(8,128)} fusion(f32[16,256,31]{2,1,0:T(8,128)S(1)} %bitcast.10, f32[12,31]{1,0:T(8,128)S(1)} %copy-done), kind=kOutput, calls=%fused_computation.14 | convolution fusion | flops 18284544 | bytes 706000 | tf_op jit(solution)/shard_map/hr,icr->hic/dot_general | solution.py:300
  23.8 1.6 collective-permute-done.got_ref
  26.2 1.4 collective-permute-start.1
  27.6 1.3 collective-permute-start.2
  28.8 2.9 %collective-permute-start.3 = (bf16[2,12,16,128]{3,2,1,0:T(8,128)(2,1)}, bf16[2,12,16,128]{3,2,1,0:T(8,128)(2,1)}, u32[]{:S(2)}, u32[]{:S(2)}) collective-permute-start(bf16[2,12,16,128]{3,2,1,0:T(8,128)(2,1)} %get-tuple-element.68), channel_id=1, source_target_pairs={{0,6},{1,7},{2,8},{3,9},{4,10},{5,11},{6,12},{7,13},{8,14},{9,15},... | collective-permute-start | bytes 294920 | tf_op jit(solution)/shard_map/ppermute | solution.py:247
  31.8 1.6 collective-permute-start.4
  34.4 37.5 %collective-permute-done.1.refs_1_ = bf16[2,12,16,128]{3,2,1,0:T(8,128)(2,1)S(1)} collective-permute-done((bf16[2,12,16,128]{3,2,1,0:T(8,128)(2,1)S(1)}, bf16[2,12,16,128]{3,2,1,0:T(8,128)(2,1)S(1)}, u32[]{:S(2)}, u32[]{:S(2)}) %collective-permute-start.1) | collective-permute-done | bytes 98336 | tf_op jit(solution)/shard_map/ppermute | solution.py:247
  71.9 2.1 %collective-permute-start.6 = (bf16[2,12,16,128]{3,2,1,0:T(8,128)(2,1)}, bf16[2,12,16,128]{3,2,1,0:T(8,128)(2,1)}, u32[]{:S(2)}, u32[]{:S(2)}) collective-permute-start(bf16[2,12,16,128]{3,2,1,0:T(8,128)(2,1)} %get-tuple-element.71), channel_id=1, source_target_pairs={{0,12},{1,13},{2,14},{3,15},{4,0},{5,1},{6,2},{7,3},{8,4},{9,5},{1... | collective-permute-start | bytes 294920 | tf_op jit(solution)/shard_map/ppermute | solution.py:247
  74.0 1.9 %collective-permute-start.7 = (bf16[2,12,16,128]{3,2,1,0:T(8,128)(2,1)}, bf16[2,12,16,128]{3,2,1,0:T(8,128)(2,1)}, u32[]{:S(2)}, u32[]{:S(2)}) collective-permute-start(bf16[2,12,16,128]{3,2,1,0:T(8,128)(2,1)} %get-tuple-element.72), channel_id=1, source_target_pairs={{0,8},{1,9},{2,10},{3,11},{4,12},{5,13},{6,14},{7,15},{8,0},{9,1},... | collective-permute-start | bytes 294920 | tf_op jit(solution)/shard_map/ppermute | solution.py:247
  77.0 4.8 %temporal_a.1 = (f32[12,256,256]{2,1,0:T(8,128)}, bf16[16,12,16,128]{3,2,1,0:T(8,128)(2,1)S(1)}) custom-call(s32[16]{0:T(128)S(1)} %fusion.13.frames_ref, bf16[16,37,16,128]{3,2,1,0:T(8,128)(2,1)S(1)} %all-to-all-done.in_ref, f32[12,16,256]{2,1,0:T(8,128)S(1)} %copy.20.bias_ref), custom_call_target="tpu_custom_call" | custom-call | flops 1000 | bytes 1000 | tf_op jit(solution)/shard_map/temporal_a/pallas_call | solution.py:219
  82.7 8.4 %all-to-all-start.2 = ((bf16[16,12,16,128]{3,2,1,0:T(8,128)(2,1)}), bf16[16,12,16,128]{3,2,1,0:T(8,128)(2,1)}, u32[]{:S(2)}, u32[]{:S(2)}) async-start(bf16[16,12,16,128]{3,2,1,0:T(8,128)(2,1)} %copy-done.6), calls=%async_computation.2 | async-start | bytes 1572864 | tf_op jit(solution)/shard_map/all_to_all | solution.py:232
  91.1 7.1 %temporal_b.1 = (bf16[16,24,16,128]{3,2,1,0:T(8,128)(2,1)}, bf16[8,12,16,128]{3,2,1,0:T(8,128)(2,1)S(1)}, bf16[8,12,16,128]{3,2,1,0:T(8,128)(2,1)S(1)}, f32[12,16,256]{2,1,0:T(8,128)S(1)}) custom-call(s32[16]{0:T(128)S(1)} %fusion.13.frames_ref, bf16[16,37,16,128]{3,2,1,0:T(8,128)(2,1)S(1)} %all-to-all-done.in_ref, ...), custom_call_target="tpu_custom_call" | custom-call | flops 999999995904 | bytes 1000 | tf_op jit(solution)/shard_map/temporal_b/pallas_call | solution.py:219
  101.1 1.7 collective-permute-start.10
  102.8 1.3 collective-permute-start.11
  104.1 2.9 %collective-permute-start.12 = (bf16[25,16,128]{2,1,0:T(8,128)(2,1)S(1)}, bf16[25,16,128]{2,1,0:T(8,128)(2,1)S(1)}, u32[]{:S(2)}, u32[]{:S(2)}) collective-permute-start(bf16[25,16,128]{2,1,0:T(8,128)(2,1)S(1)} %get-tuple-element.87), channel_id=1, source_target_pairs={{0,6},{1,7},{2,8},{3,9},{4,10},{5,11},{6,12},{7,13},{8,14},{9,15},... | collective-permute-start | bytes 307208 | tf_op jit(solution)/shard_map/ppermute | solution.py:247
  106.9 1.6 collective-permute-start.13
  109.6 4.0 %collective-permute-done.10.refs_1_ = bf16[25,16,128]{2,1,0:T(8,128)(2,1)S(1)} collective-permute-done((bf16[25,16,128]{2,1,0:T(8,128)(2,1)S(1)}, bf16[25,16,128]{2,1,0:T(8,128)(2,1)S(1)}, u32[]{:S(2)}, u32[]{:S(2)}) %collective-permute-start.10) | collective-permute-done | bytes 102432 | tf_op jit(solution)/shard_map/ppermute | solution.py:247
  114.2 2.2 %collective-permute-start.15 = (bf16[25,16,128]{2,1,0:T(8,128)(2,1)S(1)}, bf16[25,16,128]{2,1,0:T(8,128)(2,1)S(1)}, u32[]{:S(2)}, u32[]{:S(2)}) collective-permute-start(bf16[25,16,128]{2,1,0:T(8,128)(2,1)S(1)} %get-tuple-element.90), channel_id=1, source_target_pairs={{0,12},{1,13},{2,14},{3,15},{4,0},{5,1},{6,2},{7,3},{8,4},{9,5},{1... | collective-permute-start | bytes 307208 | tf_op jit(solution)/shard_map/ppermute | solution.py:247
  117.1 1.6 collective-permute-start.16
  118.7 8.9 %all-to-all-start.1 = ((bf16[16,24,16,128]{3,2,1,0:T(8,128)(2,1)}), bf16[16,24,16,128]{3,2,1,0:T(8,128)(2,1)}, u32[]{:S(2)}, u32[]{:S(2)}) async-start(bf16[16,24,16,128]{3,2,1,0:T(8,128)(2,1)} %get-tuple-element.77), calls=%async_computation.1 | async-start | bytes 3145728 | tf_op jit(solution)/shard_map/all_to_all | solution.py:232
  127.7 2.5 %collective-permute-done.16.refs_7_ = bf16[25,16,128]{2,1,0:T(8,128)(2,1)S(1)} collective-permute-done((bf16[25,16,128]{2,1,0:T(8,128)(2,1)S(1)}, bf16[25,16,128]{2,1,0:T(8,128)(2,1)S(1)}, u32[]{:S(2)}, u32[]{:S(2)}) %collective-permute-start.16) | collective-permute-done | bytes 102432 | tf_op jit(solution)/shard_map/ppermute | solution.py:247
  130.2 7.2 %spatial_bwd.1 = (bf16[1,256,1536]{2,1,0:T(8,128)(2,1)}, bf16[1,256,1536]{2,1,0:T(8,128)(2,1)}, bf16[1,256,1536]{2,1,0:T(8,128)(2,1)}) custom-call(bf16[1,256,1536]{2,1,0:T(8,128)(2,1)S(1)} %copy-done.1, bf16[1,256,1536]{2,1,0:T(8,128)(2,1)S(1)} %copy-done.3, bf16[1,256,1536]{2,1,0:T(8,128)(2,1)S(1)} %copy-done.5, ...), custom_call_target="tpu_custom_call" | custom-call | flops 999999995904 | bytes 1000 | tf_op jit(solution)/shard_map/spatial_bwd/pallas_call | solution.py:219
  137.5 1.6 finish.1
  139.1 2.7 %collective-permute-start.19 = (f32[12,31]{1,0:T(8,128)S(1)}, f32[12,31]{1,0:T(8,128)S(1)}, u32[]{:S(2)}, u32[]{:S(2)}) collective-permute-start(f32[12,31]{1,0:T(8,128)S(1)} %get-tuple-element.106), channel_id=1, source_target_pairs={{0,48},{16,32},{32,16},{48,0},{64,112},{80,96},{96,80},{112,64},{1... | collective-permute-start | bytes 4472 | tf_op jit(solution)/shard_map/ppermute | solution.py:237
  143.3 3.0 %collective-permute-done.18 = f32[12,31]{1,0:T(8,128)S(1)} collective-permute-done((f32[12,31]{1,0:T(8,128)S(1)}, f32[12,31]{1,0:T(8,128)S(1)}, u32[]{:S(2)}, u32[]{:S(2)}) %collective-permute-start.18) | collective-permute-done | bytes 1520 | tf_op jit(solution)/shard_map/ppermute | solution.py:237
  146.2 2.6 %collective-permute-start.22 = (f32[12,31]{1,0:T(8,128)S(1)}, f32[12,31]{1,0:T(8,128)S(1)}, u32[]{:S(2)}, u32[]{:S(2)}) collective-permute-start(f32[12,31]{1,0:T(8,128)S(1)} %add_add_fusion.1), channel_id=1, source_target_pairs={{0,192},{16,208},{32,224},{48,240},{64,128},{80,144},{96,160},{112... | collective-permute-start | bytes 4472 | tf_op jit(solution)/shard_map/ppermute | solution.py:237
  150.4 2.6 %collective-permute-done.21 = f32[12,31]{1,0:T(8,128)S(1)} collective-permute-done((f32[12,31]{1,0:T(8,128)S(1)}, f32[12,31]{1,0:T(8,128)S(1)}, u32[]{:S(2)}, u32[]{:S(2)}) %collective-permute-start.21) | collective-permute-done | bytes 1520 | tf_op jit(solution)/shard_map/ppermute | solution.py:237
  153.7 12.5 %all-to-all-done.1.in_ref = bf16[16,24,16,128]{3,2,1,0:T(8,128)(2,1)} async-done(((bf16[16,24,16,128]{3,2,1,0:T(8,128)(2,1)}), bf16[16,24,16,128]{3,2,1,0:T(8,128)(2,1)}, u32[]{:S(2)}, u32[]{:S(2)}) %all-to-all-start.1) | async-done | bytes 1572896 | tf_op jit(solution)/shard_map/all_to_all | solution.py:232
  166.2 2.8 %unpack.1 = (bf16[1,256,1536]{2,1,0:T(8,128)(2,1)}, bf16[1,256,1536]{2,1,0:T(8,128)(2,1)}) custom-call(bf16[16,24,16,128]{3,2,1,0:T(8,128)(2,1)} %all-to-all-done.1.in_ref), custom_call_target="tpu_custom_call" | custom-call | flops 1000 | bytes 1000 | tf_op jit(solution)/shard_map/unpack/pallas_call | solution.py:219
  (76 shorter events, 15.5 us)
Async XLA Ops:
  0.6 20.5 %copy-start = (f32[12,31]{1,0:T(8,128)S(1)}, f32[12,31]{1,0:T(8,128)}, u32[]{:S(2)}) copy-start(f32[12,31]{1,0:T(8,128)} %param.15) | copy-start | bytes 4468
  4.1 10.2 %copy-start.15 = (s32[16]{0:T(128)S(1)}, s32[16]{0:T(128)}, u32[]{:S(2)}) copy-start(s32[16]{0:T(128)} %constant.37) | copy-start | bytes 196
  4.1 10.3 %copy-start.1 = (bf16[1,256,1536]{2,1,0:T(8,128)(2,1)S(1)}, bf16[1,256,1536]{2,1,0:T(8,128)(2,1)}, u32[]{:S(2)}) copy-start(bf16[1,256,1536]{2,1,0:T(8,128)(2,1)} %q_ref.3) | copy-start | bytes 2359300
  4.1 71.8 %all-to-all-start = ((bf16[16,37,16,128]{3,2,1,0:T(8,128)(2,1)}), bf16[16,37,16,128]{3,2,1,0:T(8,128)(2,1)S(1)}, u32[]{:S(2)}, u32[]{:S(2)}) async-start(bf16[16,37,16,128]{3,2,1,0:T(8,128)(2,1)} %pack.1), calls=%async_computation | async-start | bytes 4849664 | tf_op jit(solution)/shard_map/all_to_all | solution.py:232
  21.1 52.9 %copy-start.13 = (f32[16,16,16,31]{3,2,1,0:T(8,128)}, f32[16,16,16,31]{3,2,1,0:T(8,128)S(1)}, u32[]{:S(2)}) copy-start(f32[16,16,16,31]{3,2,1,0:T(8,128)S(1)} %broadcast_in_dim.2) | copy-start | bytes 1523716
  23.6 1.7 %collective-permute-start = (bf16[8,12,16,128]{3,2,1,0:T(8,128)(2,1)S(1)}, bf16[8,12,16,128]{3,2,1,0:T(8,128)(2,1)S(1)}, u32[]{:S(2)}, u32[]{:S(2)}) collective-permute-start(bf16[8,12,16,128]{3,2,1,0:T(8,128)(2,1)S(1)} %get-tuple-element.64), channel_id=1, source_target_pairs={{0,1},{1,0},{2,3},{3,2},{4,5},{5,4},{6,7},{7,6},{8,9},{9,8},{10,11... | collective-permute-start | bytes 1179656 | tf_op jit(solution)/shard_map/ppermute | solution.py:247
  26.2 45.8 %collective-permute-start.1 = (bf16[2,12,16,128]{3,2,1,0:T(8,128)(2,1)S(1)}, bf16[2,12,16,128]{3,2,1,0:T(8,128)(2,1)S(1)}, u32[]{:S(2)}, u32[]{:S(2)}) collective-permute-start(bf16[2,12,16,128]{3,2,1,0:T(8,128)(2,1)S(1)} %get-tuple-element.66), channel_id=1, source_target_pairs={{0,2},{1,3},{2,4},{3,5},{4,6},{5,7},{6,8},{7,9},{8,10},{9,11},{10,... | collective-permute-start | bytes 294920 | tf_op jit(solution)/shard_map/ppermute | solution.py:247
  27.6 46.4 %collective-permute-start.2 = (bf16[2,12,16,128]{3,2,1,0:T(8,128)(2,1)S(1)}, bf16[2,12,16,128]{3,2,1,0:T(8,128)(2,1)S(1)}, u32[]{:S(2)}, u32[]{:S(2)}) collective-permute-start(bf16[2,12,16,128]{3,2,1,0:T(8,128)(2,1)S(1)} %get-tuple-element.67), channel_id=1, source_target_pairs={{0,14},{1,15},{2,0},{3,1},{4,2},{5,3},{6,4},{7,5},{8,6},{9,7},{10,... | collective-permute-start | bytes 294920 | tf_op jit(solution)/shard_map/ppermute | solution.py:247
  28.8 62.2 %collective-permute-start.3 = (bf16[2,12,16,128]{3,2,1,0:T(8,128)(2,1)}, bf16[2,12,16,128]{3,2,1,0:T(8,128)(2,1)}, u32[]{:S(2)}, u32[]{:S(2)}) collective-permute-start(bf16[2,12,16,128]{3,2,1,0:T(8,128)(2,1)} %get-tuple-element.68), channel_id=1, source_target_pairs={{0,6},{1,7},{2,8},{3,9},{4,10},{5,11},{6,12},{7,13},{8,14},{9,15},... | collective-permute-start | bytes 294920 | tf_op jit(solution)/shard_map/ppermute | solution.py:247
  31.8 59.3 %collective-permute-start.4 = (bf16[2,12,16,128]{3,2,1,0:T(8,128)(2,1)}, bf16[2,12,16,128]{3,2,1,0:T(8,128)(2,1)}, u32[]{:S(2)}, u32[]{:S(2)}) collective-permute-start(bf16[2,12,16,128]{3,2,1,0:T(8,128)(2,1)} %get-tuple-element.69), channel_id=1, source_target_pairs={{0,10},{1,11},{2,12},{3,13},{4,14},{5,15},{6,0},{7,1},{8,2},{9,3},... | collective-permute-start | bytes 294920 | tf_op jit(solution)/shard_map/ppermute | solution.py:247
  33.3 57.8 %collective-permute-start.5 = (bf16[2,12,16,128]{3,2,1,0:T(8,128)(2,1)}, bf16[2,12,16,128]{3,2,1,0:T(8,128)(2,1)}, u32[]{:S(2)}, u32[]{:S(2)}) collective-permute-start(bf16[2,12,16,128]{3,2,1,0:T(8,128)(2,1)} %get-tuple-element.70), channel_id=1, source_target_pairs={{0,4},{1,5},{2,6},{3,7},{4,8},{5,9},{6,10},{7,11},{8,12},{9,13},{1... | collective-permute-start | bytes 294920 | tf_op jit(solution)/shard_map/ppermute | solution.py:247
  71.9 19.2 %collective-permute-start.6 = (bf16[2,12,16,128]{3,2,1,0:T(8,128)(2,1)}, bf16[2,12,16,128]{3,2,1,0:T(8,128)(2,1)}, u32[]{:S(2)}, u32[]{:S(2)}) collective-permute-start(bf16[2,12,16,128]{3,2,1,0:T(8,128)(2,1)} %get-tuple-element.71), channel_id=1, source_target_pairs={{0,12},{1,13},{2,14},{3,15},{4,0},{5,1},{6,2},{7,3},{8,4},{9,5},{1... | collective-permute-start | bytes 294920 | tf_op jit(solution)/shard_map/ppermute | solution.py:247
  74.0 17.1 %collective-permute-start.7 = (bf16[2,12,16,128]{3,2,1,0:T(8,128)(2,1)}, bf16[2,12,16,128]{3,2,1,0:T(8,128)(2,1)}, u32[]{:S(2)}, u32[]{:S(2)}) collective-permute-start(bf16[2,12,16,128]{3,2,1,0:T(8,128)(2,1)} %get-tuple-element.72), channel_id=1, source_target_pairs={{0,8},{1,9},{2,10},{3,11},{4,12},{5,13},{6,14},{7,15},{8,0},{9,1},... | collective-permute-start | bytes 294920 | tf_op jit(solution)/shard_map/ppermute | solution.py:247
  82.7 36.0 %all-to-all-start.2 = ((bf16[16,12,16,128]{3,2,1,0:T(8,128)(2,1)}), bf16[16,12,16,128]{3,2,1,0:T(8,128)(2,1)}, u32[]{:S(2)}, u32[]{:S(2)}) async-start(bf16[16,12,16,128]{3,2,1,0:T(8,128)(2,1)} %copy-done.6), calls=%async_computation.2 | async-start | bytes 1572864 | tf_op jit(solution)/shard_map/all_to_all | solution.py:232
  98.2 2.8 %collective-permute-start.9 = (bf16[8,12,16,128]{3,2,1,0:T(8,128)(2,1)S(1)}, bf16[8,12,16,128]{3,2,1,0:T(8,128)(2,1)S(1)}, u32[]{:S(2)}, u32[]{:S(2)}) collective-permute-start(bf16[8,12,16,128]{3,2,1,0:T(8,128)(2,1)S(1)} %get-tuple-element.83), channel_id=1, source_target_pairs={{0,1},{1,0},{2,3},{3,2},{4,5},{5,4},{6,7},{7,6},{8,9},{9,8},{10,11... | collective-permute-start | bytes 1179656 | tf_op jit(solution)/shard_map/ppermute | solution.py:247
  99.6 30.6 %copy-start.3 = (bf16[1,256,1536]{2,1,0:T(8,128)(2,1)S(1)}, bf16[1,256,1536]{2,1,0:T(8,128)(2,1)}, u32[]{:S(2)}) copy-start(bf16[1,256,1536]{2,1,0:T(8,128)(2,1)} %k_ref.3) | copy-start | bytes 2359300
  99.6 30.6 %copy-start.5 = (bf16[1,256,1536]{2,1,0:T(8,128)(2,1)S(1)}, bf16[1,256,1536]{2,1,0:T(8,128)(2,1)}, u32[]{:S(2)}) copy-start(bf16[1,256,1536]{2,1,0:T(8,128)(2,1)} %v_ref.1) | copy-start | bytes 2359300
  99.6 1.3 collective-permute-start.8
  101.1 12.5 %collective-permute-start.10 = (bf16[25,16,128]{2,1,0:T(8,128)(2,1)S(1)}, bf16[25,16,128]{2,1,0:T(8,128)(2,1)S(1)}, u32[]{:S(2)}, u32[]{:S(2)}) collective-permute-start(bf16[25,16,128]{2,1,0:T(8,128)(2,1)S(1)} %get-tuple-element.85), channel_id=1, source_target_pairs={{0,2},{1,3},{2,4},{3,5},{4,6},{5,7},{6,8},{7,9},{8,10},{9,11},{10,... | collective-permute-start | bytes 307208 | tf_op jit(solution)/shard_map/ppermute | solution.py:247
  102.8 13.7 %collective-permute-start.11 = (bf16[25,16,128]{2,1,0:T(8,128)(2,1)S(1)}, bf16[25,16,128]{2,1,0:T(8,128)(2,1)S(1)}, u32[]{:S(2)}, u32[]{:S(2)}) collective-permute-start(bf16[25,16,128]{2,1,0:T(8,128)(2,1)S(1)} %get-tuple-element.86), channel_id=1, source_target_pairs={{0,14},{1,15},{2,0},{3,1},{4,2},{5,3},{6,4},{7,5},{8,6},{9,7},{10,... | collective-permute-start | bytes 307208 | tf_op jit(solution)/shard_map/ppermute | solution.py:247
  104.1 23.6 %collective-permute-start.12 = (bf16[25,16,128]{2,1,0:T(8,128)(2,1)S(1)}, bf16[25,16,128]{2,1,0:T(8,128)(2,1)S(1)}, u32[]{:S(2)}, u32[]{:S(2)}) collective-permute-start(bf16[25,16,128]{2,1,0:T(8,128)(2,1)S(1)} %get-tuple-element.87), channel_id=1, source_target_pairs={{0,6},{1,7},{2,8},{3,9},{4,10},{5,11},{6,12},{7,13},{8,14},{9,15},... | collective-permute-start | bytes 307208 | tf_op jit(solution)/shard_map/ppermute | solution.py:247
  106.9 20.7 %collective-permute-start.13 = (bf16[25,16,128]{2,1,0:T(8,128)(2,1)S(1)}, bf16[25,16,128]{2,1,0:T(8,128)(2,1)S(1)}, u32[]{:S(2)}, u32[]{:S(2)}) collective-permute-start(bf16[25,16,128]{2,1,0:T(8,128)(2,1)S(1)} %get-tuple-element.88), channel_id=1, source_target_pairs={{0,10},{1,11},{2,12},{3,13},{4,14},{5,15},{6,0},{7,1},{8,2},{9,3},... | collective-permute-start | bytes 307208 | tf_op jit(solution)/shard_map/ppermute | solution.py:247
  108.5 19.1 %collective-permute-start.14 = (bf16[25,16,128]{2,1,0:T(8,128)(2,1)S(1)}, bf16[25,16,128]{2,1,0:T(8,128)(2,1)S(1)}, u32[]{:S(2)}, u32[]{:S(2)}) collective-permute-start(bf16[25,16,128]{2,1,0:T(8,128)(2,1)S(1)} %get-tuple-element.89), channel_id=1, source_target_pairs={{0,4},{1,5},{2,6},{3,7},{4,8},{5,9},{6,10},{7,11},{8,12},{9,13},{1... | collective-permute-start | bytes 307208 | tf_op jit(solution)/shard_map/ppermute | solution.py:247
  114.2 13.4 %collective-permute-start.15 = (bf16[25,16,128]{2,1,0:T(8,128)(2,1)S(1)}, bf16[25,16,128]{2,1,0:T(8,128)(2,1)S(1)}, u32[]{:S(2)}, u32[]{:S(2)}) collective-permute-start(bf16[25,16,128]{2,1,0:T(8,128)(2,1)S(1)} %get-tuple-element.90), channel_id=1, source_target_pairs={{0,12},{1,13},{2,14},{3,15},{4,0},{5,1},{6,2},{7,3},{8,4},{9,5},{1... | collective-permute-start | bytes 307208 | tf_op jit(solution)/shard_map/ppermute | solution.py:247
  117.1 13.1 %collective-permute-start.16 = (bf16[25,16,128]{2,1,0:T(8,128)(2,1)S(1)}, bf16[25,16,128]{2,1,0:T(8,128)(2,1)S(1)}, u32[]{:S(2)}, u32[]{:S(2)}) collective-permute-start(bf16[25,16,128]{2,1,0:T(8,128)(2,1)S(1)} %get-tuple-element.91), channel_id=1, source_target_pairs={{0,8},{1,9},{2,10},{3,11},{4,12},{5,13},{6,14},{7,15},{8,0},{9,1},... | collective-permute-start | bytes 307208 | tf_op jit(solution)/shard_map/ppermute | solution.py:247
  118.7 47.5 %all-to-all-start.1 = ((bf16[16,24,16,128]{3,2,1,0:T(8,128)(2,1)}), bf16[16,24,16,128]{3,2,1,0:T(8,128)(2,1)}, u32[]{:S(2)}, u32[]{:S(2)}) async-start(bf16[16,24,16,128]{3,2,1,0:T(8,128)(2,1)} %get-tuple-element.77), calls=%async_computation.1 | async-start | bytes 3145728 | tf_op jit(solution)/shard_map/all_to_all | solution.py:232
  139.1 4.2 %collective-permute-start.19 = (f32[12,31]{1,0:T(8,128)S(1)}, f32[12,31]{1,0:T(8,128)S(1)}, u32[]{:S(2)}, u32[]{:S(2)}) collective-permute-start(f32[12,31]{1,0:T(8,128)S(1)} %get-tuple-element.106), channel_id=1, source_target_pairs={{0,48},{16,32},{32,16},{48,0},{64,112},{80,96},{96,80},{112,64},{1... | collective-permute-start | bytes 4472 | tf_op jit(solution)/shard_map/ppermute | solution.py:237
  141.8 4.4 %collective-permute-start.18 = (f32[12,31]{1,0:T(8,128)S(1)}, f32[12,31]{1,0:T(8,128)S(1)}, u32[]{:S(2)}, u32[]{:S(2)}) collective-permute-start(f32[12,31]{1,0:T(8,128)S(1)} %get-tuple-element.106), channel_id=1, source_target_pairs={{0,32},{16,48},{32,0},{48,16},{64,96},{80,112},{96,64},{112,80},{1... | collective-permute-start | bytes 4472 | tf_op jit(solution)/shard_map/ppermute | solution.py:237
  142.2 4.1 %collective-permute-start.17 = (f32[12,31]{1,0:T(8,128)S(1)}, f32[12,31]{1,0:T(8,128)S(1)}, u32[]{:S(2)}, u32[]{:S(2)}) collective-permute-start(f32[12,31]{1,0:T(8,128)S(1)} %get-tuple-element.106), channel_id=1, source_target_pairs={{0,16},{16,0},{32,48},{48,32},{64,80},{80,64},{96,112},{112,96},{1... | collective-permute-start | bytes 4472 | tf_op jit(solution)/shard_map/ppermute | solution.py:237
  146.2 4.2 %collective-permute-start.22 = (f32[12,31]{1,0:T(8,128)S(1)}, f32[12,31]{1,0:T(8,128)S(1)}, u32[]{:S(2)}, u32[]{:S(2)}) collective-permute-start(f32[12,31]{1,0:T(8,128)S(1)} %add_add_fusion.1), channel_id=1, source_target_pairs={{0,192},{16,208},{32,224},{48,240},{64,128},{80,144},{96,160},{112... | collective-permute-start | bytes 4472 | tf_op jit(solution)/shard_map/ppermute | solution.py:237
  148.8 4.2 %collective-permute-start.21 = (f32[12,31]{1,0:T(8,128)S(1)}, f32[12,31]{1,0:T(8,128)S(1)}, u32[]{:S(2)}, u32[]{:S(2)}) collective-permute-start(f32[12,31]{1,0:T(8,128)S(1)} %add_add_fusion.1), channel_id=1, source_target_pairs={{0,128},{16,144},{32,160},{48,176},{64,192},{80,208},{96,224},{112... | collective-permute-start | bytes 4472 | tf_op jit(solution)/shard_map/ppermute | solution.py:237
  149.3 3.7 %collective-permute-start.20 = (f32[12,31]{1,0:T(8,128)S(1)}, f32[12,31]{1,0:T(8,128)S(1)}, u32[]{:S(2)}, u32[]{:S(2)}) collective-permute-start(f32[12,31]{1,0:T(8,128)S(1)} %add_add_fusion.1), channel_id=1, source_target_pairs={{0,64},{16,80},{32,96},{48,112},{64,0},{80,16},{96,32},{112,48},{1... | collective-permute-start | bytes 4472 | tf_op jit(solution)/shard_map/ppermute | solution.py:237
  (11 other events, 48.1 us)

commit v5 on v4

--- a/solution.py
+++ b/solution.py
@@ -18,6 +18,7 @@
 F32 = jnp.float32
 PARAMS = pltpu.CompilerParams(vmem_limit_bytes=48 * 1024 * 1024)
 PARTS = 4
+GROUP = 3
 LONG = 10**12
 VMEM = pl.BlockSpec(memory_space=pltpu.VMEM)
 SMEM = pl.BlockSpec(memory_space=pltpu.SMEM)
@@ -80,10 +81,10 @@
         give_ref[d, tile] = low[(CHIPS + d) * TOK:(CHIPS + d + 1) * TOK]
 
 
-def put_slots(frames_ref, ref, tile, value):
+def put_frames(frames_ref, ref, i, h, value):
     low = value.astype(BF)
     for s in range(SEQ):
-        ref[frames_ref[s], tile] = low[s * TOK:(s + 1) * TOK]
+        ref[frames_ref[s], i, :, head(h)] = low[s * TOK:(s + 1) * TOK]
 
 
 def pack_kernel(clip_ref, q_ref, k_ref, up_ref, out_ref, held, made, sems, out_sems):
@@ -131,7 +132,7 @@
             give_ref[shift, h] = jnp.where(first, odd, even).astype(BF)
 
 
-def merge_kernel(keep_ref, got_ref, *outs):
+def merge_kernel(keep_ref, got_ref, bias_ref, *outs):
     for out, shift in zip(outs, (0,) + SHIFTS):
         out[0] = keep_ref[shift % CHIPS]
         out[1] = got_ref[shift % CHIPS]
@@ -162,7 +163,7 @@
         gk_ref[0, :, head(h)] = mm_tn(low, q).astype(BF)
 
 
-def temporal_a_kernel(frames_ref, in_ref, bias_ref, prob_ref, mid_ref):
+def temporal_a_kernel(frames_ref, in_ref, bias_ref, prob_ref, mid_ref, made, sems):
     row = lax.broadcasted_iota(jnp.int32, (ROWS, ROWS), 0)
     col = lax.broadcasted_iota(jnp.int32, (ROWS, ROWS), 1)
     clip = slot_rows(frames_ref, in_ref, 3 * HEADS).astype(F32)
@@ -170,12 +171,23 @@
     same = (row & (TOK - 1)) == (col & (TOK - 1))
     same &= jnp.concatenate([clip] * 2, axis=1) == jnp.concatenate([other] * 2, axis=0)
     mask = jnp.where(same, 0.0, NEG)
+    copies = []
     for h in range(HEADS):
         q, k, up = (slot_rows(frames_ref, in_ref, i * HEADS + h) for i in range(3))
         bias = jnp.broadcast_to(bias_ref[h][:, None, :], (SEQ, TOK, ROWS)).reshape(ROWS, ROWS)
         prob = softmax((mm_nt(q, k) * SCALE + bias) + mask)
         prob_ref[h] = prob
-        put_slots(frames_ref, mid_ref, h, mm_tn(prob.astype(BF), up))
+        mid = mm_tn(prob.astype(BF), up).astype(BF)
+        for s in range(SEQ):
+            made[frames_ref[s], h] = mid[s * TOK:(s + 1) * TOK]
+        if (h + 1) % GROUP == 0:
+            at = (slice(None), pl.ds(h + 1 - GROUP, GROUP))
+            copies.append(
+                pltpu.make_async_copy(made.at[at], mid_ref.at[at], sems.at[h // GROUP])
+            )
+            copies[-1].start()
+    for copy in copies:
+        copy.wait()
 
 
 def temporal_b_kernel(frames_ref, in_ref, prob_ref, *refs):
@@ -186,17 +198,23 @@
         so = jnp.concatenate([ref[x, h] for ref, x in so_at], axis=0)
         prob = prob_ref[h]
         grad_prob = mm_nt(up, so)
-        put_slots(frames_ref, out_ref, h, mm(prob.astype(BF), so))
+        put_frames(frames_ref, out_ref, 0, h, mm(prob.astype(BF), so))
         score = prob * (grad_prob - jnp.sum(prob * grad_prob, axis=-1, keepdims=True))
         bias_ref[h] = jnp.sum(score.reshape(SEQ, TOK, ROWS), axis=1)
         low = (score * SCALE).astype(BF)
-        put_slots(frames_ref, out_ref, HEADS + h, mm(low, k))
+        put_frames(frames_ref, out_ref, 1, h, mm(low, k))
         put_pairs(keep_ref, give_ref, h, mm_tn(low, q))
 
 
-def unpack_kernel(in_ref, *outs):
-    for tile in range(2 * HEADS):
-        outs[tile // HEADS][0, :, head(tile % HEADS)] = rows_of(in_ref, tile)
+def unpack_kernel(in_ref, res_ref, gq_ref, sems):
+    copies = []
+    for i, out in enumerate((res_ref, gq_ref)):
+        for u in range(SEQ):
+            rows = pl.ds(u * TOK, TOK)
+            copies.append(pltpu.make_async_copy(in_ref.at[u, i], out.at[0, rows], sems.at[i, u]))
+            copies[-1].start()
+    for copy in copies:
+        copy.wait()
 
 
 def finish_kernel(pos_ref, *refs):
@@ -220,7 +238,7 @@
         kernel,
         out_shape=tuple(outputs),
         in_specs=specs,
-        out_specs=(space,) * len(outputs),
+        out_specs=space if isinstance(space, tuple) else (space,) * len(outputs),
         scratch_shapes=scratch,
         compiler_params=params,
         cost_estimate=pl.CostEstimate(flops=estimate, bytes_accessed=1000, transcendentals=0),
@@ -308,7 +326,7 @@
     give_so, bias = lax.optimization_barrier((give_so, bias))
     got_so = move(give_so, 0, 1)
     so_messages = call(
-        merge_kernel, "merge", [VMEM] * 2, [keep_so, got_so], [units(2, HEADS)] * CHIPS
+        merge_kernel, "merge", [VMEM] * 3, [keep_so, got_so, bias], [units(2, HEADS)] * CHIPS
     )
     so = sent(so_messages)
 
@@ -319,6 +337,8 @@
         [SMEM] + [VMEM] * 2,
         [frames, there, bias],
         [probs(), units(SEQ, HEADS)],
+        [pltpu.VMEM((SEQ, HEADS, TOK, DIM), BF), pltpu.SemaphoreType.DMA((HEADS // GROUP,))],
+        space=(VMEM, HBM),
     )
     grad_mid = exchange(mid)
 
@@ -327,7 +347,7 @@
         "temporal_b",
         [SMEM] + [VMEM] * (2 + CHIPS),
         [frames, there, prob, *so],
-        [units(SEQ, 2 * HEADS)]
+        [jax.ShapeDtypeStruct((SEQ, 2, TOK, WIDTH), BF)]
         + [units(CHIPS, HEADS)] * 2
         + [jax.ShapeDtypeStruct((HEADS, SEQ, ROWS), F32)],
         estimate=LONG,
@@ -364,7 +384,15 @@
         [frame(), jax.ShapeDtypeStruct((HEADS, 2 * SEQ - 1), F32)],
     )
     total_bias = sum_of_four(sum_of_four(total, "grp", 1), "grp", 4)
-    result, grad_qt = call(unpack_kernel, "unpack", [VMEM], [returned], [frame()] * 2)
+    result, grad_qt = call(
+        unpack_kernel,
+        "unpack",
+        [VMEM],
+        [returned],
+        [frame()] * 2,
+        [pltpu.SemaphoreType.DMA((2, SEQ))],
+        space=HBM,
+    )
     return result, grad_qs, grad_ks, grad_vs, grad_qt, grad_kt, total_bias
 
 

time: 169 us -> 171 us (1.012)
    unnamed x34 -> x36, local copies, waits for them, and re-layouts: 4.5 us -> 4.5 us
  transfers between devices with their start and end apart: 26 -> 26, of which waited for: 10 -> 10; matrix products, arithmetic and copies ran while one was open for 3% -> 3% of each run, Pallas kernels for 15% -> 16%
where the time goes in v5:
time: 171 us; the launch traced here: 170 us
  waiting for transfers between devices  66.8 us (39%)
  starting transfers between devices  59.5 us (35%)
  Pallas kernels  32.6 us (19%)
  local copies, waits for them, and re-layouts  5.85 us (3%)
  matrix products  3 us (2%)
  between operations  1.75 us (1%)
    ppermute x17, waiting for transfers between devices, move(): return lax.ppermute(message, 'seq', perm)  47 us
    pallas_call x9, Pallas kernels, call(): pl.pallas_call(kernel, out_shape=tuple(outputs), in_specs=specs, out_spec...  32.6 us
    all_to_all x3, starting transfers between devices, exchange(): lax.all_to_all(packed, 'seq', split_axis=0, concat_axis=0, tiled=True)  27.4 us
    ppermute x17, starting transfers between devices, move(): return lax.ppermute(message, 'seq', perm)  25.4 us
    all_to_all x3, waiting for transfers between devices, exchange(): lax.all_to_all(packed, 'seq', split_axis=0, concat_axis=0, tiled=True)  12.5 us
    ppermute x6, waiting for transfers between devices, pair(): return lax.ppermute(terms, axis, [(i, i ^ mask) for i in range(size)])  7.3 us
    ppermute x6, starting transfers between devices, pair(): return lax.ppermute(terms, axis, [(i, i ^ mask) for i in range(size)])  6.66 us
    unnamed x36, local copies, waits for them, and re-layouts  4.5 us
  transfers between devices with their start and end apart: 26, of which 10 were waited for; matrix products, arithmetic and copies ran while one was open for 3% of the time, Pallas kernels for 16%

profile of v5, /device:TPU:1, one launch (start us, length us, event | category | flops | bytes accessed | tf_op | source)
XLA Modules:
  0.0 170.5 jit_solution(814338680462613072)
XLA Ops:
  1.3 2.8 %pack.1 = bf16[16,37,16,128]{3,2,1,0:T(8,128)(2,1)} custom-call(s32[1,1]{1,0:T(1,128)S(6)} %copy.29.clip_ref, bf16[1,256,1536]{2,1,0:T(8,128)(2,1)} %q_ref.1, bf16[1,256,1536]{2,1,0:T(8,128)(2,1)} %k_ref.1, bf16[1,256,1536]{2,1,0:T(8,128)(2,1)} %up_ref.1), custom_call_target="tpu_custom_call" | custom-call | flops 1000 | bytes 1000 | tf_op jit(solution)/shard_map/pack/pallas_call | solution.py:237
  4.1 10.1 %all-to-all-start = ((bf16[16,37,16,128]{3,2,1,0:T(8,128)(2,1)}), bf16[16,37,16,128]{3,2,1,0:T(8,128)(2,1)S(1)}, u32[]{:S(2)}, u32[]{:S(2)}) async-start(bf16[16,37,16,128]{3,2,1,0:T(8,128)(2,1)} %pack.1), calls=%async_computation | async-start | bytes 4849664 | tf_op jit(solution)/shard_map/all_to_all | solution.py:250
  16.6 4.1 %spatial_fwd.1 = (bf16[8,12,16,128]{3,2,1,0:T(8,128)(2,1)S(1)}, bf16[8,12,16,128]{3,2,1,0:T(8,128)(2,1)S(1)}, f32[12,256,256]{2,1,0:T(8,128)}) custom-call(s32[2]{0:T(128)S(1)} %pad_add_fusion.pos_ref, bf16[1,256,1536]{2,1,0:T(8,128)(2,1)S(1)} %copy-done.1, bf16[1,256,1536]{2,1,0:T(8,128)(2,1)S(1)} %copy-done.2, bf16[1,256,1536]{2,1,0:T(8,128)(2,1)S(1)} %copy-done.4), custom_call_target="tpu_custom_call" | custom-call | flops 1000 | bytes 1000 | tf_op jit(solution)/shard_map/spatial_fwd/pallas_call | solution.py:237
  21.1 1.8 %fusion.4 = f32[12,16,256]{2,0,1:T(8,128)S(1)} fusion(f32[16,256,31]{2,1,0:T(8,128)S(1)} %bitcast.10, f32[12,31]{1,0:T(8,128)S(1)} %copy-done), kind=kOutput, calls=%fused_computation.14 | convolution fusion | flops 18284544 | bytes 706000 | tf_op jit(solution)/shard_map/hr,icr->hic/dot_general | solution.py:318
  23.2 1.5 collective-permute-done.got_ref
  25.6 1.4 collective-permute-start.1
  26.9 1.3 collective-permute-start.2
  28.2 2.9 %collective-permute-start.3 = (bf16[2,12,16,128]{3,2,1,0:T(8,128)(2,1)}, bf16[2,12,16,128]{3,2,1,0:T(8,128)(2,1)}, u32[]{:S(2)}, u32[]{:S(2)}) collective-permute-start(bf16[2,12,16,128]{3,2,1,0:T(8,128)(2,1)} %get-tuple-element.69), channel_id=1, source_target_pairs={{0,6},{1,7},{2,8},{3,9},{4,10},{5,11},{6,12},{7,13},{8,14},{9,15},... | collective-permute-start | bytes 294920 | tf_op jit(solution)/shard_map/ppermute | solution.py:265
  31.1 1.6 collective-permute-start.4
  33.8 38.1 %collective-permute-done.1.refs_1_ = bf16[2,12,16,128]{3,2,1,0:T(8,128)(2,1)S(1)} collective-permute-done((bf16[2,12,16,128]{3,2,1,0:T(8,128)(2,1)S(1)}, bf16[2,12,16,128]{3,2,1,0:T(8,128)(2,1)S(1)}, u32[]{:S(2)}, u32[]{:S(2)}) %collective-permute-start.1) | collective-permute-done | bytes 98336 | tf_op jit(solution)/shard_map/ppermute | solution.py:265
  71.9 2.1 %collective-permute-start.6 = (bf16[2,12,16,128]{3,2,1,0:T(8,128)(2,1)}, bf16[2,12,16,128]{3,2,1,0:T(8,128)(2,1)}, u32[]{:S(2)}, u32[]{:S(2)}) collective-permute-start(bf16[2,12,16,128]{3,2,1,0:T(8,128)(2,1)} %get-tuple-element.72), channel_id=1, source_target_pairs={{0,12},{1,13},{2,14},{3,15},{4,0},{5,1},{6,2},{7,3},{8,4},{9,5},{1... | collective-permute-start | bytes 294920 | tf_op jit(solution)/shard_map/ppermute | solution.py:265
  74.0 1.9 %collective-permute-start.7 = (bf16[2,12,16,128]{3,2,1,0:T(8,128)(2,1)}, bf16[2,12,16,128]{3,2,1,0:T(8,128)(2,1)}, u32[]{:S(2)}, u32[]{:S(2)}) collective-permute-start(bf16[2,12,16,128]{3,2,1,0:T(8,128)(2,1)} %get-tuple-element.73), channel_id=1, source_target_pairs={{0,8},{1,9},{2,10},{3,11},{4,12},{5,13},{6,14},{7,15},{8,0},{9,1},... | collective-permute-start | bytes 294920 | tf_op jit(solution)/shard_map/ppermute | solution.py:265
  77.0 6.1 %temporal_a.1 = (f32[12,256,256]{2,1,0:T(8,128)}, bf16[16,12,16,128]{3,2,1,0:T(8,128)(2,1)S(1)}) custom-call(s32[16]{0:T(128)S(1)} %fusion.13.frames_ref, bf16[16,37,16,128]{3,2,1,0:T(8,128)(2,1)S(1)} %all-to-all-done.in_ref, f32[12,16,256]{2,1,0:T(8,128)S(1)} %copy.22.bias_ref), custom_call_target="tpu_custom_call" | custom-call | flops 1000 | bytes 1000 | tf_op jit(solution)/shard_map/temporal_a/pallas_call | solution.py:237
  84.0 8.4 %all-to-all-start.2 = ((bf16[16,12,16,128]{3,2,1,0:T(8,128)(2,1)}), bf16[16,12,16,128]{3,2,1,0:T(8,128)(2,1)}, u32[]{:S(2)}, u32[]{:S(2)}) async-start(bf16[16,12,16,128]{3,2,1,0:T(8,128)(2,1)} %copy-done.6), calls=%async_computation.2 | async-start | bytes 1572864 | tf_op jit(solution)/shard_map/all_to_all | solution.py:250
  92.5 7.1 %temporal_b.1 = (bf16[16,2,16,1536]{3,2,1,0:T(8,128)(2,1)}, bf16[8,12,16,128]{3,2,1,0:T(8,128)(2,1)S(1)}, bf16[8,12,16,128]{3,2,1,0:T(8,128)(2,1)S(1)}, f32[12,16,256]{2,1,0:T(8,128)S(1)}) custom-call(s32[16]{0:T(128)S(1)} %fusion.13.frames_ref, bf16[16,37,16,128]{3,2,1,0:T(8,128)(2,1)S(1)} %all-to-all-done.in_ref, ...), custom_call_target="tpu_custom_call" | custom-call | flops 999999995904 | bytes 1000 | tf_op jit(solution)/shard_map/temporal_b/pallas_call | solution.py:237
  102.4 1.7 collective-permute-start.10
  104.1 1.3 collective-permute-start.11
  105.4 2.9 %collective-permute-start.12 = (bf16[25,16,128]{2,1,0:T(8,128)(2,1)S(1)}, bf16[25,16,128]{2,1,0:T(8,128)(2,1)S(1)}, u32[]{:S(2)}, u32[]{:S(2)}) collective-permute-start(bf16[25,16,128]{2,1,0:T(8,128)(2,1)S(1)} %get-tuple-element.87), channel_id=1, source_target_pairs={{0,6},{1,7},{2,8},{3,9},{4,10},{5,11},{6,12},{7,13},{8,14},{9,15},... | collective-permute-start | bytes 307208 | tf_op jit(solution)/shard_map/ppermute | solution.py:265
  108.3 1.6 collective-permute-start.13
  111.0 4.0 %collective-permute-done.10.refs_1_ = bf16[25,16,128]{2,1,0:T(8,128)(2,1)S(1)} collective-permute-done((bf16[25,16,128]{2,1,0:T(8,128)(2,1)S(1)}, bf16[25,16,128]{2,1,0:T(8,128)(2,1)S(1)}, u32[]{:S(2)}, u32[]{:S(2)}) %collective-permute-start.10) | collective-permute-done | bytes 102432 | tf_op jit(solution)/shard_map/ppermute | solution.py:265
  115.5 2.2 %collective-permute-start.15 = (bf16[25,16,128]{2,1,0:T(8,128)(2,1)S(1)}, bf16[25,16,128]{2,1,0:T(8,128)(2,1)S(1)}, u32[]{:S(2)}, u32[]{:S(2)}) collective-permute-start(bf16[25,16,128]{2,1,0:T(8,128)(2,1)S(1)} %get-tuple-element.90), channel_id=1, source_target_pairs={{0,12},{1,13},{2,14},{3,15},{4,0},{5,1},{6,2},{7,3},{8,4},{9,5},{1... | collective-permute-start | bytes 307208 | tf_op jit(solution)/shard_map/ppermute | solution.py:265
  118.4 1.7 collective-permute-start.16
  120.0 8.9 %all-to-all-start.1 = ((bf16[16,2,16,1536]{3,2,1,0:T(8,128)(2,1)}), bf16[16,2,16,1536]{3,2,1,0:T(8,128)(2,1)}, u32[]{:S(2)}, u32[]{:S(2)}) async-start(bf16[16,2,16,1536]{3,2,1,0:T(8,128)(2,1)} %get-tuple-element.77), calls=%async_computation.1 | async-start | bytes 3145728 | tf_op jit(solution)/shard_map/all_to_all | solution.py:250
  129.0 2.6 %collective-permute-done.16.refs_7_ = bf16[25,16,128]{2,1,0:T(8,128)(2,1)S(1)} collective-permute-done((bf16[25,16,128]{2,1,0:T(8,128)(2,1)S(1)}, bf16[25,16,128]{2,1,0:T(8,128)(2,1)S(1)}, u32[]{:S(2)}, u32[]{:S(2)}) %collective-permute-start.16) | collective-permute-done | bytes 102432 | tf_op jit(solution)/shard_map/ppermute | solution.py:265
  131.6 7.2 %spatial_bwd.1 = (bf16[1,256,1536]{2,1,0:T(8,128)(2,1)}, bf16[1,256,1536]{2,1,0:T(8,128)(2,1)}, bf16[1,256,1536]{2,1,0:T(8,128)(2,1)}) custom-call(bf16[1,256,1536]{2,1,0:T(8,128)(2,1)S(1)} %copy-done.1, bf16[1,256,1536]{2,1,0:T(8,128)(2,1)S(1)} %copy-done.3, bf16[1,256,1536]{2,1,0:T(8,128)(2,1)S(1)} %copy-done.5, ...), custom_call_target="tpu_custom_call" | custom-call | flops 999999995904 | bytes 1000 | tf_op jit(solution)/shard_map/spatial_bwd/pallas_call | solution.py:237
  138.8 1.6 finish.1
  140.4 2.7 %collective-permute-start.19 = (f32[12,31]{1,0:T(8,128)S(1)}, f32[12,31]{1,0:T(8,128)S(1)}, u32[]{:S(2)}, u32[]{:S(2)}) collective-permute-start(f32[12,31]{1,0:T(8,128)S(1)} %get-tuple-element.106), channel_id=1, source_target_pairs={{0,48},{16,32},{32,16},{48,0},{64,112},{80,96},{96,80},{112,64},{1... | collective-permute-start | bytes 4472 | tf_op jit(solution)/shard_map/ppermute | solution.py:255
  144.6 3.0 %collective-permute-done.18 = f32[12,31]{1,0:T(8,128)S(1)} collective-permute-done((f32[12,31]{1,0:T(8,128)S(1)}, f32[12,31]{1,0:T(8,128)S(1)}, u32[]{:S(2)}, u32[]{:S(2)}) %collective-permute-start.18) | collective-permute-done | bytes 1520 | tf_op jit(solution)/shard_map/ppermute | solution.py:255
  147.6 2.6 %collective-permute-start.22 = (f32[12,31]{1,0:T(8,128)S(1)}, f32[12,31]{1,0:T(8,128)S(1)}, u32[]{:S(2)}, u32[]{:S(2)}) collective-permute-start(f32[12,31]{1,0:T(8,128)S(1)} %add_add_fusion.1), channel_id=1, source_target_pairs={{0,192},{16,208},{32,224},{48,240},{64,128},{80,144},{96,160},{112... | collective-permute-start | bytes 4472 | tf_op jit(solution)/shard_map/ppermute | solution.py:255
  151.8 2.6 %collective-permute-done.21 = f32[12,31]{1,0:T(8,128)S(1)} collective-permute-done((f32[12,31]{1,0:T(8,128)S(1)}, f32[12,31]{1,0:T(8,128)S(1)}, u32[]{:S(2)}, u32[]{:S(2)}) %collective-permute-start.21) | collective-permute-done | bytes 1520 | tf_op jit(solution)/shard_map/ppermute | solution.py:255
  155.0 12.5 %all-to-all-done.1.in_ref = bf16[16,2,16,1536]{3,2,1,0:T(8,128)(2,1)} async-done(((bf16[16,2,16,1536]{3,2,1,0:T(8,128)(2,1)}), bf16[16,2,16,1536]{3,2,1,0:T(8,128)(2,1)}, u32[]{:S(2)}, u32[]{:S(2)}) %all-to-all-start.1) | async-done | bytes 1572896 | tf_op jit(solution)/shard_map/all_to_all | solution.py:250
  167.5 2.8 %unpack.1 = (bf16[1,256,1536]{2,1,0:T(8,128)(2,1)}, bf16[1,256,1536]{2,1,0:T(8,128)(2,1)}) custom-call(bf16[16,2,16,1536]{3,2,1,0:T(8,128)(2,1)} %all-to-all-done.1.in_ref), custom_call_target="tpu_custom_call" | custom-call | flops 1000 | bytes 1000 | tf_op jit(solution)/shard_map/unpack/pallas_call | solution.py:237
  (79 shorter events, 15.7 us)
Async XLA Ops:
  0.6 20.5 %copy-start = (f32[12,31]{1,0:T(8,128)S(1)}, f32[12,31]{1,0:T(8,128)}, u32[]{:S(2)}) copy-start(f32[12,31]{1,0:T(8,128)} %param.15) | copy-start | bytes 4468
  4.1 10.2 %copy-start.16 = (s32[16]{0:T(128)S(1)}, s32[16]{0:T(128)}, u32[]{:S(2)}) copy-start(s32[16]{0:T(128)} %constant.37) | copy-start | bytes 196
  4.1 10.3 %copy-start.1 = (bf16[1,256,1536]{2,1,0:T(8,128)(2,1)S(1)}, bf16[1,256,1536]{2,1,0:T(8,128)(2,1)}, u32[]{:S(2)}) copy-start(bf16[1,256,1536]{2,1,0:T(8,128)(2,1)} %q_ref.3) | copy-start | bytes 2359300
  4.1 71.8 %all-to-all-start = ((bf16[16,37,16,128]{3,2,1,0:T(8,128)(2,1)}), bf16[16,37,16,128]{3,2,1,0:T(8,128)(2,1)S(1)}, u32[]{:S(2)}, u32[]{:S(2)}) async-start(bf16[16,37,16,128]{3,2,1,0:T(8,128)(2,1)} %pack.1), calls=%async_computation | async-start | bytes 4849664 | tf_op jit(solution)/shard_map/all_to_all | solution.py:250
  21.1 52.9 %copy-start.13 = (f32[16,16,16,31]{3,2,1,0:T(8,128)}, f32[16,16,16,31]{3,2,1,0:T(8,128)S(1)}, u32[]{:S(2)}) copy-start(f32[16,16,16,31]{3,2,1,0:T(8,128)S(1)} %broadcast_in_dim.2) | copy-start | bytes 1523716
  22.9 1.8 %collective-permute-start = (bf16[8,12,16,128]{3,2,1,0:T(8,128)(2,1)S(1)}, bf16[8,12,16,128]{3,2,1,0:T(8,128)(2,1)S(1)}, u32[]{:S(2)}, u32[]{:S(2)}) collective-permute-start(bf16[8,12,16,128]{3,2,1,0:T(8,128)(2,1)S(1)} %get-tuple-element.64), channel_id=1, source_target_pairs={{0,1},{1,0},{2,3},{3,2},{4,5},{5,4},{6,7},{7,6},{8,9},{9,8},{10,11... | collective-permute-start | bytes 1179656 | tf_op jit(solution)/shard_map/ppermute | solution.py:265
  25.6 46.4 %collective-permute-start.1 = (bf16[2,12,16,128]{3,2,1,0:T(8,128)(2,1)S(1)}, bf16[2,12,16,128]{3,2,1,0:T(8,128)(2,1)S(1)}, u32[]{:S(2)}, u32[]{:S(2)}) collective-permute-start(bf16[2,12,16,128]{3,2,1,0:T(8,128)(2,1)S(1)} %get-tuple-element.67), channel_id=1, source_target_pairs={{0,2},{1,3},{2,4},{3,5},{4,6},{5,7},{6,8},{7,9},{8,10},{9,11},{10,... | collective-permute-start | bytes 294920 | tf_op jit(solution)/shard_map/ppermute | solution.py:265
  26.9 47.0 %collective-permute-start.2 = (bf16[2,12,16,128]{3,2,1,0:T(8,128)(2,1)S(1)}, bf16[2,12,16,128]{3,2,1,0:T(8,128)(2,1)S(1)}, u32[]{:S(2)}, u32[]{:S(2)}) collective-permute-start(bf16[2,12,16,128]{3,2,1,0:T(8,128)(2,1)S(1)} %get-tuple-element.68), channel_id=1, source_target_pairs={{0,14},{1,15},{2,0},{3,1},{4,2},{5,3},{6,4},{7,5},{8,6},{9,7},{10,... | collective-permute-start | bytes 294920 | tf_op jit(solution)/shard_map/ppermute | solution.py:265
  28.2 64.2 %collective-permute-start.3 = (bf16[2,12,16,128]{3,2,1,0:T(8,128)(2,1)}, bf16[2,12,16,128]{3,2,1,0:T(8,128)(2,1)}, u32[]{:S(2)}, u32[]{:S(2)}) collective-permute-start(bf16[2,12,16,128]{3,2,1,0:T(8,128)(2,1)} %get-tuple-element.69), channel_id=1, source_target_pairs={{0,6},{1,7},{2,8},{3,9},{4,10},{5,11},{6,12},{7,13},{8,14},{9,15},... | collective-permute-start | bytes 294920 | tf_op jit(solution)/shard_map/ppermute | solution.py:265
  31.1 61.3 %collective-permute-start.4 = (bf16[2,12,16,128]{3,2,1,0:T(8,128)(2,1)}, bf16[2,12,16,128]{3,2,1,0:T(8,128)(2,1)}, u32[]{:S(2)}, u32[]{:S(2)}) collective-permute-start(bf16[2,12,16,128]{3,2,1,0:T(8,128)(2,1)} %get-tuple-element.70), channel_id=1, source_target_pairs={{0,10},{1,11},{2,12},{3,13},{4,14},{5,15},{6,0},{7,1},{8,2},{9,3},... | collective-permute-start | bytes 294920 | tf_op jit(solution)/shard_map/ppermute | solution.py:265
  32.7 59.7 %collective-permute-start.5 = (bf16[2,12,16,128]{3,2,1,0:T(8,128)(2,1)}, bf16[2,12,16,128]{3,2,1,0:T(8,128)(2,1)}, u32[]{:S(2)}, u32[]{:S(2)}) collective-permute-start(bf16[2,12,16,128]{3,2,1,0:T(8,128)(2,1)} %get-tuple-element.71), channel_id=1, source_target_pairs={{0,4},{1,5},{2,6},{3,7},{4,8},{5,9},{6,10},{7,11},{8,12},{9,13},{1... | collective-permute-start | bytes 294920 | tf_op jit(solution)/shard_map/ppermute | solution.py:265
  71.9 20.5 %collective-permute-start.6 = (bf16[2,12,16,128]{3,2,1,0:T(8,128)(2,1)}, bf16[2,12,16,128]{3,2,1,0:T(8,128)(2,1)}, u32[]{:S(2)}, u32[]{:S(2)}) collective-permute-start(bf16[2,12,16,128]{3,2,1,0:T(8,128)(2,1)} %get-tuple-element.72), channel_id=1, source_target_pairs={{0,12},{1,13},{2,14},{3,15},{4,0},{5,1},{6,2},{7,3},{8,4},{9,5},{1... | collective-permute-start | bytes 294920 | tf_op jit(solution)/shard_map/ppermute | solution.py:265
  74.0 18.5 %collective-permute-start.7 = (bf16[2,12,16,128]{3,2,1,0:T(8,128)(2,1)}, bf16[2,12,16,128]{3,2,1,0:T(8,128)(2,1)}, u32[]{:S(2)}, u32[]{:S(2)}) collective-permute-start(bf16[2,12,16,128]{3,2,1,0:T(8,128)(2,1)} %get-tuple-element.73), channel_id=1, source_target_pairs={{0,8},{1,9},{2,10},{3,11},{4,12},{5,13},{6,14},{7,15},{8,0},{9,1},... | collective-permute-start | bytes 294920 | tf_op jit(solution)/shard_map/ppermute | solution.py:265
  84.0 36.1 %all-to-all-start.2 = ((bf16[16,12,16,128]{3,2,1,0:T(8,128)(2,1)}), bf16[16,12,16,128]{3,2,1,0:T(8,128)(2,1)}, u32[]{:S(2)}, u32[]{:S(2)}) async-start(bf16[16,12,16,128]{3,2,1,0:T(8,128)(2,1)} %copy-done.6), calls=%async_computation.2 | async-start | bytes 1572864 | tf_op jit(solution)/shard_map/all_to_all | solution.py:250
  99.6 2.8 %collective-permute-start.9 = (bf16[8,12,16,128]{3,2,1,0:T(8,128)(2,1)S(1)}, bf16[8,12,16,128]{3,2,1,0:T(8,128)(2,1)S(1)}, u32[]{:S(2)}, u32[]{:S(2)}) collective-permute-start(bf16[8,12,16,128]{3,2,1,0:T(8,128)(2,1)S(1)} %get-tuple-element.83), channel_id=1, source_target_pairs={{0,1},{1,0},{2,3},{3,2},{4,5},{5,4},{6,7},{7,6},{8,9},{9,8},{10,11... | collective-permute-start | bytes 1179656 | tf_op jit(solution)/shard_map/ppermute | solution.py:265
  101.0 30.6 %copy-start.3 = (bf16[1,256,1536]{2,1,0:T(8,128)(2,1)S(1)}, bf16[1,256,1536]{2,1,0:T(8,128)(2,1)}, u32[]{:S(2)}) copy-start(bf16[1,256,1536]{2,1,0:T(8,128)(2,1)} %k_ref.3) | copy-start | bytes 2359300
  101.0 30.6 %copy-start.5 = (bf16[1,256,1536]{2,1,0:T(8,128)(2,1)S(1)}, bf16[1,256,1536]{2,1,0:T(8,128)(2,1)}, u32[]{:S(2)}) copy-start(bf16[1,256,1536]{2,1,0:T(8,128)(2,1)} %v_ref.1) | copy-start | bytes 2359300
  101.0 1.3 collective-permute-start.8
  102.4 12.5 %collective-permute-start.10 = (bf16[25,16,128]{2,1,0:T(8,128)(2,1)S(1)}, bf16[25,16,128]{2,1,0:T(8,128)(2,1)S(1)}, u32[]{:S(2)}, u32[]{:S(2)}) collective-permute-start(bf16[25,16,128]{2,1,0:T(8,128)(2,1)S(1)} %get-tuple-element.85), channel_id=1, source_target_pairs={{0,2},{1,3},{2,4},{3,5},{4,6},{5,7},{6,8},{7,9},{8,10},{9,11},{10,... | collective-permute-start | bytes 307208 | tf_op jit(solution)/shard_map/ppermute | solution.py:265
  104.1 13.6 %collective-permute-start.11 = (bf16[25,16,128]{2,1,0:T(8,128)(2,1)S(1)}, bf16[25,16,128]{2,1,0:T(8,128)(2,1)S(1)}, u32[]{:S(2)}, u32[]{:S(2)}) collective-permute-start(bf16[25,16,128]{2,1,0:T(8,128)(2,1)S(1)} %get-tuple-element.86), channel_id=1, source_target_pairs={{0,14},{1,15},{2,0},{3,1},{4,2},{5,3},{6,4},{7,5},{8,6},{9,7},{10,... | collective-permute-start | bytes 307208 | tf_op jit(solution)/shard_map/ppermute | solution.py:265
  105.4 23.5 %collective-permute-start.12 = (bf16[25,16,128]{2,1,0:T(8,128)(2,1)S(1)}, bf16[25,16,128]{2,1,0:T(8,128)(2,1)S(1)}, u32[]{:S(2)}, u32[]{:S(2)}) collective-permute-start(bf16[25,16,128]{2,1,0:T(8,128)(2,1)S(1)} %get-tuple-element.87), channel_id=1, source_target_pairs={{0,6},{1,7},{2,8},{3,9},{4,10},{5,11},{6,12},{7,13},{8,14},{9,15},... | collective-permute-start | bytes 307208 | tf_op jit(solution)/shard_map/ppermute | solution.py:265
  108.3 20.7 %collective-permute-start.13 = (bf16[25,16,128]{2,1,0:T(8,128)(2,1)S(1)}, bf16[25,16,128]{2,1,0:T(8,128)(2,1)S(1)}, u32[]{:S(2)}, u32[]{:S(2)}) collective-permute-start(bf16[25,16,128]{2,1,0:T(8,128)(2,1)S(1)} %get-tuple-element.88), channel_id=1, source_target_pairs={{0,10},{1,11},{2,12},{3,13},{4,14},{5,15},{6,0},{7,1},{8,2},{9,3},... | collective-permute-start | bytes 307208 | tf_op jit(solution)/shard_map/ppermute | solution.py:265
  109.9 19.1 %collective-permute-start.14 = (bf16[25,16,128]{2,1,0:T(8,128)(2,1)S(1)}, bf16[25,16,128]{2,1,0:T(8,128)(2,1)S(1)}, u32[]{:S(2)}, u32[]{:S(2)}) collective-permute-start(bf16[25,16,128]{2,1,0:T(8,128)(2,1)S(1)} %get-tuple-element.89), channel_id=1, source_target_pairs={{0,4},{1,5},{2,6},{3,7},{4,8},{5,9},{6,10},{7,11},{8,12},{9,13},{1... | collective-permute-start | bytes 307208 | tf_op jit(solution)/shard_map/ppermute | solution.py:265
  115.5 13.4 %collective-permute-start.15 = (bf16[25,16,128]{2,1,0:T(8,128)(2,1)S(1)}, bf16[25,16,128]{2,1,0:T(8,128)(2,1)S(1)}, u32[]{:S(2)}, u32[]{:S(2)}) collective-permute-start(bf16[25,16,128]{2,1,0:T(8,128)(2,1)S(1)} %get-tuple-element.90), channel_id=1, source_target_pairs={{0,12},{1,13},{2,14},{3,15},{4,0},{5,1},{6,2},{7,3},{8,4},{9,5},{1... | collective-permute-start | bytes 307208 | tf_op jit(solution)/shard_map/ppermute | solution.py:265
  118.4 13.2 %collective-permute-start.16 = (bf16[25,16,128]{2,1,0:T(8,128)(2,1)S(1)}, bf16[25,16,128]{2,1,0:T(8,128)(2,1)S(1)}, u32[]{:S(2)}, u32[]{:S(2)}) collective-permute-start(bf16[25,16,128]{2,1,0:T(8,128)(2,1)S(1)} %get-tuple-element.91), channel_id=1, source_target_pairs={{0,8},{1,9},{2,10},{3,11},{4,12},{5,13},{6,14},{7,15},{8,0},{9,1},... | collective-permute-start | bytes 307208 | tf_op jit(solution)/shard_map/ppermute | solution.py:265
  120.0 47.4 %all-to-all-start.1 = ((bf16[16,2,16,1536]{3,2,1,0:T(8,128)(2,1)}), bf16[16,2,16,1536]{3,2,1,0:T(8,128)(2,1)}, u32[]{:S(2)}, u32[]{:S(2)}) async-start(bf16[16,2,16,1536]{3,2,1,0:T(8,128)(2,1)} %get-tuple-element.77), calls=%async_computation.1 | async-start | bytes 3145728 | tf_op jit(solution)/shard_map/all_to_all | solution.py:250
  140.4 4.2 %collective-permute-start.19 = (f32[12,31]{1,0:T(8,128)S(1)}, f32[12,31]{1,0:T(8,128)S(1)}, u32[]{:S(2)}, u32[]{:S(2)}) collective-permute-start(f32[12,31]{1,0:T(8,128)S(1)} %get-tuple-element.106), channel_id=1, source_target_pairs={{0,48},{16,32},{32,16},{48,0},{64,112},{80,96},{96,80},{112,64},{1... | collective-permute-start | bytes 4472 | tf_op jit(solution)/shard_map/ppermute | solution.py:255
  143.2 4.4 %collective-permute-start.18 = (f32[12,31]{1,0:T(8,128)S(1)}, f32[12,31]{1,0:T(8,128)S(1)}, u32[]{:S(2)}, u32[]{:S(2)}) collective-permute-start(f32[12,31]{1,0:T(8,128)S(1)} %get-tuple-element.106), channel_id=1, source_target_pairs={{0,32},{16,48},{32,0},{48,16},{64,96},{80,112},{96,64},{112,80},{1... | collective-permute-start | bytes 4472 | tf_op jit(solution)/shard_map/ppermute | solution.py:255
  143.5 4.1 %collective-permute-start.17 = (f32[12,31]{1,0:T(8,128)S(1)}, f32[12,31]{1,0:T(8,128)S(1)}, u32[]{:S(2)}, u32[]{:S(2)}) collective-permute-start(f32[12,31]{1,0:T(8,128)S(1)} %get-tuple-element.106), channel_id=1, source_target_pairs={{0,16},{16,0},{32,48},{48,32},{64,80},{80,64},{96,112},{112,96},{1... | collective-permute-start | bytes 4472 | tf_op jit(solution)/shard_map/ppermute | solution.py:255
  147.6 4.2 %collective-permute-start.22 = (f32[12,31]{1,0:T(8,128)S(1)}, f32[12,31]{1,0:T(8,128)S(1)}, u32[]{:S(2)}, u32[]{:S(2)}) collective-permute-start(f32[12,31]{1,0:T(8,128)S(1)} %add_add_fusion.1), channel_id=1, source_target_pairs={{0,192},{16,208},{32,224},{48,240},{64,128},{80,144},{96,160},{112... | collective-permute-start | bytes 4472 | tf_op jit(solution)/shard_map/ppermute | solution.py:255
  150.2 4.2 %collective-permute-start.21 = (f32[12,31]{1,0:T(8,128)S(1)}, f32[12,31]{1,0:T(8,128)S(1)}, u32[]{:S(2)}, u32[]{:S(2)}) collective-permute-start(f32[12,31]{1,0:T(8,128)S(1)} %add_add_fusion.1), channel_id=1, source_target_pairs={{0,128},{16,144},{32,160},{48,176},{64,192},{80,208},{96,224},{112... | collective-permute-start | bytes 4472 | tf_op jit(solution)/shard_map/ppermute | solution.py:255
  150.7 3.7 %collective-permute-start.20 = (f32[12,31]{1,0:T(8,128)S(1)}, f32[12,31]{1,0:T(8,128)S(1)}, u32[]{:S(2)}, u32[]{:S(2)}) collective-permute-start(f32[12,31]{1,0:T(8,128)S(1)} %add_add_fusion.1), channel_id=1, source_target_pairs={{0,64},{16,80},{32,96},{48,112},{64,0},{80,16},{96,32},{112,48},{1... | collective-permute-start | bytes 4472 | tf_op jit(solution)/shard_map/ppermute | solution.py:255
  (12 other events, 50.0 us)

commit v6 on v5

--- a/solution.py
+++ b/solution.py
@@ -7,6 +7,7 @@
 
 HEADS = 12
 DIM = 128
+RELS = 31
 SEQ = 16
 CHIPS = 8
 TOK = 16
@@ -16,9 +17,8 @@
 NEG = -1e30
 BF = jnp.bfloat16
 F32 = jnp.float32
-PARAMS = pltpu.CompilerParams(vmem_limit_bytes=48 * 1024 * 1024)
+PARAMS = pltpu.CompilerParams(vmem_limit_bytes=24 * 1024 * 1024)
 PARTS = 4
-GROUP = 3
 LONG = 10**12
 VMEM = pl.BlockSpec(memory_space=pltpu.VMEM)
 SMEM = pl.BlockSpec(memory_space=pltpu.SMEM)
@@ -132,7 +132,7 @@
             give_ref[shift, h] = jnp.where(first, odd, even).astype(BF)
 
 
-def merge_kernel(keep_ref, got_ref, bias_ref, *outs):
+def merge_kernel(keep_ref, got_ref, *outs):
     for out, shift in zip(outs, (0,) + SHIFTS):
         out[0] = keep_ref[shift % CHIPS]
         out[1] = got_ref[shift % CHIPS]
@@ -163,7 +163,16 @@
         gk_ref[0, :, head(h)] = mm_tn(low, q).astype(BF)
 
 
-def temporal_a_kernel(frames_ref, in_ref, bias_ref, prob_ref, mid_ref, made, sems):
+def bias_kernel(rel_ref, offsets_ref, out_ref):
+    offsets = offsets_ref[...]
+    for h in range(HEADS):
+        table = jnp.zeros((SEQ, ROWS), F32)
+        for r in range(RELS):
+            table = jnp.where(offsets == r, rel_ref[h, r], table)
+        out_ref[h] = table
+
+
+def temporal_a_kernel(frames_ref, in_ref, bias_ref, prob_ref, mid_ref):
     row = lax.broadcasted_iota(jnp.int32, (ROWS, ROWS), 0)
     col = lax.broadcasted_iota(jnp.int32, (ROWS, ROWS), 1)
     clip = slot_rows(frames_ref, in_ref, 3 * HEADS).astype(F32)
@@ -171,7 +180,6 @@
     same = (row & (TOK - 1)) == (col & (TOK - 1))
     same &= jnp.concatenate([clip] * 2, axis=1) == jnp.concatenate([other] * 2, axis=0)
     mask = jnp.where(same, 0.0, NEG)
-    copies = []
     for h in range(HEADS):
         q, k, up = (slot_rows(frames_ref, in_ref, i * HEADS + h) for i in range(3))
         bias = jnp.broadcast_to(bias_ref[h][:, None, :], (SEQ, TOK, ROWS)).reshape(ROWS, ROWS)
@@ -179,15 +187,7 @@
         prob_ref[h] = prob
         mid = mm_tn(prob.astype(BF), up).astype(BF)
         for s in range(SEQ):
-            made[frames_ref[s], h] = mid[s * TOK:(s + 1) * TOK]
-        if (h + 1) % GROUP == 0:
-            at = (slice(None), pl.ds(h + 1 - GROUP, GROUP))
-            copies.append(
-                pltpu.make_async_copy(made.at[at], mid_ref.at[at], sems.at[h // GROUP])
-            )
-            copies[-1].start()
-    for copy in copies:
-        copy.wait()
+            mid_ref[frames_ref[s], h] = mid[s * TOK:(s + 1) * TOK]
 
 
 def temporal_b_kernel(frames_ref, in_ref, prob_ref, *refs):
@@ -230,7 +230,7 @@
             mine = ((z - shift) & (CHIPS - 1)) == chip
             total += jnp.where(mine, ref[2 * HEADS].astype(F32), 0.0)
     total = total + pltpu.roll(total, DIM - 32, 1) + pltpu.roll(total, DIM - 64, 1)
-    bias_ref[...] = total[:HEADS, :2 * SEQ - 1]
+    bias_ref[...] = total[:HEADS, :RELS]
 
 
 def call(kernel, name, specs, inputs, outputs, scratch=(), estimate=1000, params=PARAMS, space=VMEM):
@@ -238,7 +238,7 @@
         kernel,
         out_shape=tuple(outputs),
         in_specs=specs,
-        out_specs=space if isinstance(space, tuple) else (space,) * len(outputs),
+        out_specs=(space,) * len(outputs),
         scratch_shapes=scratch,
         compiler_params=params,
         cost_estimate=pl.CostEstimate(flops=estimate, bytes_accessed=1000, transcendentals=0),
@@ -276,12 +276,6 @@
         parts.append(jnp.pad(part, ((0, TOK - HEADS), (0, 1))))
         terms = terms - part
     return jnp.pad(jnp.concatenate(parts, axis=1), ((0, 0), (0, DIM - 96))).astype(BF)
-
-
-def offsets_table(frames):
-    offset = frames[:, None] - frames[None, :] + (SEQ - 1)
-    slots = jnp.arange(2 * SEQ - 1, dtype=jnp.int32)
-    return (offset[:, :, None] == slots[None, None, :]).astype(F32)
 
 
 def per_device(
@@ -314,8 +308,15 @@
 
     spatial = [q_spatial, k_spatial, v_spatial]
     spatial, rel_bias, frames, _ = lax.optimization_barrier((spatial, rel_bias, frames, packed))
-    wide = jnp.repeat(offsets_table(frames), TOK, axis=1)
-    bias = jnp.einsum("hr,icr->hic", rel_bias, wide, precision=lax.Precision.HIGHEST)
+    offsets = frames[:, None] - jnp.repeat(frames, TOK)[None, :] + (SEQ - 1)
+    (bias,) = call(
+        bias_kernel,
+        "bias",
+        [SMEM, VMEM],
+        [rel_bias, offsets],
+        [jax.ShapeDtypeStruct((HEADS, SEQ, ROWS), F32)],
+    )
+    wide = (offsets[:, :, None] == jnp.arange(RELS, dtype=jnp.int32)).astype(F32)
     keep_so, give_so, sp_prob = call(
         spatial_fwd_kernel,
         "spatial_fwd",
@@ -326,7 +327,7 @@
     give_so, bias = lax.optimization_barrier((give_so, bias))
     got_so = move(give_so, 0, 1)
     so_messages = call(
-        merge_kernel, "merge", [VMEM] * 3, [keep_so, got_so, bias], [units(2, HEADS)] * CHIPS
+        merge_kernel, "merge", [VMEM] * 2, [keep_so, got_so], [units(2, HEADS)] * CHIPS
     )
     so = sent(so_messages)
 
@@ -337,8 +338,6 @@
         [SMEM] + [VMEM] * 2,
         [frames, there, bias],
         [probs(), units(SEQ, HEADS)],
-        [pltpu.VMEM((SEQ, HEADS, TOK, DIM), BF), pltpu.SemaphoreType.DMA((HEADS // GROUP,))],
-        space=(VMEM, HBM),
     )
     grad_mid = exchange(mid)
 
@@ -381,7 +380,7 @@
         "finish",
         [SMEM] + [VMEM] * CHIPS,
         [pos, *last],
-        [frame(), jax.ShapeDtypeStruct((HEADS, 2 * SEQ - 1), F32)],
+        [frame(), jax.ShapeDtypeStruct((HEADS, RELS), F32)],
     )
     total_bias = sum_of_four(sum_of_four(total, "grp", 1), "grp", 4)
     result, grad_qt = call(

time: 171 us -> 170 us (level)
  local copies, waits for them, and re-layouts: 5.85 us -> 15.9 us
  Pallas kernels: 32.6 us -> 26.5 us
  matrix products: 3 us -> 0.42 us
  waiting for transfers between devices: 66.8 us -> 64.9 us
    unnamed x36 -> x48, local copies, waits for them, and re-layouts: 4.5 us -> 15.7 us
    pallas_call x9 -> x10, Pallas kernels: 32.6 us -> 26.5 us  [call(): pl.pallas_call(kernel, out_shape=tuple(outputs), in_specs=specs, out_spec...]
    all_to_all x3, waiting for transfers between devices: 12.5 us -> 10.7 us  [exchange(): lax.all_to_all(packed, 'seq', split_axis=0, concat_axis=0, tiled=True)]
    dot_general x1 -> x0, matrix products: 1.8 us -> none  [per_device(): jnp.einsum('hr,icr->hic', rel_bias, wide, precision=lax.Precision.HIGHEST)]
  transfers between devices with their start and end apart: 26 -> 26, of which waited for: 10 -> 10; matrix products, arithmetic and copies ran while one was open for 3% -> 1% of each run, Pallas kernels for 16% -> 12%
where the time goes in v6:
time: 170 us
  waiting for transfers between devices  64.9 us (38%)
  starting transfers between devices  59.3 us (35%)
  Pallas kernels  26.5 us (16%)
  local copies, waits for them, and re-layouts  15.9 us (9%)
  between operations  1.7 us (1%)
    ppermute x17, waiting for transfers between devices, move(): return lax.ppermute(message, 'seq', perm)  46.8 us
    ppermute x17, starting transfers between devices, move(): return lax.ppermute(message, 'seq', perm)  26.8 us
    pallas_call x10, Pallas kernels, call(): pl.pallas_call(kernel, out_shape=tuple(outputs), in_specs=specs, out_spec...  26.5 us
    all_to_all x3, starting transfers between devices, exchange(): lax.all_to_all(packed, 'seq', split_axis=0, concat_axis=0, tiled=True)  25.9 us
    unnamed x48, local copies, waits for them, and re-layouts  15.7 us
    all_to_all x3, waiting for transfers between devices, exchange(): lax.all_to_all(packed, 'seq', split_axis=0, concat_axis=0, tiled=True)  10.7 us
    ppermute x6, waiting for transfers between devices, pair(): return lax.ppermute(terms, axis, [(i, i ^ mask) for i in range(size)])  7.46 us
    ppermute x6, starting transfers between devices, pair(): return lax.ppermute(terms, axis, [(i, i ^ mask) for i in range(size)])  6.65 us
  transfers between devices with their start and end apart: 26, of which 10 were waited for; matrix products, arithmetic and copies ran while one was open for 1% of the time, Pallas kernels for 12%

profile of v6, /device:TPU:1, one launch (start us, length us, event | category | flops | bytes accessed | tf_op | source)
XLA Modules:
  0.0 169.5 jit_solution(2468547951781419509)
XLA Ops:
  1.3 2.8 %pack.1 = bf16[16,37,16,128]{3,2,1,0:T(8,128)(2,1)} custom-call(s32[1,1]{1,0:T(1,128)S(6)} %copy.20.clip_ref, bf16[1,256,1536]{2,1,0:T(8,128)(2,1)} %q_ref.1, bf16[1,256,1536]{2,1,0:T(8,128)(2,1)} %k_ref.1, bf16[1,256,1536]{2,1,0:T(8,128)(2,1)} %up_ref.1), custom_call_target="tpu_custom_call" | custom-call | flops 1000 | bytes 1000 | tf_op jit(solution)/shard_map/pack/pallas_call | solution.py:237
  4.1 10.1 %all-to-all-start = ((bf16[16,37,16,128]{3,2,1,0:T(8,128)(2,1)}), bf16[16,37,16,128]{3,2,1,0:T(8,128)(2,1)S(1)}, u32[]{:S(2)}, u32[]{:S(2)}) async-start(bf16[16,37,16,128]{3,2,1,0:T(8,128)(2,1)} %pack.1), calls=%async_computation | async-start | bytes 4849664 | tf_op jit(solution)/shard_map/all_to_all | solution.py:250
  18.0 2.6 %spatial_fwd.1 = (bf16[8,12,16,128]{3,2,1,0:T(8,128)(2,1)S(1)}, bf16[8,12,16,128]{3,2,1,0:T(8,128)(2,1)S(1)}, f32[12,256,256]{2,1,0:T(8,128)S(1)}) custom-call(s32[2]{0:T(128)S(1)} %pad_add_fusion.pos_ref, bf16[1,256,1536]{2,1,0:T(8,128)(2,1)S(1)} %copy-done.1, bf16[1,256,1536]{2,1,0:T(8,128)(2,1)S(1)} %copy-done.2, bf16[1,256,1536]{2,1,0:T(8,128)(2,1)S(1)} %copy-done.4), custom_call_target="tpu_custom_call" | custom-call | flops 1000 | bytes 1000 | tf_op jit(solution)/shard_map/spatial_fwd/pallas_call | solution.py:237
  20.6 1.6 copy-done.14
  22.3 1.6 collective-permute-done.got_ref
  27.4 2.9 %collective-permute-start.3 = (bf16[2,12,16,128]{3,2,1,0:T(8,128)(2,1)}, bf16[2,12,16,128]{3,2,1,0:T(8,128)(2,1)}, u32[]{:S(2)}, u32[]{:S(2)}) collective-permute-start(bf16[2,12,16,128]{3,2,1,0:T(8,128)(2,1)} %get-tuple-element.68), channel_id=1, source_target_pairs={{0,6},{1,7},{2,8},{3,9},{4,10},{5,11},{6,12},{7,13},{8,14},{9,15},... | collective-permute-start | bytes 294920 | tf_op jit(solution)/shard_map/ppermute | solution.py:265
  30.3 1.6 collective-permute-start.4
  33.0 39.0 %collective-permute-done.1.refs_1_ = bf16[2,12,16,128]{3,2,1,0:T(8,128)(2,1)S(1)} collective-permute-done((bf16[2,12,16,128]{3,2,1,0:T(8,128)(2,1)S(1)}, bf16[2,12,16,128]{3,2,1,0:T(8,128)(2,1)S(1)}, u32[]{:S(2)}, u32[]{:S(2)}) %collective-permute-start.1) | collective-permute-done | bytes 98336 | tf_op jit(solution)/shard_map/ppermute | solution.py:265
  72.5 2.1 %collective-permute-start.6 = (bf16[2,12,16,128]{3,2,1,0:T(8,128)(2,1)}, bf16[2,12,16,128]{3,2,1,0:T(8,128)(2,1)}, u32[]{:S(2)}, u32[]{:S(2)}) collective-permute-start(bf16[2,12,16,128]{3,2,1,0:T(8,128)(2,1)} %get-tuple-element.71), channel_id=1, source_target_pairs={{0,12},{1,13},{2,14},{3,15},{4,0},{5,1},{6,2},{7,3},{8,4},{9,5},{1... | collective-permute-start | bytes 294920 | tf_op jit(solution)/shard_map/ppermute | solution.py:265
  75.3 1.7 collective-permute-start.7
  76.9 3.3 %temporal_a.1 = (f32[12,256,256]{2,1,0:T(8,128)S(1)}, bf16[16,12,16,128]{3,2,1,0:T(8,128)(2,1)S(1)}) custom-call(s32[16]{0:T(128)S(1)} %fusion.11.frames_ref, bf16[16,37,16,128]{3,2,1,0:T(8,128)(2,1)S(1)} %all-to-all-done.in_ref, f32[12,16,256]{2,1,0:T(8,128)S(1)} %bias.1.bias_ref), custom_call_target="tpu_custom_call" | custom-call | flops 1000 | bytes 1000 | tf_op jit(solution)/shard_map/temporal_a/pallas_call | solution.py:237
  81.1 1.7 copy-done.16
  82.8 8.7 %all-to-all-start.2 = ((bf16[16,12,16,128]{3,2,1,0:T(8,128)(2,1)}), bf16[16,12,16,128]{3,2,1,0:T(8,128)(2,1)}, u32[]{:S(2)}, u32[]{:S(2)}) async-start(bf16[16,12,16,128]{3,2,1,0:T(8,128)(2,1)} %copy-done.6), calls=%async_computation.2 | async-start | bytes 1572864 | tf_op jit(solution)/shard_map/all_to_all | solution.py:250
  91.5 1.9 %copy-done.17 = f32[12,256,256]{2,1,0:T(8,128)S(1)} copy-done((f32[12,256,256]{2,1,0:T(8,128)S(1)}, f32[12,256,256]{2,1,0:T(8,128)}, u32[]{:S(2)}) %copy-start.17) | copy-done | bytes 3145752
  95.2 5.0 %temporal_b.1 = (bf16[16,2,16,1536]{3,2,1,0:T(8,128)(2,1)S(1)}, bf16[8,12,16,128]{3,2,1,0:T(8,128)(2,1)S(1)}, bf16[8,12,16,128]{3,2,1,0:T(8,128)(2,1)S(1)}, f32[12,16,256]{2,1,0:T(8,128)S(1)}) custom-call(s32[16]{0:T(128)S(1)} %fusion.11.frames_ref, bf16[16,37,16,128]{3,2,1,0:T(8,128)(2,1)S(1)} %all-to-all-done.in_ref, f32[12,256,256]{2,1,0:T(8,128)S(1)} %copy-done.17, ...), custom_call_target="tpu_custom_call" | custom-call | flops 999999995904 | bytes 1000 | tf_op jit(solution)/shard_map/temporal_b/pallas_call | solution.py:237
  103.4 1.7 collective-permute-start.10
  106.3 2.9 %collective-permute-start.12 = (bf16[25,16,128]{2,1,0:T(8,128)(2,1)S(1)}, bf16[25,16,128]{2,1,0:T(8,128)(2,1)S(1)}, u32[]{:S(2)}, u32[]{:S(2)}) collective-permute-start(bf16[25,16,128]{2,1,0:T(8,128)(2,1)S(1)} %get-tuple-element.87), channel_id=1, source_target_pairs={{0,6},{1,7},{2,8},{3,9},{4,10},{5,11},{6,12},{7,13},{8,14},{9,15},... | collective-permute-start | bytes 307208 | tf_op jit(solution)/shard_map/ppermute | solution.py:265
  109.2 1.6 collective-permute-start.13
  111.9 2.1 %collective-permute-done.10.refs_1_ = bf16[25,16,128]{2,1,0:T(8,128)(2,1)S(1)} collective-permute-done((bf16[25,16,128]{2,1,0:T(8,128)(2,1)S(1)}, bf16[25,16,128]{2,1,0:T(8,128)(2,1)S(1)}, u32[]{:S(2)}, u32[]{:S(2)}) %collective-permute-start.10) | collective-permute-done | bytes 102432 | tf_op jit(solution)/shard_map/ppermute | solution.py:265
  114.6 2.2 %collective-permute-start.15 = (bf16[25,16,128]{2,1,0:T(8,128)(2,1)S(1)}, bf16[25,16,128]{2,1,0:T(8,128)(2,1)S(1)}, u32[]{:S(2)}, u32[]{:S(2)}) collective-permute-start(bf16[25,16,128]{2,1,0:T(8,128)(2,1)S(1)} %get-tuple-element.90), channel_id=1, source_target_pairs={{0,12},{1,13},{2,14},{3,15},{4,0},{5,1},{6,2},{7,3},{8,4},{9,5},{1... | collective-permute-start | bytes 307208 | tf_op jit(solution)/shard_map/ppermute | solution.py:265
  117.5 3.5 %collective-permute-start.16 = (bf16[25,16,128]{2,1,0:T(8,128)(2,1)S(1)}, bf16[25,16,128]{2,1,0:T(8,128)(2,1)S(1)}, u32[]{:S(2)}, u32[]{:S(2)}) collective-permute-start(bf16[25,16,128]{2,1,0:T(8,128)(2,1)S(1)} %get-tuple-element.91), channel_id=1, source_target_pairs={{0,8},{1,9},{2,10},{3,11},{4,12},{5,13},{6,14},{7,15},{8,0},{9,1},... | collective-permute-start | bytes 307208 | tf_op jit(solution)/shard_map/ppermute | solution.py:265
  120.9 7.1 %all-to-all-start.1 = ((bf16[16,2,16,1536]{3,2,1,0:T(8,128)(2,1)}), bf16[16,2,16,1536]{3,2,1,0:T(8,128)(2,1)}, u32[]{:S(2)}, u32[]{:S(2)}) async-start(bf16[16,2,16,1536]{3,2,1,0:T(8,128)(2,1)} %copy-done), calls=%async_computation.1 | async-start | bytes 3145728 | tf_op jit(solution)/shard_map/all_to_all | solution.py:250
  128.1 3.2 %collective-permute-done.16.refs_7_ = bf16[25,16,128]{2,1,0:T(8,128)(2,1)S(1)} collective-permute-done((bf16[25,16,128]{2,1,0:T(8,128)(2,1)S(1)}, bf16[25,16,128]{2,1,0:T(8,128)(2,1)S(1)}, u32[]{:S(2)}, u32[]{:S(2)}) %collective-permute-start.16) | collective-permute-done | bytes 102432 | tf_op jit(solution)/shard_map/ppermute | solution.py:265
  131.3 1.9 %copy-done.15 = f32[12,256,256]{2,1,0:T(8,128)S(1)} copy-done((f32[12,256,256]{2,1,0:T(8,128)S(1)}, f32[12,256,256]{2,1,0:T(8,128)}, u32[]{:S(2)}) %copy-start.15) | copy-done | bytes 3145752
  133.2 6.3 %spatial_bwd.1 = (bf16[1,256,1536]{2,1,0:T(8,128)(2,1)}, bf16[1,256,1536]{2,1,0:T(8,128)(2,1)}, bf16[1,256,1536]{2,1,0:T(8,128)(2,1)}) custom-call(bf16[1,256,1536]{2,1,0:T(8,128)(2,1)S(1)} %copy-done.1, bf16[1,256,1536]{2,1,0:T(8,128)(2,1)S(1)} %copy-done.3, bf16[1,256,1536]{2,1,0:T(8,128)(2,1)S(1)} %copy-done.5, f32[12,256,256]{2,1,0:T(8,128)S(1)} %copy-done.15, ...), custom_call_target="tpu_custom_call" | custom-call | flops 999999995904 | bytes 1000 | tf_op jit(solution)/shard_map/spatial_bwd/pallas_call | solution.py:237
  139.6 1.6 finish.1
  141.2 2.7 %collective-permute-start.19 = (f32[12,31]{1,0:T(8,128)S(1)}, f32[12,31]{1,0:T(8,128)S(1)}, u32[]{:S(2)}, u32[]{:S(2)}) collective-permute-start(f32[12,31]{1,0:T(8,128)S(1)} %get-tuple-element.106), channel_id=1, source_target_pairs={{0,48},{16,32},{32,16},{48,0},{64,112},{80,96},{96,80},{112,64},{1... | collective-permute-start | bytes 4472 | tf_op jit(solution)/shard_map/ppermute | solution.py:255
  145.3 3.0 %collective-permute-done.18 = f32[12,31]{1,0:T(8,128)S(1)} collective-permute-done((f32[12,31]{1,0:T(8,128)S(1)}, f32[12,31]{1,0:T(8,128)S(1)}, u32[]{:S(2)}, u32[]{:S(2)}) %collective-permute-start.18) | collective-permute-done | bytes 1520 | tf_op jit(solution)/shard_map/ppermute | solution.py:255
  148.3 2.6 %collective-permute-start.22 = (f32[12,31]{1,0:T(8,128)S(1)}, f32[12,31]{1,0:T(8,128)S(1)}, u32[]{:S(2)}, u32[]{:S(2)}) collective-permute-start(f32[12,31]{1,0:T(8,128)S(1)} %add_add_fusion.1), channel_id=1, source_target_pairs={{0,192},{16,208},{32,224},{48,240},{64,128},{80,144},{96,160},{112... | collective-permute-start | bytes 4472 | tf_op jit(solution)/shard_map/ppermute | solution.py:255
  152.5 2.8 %collective-permute-done.21 = f32[12,31]{1,0:T(8,128)S(1)} collective-permute-done((f32[12,31]{1,0:T(8,128)S(1)}, f32[12,31]{1,0:T(8,128)S(1)}, u32[]{:S(2)}, u32[]{:S(2)}) %collective-permute-start.21) | collective-permute-done | bytes 1520 | tf_op jit(solution)/shard_map/ppermute | solution.py:255
  155.9 10.6 %all-to-all-done.1.in_ref = bf16[16,2,16,1536]{3,2,1,0:T(8,128)(2,1)} async-done(((bf16[16,2,16,1536]{3,2,1,0:T(8,128)(2,1)}), bf16[16,2,16,1536]{3,2,1,0:T(8,128)(2,1)}, u32[]{:S(2)}, u32[]{:S(2)}) %all-to-all-start.1) | async-done | bytes 1572896 | tf_op jit(solution)/shard_map/all_to_all | solution.py:250
  166.6 2.8 %unpack.1 = (bf16[1,256,1536]{2,1,0:T(8,128)(2,1)}, bf16[1,256,1536]{2,1,0:T(8,128)(2,1)}) custom-call(bf16[16,2,16,1536]{3,2,1,0:T(8,128)(2,1)} %all-to-all-done.1.in_ref), custom_call_target="tpu_custom_call" | custom-call | flops 1000 | bytes 1000 | tf_op jit(solution)/shard_map/unpack/pallas_call | solution.py:237
  (89 shorter events, 22.8 us)
Async XLA Ops:
  4.1 10.2 %copy-start.22 = (s32[16]{0:T(128)S(1)}, s32[16]{0:T(128)}, u32[]{:S(2)}) copy-start(s32[16]{0:T(128)} %constant.37) | copy-start | bytes 196
  4.1 10.2 %copy-start.23 = (s32[16]{0:T(128)S(1)}, s32[16]{0:T(128)}, u32[]{:S(2)}) copy-start(s32[16]{0:T(128)} %constant.21.clone) | copy-start | bytes 196
  4.1 10.4 %copy-start.13 = (f32[12,31]{1,0:T(8,128)S(1)}, f32[12,31]{1,0:T(8,128)}, u32[]{:S(2)}) copy-start(f32[12,31]{1,0:T(8,128)} %rel_ref) | copy-start | bytes 4468
  4.1 11.6 %copy-start.1 = (bf16[1,256,1536]{2,1,0:T(8,128)(2,1)S(1)}, bf16[1,256,1536]{2,1,0:T(8,128)(2,1)}, u32[]{:S(2)}) copy-start(bf16[1,256,1536]{2,1,0:T(8,128)(2,1)} %q_ref.3) | copy-start | bytes 2359300
  4.1 72.8 %all-to-all-start = ((bf16[16,37,16,128]{3,2,1,0:T(8,128)(2,1)}), bf16[16,37,16,128]{3,2,1,0:T(8,128)(2,1)S(1)}, u32[]{:S(2)}, u32[]{:S(2)}) async-start(bf16[16,37,16,128]{3,2,1,0:T(8,128)(2,1)} %pack.1), calls=%async_computation | async-start | bytes 4849664 | tf_op jit(solution)/shard_map/all_to_all | solution.py:250
  22.2 1.7 %collective-permute-start = (bf16[8,12,16,128]{3,2,1,0:T(8,128)(2,1)S(1)}, bf16[8,12,16,128]{3,2,1,0:T(8,128)(2,1)S(1)}, u32[]{:S(2)}, u32[]{:S(2)}) collective-permute-start(bf16[8,12,16,128]{3,2,1,0:T(8,128)(2,1)S(1)} %get-tuple-element.64), channel_id=1, source_target_pairs={{0,1},{1,0},{2,3},{3,2},{4,5},{5,4},{6,7},{7,6},{8,9},{9,8},{10,11... | collective-permute-start | bytes 1179656 | tf_op jit(solution)/shard_map/ppermute | solution.py:265
  24.7 47.2 %collective-permute-start.1 = (bf16[2,12,16,128]{3,2,1,0:T(8,128)(2,1)S(1)}, bf16[2,12,16,128]{3,2,1,0:T(8,128)(2,1)S(1)}, u32[]{:S(2)}, u32[]{:S(2)}) collective-permute-start(bf16[2,12,16,128]{3,2,1,0:T(8,128)(2,1)S(1)} %get-tuple-element.66), channel_id=1, source_target_pairs={{0,2},{1,3},{2,4},{3,5},{4,6},{5,7},{6,8},{7,9},{8,10},{9,11},{10,... | collective-permute-start | bytes 294920 | tf_op jit(solution)/shard_map/ppermute | solution.py:265
  26.1 48.5 %collective-permute-start.2 = (bf16[2,12,16,128]{3,2,1,0:T(8,128)(2,1)S(1)}, bf16[2,12,16,128]{3,2,1,0:T(8,128)(2,1)S(1)}, u32[]{:S(2)}, u32[]{:S(2)}) collective-permute-start(bf16[2,12,16,128]{3,2,1,0:T(8,128)(2,1)S(1)} %get-tuple-element.67), channel_id=1, source_target_pairs={{0,14},{1,15},{2,0},{3,1},{4,2},{5,3},{6,4},{7,5},{8,6},{9,7},{10,... | collective-permute-start | bytes 294920 | tf_op jit(solution)/shard_map/ppermute | solution.py:265
  27.4 64.1 %collective-permute-start.3 = (bf16[2,12,16,128]{3,2,1,0:T(8,128)(2,1)}, bf16[2,12,16,128]{3,2,1,0:T(8,128)(2,1)}, u32[]{:S(2)}, u32[]{:S(2)}) collective-permute-start(bf16[2,12,16,128]{3,2,1,0:T(8,128)(2,1)} %get-tuple-element.68), channel_id=1, source_target_pairs={{0,6},{1,7},{2,8},{3,9},{4,10},{5,11},{6,12},{7,13},{8,14},{9,15},... | collective-permute-start | bytes 294920 | tf_op jit(solution)/shard_map/ppermute | solution.py:265
  30.3 61.2 %collective-permute-start.4 = (bf16[2,12,16,128]{3,2,1,0:T(8,128)(2,1)}, bf16[2,12,16,128]{3,2,1,0:T(8,128)(2,1)}, u32[]{:S(2)}, u32[]{:S(2)}) collective-permute-start(bf16[2,12,16,128]{3,2,1,0:T(8,128)(2,1)} %get-tuple-element.69), channel_id=1, source_target_pairs={{0,10},{1,11},{2,12},{3,13},{4,14},{5,15},{6,0},{7,1},{8,2},{9,3},... | collective-permute-start | bytes 294920 | tf_op jit(solution)/shard_map/ppermute | solution.py:265
  31.9 59.6 %collective-permute-start.5 = (bf16[2,12,16,128]{3,2,1,0:T(8,128)(2,1)}, bf16[2,12,16,128]{3,2,1,0:T(8,128)(2,1)}, u32[]{:S(2)}, u32[]{:S(2)}) collective-permute-start(bf16[2,12,16,128]{3,2,1,0:T(8,128)(2,1)} %get-tuple-element.70), channel_id=1, source_target_pairs={{0,4},{1,5},{2,6},{3,7},{4,8},{5,9},{6,10},{7,11},{8,12},{9,13},{1... | collective-permute-start | bytes 294920 | tf_op jit(solution)/shard_map/ppermute | solution.py:265
  72.5 19.0 %collective-permute-start.6 = (bf16[2,12,16,128]{3,2,1,0:T(8,128)(2,1)}, bf16[2,12,16,128]{3,2,1,0:T(8,128)(2,1)}, u32[]{:S(2)}, u32[]{:S(2)}) collective-permute-start(bf16[2,12,16,128]{3,2,1,0:T(8,128)(2,1)} %get-tuple-element.71), channel_id=1, source_target_pairs={{0,12},{1,13},{2,14},{3,15},{4,0},{5,1},{6,2},{7,3},{8,4},{9,5},{1... | collective-permute-start | bytes 294920 | tf_op jit(solution)/shard_map/ppermute | solution.py:265
  75.3 16.3 %collective-permute-start.7 = (bf16[2,12,16,128]{3,2,1,0:T(8,128)(2,1)}, bf16[2,12,16,128]{3,2,1,0:T(8,128)(2,1)}, u32[]{:S(2)}, u32[]{:S(2)}) collective-permute-start(bf16[2,12,16,128]{3,2,1,0:T(8,128)(2,1)} %get-tuple-element.72), channel_id=1, source_target_pairs={{0,8},{1,9},{2,10},{3,11},{4,12},{5,13},{6,14},{7,15},{8,0},{9,1},... | collective-permute-start | bytes 294920 | tf_op jit(solution)/shard_map/ppermute | solution.py:265
  82.8 38.1 %all-to-all-start.2 = ((bf16[16,12,16,128]{3,2,1,0:T(8,128)(2,1)}), bf16[16,12,16,128]{3,2,1,0:T(8,128)(2,1)}, u32[]{:S(2)}, u32[]{:S(2)}) async-start(bf16[16,12,16,128]{3,2,1,0:T(8,128)(2,1)} %copy-done.6), calls=%async_computation.2 | async-start | bytes 1572864 | tf_op jit(solution)/shard_map/all_to_all | solution.py:250
  101.4 29.9 %copy-start.3 = (bf16[1,256,1536]{2,1,0:T(8,128)(2,1)S(1)}, bf16[1,256,1536]{2,1,0:T(8,128)(2,1)}, u32[]{:S(2)}) copy-start(bf16[1,256,1536]{2,1,0:T(8,128)(2,1)} %k_ref.3) | copy-start | bytes 2359300
  101.4 29.9 %copy-start.5 = (bf16[1,256,1536]{2,1,0:T(8,128)(2,1)S(1)}, bf16[1,256,1536]{2,1,0:T(8,128)(2,1)}, u32[]{:S(2)}) copy-start(bf16[1,256,1536]{2,1,0:T(8,128)(2,1)} %v_ref.1) | copy-start | bytes 2359300
  101.4 1.9 %collective-permute-start.9 = (bf16[8,12,16,128]{3,2,1,0:T(8,128)(2,1)S(1)}, bf16[8,12,16,128]{3,2,1,0:T(8,128)(2,1)S(1)}, u32[]{:S(2)}, u32[]{:S(2)}) collective-permute-start(bf16[8,12,16,128]{3,2,1,0:T(8,128)(2,1)S(1)} %get-tuple-element.83), channel_id=1, source_target_pairs={{0,1},{1,0},{2,3},{3,2},{4,5},{5,4},{6,7},{7,6},{8,9},{9,8},{10,11... | collective-permute-start | bytes 1179656 | tf_op jit(solution)/shard_map/ppermute | solution.py:265
  102.0 1.2 collective-permute-start.8
  103.4 10.6 %collective-permute-start.10 = (bf16[25,16,128]{2,1,0:T(8,128)(2,1)S(1)}, bf16[25,16,128]{2,1,0:T(8,128)(2,1)S(1)}, u32[]{:S(2)}, u32[]{:S(2)}) collective-permute-start(bf16[25,16,128]{2,1,0:T(8,128)(2,1)S(1)} %get-tuple-element.85), channel_id=1, source_target_pairs={{0,2},{1,3},{2,4},{3,5},{4,6},{5,7},{6,8},{7,9},{8,10},{9,11},{10,... | collective-permute-start | bytes 307208 | tf_op jit(solution)/shard_map/ppermute | solution.py:265
  105.0 11.8 %collective-permute-start.11 = (bf16[25,16,128]{2,1,0:T(8,128)(2,1)S(1)}, bf16[25,16,128]{2,1,0:T(8,128)(2,1)S(1)}, u32[]{:S(2)}, u32[]{:S(2)}) collective-permute-start(bf16[25,16,128]{2,1,0:T(8,128)(2,1)S(1)} %get-tuple-element.86), channel_id=1, source_target_pairs={{0,14},{1,15},{2,0},{3,1},{4,2},{5,3},{6,4},{7,5},{8,6},{9,7},{10,... | collective-permute-start | bytes 307208 | tf_op jit(solution)/shard_map/ppermute | solution.py:265
  106.3 21.7 %collective-permute-start.12 = (bf16[25,16,128]{2,1,0:T(8,128)(2,1)S(1)}, bf16[25,16,128]{2,1,0:T(8,128)(2,1)S(1)}, u32[]{:S(2)}, u32[]{:S(2)}) collective-permute-start(bf16[25,16,128]{2,1,0:T(8,128)(2,1)S(1)} %get-tuple-element.87), channel_id=1, source_target_pairs={{0,6},{1,7},{2,8},{3,9},{4,10},{5,11},{6,12},{7,13},{8,14},{9,15},... | collective-permute-start | bytes 307208 | tf_op jit(solution)/shard_map/ppermute | solution.py:265
  109.2 18.8 %collective-permute-start.13 = (bf16[25,16,128]{2,1,0:T(8,128)(2,1)S(1)}, bf16[25,16,128]{2,1,0:T(8,128)(2,1)S(1)}, u32[]{:S(2)}, u32[]{:S(2)}) collective-permute-start(bf16[25,16,128]{2,1,0:T(8,128)(2,1)S(1)} %get-tuple-element.88), channel_id=1, source_target_pairs={{0,10},{1,11},{2,12},{3,13},{4,14},{5,15},{6,0},{7,1},{8,2},{9,3},... | collective-permute-start | bytes 307208 | tf_op jit(solution)/shard_map/ppermute | solution.py:265
  110.8 17.3 %collective-permute-start.14 = (bf16[25,16,128]{2,1,0:T(8,128)(2,1)S(1)}, bf16[25,16,128]{2,1,0:T(8,128)(2,1)S(1)}, u32[]{:S(2)}, u32[]{:S(2)}) collective-permute-start(bf16[25,16,128]{2,1,0:T(8,128)(2,1)S(1)} %get-tuple-element.89), channel_id=1, source_target_pairs={{0,4},{1,5},{2,6},{3,7},{4,8},{5,9},{6,10},{7,11},{8,12},{9,13},{1... | collective-permute-start | bytes 307208 | tf_op jit(solution)/shard_map/ppermute | solution.py:265
  114.6 13.4 %collective-permute-start.15 = (bf16[25,16,128]{2,1,0:T(8,128)(2,1)S(1)}, bf16[25,16,128]{2,1,0:T(8,128)(2,1)S(1)}, u32[]{:S(2)}, u32[]{:S(2)}) collective-permute-start(bf16[25,16,128]{2,1,0:T(8,128)(2,1)S(1)} %get-tuple-element.90), channel_id=1, source_target_pairs={{0,12},{1,13},{2,14},{3,15},{4,0},{5,1},{6,2},{7,3},{8,4},{9,5},{1... | collective-permute-start | bytes 307208 | tf_op jit(solution)/shard_map/ppermute | solution.py:265
  117.5 13.8 %collective-permute-start.16 = (bf16[25,16,128]{2,1,0:T(8,128)(2,1)S(1)}, bf16[25,16,128]{2,1,0:T(8,128)(2,1)S(1)}, u32[]{:S(2)}, u32[]{:S(2)}) collective-permute-start(bf16[25,16,128]{2,1,0:T(8,128)(2,1)S(1)} %get-tuple-element.91), channel_id=1, source_target_pairs={{0,8},{1,9},{2,10},{3,11},{4,12},{5,13},{6,14},{7,15},{8,0},{9,1},... | collective-permute-start | bytes 307208 | tf_op jit(solution)/shard_map/ppermute | solution.py:265
  120.9 45.6 %all-to-all-start.1 = ((bf16[16,2,16,1536]{3,2,1,0:T(8,128)(2,1)}), bf16[16,2,16,1536]{3,2,1,0:T(8,128)(2,1)}, u32[]{:S(2)}, u32[]{:S(2)}) async-start(bf16[16,2,16,1536]{3,2,1,0:T(8,128)(2,1)} %copy-done), calls=%async_computation.1 | async-start | bytes 3145728 | tf_op jit(solution)/shard_map/all_to_all | solution.py:250
  141.2 4.2 %collective-permute-start.19 = (f32[12,31]{1,0:T(8,128)S(1)}, f32[12,31]{1,0:T(8,128)S(1)}, u32[]{:S(2)}, u32[]{:S(2)}) collective-permute-start(f32[12,31]{1,0:T(8,128)S(1)} %get-tuple-element.106), channel_id=1, source_target_pairs={{0,48},{16,32},{32,16},{48,0},{64,112},{80,96},{96,80},{112,64},{1... | collective-permute-start | bytes 4472 | tf_op jit(solution)/shard_map/ppermute | solution.py:255
  143.9 4.4 %collective-permute-start.18 = (f32[12,31]{1,0:T(8,128)S(1)}, f32[12,31]{1,0:T(8,128)S(1)}, u32[]{:S(2)}, u32[]{:S(2)}) collective-permute-start(f32[12,31]{1,0:T(8,128)S(1)} %get-tuple-element.106), channel_id=1, source_target_pairs={{0,32},{16,48},{32,0},{48,16},{64,96},{80,112},{96,64},{112,80},{1... | collective-permute-start | bytes 4472 | tf_op jit(solution)/shard_map/ppermute | solution.py:255
  144.3 4.1 %collective-permute-start.17 = (f32[12,31]{1,0:T(8,128)S(1)}, f32[12,31]{1,0:T(8,128)S(1)}, u32[]{:S(2)}, u32[]{:S(2)}) collective-permute-start(f32[12,31]{1,0:T(8,128)S(1)} %get-tuple-element.106), channel_id=1, source_target_pairs={{0,16},{16,0},{32,48},{48,32},{64,80},{80,64},{96,112},{112,96},{1... | collective-permute-start | bytes 4472 | tf_op jit(solution)/shard_map/ppermute | solution.py:255
  148.3 4.2 %collective-permute-start.22 = (f32[12,31]{1,0:T(8,128)S(1)}, f32[12,31]{1,0:T(8,128)S(1)}, u32[]{:S(2)}, u32[]{:S(2)}) collective-permute-start(f32[12,31]{1,0:T(8,128)S(1)} %add_add_fusion.1), channel_id=1, source_target_pairs={{0,192},{16,208},{32,224},{48,240},{64,128},{80,144},{96,160},{112... | collective-permute-start | bytes 4472 | tf_op jit(solution)/shard_map/ppermute | solution.py:255
  150.9 4.4 %collective-permute-start.21 = (f32[12,31]{1,0:T(8,128)S(1)}, f32[12,31]{1,0:T(8,128)S(1)}, u32[]{:S(2)}, u32[]{:S(2)}) collective-permute-start(f32[12,31]{1,0:T(8,128)S(1)} %add_add_fusion.1), channel_id=1, source_target_pairs={{0,128},{16,144},{32,160},{48,176},{64,192},{80,208},{96,224},{112... | collective-permute-start | bytes 4472 | tf_op jit(solution)/shard_map/ppermute | solution.py:255
  151.4 3.9 %collective-permute-start.20 = (f32[12,31]{1,0:T(8,128)S(1)}, f32[12,31]{1,0:T(8,128)S(1)}, u32[]{:S(2)}, u32[]{:S(2)}) collective-permute-start(f32[12,31]{1,0:T(8,128)S(1)} %add_add_fusion.1), channel_id=1, source_target_pairs={{0,64},{16,80},{32,96},{48,112},{64,0},{80,16},{96,32},{112,48},{1... | collective-permute-start | bytes 4472 | tf_op jit(solution)/shard_map/ppermute | solution.py:255
  (18 other events, 35.9 us)

commit v7 on v6

--- a/solution.py
+++ b/solution.py
@@ -17,7 +17,7 @@
 NEG = -1e30
 BF = jnp.bfloat16
 F32 = jnp.float32
-PARAMS = pltpu.CompilerParams(vmem_limit_bytes=24 * 1024 * 1024)
+PARAMS = pltpu.CompilerParams(vmem_limit_bytes=48 * 1024 * 1024)
 PARTS = 4
 LONG = 10**12
 VMEM = pl.BlockSpec(memory_space=pltpu.VMEM)
@@ -172,48 +172,62 @@
         out_ref[h] = table
 
 
-def temporal_a_kernel(frames_ref, in_ref, bias_ref, prob_ref, mid_ref):
+def temporal_mask(frames_ref, in_ref):
     row = lax.broadcasted_iota(jnp.int32, (ROWS, ROWS), 0)
     col = lax.broadcasted_iota(jnp.int32, (ROWS, ROWS), 1)
     clip = slot_rows(frames_ref, in_ref, 3 * HEADS).astype(F32)
     other = clip.T
     same = (row & (TOK - 1)) == (col & (TOK - 1))
     same &= jnp.concatenate([clip] * 2, axis=1) == jnp.concatenate([other] * 2, axis=0)
-    mask = jnp.where(same, 0.0, NEG)
+    return jnp.where(same, 0.0, NEG)
+
+
+def temporal_prob(q, k, bias, mask):
+    bias = jnp.broadcast_to(bias[:, None, :], (SEQ, TOK, ROWS)).reshape(ROWS, ROWS)
+    return softmax((mm_nt(q, k) * SCALE + bias) + mask)
+
+
+def temporal_a_kernel(frames_ref, in_ref, bias_ref, mid_ref):
+    mask = temporal_mask(frames_ref, in_ref)
     for h in range(HEADS):
         q, k, up = (slot_rows(frames_ref, in_ref, i * HEADS + h) for i in range(3))
-        bias = jnp.broadcast_to(bias_ref[h][:, None, :], (SEQ, TOK, ROWS)).reshape(ROWS, ROWS)
-        prob = softmax((mm_nt(q, k) * SCALE + bias) + mask)
-        prob_ref[h] = prob
+        prob = temporal_prob(q, k, bias_ref[h], mask)
         mid = mm_tn(prob.astype(BF), up).astype(BF)
         for s in range(SEQ):
             mid_ref[frames_ref[s], h] = mid[s * TOK:(s + 1) * TOK]
 
 
-def temporal_b_kernel(frames_ref, in_ref, prob_ref, *refs):
-    so_refs, (out_ref, keep_ref, give_ref, bias_ref) = dict(zip((0,) + SHIFTS, refs)), refs[-4:]
+def temporal_b_kernel(frames_ref, in_ref, bias_ref, *refs):
+    so_refs, (out_ref, keep_ref, give_ref, rows_ref) = dict(zip((0,) + SHIFTS, refs)), refs[-4:]
     so_at = [(so_refs[d if d <= CHIPS // 2 else d - CHIPS], x) for d, x in SLOTS]
+    mask = temporal_mask(frames_ref, in_ref)
     for h in range(HEADS):
         q, k, up = (slot_rows(frames_ref, in_ref, i * HEADS + h) for i in range(3))
         so = jnp.concatenate([ref[x, h] for ref, x in so_at], axis=0)
-        prob = prob_ref[h]
+        prob = temporal_prob(q, k, bias_ref[h], mask)
         grad_prob = mm_nt(up, so)
         put_frames(frames_ref, out_ref, 0, h, mm(prob.astype(BF), so))
         score = prob * (grad_prob - jnp.sum(prob * grad_prob, axis=-1, keepdims=True))
-        bias_ref[h] = jnp.sum(score.reshape(SEQ, TOK, ROWS), axis=1)
+        rows_ref[h] = jnp.sum(score.reshape(SEQ, TOK, ROWS), axis=1)
         low = (score * SCALE).astype(BF)
         put_frames(frames_ref, out_ref, 1, h, mm(low, k))
         put_pairs(keep_ref, give_ref, h, mm_tn(low, q))
 
 
-def unpack_kernel(in_ref, res_ref, gq_ref, sems):
-    copies = []
-    for i, out in enumerate((res_ref, gq_ref)):
-        for u in range(SEQ):
-            rows = pl.ds(u * TOK, TOK)
-            copies.append(pltpu.make_async_copy(in_ref.at[u, i], out.at[0, rows], sems.at[i, u]))
-            copies[-1].start()
-    for copy in copies:
+def unpack_kernel(in_ref, res_ref, gq_ref, held, in_sems, out_sems):
+    pieces = [(u, i) for u in range(SEQ) for i in range(2)]
+    ins = [
+        pltpu.make_async_copy(in_ref.at[u, i], held.at[u, i], in_sems.at[u, i]) for u, i in pieces
+    ]
+    for copy in ins:
+        copy.start()
+    outs = []
+    for copy, (u, i) in zip(ins, pieces):
+        copy.wait()
+        out = (res_ref, gq_ref)[i].at[0, pl.ds(u * TOK, TOK)]
+        outs.append(pltpu.make_async_copy(held.at[u, i], out, out_sems.at[u, i]))
+        outs[-1].start()
+    for copy in outs:
         copy.wait()
 
 
@@ -332,12 +346,12 @@
     so = sent(so_messages)
 
     there, _, bias = lax.optimization_barrier((there, so_messages, bias))
-    prob, mid = call(
+    (mid,) = call(
         temporal_a_kernel,
         "temporal_a",
         [SMEM] + [VMEM] * 2,
         [frames, there, bias],
-        [probs(), units(SEQ, HEADS)],
+        [units(SEQ, HEADS)],
     )
     grad_mid = exchange(mid)
 
@@ -345,7 +359,7 @@
         temporal_b_kernel,
         "temporal_b",
         [SMEM] + [VMEM] * (2 + CHIPS),
-        [frames, there, prob, *so],
+        [frames, there, bias, *so],
         [jax.ShapeDtypeStruct((SEQ, 2, TOK, WIDTH), BF)]
         + [units(CHIPS, HEADS)] * 2
         + [jax.ShapeDtypeStruct((HEADS, SEQ, ROWS), F32)],
@@ -386,10 +400,14 @@
     result, grad_qt = call(
         unpack_kernel,
         "unpack",
-        [VMEM],
+        [HBM],
         [returned],
         [frame()] * 2,
-        [pltpu.SemaphoreType.DMA((2, SEQ))],
+        [
+            pltpu.VMEM((SEQ, 2, TOK, WIDTH), BF),
+            pltpu.SemaphoreType.DMA((SEQ, 2)),
+            pltpu.SemaphoreType.DMA((SEQ, 2)),
+        ],
         space=HBM,
     )
     return result, grad_qs, grad_ks, grad_vs, grad_qt, grad_kt, total_bias

time: 170 us -> 167 us (0.982)
  local copies, waits for them, and re-layouts: 15.9 us -> 6.68 us
  Pallas kernels: 26.5 us -> 32.3 us
    unnamed x48 -> x30, local copies, waits for them, and re-layouts: 15.7 us -> 6.52 us
    pallas_call x10, Pallas kernels: 26.5 us -> 32.3 us  [call(): pl.pallas_call(kernel, out_shape=tuple(outputs), in_specs=specs, out_spec...]
  transfers between devices with their start and end apart: 26 -> 26, of which waited for: 10 -> 10; matrix products, arithmetic and copies ran while one was open for 1% -> 1% of each run, Pallas kernels for 12% -> 16%
where the time goes in v7:
time: 167 us
  waiting for transfers between devices  64 us (38%)
  starting transfers between devices  60.6 us (36%)
  Pallas kernels  32.3 us (19%)
  local copies, waits for them, and re-layouts  6.68 us (4%)
    ppermute x17, waiting for transfers between devices, move(): return lax.ppermute(message, 'seq', perm)  46.9 us
    pallas_call x10, Pallas kernels, call(): pl.pallas_call(kernel, out_shape=tuple(outputs), in_specs=specs, out_spec...  32.3 us
    ppermute x17, starting transfers between devices, move(): return lax.ppermute(message, 'seq', perm)  27.6 us
    all_to_all x3, starting transfers between devices, exchange(): lax.all_to_all(packed, 'seq', split_axis=0, concat_axis=0, tiled=True)  25.3 us
    all_to_all x3, waiting for transfers between devices, exchange(): lax.all_to_all(packed, 'seq', split_axis=0, concat_axis=0, tiled=True)  9.08 us
    ppermute x6, waiting for transfers between devices, pair(): return lax.ppermute(terms, axis, [(i, i ^ mask) for i in range(size)])  8.02 us
    ppermute x6, starting transfers between devices, pair(): return lax.ppermute(terms, axis, [(i, i ^ mask) for i in range(size)])  7.77 us
    unnamed x30, local copies, waits for them, and re-layouts  6.52 us
  transfers between devices with their start and end apart: 26, of which 10 were waited for; matrix products, arithmetic and copies ran while one was open for 1% of the time, Pallas kernels for 16%

profile of v7, /device:TPU:1, one launch (start us, length us, event | category | flops | bytes accessed | tf_op | source)
XLA Modules:
  0.0 166.5 jit_solution(5760002955969227349)
XLA Ops:
  1.3 2.7 %pack.1 = bf16[16,37,16,128]{3,2,1,0:T(8,128)(2,1)} custom-call(s32[1,1]{1,0:T(1,128)S(6)} %copy.20.clip_ref, bf16[1,256,1536]{2,1,0:T(8,128)(2,1)} %q_ref.1, bf16[1,256,1536]{2,1,0:T(8,128)(2,1)} %k_ref.1, bf16[1,256,1536]{2,1,0:T(8,128)(2,1)} %up_ref.1), custom_call_target="tpu_custom_call" | custom-call | flops 1000 | bytes 1000 | tf_op jit(solution)/shard_map/pack/pallas_call | solution.py:251
  4.1 10.1 %all-to-all-start = ((bf16[16,37,16,128]{3,2,1,0:T(8,128)(2,1)}), bf16[16,37,16,128]{3,2,1,0:T(8,128)(2,1)S(1)}, u32[]{:S(2)}, u32[]{:S(2)}) async-start(bf16[16,37,16,128]{3,2,1,0:T(8,128)(2,1)} %pack.1), calls=%async_computation | async-start | bytes 4849664 | tf_op jit(solution)/shard_map/all_to_all | solution.py:264
  17.9 4.1 %spatial_fwd.1 = (bf16[8,12,16,128]{3,2,1,0:T(8,128)(2,1)S(1)}, bf16[8,12,16,128]{3,2,1,0:T(8,128)(2,1)S(1)}, f32[12,256,256]{2,1,0:T(8,128)}) custom-call(s32[2]{0:T(128)S(1)} %pad_add_fusion.pos_ref, bf16[1,256,1536]{2,1,0:T(8,128)(2,1)S(1)} %copy-done.1, bf16[1,256,1536]{2,1,0:T(8,128)(2,1)S(1)} %copy-done.2, bf16[1,256,1536]{2,1,0:T(8,128)(2,1)S(1)} %copy-done.4), custom_call_target="tpu_custom_call" | custom-call | flops 1000 | bytes 1000 | tf_op jit(solution)/shard_map/spatial_fwd/pallas_call | solution.py:251
  22.2 1.6 collective-permute-done.got_ref
  24.6 1.4 collective-permute-start.1
  26.0 1.3 collective-permute-start.2
  27.3 2.9 %collective-permute-start.3 = (bf16[2,12,16,128]{3,2,1,0:T(8,128)(2,1)}, bf16[2,12,16,128]{3,2,1,0:T(8,128)(2,1)}, u32[]{:S(2)}, u32[]{:S(2)}) collective-permute-start(bf16[2,12,16,128]{3,2,1,0:T(8,128)(2,1)} %get-tuple-element.66), channel_id=1, source_target_pairs={{0,6},{1,7},{2,8},{3,9},{4,10},{5,11},{6,12},{7,13},{8,14},{9,15},... | collective-permute-start | bytes 294920 | tf_op jit(solution)/shard_map/ppermute | solution.py:279
  30.2 1.6 collective-permute-start.4
  32.8 39.1 %collective-permute-done.1.refs_1_ = bf16[2,12,16,128]{3,2,1,0:T(8,128)(2,1)S(1)} collective-permute-done((bf16[2,12,16,128]{3,2,1,0:T(8,128)(2,1)S(1)}, bf16[2,12,16,128]{3,2,1,0:T(8,128)(2,1)S(1)}, u32[]{:S(2)}, u32[]{:S(2)}) %collective-permute-start.1) | collective-permute-done | bytes 98336 | tf_op jit(solution)/shard_map/ppermute | solution.py:279
  72.5 2.1 %collective-permute-start.6 = (bf16[2,12,16,128]{3,2,1,0:T(8,128)(2,1)}, bf16[2,12,16,128]{3,2,1,0:T(8,128)(2,1)}, u32[]{:S(2)}, u32[]{:S(2)}) collective-permute-start(bf16[2,12,16,128]{3,2,1,0:T(8,128)(2,1)} %get-tuple-element.69), channel_id=1, source_target_pairs={{0,12},{1,13},{2,14},{3,15},{4,0},{5,1},{6,2},{7,3},{8,4},{9,5},{1... | collective-permute-start | bytes 294920 | tf_op jit(solution)/shard_map/ppermute | solution.py:279
  75.2 1.7 collective-permute-start.7
  76.9 4.2 %temporal_a.1 = bf16[16,12,16,128]{3,2,1,0:T(8,128)(2,1)} custom-call(s32[16]{0:T(128)S(1)} %fusion.11.frames_ref, bf16[16,37,16,128]{3,2,1,0:T(8,128)(2,1)S(1)} %all-to-all-done.in_ref, f32[12,16,256]{2,1,0:T(8,128)S(1)} %bias.1.bias_ref), custom_call_target="tpu_custom_call" | custom-call | flops 1000 | bytes 1000 | tf_op jit(solution)/shard_map/temporal_a/pallas_call | solution.py:251
  81.1 8.7 %all-to-all-start.2 = ((bf16[16,12,16,128]{3,2,1,0:T(8,128)(2,1)}), bf16[16,12,16,128]{3,2,1,0:T(8,128)(2,1)}, u32[]{:S(2)}, u32[]{:S(2)}) async-start(bf16[16,12,16,128]{3,2,1,0:T(8,128)(2,1)} %temporal_a.1), calls=%async_computation.2 | async-start | bytes 1572864 | tf_op jit(solution)/shard_map/all_to_all | solution.py:264
  91.6 7.2 %temporal_b.1 = (bf16[16,2,16,1536]{3,2,1,0:T(8,128)(2,1)S(1)}, bf16[8,12,16,128]{3,2,1,0:T(8,128)(2,1)S(1)}, bf16[8,12,16,128]{3,2,1,0:T(8,128)(2,1)S(1)}, f32[12,16,256]{2,1,0:T(8,128)S(1)}) custom-call(s32[16]{0:T(128)S(1)} %fusion.11.frames_ref, bf16[16,37,16,128]{3,2,1,0:T(8,128)(2,1)S(1)} %all-to-all-done.in_ref, f32[12,16,256]{2,1,0:T(8,128)S(1)} %bias.1.bias_ref, ...), custom_call_target="tpu_custom_call" | custom-call | flops 999999995904 | bytes 1000 | tf_op jit(solution)/shard_map/temporal_b/pallas_call | solution.py:251
  102.6 1.6 collective-permute-start.10
  105.4 3.0 %collective-permute-start.12 = (bf16[25,16,128]{2,1,0:T(8,128)(2,1)}, bf16[25,16,128]{2,1,0:T(8,128)(2,1)S(1)}, u32[]{:S(2)}, u32[]{:S(2)}) collective-permute-start(bf16[25,16,128]{2,1,0:T(8,128)(2,1)} %get-tuple-element.83), channel_id=1, source_target_pairs={{0,6},{1,7},{2,8},{3,9},{4,10},{5,11},{6,12},{7,13},{8,14},{9,15},... | collective-permute-start | bytes 307208 | tf_op jit(solution)/shard_map/ppermute | solution.py:279
  108.4 1.5 collective-permute-start.13
  112.3 2.2 %collective-permute-start.15 = (bf16[25,16,128]{2,1,0:T(8,128)(2,1)S(1)}, bf16[25,16,128]{2,1,0:T(8,128)(2,1)S(1)}, u32[]{:S(2)}, u32[]{:S(2)}) collective-permute-start(bf16[25,16,128]{2,1,0:T(8,128)(2,1)S(1)} %get-tuple-element.86), channel_id=1, source_target_pairs={{0,12},{1,13},{2,14},{3,15},{4,0},{5,1},{6,2},{7,3},{8,4},{9,5},{1... | collective-permute-start | bytes 307208 | tf_op jit(solution)/shard_map/ppermute | solution.py:279
  114.5 4.4 %collective-permute-start.16 = (bf16[25,16,128]{2,1,0:T(8,128)(2,1)S(1)}, bf16[25,16,128]{2,1,0:T(8,128)(2,1)S(1)}, u32[]{:S(2)}, u32[]{:S(2)}) collective-permute-start(bf16[25,16,128]{2,1,0:T(8,128)(2,1)S(1)} %get-tuple-element.87), channel_id=1, source_target_pairs={{0,8},{1,9},{2,10},{3,11},{4,12},{5,13},{6,14},{7,15},{8,0},{9,1},... | collective-permute-start | bytes 307208 | tf_op jit(solution)/shard_map/ppermute | solution.py:279
  118.9 6.4 %all-to-all-start.1 = ((bf16[16,2,16,1536]{3,2,1,0:T(8,128)(2,1)}), bf16[16,2,16,1536]{3,2,1,0:T(8,128)(2,1)}, u32[]{:S(2)}, u32[]{:S(2)}) async-start(bf16[16,2,16,1536]{3,2,1,0:T(8,128)(2,1)} %copy-done), calls=%async_computation.1 | async-start | bytes 3145728 | tf_op jit(solution)/shard_map/all_to_all | solution.py:264
  125.4 4.1 %collective-permute-done.16.refs_7_ = bf16[25,16,128]{2,1,0:T(8,128)(2,1)S(1)} collective-permute-done((bf16[25,16,128]{2,1,0:T(8,128)(2,1)S(1)}, bf16[25,16,128]{2,1,0:T(8,128)(2,1)S(1)}, u32[]{:S(2)}, u32[]{:S(2)}) %collective-permute-start.16) | collective-permute-done | bytes 102432 | tf_op jit(solution)/shard_map/ppermute | solution.py:279
  129.5 7.2 %spatial_bwd.1 = (bf16[1,256,1536]{2,1,0:T(8,128)(2,1)}, bf16[1,256,1536]{2,1,0:T(8,128)(2,1)}, bf16[1,256,1536]{2,1,0:T(8,128)(2,1)}) custom-call(bf16[1,256,1536]{2,1,0:T(8,128)(2,1)S(1)} %copy-done.1, bf16[1,256,1536]{2,1,0:T(8,128)(2,1)S(1)} %copy-done.3, bf16[1,256,1536]{2,1,0:T(8,128)(2,1)S(1)} %copy-done.5, ...), custom_call_target="tpu_custom_call" | custom-call | flops 999999995904 | bytes 1000 | tf_op jit(solution)/shard_map/spatial_bwd/pallas_call | solution.py:251
  136.7 1.6 finish.1
  138.3 1.3 collective-permute-start.17
  139.6 2.6 %collective-permute-start.18 = (f32[12,31]{1,0:T(8,128)S(1)}, f32[12,31]{1,0:T(8,128)S(1)}, u32[]{:S(2)}, u32[]{:S(2)}) collective-permute-start(f32[12,31]{1,0:T(8,128)S(1)} %get-tuple-element.102), channel_id=1, source_target_pairs={{0,32},{16,48},{32,0},{48,16},{64,96},{80,112},{96,64},{112,80},{1... | collective-permute-start | bytes 4472 | tf_op jit(solution)/shard_map/ppermute | solution.py:269
  142.2 1.8 %collective-permute-done.18 = f32[12,31]{1,0:T(8,128)S(1)} collective-permute-done((f32[12,31]{1,0:T(8,128)S(1)}, f32[12,31]{1,0:T(8,128)S(1)}, u32[]{:S(2)}, u32[]{:S(2)}) %collective-permute-start.18) | collective-permute-done | bytes 1520 | tf_op jit(solution)/shard_map/ppermute | solution.py:269
  144.0 2.3 %collective-permute-done.19 = f32[12,31]{1,0:T(8,128)S(1)} collective-permute-done((f32[12,31]{1,0:T(8,128)S(1)}, f32[12,31]{1,0:T(8,128)S(1)}, u32[]{:S(2)}, u32[]{:S(2)}) %collective-permute-start.19) | collective-permute-done | bytes 1520 | tf_op jit(solution)/shard_map/ppermute | solution.py:269
  147.6 2.4 %collective-permute-start.21 = (f32[12,31]{1,0:T(8,128)S(1)}, f32[12,31]{1,0:T(8,128)S(1)}, u32[]{:S(2)}, u32[]{:S(2)}) collective-permute-start(f32[12,31]{1,0:T(8,128)S(1)} %add_add_fusion.1), channel_id=1, source_target_pairs={{0,128},{16,144},{32,160},{48,176},{64,192},{80,208},{96,224},{112... | collective-permute-start | bytes 4472 | tf_op jit(solution)/shard_map/ppermute | solution.py:269
  150.2 1.8 %collective-permute-done.21 = f32[12,31]{1,0:T(8,128)S(1)} collective-permute-done((f32[12,31]{1,0:T(8,128)S(1)}, f32[12,31]{1,0:T(8,128)S(1)}, u32[]{:S(2)}, u32[]{:S(2)}) %collective-permute-start.21) | collective-permute-done | bytes 1520 | tf_op jit(solution)/shard_map/ppermute | solution.py:269
  152.0 2.2 %collective-permute-done.22 = f32[12,31]{1,0:T(8,128)S(1)} collective-permute-done((f32[12,31]{1,0:T(8,128)S(1)}, f32[12,31]{1,0:T(8,128)S(1)}, u32[]{:S(2)}, u32[]{:S(2)}) %collective-permute-start.22) | collective-permute-done | bytes 1520 | tf_op jit(solution)/shard_map/ppermute | solution.py:269
  154.7 9.1 %all-to-all-done.1.in_ref = bf16[16,2,16,1536]{3,2,1,0:T(8,128)(2,1)} async-done(((bf16[16,2,16,1536]{3,2,1,0:T(8,128)(2,1)}), bf16[16,2,16,1536]{3,2,1,0:T(8,128)(2,1)}, u32[]{:S(2)}, u32[]{:S(2)}) %all-to-all-start.1) | async-done | bytes 1572896 | tf_op jit(solution)/shard_map/all_to_all | solution.py:264
  163.8 2.6 %unpack.1 = (bf16[1,256,1536]{2,1,0:T(8,128)(2,1)}, bf16[1,256,1536]{2,1,0:T(8,128)(2,1)}) custom-call(bf16[16,2,16,1536]{3,2,1,0:T(8,128)(2,1)} %all-to-all-done.1.in_ref), custom_call_target="tpu_custom_call" | custom-call | flops 1000 | bytes 1000 | tf_op jit(solution)/shard_map/unpack/pallas_call | solution.py:251
  (71 shorter events, 18.2 us)
Async XLA Ops:
  4.0 10.2 %copy-start.13 = (s32[16]{0:T(128)S(1)}, s32[16]{0:T(128)}, u32[]{:S(2)}) copy-start(s32[16]{0:T(128)} %constant.21.clone) | copy-start | bytes 196
  4.0 10.2 %copy-start.14 = (s32[16]{0:T(128)S(1)}, s32[16]{0:T(128)}, u32[]{:S(2)}) copy-start(s32[16]{0:T(128)} %constant.37) | copy-start | bytes 196
  4.0 10.4 %copy-start.8 = (f32[12,31]{1,0:T(8,128)S(1)}, f32[12,31]{1,0:T(8,128)}, u32[]{:S(2)}) copy-start(f32[12,31]{1,0:T(8,128)} %rel_ref) | copy-start | bytes 4468
  4.1 11.6 %copy-start.1 = (bf16[1,256,1536]{2,1,0:T(8,128)(2,1)S(1)}, bf16[1,256,1536]{2,1,0:T(8,128)(2,1)}, u32[]{:S(2)}) copy-start(bf16[1,256,1536]{2,1,0:T(8,128)(2,1)} %q_ref.3) | copy-start | bytes 2359300
  4.1 72.8 %all-to-all-start = ((bf16[16,37,16,128]{3,2,1,0:T(8,128)(2,1)}), bf16[16,37,16,128]{3,2,1,0:T(8,128)(2,1)S(1)}, u32[]{:S(2)}, u32[]{:S(2)}) async-start(bf16[16,37,16,128]{3,2,1,0:T(8,128)(2,1)} %pack.1), calls=%async_computation | async-start | bytes 4849664 | tf_op jit(solution)/shard_map/all_to_all | solution.py:264
  22.0 1.7 %collective-permute-start = (bf16[8,12,16,128]{3,2,1,0:T(8,128)(2,1)S(1)}, bf16[8,12,16,128]{3,2,1,0:T(8,128)(2,1)S(1)}, u32[]{:S(2)}, u32[]{:S(2)}) collective-permute-start(bf16[8,12,16,128]{3,2,1,0:T(8,128)(2,1)S(1)} %get-tuple-element.62), channel_id=1, source_target_pairs={{0,1},{1,0},{2,3},{3,2},{4,5},{5,4},{6,7},{7,6},{8,9},{9,8},{10,11... | collective-permute-start | bytes 1179656 | tf_op jit(solution)/shard_map/ppermute | solution.py:279
  24.6 47.3 %collective-permute-start.1 = (bf16[2,12,16,128]{3,2,1,0:T(8,128)(2,1)S(1)}, bf16[2,12,16,128]{3,2,1,0:T(8,128)(2,1)S(1)}, u32[]{:S(2)}, u32[]{:S(2)}) collective-permute-start(bf16[2,12,16,128]{3,2,1,0:T(8,128)(2,1)S(1)} %get-tuple-element.64), channel_id=1, source_target_pairs={{0,2},{1,3},{2,4},{3,5},{4,6},{5,7},{6,8},{7,9},{8,10},{9,11},{10,... | collective-permute-start | bytes 294920 | tf_op jit(solution)/shard_map/ppermute | solution.py:279
  26.0 48.6 %collective-permute-start.2 = (bf16[2,12,16,128]{3,2,1,0:T(8,128)(2,1)S(1)}, bf16[2,12,16,128]{3,2,1,0:T(8,128)(2,1)S(1)}, u32[]{:S(2)}, u32[]{:S(2)}) collective-permute-start(bf16[2,12,16,128]{3,2,1,0:T(8,128)(2,1)S(1)} %get-tuple-element.65), channel_id=1, source_target_pairs={{0,14},{1,15},{2,0},{3,1},{4,2},{5,3},{6,4},{7,5},{8,6},{9,7},{10,... | collective-permute-start | bytes 294920 | tf_op jit(solution)/shard_map/ppermute | solution.py:279
  27.3 62.5 %collective-permute-start.3 = (bf16[2,12,16,128]{3,2,1,0:T(8,128)(2,1)}, bf16[2,12,16,128]{3,2,1,0:T(8,128)(2,1)}, u32[]{:S(2)}, u32[]{:S(2)}) collective-permute-start(bf16[2,12,16,128]{3,2,1,0:T(8,128)(2,1)} %get-tuple-element.66), channel_id=1, source_target_pairs={{0,6},{1,7},{2,8},{3,9},{4,10},{5,11},{6,12},{7,13},{8,14},{9,15},... | collective-permute-start | bytes 294920 | tf_op jit(solution)/shard_map/ppermute | solution.py:279
  30.2 59.6 %collective-permute-start.4 = (bf16[2,12,16,128]{3,2,1,0:T(8,128)(2,1)}, bf16[2,12,16,128]{3,2,1,0:T(8,128)(2,1)}, u32[]{:S(2)}, u32[]{:S(2)}) collective-permute-start(bf16[2,12,16,128]{3,2,1,0:T(8,128)(2,1)} %get-tuple-element.67), channel_id=1, source_target_pairs={{0,10},{1,11},{2,12},{3,13},{4,14},{5,15},{6,0},{7,1},{8,2},{9,3},... | collective-permute-start | bytes 294920 | tf_op jit(solution)/shard_map/ppermute | solution.py:279
  31.7 58.0 %collective-permute-start.5 = (bf16[2,12,16,128]{3,2,1,0:T(8,128)(2,1)}, bf16[2,12,16,128]{3,2,1,0:T(8,128)(2,1)}, u32[]{:S(2)}, u32[]{:S(2)}) collective-permute-start(bf16[2,12,16,128]{3,2,1,0:T(8,128)(2,1)} %get-tuple-element.68), channel_id=1, source_target_pairs={{0,4},{1,5},{2,6},{3,7},{4,8},{5,9},{6,10},{7,11},{8,12},{9,13},{1... | collective-permute-start | bytes 294920 | tf_op jit(solution)/shard_map/ppermute | solution.py:279
  72.5 17.3 %collective-permute-start.6 = (bf16[2,12,16,128]{3,2,1,0:T(8,128)(2,1)}, bf16[2,12,16,128]{3,2,1,0:T(8,128)(2,1)}, u32[]{:S(2)}, u32[]{:S(2)}) collective-permute-start(bf16[2,12,16,128]{3,2,1,0:T(8,128)(2,1)} %get-tuple-element.69), channel_id=1, source_target_pairs={{0,12},{1,13},{2,14},{3,15},{4,0},{5,1},{6,2},{7,3},{8,4},{9,5},{1... | collective-permute-start | bytes 294920 | tf_op jit(solution)/shard_map/ppermute | solution.py:279
  75.2 14.6 %collective-permute-start.7 = (bf16[2,12,16,128]{3,2,1,0:T(8,128)(2,1)}, bf16[2,12,16,128]{3,2,1,0:T(8,128)(2,1)}, u32[]{:S(2)}, u32[]{:S(2)}) collective-permute-start(bf16[2,12,16,128]{3,2,1,0:T(8,128)(2,1)} %get-tuple-element.70), channel_id=1, source_target_pairs={{0,8},{1,9},{2,10},{3,11},{4,12},{5,13},{6,14},{7,15},{8,0},{9,1},... | collective-permute-start | bytes 294920 | tf_op jit(solution)/shard_map/ppermute | solution.py:279
  81.1 37.8 %all-to-all-start.2 = ((bf16[16,12,16,128]{3,2,1,0:T(8,128)(2,1)}), bf16[16,12,16,128]{3,2,1,0:T(8,128)(2,1)}, u32[]{:S(2)}, u32[]{:S(2)}) async-start(bf16[16,12,16,128]{3,2,1,0:T(8,128)(2,1)} %temporal_a.1), calls=%async_computation.2 | async-start | bytes 1572864 | tf_op jit(solution)/shard_map/all_to_all | solution.py:264
  100.0 29.5 %copy-start.3 = (bf16[1,256,1536]{2,1,0:T(8,128)(2,1)S(1)}, bf16[1,256,1536]{2,1,0:T(8,128)(2,1)}, u32[]{:S(2)}) copy-start(bf16[1,256,1536]{2,1,0:T(8,128)(2,1)} %k_ref.3) | copy-start | bytes 2359300
  100.0 29.5 %copy-start.5 = (bf16[1,256,1536]{2,1,0:T(8,128)(2,1)S(1)}, bf16[1,256,1536]{2,1,0:T(8,128)(2,1)}, u32[]{:S(2)}) copy-start(bf16[1,256,1536]{2,1,0:T(8,128)(2,1)} %v_ref.1) | copy-start | bytes 2359300
  100.0 1.9 %collective-permute-start.9 = (bf16[8,12,16,128]{3,2,1,0:T(8,128)(2,1)S(1)}, bf16[8,12,16,128]{3,2,1,0:T(8,128)(2,1)S(1)}, u32[]{:S(2)}, u32[]{:S(2)}) collective-permute-start(bf16[8,12,16,128]{3,2,1,0:T(8,128)(2,1)S(1)} %get-tuple-element.79), channel_id=1, source_target_pairs={{0,1},{1,0},{2,3},{3,2},{4,5},{5,4},{6,7},{7,6},{8,9},{9,8},{10,11... | collective-permute-start | bytes 1179656 | tf_op jit(solution)/shard_map/ppermute | solution.py:279
  100.6 1.2 collective-permute-start.8
  102.6 9.6 %collective-permute-start.10 = (bf16[25,16,128]{2,1,0:T(8,128)(2,1)S(1)}, bf16[25,16,128]{2,1,0:T(8,128)(2,1)S(1)}, u32[]{:S(2)}, u32[]{:S(2)}) collective-permute-start(bf16[25,16,128]{2,1,0:T(8,128)(2,1)S(1)} %get-tuple-element.81), channel_id=1, source_target_pairs={{0,2},{1,3},{2,4},{3,5},{4,6},{5,7},{6,8},{7,9},{8,10},{9,11},{10,... | collective-permute-start | bytes 307208 | tf_op jit(solution)/shard_map/ppermute | solution.py:279
  104.2 10.2 %collective-permute-start.11 = (bf16[25,16,128]{2,1,0:T(8,128)(2,1)S(1)}, bf16[25,16,128]{2,1,0:T(8,128)(2,1)S(1)}, u32[]{:S(2)}, u32[]{:S(2)}) collective-permute-start(bf16[25,16,128]{2,1,0:T(8,128)(2,1)S(1)} %get-tuple-element.82), channel_id=1, source_target_pairs={{0,14},{1,15},{2,0},{3,1},{4,2},{5,3},{6,4},{7,5},{8,6},{9,7},{10,... | collective-permute-start | bytes 307208 | tf_op jit(solution)/shard_map/ppermute | solution.py:279
  105.4 19.9 %collective-permute-start.12 = (bf16[25,16,128]{2,1,0:T(8,128)(2,1)}, bf16[25,16,128]{2,1,0:T(8,128)(2,1)S(1)}, u32[]{:S(2)}, u32[]{:S(2)}) collective-permute-start(bf16[25,16,128]{2,1,0:T(8,128)(2,1)} %get-tuple-element.83), channel_id=1, source_target_pairs={{0,6},{1,7},{2,8},{3,9},{4,10},{5,11},{6,12},{7,13},{8,14},{9,15},... | collective-permute-start | bytes 307208 | tf_op jit(solution)/shard_map/ppermute | solution.py:279
  108.4 16.9 %collective-permute-start.13 = (bf16[25,16,128]{2,1,0:T(8,128)(2,1)}, bf16[25,16,128]{2,1,0:T(8,128)(2,1)S(1)}, u32[]{:S(2)}, u32[]{:S(2)}) collective-permute-start(bf16[25,16,128]{2,1,0:T(8,128)(2,1)} %get-tuple-element.84), channel_id=1, source_target_pairs={{0,10},{1,11},{2,12},{3,13},{4,14},{5,15},{6,0},{7,1},{8,2},{9,3},... | collective-permute-start | bytes 307208 | tf_op jit(solution)/shard_map/ppermute | solution.py:279
  109.9 15.4 %collective-permute-start.14 = (bf16[25,16,128]{2,1,0:T(8,128)(2,1)}, bf16[25,16,128]{2,1,0:T(8,128)(2,1)S(1)}, u32[]{:S(2)}, u32[]{:S(2)}) collective-permute-start(bf16[25,16,128]{2,1,0:T(8,128)(2,1)} %get-tuple-element.85), channel_id=1, source_target_pairs={{0,4},{1,5},{2,6},{3,7},{4,8},{5,9},{6,10},{7,11},{8,12},{9,13},{1... | collective-permute-start | bytes 307208 | tf_op jit(solution)/shard_map/ppermute | solution.py:279
  112.3 13.1 %collective-permute-start.15 = (bf16[25,16,128]{2,1,0:T(8,128)(2,1)S(1)}, bf16[25,16,128]{2,1,0:T(8,128)(2,1)S(1)}, u32[]{:S(2)}, u32[]{:S(2)}) collective-permute-start(bf16[25,16,128]{2,1,0:T(8,128)(2,1)S(1)} %get-tuple-element.86), channel_id=1, source_target_pairs={{0,12},{1,13},{2,14},{3,15},{4,0},{5,1},{6,2},{7,3},{8,4},{9,5},{1... | collective-permute-start | bytes 307208 | tf_op jit(solution)/shard_map/ppermute | solution.py:279
  114.5 15.0 %collective-permute-start.16 = (bf16[25,16,128]{2,1,0:T(8,128)(2,1)S(1)}, bf16[25,16,128]{2,1,0:T(8,128)(2,1)S(1)}, u32[]{:S(2)}, u32[]{:S(2)}) collective-permute-start(bf16[25,16,128]{2,1,0:T(8,128)(2,1)S(1)} %get-tuple-element.87), channel_id=1, source_target_pairs={{0,8},{1,9},{2,10},{3,11},{4,12},{5,13},{6,14},{7,15},{8,0},{9,1},... | collective-permute-start | bytes 307208 | tf_op jit(solution)/shard_map/ppermute | solution.py:279
  118.9 44.9 %all-to-all-start.1 = ((bf16[16,2,16,1536]{3,2,1,0:T(8,128)(2,1)}), bf16[16,2,16,1536]{3,2,1,0:T(8,128)(2,1)}, u32[]{:S(2)}, u32[]{:S(2)}) async-start(bf16[16,2,16,1536]{3,2,1,0:T(8,128)(2,1)} %copy-done), calls=%async_computation.1 | async-start | bytes 3145728 | tf_op jit(solution)/shard_map/all_to_all | solution.py:264
  138.3 3.9 %collective-permute-start.17 = (f32[12,31]{1,0:T(8,128)S(1)}, f32[12,31]{1,0:T(8,128)S(1)}, u32[]{:S(2)}, u32[]{:S(2)}) collective-permute-start(f32[12,31]{1,0:T(8,128)S(1)} %get-tuple-element.102), channel_id=1, source_target_pairs={{0,16},{16,0},{32,48},{48,32},{64,80},{80,64},{96,112},{112,96},{1... | collective-permute-start | bytes 4472 | tf_op jit(solution)/shard_map/ppermute | solution.py:269
  139.6 4.4 %collective-permute-start.18 = (f32[12,31]{1,0:T(8,128)S(1)}, f32[12,31]{1,0:T(8,128)S(1)}, u32[]{:S(2)}, u32[]{:S(2)}) collective-permute-start(f32[12,31]{1,0:T(8,128)S(1)} %get-tuple-element.102), channel_id=1, source_target_pairs={{0,32},{16,48},{32,0},{48,16},{64,96},{80,112},{96,64},{112,80},{1... | collective-permute-start | bytes 4472 | tf_op jit(solution)/shard_map/ppermute | solution.py:269
  142.2 4.1 %collective-permute-start.19 = (f32[12,31]{1,0:T(8,128)S(1)}, f32[12,31]{1,0:T(8,128)S(1)}, u32[]{:S(2)}, u32[]{:S(2)}) collective-permute-start(f32[12,31]{1,0:T(8,128)S(1)} %get-tuple-element.102), channel_id=1, source_target_pairs={{0,48},{16,32},{32,16},{48,0},{64,112},{80,96},{96,80},{112,64},{1... | collective-permute-start | bytes 4472 | tf_op jit(solution)/shard_map/ppermute | solution.py:269
  146.3 3.9 %collective-permute-start.20 = (f32[12,31]{1,0:T(8,128)S(1)}, f32[12,31]{1,0:T(8,128)S(1)}, u32[]{:S(2)}, u32[]{:S(2)}) collective-permute-start(f32[12,31]{1,0:T(8,128)S(1)} %add_add_fusion.1), channel_id=1, source_target_pairs={{0,64},{16,80},{32,96},{48,112},{64,0},{80,16},{96,32},{112,48},{1... | collective-permute-start | bytes 4472 | tf_op jit(solution)/shard_map/ppermute | solution.py:269
  147.6 4.4 %collective-permute-start.21 = (f32[12,31]{1,0:T(8,128)S(1)}, f32[12,31]{1,0:T(8,128)S(1)}, u32[]{:S(2)}, u32[]{:S(2)}) collective-permute-start(f32[12,31]{1,0:T(8,128)S(1)} %add_add_fusion.1), channel_id=1, source_target_pairs={{0,128},{16,144},{32,160},{48,176},{64,192},{80,208},{96,224},{112... | collective-permute-start | bytes 4472 | tf_op jit(solution)/shard_map/ppermute | solution.py:269
  150.0 4.1 %collective-permute-start.22 = (f32[12,31]{1,0:T(8,128)S(1)}, f32[12,31]{1,0:T(8,128)S(1)}, u32[]{:S(2)}, u32[]{:S(2)}) collective-permute-start(f32[12,31]{1,0:T(8,128)S(1)} %add_add_fusion.1), channel_id=1, source_target_pairs={{0,192},{16,208},{32,224},{48,240},{64,128},{80,144},{96,160},{112... | collective-permute-start | bytes 4472 | tf_op jit(solution)/shard_map/ppermute | solution.py:269
  (9 other events, 16.2 us)

commit v8 on v7

--- a/solution.py
+++ b/solution.py
@@ -214,23 +214,6 @@
         put_pairs(keep_ref, give_ref, h, mm_tn(low, q))
 
 
-def unpack_kernel(in_ref, res_ref, gq_ref, held, in_sems, out_sems):
-    pieces = [(u, i) for u in range(SEQ) for i in range(2)]
-    ins = [
-        pltpu.make_async_copy(in_ref.at[u, i], held.at[u, i], in_sems.at[u, i]) for u, i in pieces
-    ]
-    for copy in ins:
-        copy.start()
-    outs = []
-    for copy, (u, i) in zip(ins, pieces):
-        copy.wait()
-        out = (res_ref, gq_ref)[i].at[0, pl.ds(u * TOK, TOK)]
-        outs.append(pltpu.make_async_copy(held.at[u, i], out, out_sems.at[u, i]))
-        outs[-1].start()
-    for copy in outs:
-        copy.wait()
-
-
 def finish_kernel(pos_ref, *refs):
     messages, (gk_ref, bias_ref) = refs[:CHIPS], refs[CHIPS:]
     for ref, shift in zip(messages, (0,) + SHIFTS):
@@ -397,19 +380,7 @@
         [frame(), jax.ShapeDtypeStruct((HEADS, RELS), F32)],
     )
     total_bias = sum_of_four(sum_of_four(total, "grp", 1), "grp", 4)
-    result, grad_qt = call(
-        unpack_kernel,
-        "unpack",
-        [HBM],
-        [returned],
-        [frame()] * 2,
-        [
-            pltpu.VMEM((SEQ, 2, TOK, WIDTH), BF),
-            pltpu.SemaphoreType.DMA((SEQ, 2)),
-            pltpu.SemaphoreType.DMA((SEQ, 2)),
-        ],
-        space=HBM,
-    )
+    result, grad_qt = (returned[:, i].reshape(1, ROWS, WIDTH) for i in range(2))
     return result, grad_qs, grad_ks, grad_vs, grad_qt, grad_kt, total_bias
 
 

time: 167 us -> 167 us (level)
  local copies, waits for them, and re-layouts: 6.68 us -> 9.3 us
  Pallas kernels: 32.3 us -> 29.8 us
    slice x0 -> x1, local copies, waits for them, and re-layouts: none -> 2.61 us  [per_device(): result, grad_qt = (returned[:, i].reshape(1, ROWS, WIDTH) for i in range(2))]
    pallas_call x10 -> x9, Pallas kernels: 32.3 us -> 29.8 us  [call(): pl.pallas_call(kernel, out_shape=tuple(outputs), in_specs=specs, out_spec...]
where the time goes in v8:
time: 167 us; the launch traced here: 166 us
  waiting for transfers between devices  63.9 us (38%)
  starting transfers between devices  60.6 us (36%)
  Pallas kernels  29.8 us (18%)
  local copies, waits for them, and re-layouts  9.3 us (6%)
    ppermute x17, waiting for transfers between devices, move(): return lax.ppermute(message, 'seq', perm)  46.8 us
    pallas_call x9, Pallas kernels, call(): pl.pallas_call(kernel, out_shape=tuple(outputs), in_specs=specs, out_spec...  29.8 us
    ppermute x17, starting transfers between devices, move(): return lax.ppermute(message, 'seq', perm)  27.6 us
    all_to_all x3, starting transfers between devices, exchange(): lax.all_to_all(packed, 'seq', split_axis=0, concat_axis=0, tiled=True)  25.2 us
    all_to_all x3, waiting for transfers between devices, exchange(): lax.all_to_all(packed, 'seq', split_axis=0, concat_axis=0, tiled=True)  9.07 us
    ppermute x6, waiting for transfers between devices, pair(): return lax.ppermute(terms, axis, [(i, i ^ mask) for i in range(size)])  8.02 us
    ppermute x6, starting transfers between devices, pair(): return lax.ppermute(terms, axis, [(i, i ^ mask) for i in range(size)])  7.78 us
    unnamed x30, local copies, waits for them, and re-layouts  6.52 us
  transfers between devices with their start and end apart: 26, of which 10 were waited for; matrix products, arithmetic and copies ran while one was open for 1% of the time, Pallas kernels for 16%

profile of v8, /device:TPU:1, one launch (start us, length us, event | category | flops | bytes accessed | tf_op | source)
XLA Modules:
  0.0 166.4 jit_solution(6269902761795252904)
XLA Ops:
  1.3 2.7 %pack.1 = bf16[16,37,16,128]{3,2,1,0:T(8,128)(2,1)} custom-call(s32[1,1]{1,0:T(1,128)S(6)} %copy.20.clip_ref, bf16[1,256,1536]{2,1,0:T(8,128)(2,1)} %q_ref.1, bf16[1,256,1536]{2,1,0:T(8,128)(2,1)} %k_ref.1, bf16[1,256,1536]{2,1,0:T(8,128)(2,1)} %up_ref.1), custom_call_target="tpu_custom_call" | custom-call | flops 1000 | bytes 1000 | tf_op jit(solution)/shard_map/pack/pallas_call | solution.py:234
  4.1 10.1 %all-to-all-start = ((bf16[16,37,16,128]{3,2,1,0:T(8,128)(2,1)}), bf16[16,37,16,128]{3,2,1,0:T(8,128)(2,1)S(1)}, u32[]{:S(2)}, u32[]{:S(2)}) async-start(bf16[16,37,16,128]{3,2,1,0:T(8,128)(2,1)} %pack.1), calls=%async_computation | async-start | bytes 4849664 | tf_op jit(solution)/shard_map/all_to_all | solution.py:247
  17.9 4.2 %spatial_fwd.1 = (bf16[8,12,16,128]{3,2,1,0:T(8,128)(2,1)S(1)}, bf16[8,12,16,128]{3,2,1,0:T(8,128)(2,1)S(1)}, f32[12,256,256]{2,1,0:T(8,128)}) custom-call(s32[2]{0:T(128)S(1)} %pad_add_fusion.pos_ref, bf16[1,256,1536]{2,1,0:T(8,128)(2,1)S(1)} %copy-done.1, bf16[1,256,1536]{2,1,0:T(8,128)(2,1)S(1)} %copy-done.2, bf16[1,256,1536]{2,1,0:T(8,128)(2,1)S(1)} %copy-done.4), custom_call_target="tpu_custom_call" | custom-call | flops 1000 | bytes 1000 | tf_op jit(solution)/shard_map/spatial_fwd/pallas_call | solution.py:234
  22.2 1.6 collective-permute-done.got_ref
  24.6 1.4 collective-permute-start.1
  26.0 1.3 collective-permute-start.2
  27.3 2.9 %collective-permute-start.3 = (bf16[2,12,16,128]{3,2,1,0:T(8,128)(2,1)}, bf16[2,12,16,128]{3,2,1,0:T(8,128)(2,1)}, u32[]{:S(2)}, u32[]{:S(2)}) collective-permute-start(bf16[2,12,16,128]{3,2,1,0:T(8,128)(2,1)} %get-tuple-element.64), channel_id=1, source_target_pairs={{0,6},{1,7},{2,8},{3,9},{4,10},{5,11},{6,12},{7,13},{8,14},{9,15},... | collective-permute-start | bytes 294920 | tf_op jit(solution)/shard_map/ppermute | solution.py:262
  30.2 1.6 collective-permute-start.4
  32.8 39.0 %collective-permute-done.1.refs_1_ = bf16[2,12,16,128]{3,2,1,0:T(8,128)(2,1)S(1)} collective-permute-done((bf16[2,12,16,128]{3,2,1,0:T(8,128)(2,1)S(1)}, bf16[2,12,16,128]{3,2,1,0:T(8,128)(2,1)S(1)}, u32[]{:S(2)}, u32[]{:S(2)}) %collective-permute-start.1) | collective-permute-done | bytes 98336 | tf_op jit(solution)/shard_map/ppermute | solution.py:262
  72.5 2.1 %collective-permute-start.6 = (bf16[2,12,16,128]{3,2,1,0:T(8,128)(2,1)}, bf16[2,12,16,128]{3,2,1,0:T(8,128)(2,1)}, u32[]{:S(2)}, u32[]{:S(2)}) collective-permute-start(bf16[2,12,16,128]{3,2,1,0:T(8,128)(2,1)} %get-tuple-element.67), channel_id=1, source_target_pairs={{0,12},{1,13},{2,14},{3,15},{4,0},{5,1},{6,2},{7,3},{8,4},{9,5},{1... | collective-permute-start | bytes 294920 | tf_op jit(solution)/shard_map/ppermute | solution.py:262
  75.2 1.7 collective-permute-start.7
  76.9 4.2 %temporal_a.1 = bf16[16,12,16,128]{3,2,1,0:T(8,128)(2,1)} custom-call(s32[16]{0:T(128)S(1)} %fusion.11.frames_ref, bf16[16,37,16,128]{3,2,1,0:T(8,128)(2,1)S(1)} %all-to-all-done.in_ref, f32[12,16,256]{2,1,0:T(8,128)S(1)} %bias.1.bias_ref), custom_call_target="tpu_custom_call" | custom-call | flops 1000 | bytes 1000 | tf_op jit(solution)/shard_map/temporal_a/pallas_call | solution.py:234
  81.1 8.7 %all-to-all-start.2 = ((bf16[16,12,16,128]{3,2,1,0:T(8,128)(2,1)}), bf16[16,12,16,128]{3,2,1,0:T(8,128)(2,1)}, u32[]{:S(2)}, u32[]{:S(2)}) async-start(bf16[16,12,16,128]{3,2,1,0:T(8,128)(2,1)} %temporal_a.1), calls=%async_computation.2 | async-start | bytes 1572864 | tf_op jit(solution)/shard_map/all_to_all | solution.py:247
  91.6 7.2 %temporal_b.1 = (bf16[16,2,16,1536]{3,2,1,0:T(8,128)(2,1)S(1)}, bf16[8,12,16,128]{3,2,1,0:T(8,128)(2,1)S(1)}, bf16[8,12,16,128]{3,2,1,0:T(8,128)(2,1)S(1)}, f32[12,16,256]{2,1,0:T(8,128)S(1)}) custom-call(s32[16]{0:T(128)S(1)} %fusion.11.frames_ref, bf16[16,37,16,128]{3,2,1,0:T(8,128)(2,1)S(1)} %all-to-all-done.in_ref, f32[12,16,256]{2,1,0:T(8,128)S(1)} %bias.1.bias_ref, ...), custom_call_target="tpu_custom_call" | custom-call | flops 999999995904 | bytes 1000 | tf_op jit(solution)/shard_map/temporal_b/pallas_call | solution.py:234
  102.6 1.6 collective-permute-start.10
  105.4 3.0 %collective-permute-start.12 = (bf16[25,16,128]{2,1,0:T(8,128)(2,1)}, bf16[25,16,128]{2,1,0:T(8,128)(2,1)S(1)}, u32[]{:S(2)}, u32[]{:S(2)}) collective-permute-start(bf16[25,16,128]{2,1,0:T(8,128)(2,1)} %get-tuple-element.80), channel_id=1, source_target_pairs={{0,6},{1,7},{2,8},{3,9},{4,10},{5,11},{6,12},{7,13},{8,14},{9,15},... | collective-permute-start | bytes 307208 | tf_op jit(solution)/shard_map/ppermute | solution.py:262
  108.4 1.5 collective-permute-start.13
  112.2 2.2 %collective-permute-start.15 = (bf16[25,16,128]{2,1,0:T(8,128)(2,1)S(1)}, bf16[25,16,128]{2,1,0:T(8,128)(2,1)S(1)}, u32[]{:S(2)}, u32[]{:S(2)}) collective-permute-start(bf16[25,16,128]{2,1,0:T(8,128)(2,1)S(1)} %get-tuple-element.83), channel_id=1, source_target_pairs={{0,12},{1,13},{2,14},{3,15},{4,0},{5,1},{6,2},{7,3},{8,4},{9,5},{1... | collective-permute-start | bytes 307208 | tf_op jit(solution)/shard_map/ppermute | solution.py:262
  114.5 4.4 %collective-permute-start.16 = (bf16[25,16,128]{2,1,0:T(8,128)(2,1)S(1)}, bf16[25,16,128]{2,1,0:T(8,128)(2,1)S(1)}, u32[]{:S(2)}, u32[]{:S(2)}) collective-permute-start(bf16[25,16,128]{2,1,0:T(8,128)(2,1)S(1)} %get-tuple-element.84), channel_id=1, source_target_pairs={{0,8},{1,9},{2,10},{3,11},{4,12},{5,13},{6,14},{7,15},{8,0},{9,1},... | collective-permute-start | bytes 307208 | tf_op jit(solution)/shard_map/ppermute | solution.py:262
  118.9 6.4 %all-to-all-start.1 = ((bf16[16,2,16,1536]{3,2,1,0:T(8,128)(2,1)}), bf16[16,2,16,1536]{3,2,1,0:T(8,128)(2,1)}, u32[]{:S(2)}, u32[]{:S(2)}) async-start(bf16[16,2,16,1536]{3,2,1,0:T(8,128)(2,1)} %copy-done), calls=%async_computation.1 | async-start | bytes 3145728 | tf_op jit(solution)/shard_map/all_to_all | solution.py:247
  125.3 4.1 %collective-permute-done.16.refs_7_ = bf16[25,16,128]{2,1,0:T(8,128)(2,1)S(1)} collective-permute-done((bf16[25,16,128]{2,1,0:T(8,128)(2,1)S(1)}, bf16[25,16,128]{2,1,0:T(8,128)(2,1)S(1)}, u32[]{:S(2)}, u32[]{:S(2)}) %collective-permute-start.16) | collective-permute-done | bytes 102432 | tf_op jit(solution)/shard_map/ppermute | solution.py:262
  129.5 7.2 %spatial_bwd.1 = (bf16[1,256,1536]{2,1,0:T(8,128)(2,1)}, bf16[1,256,1536]{2,1,0:T(8,128)(2,1)}, bf16[1,256,1536]{2,1,0:T(8,128)(2,1)}) custom-call(bf16[1,256,1536]{2,1,0:T(8,128)(2,1)S(1)} %copy-done.1, bf16[1,256,1536]{2,1,0:T(8,128)(2,1)S(1)} %copy-done.3, bf16[1,256,1536]{2,1,0:T(8,128)(2,1)S(1)} %copy-done.5, ...), custom_call_target="tpu_custom_call" | custom-call | flops 999999995904 | bytes 1000 | tf_op jit(solution)/shard_map/spatial_bwd/pallas_call | solution.py:234
  136.7 1.6 finish.1
  138.3 1.3 collective-permute-start.17
  139.6 2.6 %collective-permute-start.18 = (f32[12,31]{1,0:T(8,128)S(1)}, f32[12,31]{1,0:T(8,128)S(1)}, u32[]{:S(2)}, u32[]{:S(2)}) collective-permute-start(f32[12,31]{1,0:T(8,128)S(1)} %get-tuple-element.98), channel_id=1, source_target_pairs={{0,32},{16,48},{32,0},{48,16},{64,96},{80,112},{96,64},{112,80},{1... | collective-permute-start | bytes 4472 | tf_op jit(solution)/shard_map/ppermute | solution.py:252
  142.2 1.8 %collective-permute-done.18 = f32[12,31]{1,0:T(8,128)S(1)} collective-permute-done((f32[12,31]{1,0:T(8,128)S(1)}, f32[12,31]{1,0:T(8,128)S(1)}, u32[]{:S(2)}, u32[]{:S(2)}) %collective-permute-start.18) | collective-permute-done | bytes 1520 | tf_op jit(solution)/shard_map/ppermute | solution.py:252
  144.0 2.3 %collective-permute-done.19 = f32[12,31]{1,0:T(8,128)S(1)} collective-permute-done((f32[12,31]{1,0:T(8,128)S(1)}, f32[12,31]{1,0:T(8,128)S(1)}, u32[]{:S(2)}, u32[]{:S(2)}) %collective-permute-start.19) | collective-permute-done | bytes 1520 | tf_op jit(solution)/shard_map/ppermute | solution.py:252
  147.6 2.5 %collective-permute-start.21 = (f32[12,31]{1,0:T(8,128)S(1)}, f32[12,31]{1,0:T(8,128)S(1)}, u32[]{:S(2)}, u32[]{:S(2)}) collective-permute-start(f32[12,31]{1,0:T(8,128)S(1)} %add_add_fusion.1), channel_id=1, source_target_pairs={{0,128},{16,144},{32,160},{48,176},{64,192},{80,208},{96,224},{112... | collective-permute-start | bytes 4472 | tf_op jit(solution)/shard_map/ppermute | solution.py:252
  150.2 1.8 %collective-permute-done.21 = f32[12,31]{1,0:T(8,128)S(1)} collective-permute-done((f32[12,31]{1,0:T(8,128)S(1)}, f32[12,31]{1,0:T(8,128)S(1)}, u32[]{:S(2)}, u32[]{:S(2)}) %collective-permute-start.21) | collective-permute-done | bytes 1520 | tf_op jit(solution)/shard_map/ppermute | solution.py:252
  152.0 2.2 %collective-permute-done.22 = f32[12,31]{1,0:T(8,128)S(1)} collective-permute-done((f32[12,31]{1,0:T(8,128)S(1)}, f32[12,31]{1,0:T(8,128)S(1)}, u32[]{:S(2)}, u32[]{:S(2)}) %collective-permute-start.22) | collective-permute-done | bytes 1520 | tf_op jit(solution)/shard_map/ppermute | solution.py:252
  154.7 9.1 %all-to-all-done.1 = bf16[16,2,16,1536]{3,2,1,0:T(8,128)(2,1)} async-done(((bf16[16,2,16,1536]{3,2,1,0:T(8,128)(2,1)}), bf16[16,2,16,1536]{3,2,1,0:T(8,128)(2,1)}, u32[]{:S(2)}, u32[]{:S(2)}) %all-to-all-start.1) | async-done | bytes 1572896 | tf_op jit(solution)/shard_map/all_to_all | solution.py:247
  163.8 2.6 %fusion.12 = (bf16[16,1,16,1536]{3,2,1,0:T(8,128)(2,1)}, bf16[16,1,16,1536]{3,2,1,0:T(8,128)(2,1)}) fusion(bf16[16,2,16,1536]{3,2,1,0:T(8,128)(2,1)} %all-to-all-done.1), kind=kLoop, calls=%fused_computation.27 | loop fusion | bytes 3145728 | tf_op jit(solution)/shard_map/slice | solution.py:383
  (71 shorter events, 18.2 us)
Async XLA Ops:
  4.0 10.2 %copy-start.13 = (s32[16]{0:T(128)S(1)}, s32[16]{0:T(128)}, u32[]{:S(2)}) copy-start(s32[16]{0:T(128)} %constant.21.clone) | copy-start | bytes 196
  4.0 10.2 %copy-start.14 = (s32[16]{0:T(128)S(1)}, s32[16]{0:T(128)}, u32[]{:S(2)}) copy-start(s32[16]{0:T(128)} %constant.37) | copy-start | bytes 196
  4.0 10.4 %copy-start.8 = (f32[12,31]{1,0:T(8,128)S(1)}, f32[12,31]{1,0:T(8,128)}, u32[]{:S(2)}) copy-start(f32[12,31]{1,0:T(8,128)} %rel_ref) | copy-start | bytes 4468
  4.1 11.6 %copy-start.1 = (bf16[1,256,1536]{2,1,0:T(8,128)(2,1)S(1)}, bf16[1,256,1536]{2,1,0:T(8,128)(2,1)}, u32[]{:S(2)}) copy-start(bf16[1,256,1536]{2,1,0:T(8,128)(2,1)} %q_ref.3) | copy-start | bytes 2359300
  4.1 72.8 %all-to-all-start = ((bf16[16,37,16,128]{3,2,1,0:T(8,128)(2,1)}), bf16[16,37,16,128]{3,2,1,0:T(8,128)(2,1)S(1)}, u32[]{:S(2)}, u32[]{:S(2)}) async-start(bf16[16,37,16,128]{3,2,1,0:T(8,128)(2,1)} %pack.1), calls=%async_computation | async-start | bytes 4849664 | tf_op jit(solution)/shard_map/all_to_all | solution.py:247
  22.1 1.7 %collective-permute-start = (bf16[8,12,16,128]{3,2,1,0:T(8,128)(2,1)S(1)}, bf16[8,12,16,128]{3,2,1,0:T(8,128)(2,1)S(1)}, u32[]{:S(2)}, u32[]{:S(2)}) collective-permute-start(bf16[8,12,16,128]{3,2,1,0:T(8,128)(2,1)S(1)} %get-tuple-element.60), channel_id=1, source_target_pairs={{0,1},{1,0},{2,3},{3,2},{4,5},{5,4},{6,7},{7,6},{8,9},{9,8},{10,11... | collective-permute-start | bytes 1179656 | tf_op jit(solution)/shard_map/ppermute | solution.py:262
  24.6 47.3 %collective-permute-start.1 = (bf16[2,12,16,128]{3,2,1,0:T(8,128)(2,1)S(1)}, bf16[2,12,16,128]{3,2,1,0:T(8,128)(2,1)S(1)}, u32[]{:S(2)}, u32[]{:S(2)}) collective-permute-start(bf16[2,12,16,128]{3,2,1,0:T(8,128)(2,1)S(1)} %get-tuple-element.62), channel_id=1, source_target_pairs={{0,2},{1,3},{2,4},{3,5},{4,6},{5,7},{6,8},{7,9},{8,10},{9,11},{10,... | collective-permute-start | bytes 294920 | tf_op jit(solution)/shard_map/ppermute | solution.py:262
  26.0 48.6 %collective-permute-start.2 = (bf16[2,12,16,128]{3,2,1,0:T(8,128)(2,1)S(1)}, bf16[2,12,16,128]{3,2,1,0:T(8,128)(2,1)S(1)}, u32[]{:S(2)}, u32[]{:S(2)}) collective-permute-start(bf16[2,12,16,128]{3,2,1,0:T(8,128)(2,1)S(1)} %get-tuple-element.63), channel_id=1, source_target_pairs={{0,14},{1,15},{2,0},{3,1},{4,2},{5,3},{6,4},{7,5},{8,6},{9,7},{10,... | collective-permute-start | bytes 294920 | tf_op jit(solution)/shard_map/ppermute | solution.py:262
  27.3 62.5 %collective-permute-start.3 = (bf16[2,12,16,128]{3,2,1,0:T(8,128)(2,1)}, bf16[2,12,16,128]{3,2,1,0:T(8,128)(2,1)}, u32[]{:S(2)}, u32[]{:S(2)}) collective-permute-start(bf16[2,12,16,128]{3,2,1,0:T(8,128)(2,1)} %get-tuple-element.64), channel_id=1, source_target_pairs={{0,6},{1,7},{2,8},{3,9},{4,10},{5,11},{6,12},{7,13},{8,14},{9,15},... | collective-permute-start | bytes 294920 | tf_op jit(solution)/shard_map/ppermute | solution.py:262
  30.2 59.6 %collective-permute-start.4 = (bf16[2,12,16,128]{3,2,1,0:T(8,128)(2,1)}, bf16[2,12,16,128]{3,2,1,0:T(8,128)(2,1)}, u32[]{:S(2)}, u32[]{:S(2)}) collective-permute-start(bf16[2,12,16,128]{3,2,1,0:T(8,128)(2,1)} %get-tuple-element.65), channel_id=1, source_target_pairs={{0,10},{1,11},{2,12},{3,13},{4,14},{5,15},{6,0},{7,1},{8,2},{9,3},... | collective-permute-start | bytes 294920 | tf_op jit(solution)/shard_map/ppermute | solution.py:262
  31.8 58.0 %collective-permute-start.5 = (bf16[2,12,16,128]{3,2,1,0:T(8,128)(2,1)}, bf16[2,12,16,128]{3,2,1,0:T(8,128)(2,1)}, u32[]{:S(2)}, u32[]{:S(2)}) collective-permute-start(bf16[2,12,16,128]{3,2,1,0:T(8,128)(2,1)} %get-tuple-element.66), channel_id=1, source_target_pairs={{0,4},{1,5},{2,6},{3,7},{4,8},{5,9},{6,10},{7,11},{8,12},{9,13},{1... | collective-permute-start | bytes 294920 | tf_op jit(solution)/shard_map/ppermute | solution.py:262
  72.5 17.3 %collective-permute-start.6 = (bf16[2,12,16,128]{3,2,1,0:T(8,128)(2,1)}, bf16[2,12,16,128]{3,2,1,0:T(8,128)(2,1)}, u32[]{:S(2)}, u32[]{:S(2)}) collective-permute-start(bf16[2,12,16,128]{3,2,1,0:T(8,128)(2,1)} %get-tuple-element.67), channel_id=1, source_target_pairs={{0,12},{1,13},{2,14},{3,15},{4,0},{5,1},{6,2},{7,3},{8,4},{9,5},{1... | collective-permute-start | bytes 294920 | tf_op jit(solution)/shard_map/ppermute | solution.py:262
  75.2 14.6 %collective-permute-start.7 = (bf16[2,12,16,128]{3,2,1,0:T(8,128)(2,1)}, bf16[2,12,16,128]{3,2,1,0:T(8,128)(2,1)}, u32[]{:S(2)}, u32[]{:S(2)}) collective-permute-start(bf16[2,12,16,128]{3,2,1,0:T(8,128)(2,1)} %get-tuple-element.68), channel_id=1, source_target_pairs={{0,8},{1,9},{2,10},{3,11},{4,12},{5,13},{6,14},{7,15},{8,0},{9,1},... | collective-permute-start | bytes 294920 | tf_op jit(solution)/shard_map/ppermute | solution.py:262
  81.1 37.8 %all-to-all-start.2 = ((bf16[16,12,16,128]{3,2,1,0:T(8,128)(2,1)}), bf16[16,12,16,128]{3,2,1,0:T(8,128)(2,1)}, u32[]{:S(2)}, u32[]{:S(2)}) async-start(bf16[16,12,16,128]{3,2,1,0:T(8,128)(2,1)} %temporal_a.1), calls=%async_computation.2 | async-start | bytes 1572864 | tf_op jit(solution)/shard_map/all_to_all | solution.py:247
  100.0 29.5 %copy-start.3 = (bf16[1,256,1536]{2,1,0:T(8,128)(2,1)S(1)}, bf16[1,256,1536]{2,1,0:T(8,128)(2,1)}, u32[]{:S(2)}) copy-start(bf16[1,256,1536]{2,1,0:T(8,128)(2,1)} %k_ref.3) | copy-start | bytes 2359300
  100.0 29.5 %copy-start.5 = (bf16[1,256,1536]{2,1,0:T(8,128)(2,1)S(1)}, bf16[1,256,1536]{2,1,0:T(8,128)(2,1)}, u32[]{:S(2)}) copy-start(bf16[1,256,1536]{2,1,0:T(8,128)(2,1)} %v_ref.1) | copy-start | bytes 2359300
  100.0 1.9 %collective-permute-start.9 = (bf16[8,12,16,128]{3,2,1,0:T(8,128)(2,1)S(1)}, bf16[8,12,16,128]{3,2,1,0:T(8,128)(2,1)S(1)}, u32[]{:S(2)}, u32[]{:S(2)}) collective-permute-start(bf16[8,12,16,128]{3,2,1,0:T(8,128)(2,1)S(1)} %get-tuple-element.76), channel_id=1, source_target_pairs={{0,1},{1,0},{2,3},{3,2},{4,5},{5,4},{6,7},{7,6},{8,9},{9,8},{10,11... | collective-permute-start | bytes 1179656 | tf_op jit(solution)/shard_map/ppermute | solution.py:262
  100.6 1.2 collective-permute-start.8
  102.6 9.6 %collective-permute-start.10 = (bf16[25,16,128]{2,1,0:T(8,128)(2,1)S(1)}, bf16[25,16,128]{2,1,0:T(8,128)(2,1)S(1)}, u32[]{:S(2)}, u32[]{:S(2)}) collective-permute-start(bf16[25,16,128]{2,1,0:T(8,128)(2,1)S(1)} %get-tuple-element.78), channel_id=1, source_target_pairs={{0,2},{1,3},{2,4},{3,5},{4,6},{5,7},{6,8},{7,9},{8,10},{9,11},{10,... | collective-permute-start | bytes 307208 | tf_op jit(solution)/shard_map/ppermute | solution.py:262
  104.2 10.2 %collective-permute-start.11 = (bf16[25,16,128]{2,1,0:T(8,128)(2,1)S(1)}, bf16[25,16,128]{2,1,0:T(8,128)(2,1)S(1)}, u32[]{:S(2)}, u32[]{:S(2)}) collective-permute-start(bf16[25,16,128]{2,1,0:T(8,128)(2,1)S(1)} %get-tuple-element.79), channel_id=1, source_target_pairs={{0,14},{1,15},{2,0},{3,1},{4,2},{5,3},{6,4},{7,5},{8,6},{9,7},{10,... | collective-permute-start | bytes 307208 | tf_op jit(solution)/shard_map/ppermute | solution.py:262
  105.4 19.9 %collective-permute-start.12 = (bf16[25,16,128]{2,1,0:T(8,128)(2,1)}, bf16[25,16,128]{2,1,0:T(8,128)(2,1)S(1)}, u32[]{:S(2)}, u32[]{:S(2)}) collective-permute-start(bf16[25,16,128]{2,1,0:T(8,128)(2,1)} %get-tuple-element.80), channel_id=1, source_target_pairs={{0,6},{1,7},{2,8},{3,9},{4,10},{5,11},{6,12},{7,13},{8,14},{9,15},... | collective-permute-start | bytes 307208 | tf_op jit(solution)/shard_map/ppermute | solution.py:262
  108.4 16.9 %collective-permute-start.13 = (bf16[25,16,128]{2,1,0:T(8,128)(2,1)}, bf16[25,16,128]{2,1,0:T(8,128)(2,1)S(1)}, u32[]{:S(2)}, u32[]{:S(2)}) collective-permute-start(bf16[25,16,128]{2,1,0:T(8,128)(2,1)} %get-tuple-element.81), channel_id=1, source_target_pairs={{0,10},{1,11},{2,12},{3,13},{4,14},{5,15},{6,0},{7,1},{8,2},{9,3},... | collective-permute-start | bytes 307208 | tf_op jit(solution)/shard_map/ppermute | solution.py:262
  109.9 15.4 %collective-permute-start.14 = (bf16[25,16,128]{2,1,0:T(8,128)(2,1)}, bf16[25,16,128]{2,1,0:T(8,128)(2,1)S(1)}, u32[]{:S(2)}, u32[]{:S(2)}) collective-permute-start(bf16[25,16,128]{2,1,0:T(8,128)(2,1)} %get-tuple-element.82), channel_id=1, source_target_pairs={{0,4},{1,5},{2,6},{3,7},{4,8},{5,9},{6,10},{7,11},{8,12},{9,13},{1... | collective-permute-start | bytes 307208 | tf_op jit(solution)/shard_map/ppermute | solution.py:262
  112.2 13.1 %collective-permute-start.15 = (bf16[25,16,128]{2,1,0:T(8,128)(2,1)S(1)}, bf16[25,16,128]{2,1,0:T(8,128)(2,1)S(1)}, u32[]{:S(2)}, u32[]{:S(2)}) collective-permute-start(bf16[25,16,128]{2,1,0:T(8,128)(2,1)S(1)} %get-tuple-element.83), channel_id=1, source_target_pairs={{0,12},{1,13},{2,14},{3,15},{4,0},{5,1},{6,2},{7,3},{8,4},{9,5},{1... | collective-permute-start | bytes 307208 | tf_op jit(solution)/shard_map/ppermute | solution.py:262
  114.5 15.0 %collective-permute-start.16 = (bf16[25,16,128]{2,1,0:T(8,128)(2,1)S(1)}, bf16[25,16,128]{2,1,0:T(8,128)(2,1)S(1)}, u32[]{:S(2)}, u32[]{:S(2)}) collective-permute-start(bf16[25,16,128]{2,1,0:T(8,128)(2,1)S(1)} %get-tuple-element.84), channel_id=1, source_target_pairs={{0,8},{1,9},{2,10},{3,11},{4,12},{5,13},{6,14},{7,15},{8,0},{9,1},... | collective-permute-start | bytes 307208 | tf_op jit(solution)/shard_map/ppermute | solution.py:262
  118.9 44.9 %all-to-all-start.1 = ((bf16[16,2,16,1536]{3,2,1,0:T(8,128)(2,1)}), bf16[16,2,16,1536]{3,2,1,0:T(8,128)(2,1)}, u32[]{:S(2)}, u32[]{:S(2)}) async-start(bf16[16,2,16,1536]{3,2,1,0:T(8,128)(2,1)} %copy-done), calls=%async_computation.1 | async-start | bytes 3145728 | tf_op jit(solution)/shard_map/all_to_all | solution.py:247
  138.3 3.9 %collective-permute-start.17 = (f32[12,31]{1,0:T(8,128)S(1)}, f32[12,31]{1,0:T(8,128)S(1)}, u32[]{:S(2)}, u32[]{:S(2)}) collective-permute-start(f32[12,31]{1,0:T(8,128)S(1)} %get-tuple-element.98), channel_id=1, source_target_pairs={{0,16},{16,0},{32,48},{48,32},{64,80},{80,64},{96,112},{112,96},{1... | collective-permute-start | bytes 4472 | tf_op jit(solution)/shard_map/ppermute | solution.py:252
  139.6 4.4 %collective-permute-start.18 = (f32[12,31]{1,0:T(8,128)S(1)}, f32[12,31]{1,0:T(8,128)S(1)}, u32[]{:S(2)}, u32[]{:S(2)}) collective-permute-start(f32[12,31]{1,0:T(8,128)S(1)} %get-tuple-element.98), channel_id=1, source_target_pairs={{0,32},{16,48},{32,0},{48,16},{64,96},{80,112},{96,64},{112,80},{1... | collective-permute-start | bytes 4472 | tf_op jit(solution)/shard_map/ppermute | solution.py:252
  142.2 4.1 %collective-permute-start.19 = (f32[12,31]{1,0:T(8,128)S(1)}, f32[12,31]{1,0:T(8,128)S(1)}, u32[]{:S(2)}, u32[]{:S(2)}) collective-permute-start(f32[12,31]{1,0:T(8,128)S(1)} %get-tuple-element.98), channel_id=1, source_target_pairs={{0,48},{16,32},{32,16},{48,0},{64,112},{80,96},{96,80},{112,64},{1... | collective-permute-start | bytes 4472 | tf_op jit(solution)/shard_map/ppermute | solution.py:252
  146.4 3.9 %collective-permute-start.20 = (f32[12,31]{1,0:T(8,128)S(1)}, f32[12,31]{1,0:T(8,128)S(1)}, u32[]{:S(2)}, u32[]{:S(2)}) collective-permute-start(f32[12,31]{1,0:T(8,128)S(1)} %add_add_fusion.1), channel_id=1, source_target_pairs={{0,64},{16,80},{32,96},{48,112},{64,0},{80,16},{96,32},{112,48},{1... | collective-permute-start | bytes 4472 | tf_op jit(solution)/shard_map/ppermute | solution.py:252
  147.6 4.4 %collective-permute-start.21 = (f32[12,31]{1,0:T(8,128)S(1)}, f32[12,31]{1,0:T(8,128)S(1)}, u32[]{:S(2)}, u32[]{:S(2)}) collective-permute-start(f32[12,31]{1,0:T(8,128)S(1)} %add_add_fusion.1), channel_id=1, source_target_pairs={{0,128},{16,144},{32,160},{48,176},{64,192},{80,208},{96,224},{112... | collective-permute-start | bytes 4472 | tf_op jit(solution)/shard_map/ppermute | solution.py:252
  150.0 4.1 %collective-permute-start.22 = (f32[12,31]{1,0:T(8,128)S(1)}, f32[12,31]{1,0:T(8,128)S(1)}, u32[]{:S(2)}, u32[]{:S(2)}) collective-permute-start(f32[12,31]{1,0:T(8,128)S(1)} %add_add_fusion.1), channel_id=1, source_target_pairs={{0,192},{16,208},{32,224},{48,240},{64,128},{80,144},{96,160},{112... | collective-permute-start | bytes 4472 | tf_op jit(solution)/shard_map/ppermute | solution.py:252
  (9 other events, 16.2 us)

commit v9 on v8

--- a/solution.py
+++ b/solution.py
@@ -19,7 +19,7 @@
 F32 = jnp.float32
 PARAMS = pltpu.CompilerParams(vmem_limit_bytes=48 * 1024 * 1024)
 PARTS = 4
-LONG = 10**12
+LONG = 10**11
 VMEM = pl.BlockSpec(memory_space=pltpu.VMEM)
 SMEM = pl.BlockSpec(memory_space=pltpu.SMEM)
 HBM = pl.BlockSpec(memory_space=pltpu.HBM)
@@ -214,6 +214,17 @@
         put_pairs(keep_ref, give_ref, h, mm_tn(low, q))
 
 
+def unpack_kernel(in_ref, res_ref, gq_ref, sems):
+    copies = []
+    for u in range(SEQ):
+        for i, out in enumerate((res_ref, gq_ref)):
+            rows = pl.ds(u * TOK, TOK)
+            copies.append(pltpu.make_async_copy(in_ref.at[u, i], out.at[0, rows], sems.at[u, i]))
+            copies[-1].start()
+    for copy in copies:
+        copy.wait()
+
+
 def finish_kernel(pos_ref, *refs):
     messages, (gk_ref, bias_ref) = refs[:CHIPS], refs[CHIPS:]
     for ref, shift in zip(messages, (0,) + SHIFTS):
@@ -380,7 +391,15 @@
         [frame(), jax.ShapeDtypeStruct((HEADS, RELS), F32)],
     )
     total_bias = sum_of_four(sum_of_four(total, "grp", 1), "grp", 4)
-    result, grad_qt = (returned[:, i].reshape(1, ROWS, WIDTH) for i in range(2))
+    result, grad_qt = call(
+        unpack_kernel,
+        "unpack",
+        [VMEM],
+        [returned],
+        [frame()] * 2,
+        [pltpu.SemaphoreType.DMA((SEQ, 2))],
+        space=HBM,
+    )
     return result, grad_qs, grad_ks, grad_vs, grad_qt, grad_kt, total_bias
 
 

time: 167 us -> 166 us (level)
  Pallas kernels: 29.8 us -> 31.8 us
  waiting for transfers between devices: 63.9 us -> 62 us
    slice x1 -> x0, local copies, waits for them, and re-layouts: 2.61 us -> none  [per_device(): result, grad_qt = (returned[:, i].reshape(1, ROWS, WIDTH) for i in range(2))]
    pallas_call x9 -> x10, Pallas kernels: 29.8 us -> 31.8 us  [call(): pl.pallas_call(kernel, out_shape=tuple(outputs), in_specs=specs, out_spec...]
    all_to_all x3, waiting for transfers between devices: 9.07 us -> 7.25 us  [exchange(): lax.all_to_all(packed, 'seq', split_axis=0, concat_axis=0, tiled=True)]
  transfers between devices with their start and end apart: 26 -> 26, of which waited for: 10 -> 10; matrix products, arithmetic and copies ran while one was open for 1% -> 1% of each run, Pallas kernels for 16% -> 17%
where the time goes in v9:
time: 166 us; the launch traced here: 165 us
  waiting for transfers between devices  62 us (37%)
  starting transfers between devices  60.7 us (37%)
  Pallas kernels  31.8 us (19%)
  local copies, waits for them, and re-layouts  7.81 us (5%)
    ppermute x17, waiting for transfers between devices, move(): return lax.ppermute(message, 'seq', perm)  46.9 us
    pallas_call x10, Pallas kernels, call(): pl.pallas_call(kernel, out_shape=tuple(outputs), in_specs=specs, out_spec...  31.8 us
    ppermute x17, starting transfers between devices, move(): return lax.ppermute(message, 'seq', perm)  27.7 us
    all_to_all x3, starting transfers between devices, exchange(): lax.all_to_all(packed, 'seq', split_axis=0, concat_axis=0, tiled=True)  25.2 us
    ppermute x6, waiting for transfers between devices, pair(): return lax.ppermute(terms, axis, [(i, i ^ mask) for i in range(size)])  7.81 us
    ppermute x6, starting transfers between devices, pair(): return lax.ppermute(terms, axis, [(i, i ^ mask) for i in range(size)])  7.79 us
    unnamed x30, local copies, waits for them, and re-layouts  7.65 us
    all_to_all x3, waiting for transfers between devices, exchange(): lax.all_to_all(packed, 'seq', split_axis=0, concat_axis=0, tiled=True)  7.25 us
  transfers between devices with their start and end apart: 26, of which 10 were waited for; matrix products, arithmetic and copies ran while one was open for 1% of the time, Pallas kernels for 17%

profile of v9, /device:TPU:1, one launch (start us, length us, event | category | flops | bytes accessed | tf_op | source)
XLA Modules:
  0.0 165.2 jit_solution(15550701168114262229)
XLA Ops:
  1.3 2.7 %pack.1 = bf16[16,37,16,128]{3,2,1,0:T(8,128)(2,1)} custom-call(s32[1,1]{1,0:T(1,128)S(6)} %copy.20.clip_ref, bf16[1,256,1536]{2,1,0:T(8,128)(2,1)} %q_ref.1, bf16[1,256,1536]{2,1,0:T(8,128)(2,1)} %k_ref.1, bf16[1,256,1536]{2,1,0:T(8,128)(2,1)} %up_ref.1), custom_call_target="tpu_custom_call" | custom-call | flops 1000 | bytes 1000 | tf_op jit(solution)/shard_map/pack/pallas_call | solution.py:245
  4.1 10.1 %all-to-all-start = ((bf16[16,37,16,128]{3,2,1,0:T(8,128)(2,1)}), bf16[16,37,16,128]{3,2,1,0:T(8,128)(2,1)S(1)}, u32[]{:S(2)}, u32[]{:S(2)}) async-start(bf16[16,37,16,128]{3,2,1,0:T(8,128)(2,1)} %pack.1), calls=%async_computation | async-start | bytes 4849664 | tf_op jit(solution)/shard_map/all_to_all | solution.py:258
  17.9 4.1 %spatial_fwd.1 = (bf16[8,12,16,128]{3,2,1,0:T(8,128)(2,1)S(1)}, bf16[8,12,16,128]{3,2,1,0:T(8,128)(2,1)S(1)}, f32[12,256,256]{2,1,0:T(8,128)}) custom-call(s32[2]{0:T(128)S(1)} %pad_add_fusion.pos_ref, bf16[1,256,1536]{2,1,0:T(8,128)(2,1)S(1)} %copy-done.1, bf16[1,256,1536]{2,1,0:T(8,128)(2,1)S(1)} %copy-done.2, bf16[1,256,1536]{2,1,0:T(8,128)(2,1)S(1)} %copy-done.4), custom_call_target="tpu_custom_call" | custom-call | flops 1000 | bytes 1000 | tf_op jit(solution)/shard_map/spatial_fwd/pallas_call | solution.py:245
  22.2 1.6 collective-permute-done.got_ref
  24.6 1.4 collective-permute-start.1
  26.0 1.3 collective-permute-start.2
  27.2 2.9 %collective-permute-start.3 = (bf16[2,12,16,128]{3,2,1,0:T(8,128)(2,1)}, bf16[2,12,16,128]{3,2,1,0:T(8,128)(2,1)}, u32[]{:S(2)}, u32[]{:S(2)}) collective-permute-start(bf16[2,12,16,128]{3,2,1,0:T(8,128)(2,1)} %get-tuple-element.66), channel_id=1, source_target_pairs={{0,6},{1,7},{2,8},{3,9},{4,10},{5,11},{6,12},{7,13},{8,14},{9,15},... | collective-permute-start | bytes 294920 | tf_op jit(solution)/shard_map/ppermute | solution.py:273
  30.2 1.6 collective-permute-start.4
  32.8 39.1 %collective-permute-done.1.refs_1_ = bf16[2,12,16,128]{3,2,1,0:T(8,128)(2,1)S(1)} collective-permute-done((bf16[2,12,16,128]{3,2,1,0:T(8,128)(2,1)S(1)}, bf16[2,12,16,128]{3,2,1,0:T(8,128)(2,1)S(1)}, u32[]{:S(2)}, u32[]{:S(2)}) %collective-permute-start.1) | collective-permute-done | bytes 98336 | tf_op jit(solution)/shard_map/ppermute | solution.py:273
  72.5 2.1 %collective-permute-start.6 = (bf16[2,12,16,128]{3,2,1,0:T(8,128)(2,1)}, bf16[2,12,16,128]{3,2,1,0:T(8,128)(2,1)}, u32[]{:S(2)}, u32[]{:S(2)}) collective-permute-start(bf16[2,12,16,128]{3,2,1,0:T(8,128)(2,1)} %get-tuple-element.69), channel_id=1, source_target_pairs={{0,12},{1,13},{2,14},{3,15},{4,0},{5,1},{6,2},{7,3},{8,4},{9,5},{1... | collective-permute-start | bytes 294920 | tf_op jit(solution)/shard_map/ppermute | solution.py:273
  75.2 1.7 %collective-permute-start.7 = (bf16[2,12,16,128]{3,2,1,0:T(8,128)(2,1)}, bf16[2,12,16,128]{3,2,1,0:T(8,128)(2,1)}, u32[]{:S(2)}, u32[]{:S(2)}) collective-permute-start(bf16[2,12,16,128]{3,2,1,0:T(8,128)(2,1)} %get-tuple-element.70), channel_id=1, source_target_pairs={{0,8},{1,9},{2,10},{3,11},{4,12},{5,13},{6,14},{7,15},{8,0},{9,1},... | collective-permute-start | bytes 294920 | tf_op jit(solution)/shard_map/ppermute | solution.py:273
  76.9 4.2 %temporal_a.1 = bf16[16,12,16,128]{3,2,1,0:T(8,128)(2,1)} custom-call(s32[16]{0:T(128)S(1)} %fusion.11.frames_ref, bf16[16,37,16,128]{3,2,1,0:T(8,128)(2,1)S(1)} %all-to-all-done.in_ref, f32[12,16,256]{2,1,0:T(8,128)S(1)} %bias.1.bias_ref), custom_call_target="tpu_custom_call" | custom-call | flops 1000 | bytes 1000 | tf_op jit(solution)/shard_map/temporal_a/pallas_call | solution.py:245
  81.1 8.7 %all-to-all-start.2 = ((bf16[16,12,16,128]{3,2,1,0:T(8,128)(2,1)}), bf16[16,12,16,128]{3,2,1,0:T(8,128)(2,1)}, u32[]{:S(2)}, u32[]{:S(2)}) async-start(bf16[16,12,16,128]{3,2,1,0:T(8,128)(2,1)} %temporal_a.1), calls=%async_computation.2 | async-start | bytes 1572864 | tf_op jit(solution)/shard_map/all_to_all | solution.py:258
  91.6 7.2 %temporal_b.1 = (bf16[16,2,16,1536]{3,2,1,0:T(8,128)(2,1)S(1)}, bf16[8,12,16,128]{3,2,1,0:T(8,128)(2,1)S(1)}, bf16[8,12,16,128]{3,2,1,0:T(8,128)(2,1)S(1)}, f32[12,16,256]{2,1,0:T(8,128)S(1)}) custom-call(s32[16]{0:T(128)S(1)} %fusion.11.frames_ref, bf16[16,37,16,128]{3,2,1,0:T(8,128)(2,1)S(1)} %all-to-all-done.in_ref, f32[12,16,256]{2,1,0:T(8,128)S(1)} %bias.1.bias_ref, ...), custom_call_target="tpu_custom_call" | custom-call | flops 99999997952 | bytes 1000 | tf_op jit(solution)/shard_map/temporal_b/pallas_call | solution.py:245
  102.7 1.6 collective-permute-start.10
  105.5 3.0 %collective-permute-start.12 = (bf16[25,16,128]{2,1,0:T(8,128)(2,1)}, bf16[25,16,128]{2,1,0:T(8,128)(2,1)}, u32[]{:S(2)}, u32[]{:S(2)}) collective-permute-start(bf16[25,16,128]{2,1,0:T(8,128)(2,1)} %get-tuple-element.83), channel_id=1, source_target_pairs={{0,6},{1,7},{2,8},{3,9},{4,10},{5,11},{6,12},{7,13},{8,14},{9,15},... | collective-permute-start | bytes 307208 | tf_op jit(solution)/shard_map/ppermute | solution.py:273
  108.5 1.5 collective-permute-start.13
  112.3 2.2 %collective-permute-start.15 = (bf16[25,16,128]{2,1,0:T(8,128)(2,1)}, bf16[25,16,128]{2,1,0:T(8,128)(2,1)}, u32[]{:S(2)}, u32[]{:S(2)}) collective-permute-start(bf16[25,16,128]{2,1,0:T(8,128)(2,1)} %get-tuple-element.86), channel_id=1, source_target_pairs={{0,12},{1,13},{2,14},{3,15},{4,0},{5,1},{6,2},{7,3},{8,4},{9,5},{1... | collective-permute-start | bytes 307208 | tf_op jit(solution)/shard_map/ppermute | solution.py:273
  114.5 4.5 %collective-permute-start.16 = (bf16[25,16,128]{2,1,0:T(8,128)(2,1)}, bf16[25,16,128]{2,1,0:T(8,128)(2,1)}, u32[]{:S(2)}, u32[]{:S(2)}) collective-permute-start(bf16[25,16,128]{2,1,0:T(8,128)(2,1)} %get-tuple-element.87), channel_id=1, source_target_pairs={{0,8},{1,9},{2,10},{3,11},{4,12},{5,13},{6,14},{7,15},{8,0},{9,1},... | collective-permute-start | bytes 307208 | tf_op jit(solution)/shard_map/ppermute | solution.py:273
  118.9 6.4 %all-to-all-start.1 = ((bf16[16,2,16,1536]{3,2,1,0:T(8,128)(2,1)}), bf16[16,2,16,1536]{3,2,1,0:T(8,128)(2,1)S(1)}, u32[]{:S(2)}, u32[]{:S(2)}) async-start(bf16[16,2,16,1536]{3,2,1,0:T(8,128)(2,1)} %copy-done), calls=%async_computation.1 | async-start | bytes 3145728 | tf_op jit(solution)/shard_map/all_to_all | solution.py:258
  125.4 4.3 %collective-permute-done.16.refs_7_ = bf16[25,16,128]{2,1,0:T(8,128)(2,1)} collective-permute-done((bf16[25,16,128]{2,1,0:T(8,128)(2,1)}, bf16[25,16,128]{2,1,0:T(8,128)(2,1)}, u32[]{:S(2)}, u32[]{:S(2)}) %collective-permute-start.16) | collective-permute-done | bytes 102432 | tf_op jit(solution)/shard_map/ppermute | solution.py:273
  130.8 7.2 %spatial_bwd.1 = (bf16[1,256,1536]{2,1,0:T(8,128)(2,1)}, bf16[1,256,1536]{2,1,0:T(8,128)(2,1)}, bf16[1,256,1536]{2,1,0:T(8,128)(2,1)}) custom-call(bf16[1,256,1536]{2,1,0:T(8,128)(2,1)S(1)} %copy-done.1, bf16[1,256,1536]{2,1,0:T(8,128)(2,1)S(1)} %copy-done.3, bf16[1,256,1536]{2,1,0:T(8,128)(2,1)S(1)} %copy-done.5, ...), custom_call_target="tpu_custom_call" | custom-call | flops 99999997952 | bytes 1000 | tf_op jit(solution)/shard_map/spatial_bwd/pallas_call | solution.py:245
  138.0 2.2 %finish.1 = (bf16[1,256,1536]{2,1,0:T(8,128)(2,1)}, f32[12,31]{1,0:T(8,128)S(1)}) custom-call(s32[2]{0:T(128)S(1)} %copy-done.8, bf16[25,16,128]{2,1,0:T(8,128)(2,1)S(1)} %get-tuple-element.93.refs_0_, bf16[25,16,128]{2,1,0:T(8,128)(2,1)S(1)} %collective-permute-done.10.refs_1_, bf16[25,16,128]{2,1,0:T(8,128)(2,1)S(1)} %collective-permute-done.11.refs_2_, ...), custom_call_target="tpu_custom_call" | custom-call | flops 1000 | bytes 1000 | tf_op jit(solution)/shard_map/finish/pallas_call | solution.py:245
  140.2 1.3 collective-permute-start.17
  141.5 2.6 %collective-permute-start.18 = (f32[12,31]{1,0:T(8,128)S(1)}, f32[12,31]{1,0:T(8,128)S(1)}, u32[]{:S(2)}, u32[]{:S(2)}) collective-permute-start(f32[12,31]{1,0:T(8,128)S(1)} %get-tuple-element.102), channel_id=1, source_target_pairs={{0,32},{16,48},{32,0},{48,16},{64,96},{80,112},{96,64},{112,80},{1... | collective-permute-start | bytes 4472 | tf_op jit(solution)/shard_map/ppermute | solution.py:263
  144.1 1.7 %collective-permute-done.18 = f32[12,31]{1,0:T(8,128)S(1)} collective-permute-done((f32[12,31]{1,0:T(8,128)S(1)}, f32[12,31]{1,0:T(8,128)S(1)}, u32[]{:S(2)}, u32[]{:S(2)}) %collective-permute-start.18) | collective-permute-done | bytes 1520 | tf_op jit(solution)/shard_map/ppermute | solution.py:263
  145.8 2.3 %collective-permute-done.19 = f32[12,31]{1,0:T(8,128)S(1)} collective-permute-done((f32[12,31]{1,0:T(8,128)S(1)}, f32[12,31]{1,0:T(8,128)S(1)}, u32[]{:S(2)}, u32[]{:S(2)}) %collective-permute-start.19) | collective-permute-done | bytes 1520 | tf_op jit(solution)/shard_map/ppermute | solution.py:263
  149.3 2.5 %collective-permute-start.21 = (f32[12,31]{1,0:T(8,128)S(1)}, f32[12,31]{1,0:T(8,128)S(1)}, u32[]{:S(2)}, u32[]{:S(2)}) collective-permute-start(f32[12,31]{1,0:T(8,128)S(1)} %add_add_fusion.1), channel_id=1, source_target_pairs={{0,128},{16,144},{32,160},{48,176},{64,192},{80,208},{96,224},{112... | collective-permute-start | bytes 4472 | tf_op jit(solution)/shard_map/ppermute | solution.py:263
  152.0 1.6 collective-permute-done.21
  153.6 2.2 %collective-permute-done.22 = f32[12,31]{1,0:T(8,128)S(1)} collective-permute-done((f32[12,31]{1,0:T(8,128)S(1)}, f32[12,31]{1,0:T(8,128)S(1)}, u32[]{:S(2)}, u32[]{:S(2)}) %collective-permute-start.22) | collective-permute-done | bytes 1520 | tf_op jit(solution)/shard_map/ppermute | solution.py:263
  156.4 7.2 %all-to-all-done.1.in_ref = bf16[16,2,16,1536]{3,2,1,0:T(8,128)(2,1)S(1)} async-done(((bf16[16,2,16,1536]{3,2,1,0:T(8,128)(2,1)}), bf16[16,2,16,1536]{3,2,1,0:T(8,128)(2,1)S(1)}, u32[]{:S(2)}, u32[]{:S(2)}) %all-to-all-start.1) | async-done | bytes 1572896 | tf_op jit(solution)/shard_map/all_to_all | solution.py:258
  163.6 1.4 unpack.1
  (71 shorter events, 19.3 us)
Async XLA Ops:
  4.0 10.2 %copy-start.13 = (s32[16]{0:T(128)S(1)}, s32[16]{0:T(128)}, u32[]{:S(2)}) copy-start(s32[16]{0:T(128)} %constant.21.clone) | copy-start | bytes 196
  4.0 10.2 %copy-start.14 = (s32[16]{0:T(128)S(1)}, s32[16]{0:T(128)}, u32[]{:S(2)}) copy-start(s32[16]{0:T(128)} %constant.37) | copy-start | bytes 196
  4.0 10.4 %copy-start.6 = (f32[12,31]{1,0:T(8,128)S(1)}, f32[12,31]{1,0:T(8,128)}, u32[]{:S(2)}) copy-start(f32[12,31]{1,0:T(8,128)} %rel_ref) | copy-start | bytes 4468
  4.1 11.6 %copy-start.1 = (bf16[1,256,1536]{2,1,0:T(8,128)(2,1)S(1)}, bf16[1,256,1536]{2,1,0:T(8,128)(2,1)}, u32[]{:S(2)}) copy-start(bf16[1,256,1536]{2,1,0:T(8,128)(2,1)} %q_ref.3) | copy-start | bytes 2359300
  4.1 72.8 %all-to-all-start = ((bf16[16,37,16,128]{3,2,1,0:T(8,128)(2,1)}), bf16[16,37,16,128]{3,2,1,0:T(8,128)(2,1)S(1)}, u32[]{:S(2)}, u32[]{:S(2)}) async-start(bf16[16,37,16,128]{3,2,1,0:T(8,128)(2,1)} %pack.1), calls=%async_computation | async-start | bytes 4849664 | tf_op jit(solution)/shard_map/all_to_all | solution.py:258
  17.9 63.2 %copy-start.7 = (s32[2]{0:T(128)}, s32[2]{0:T(128)S(1)}, u32[]{:S(2)}) copy-start(s32[2]{0:T(128)S(1)} %pad_add_fusion.pos_ref) | copy-start | bytes 28
  22.0 1.7 %collective-permute-start = (bf16[8,12,16,128]{3,2,1,0:T(8,128)(2,1)S(1)}, bf16[8,12,16,128]{3,2,1,0:T(8,128)(2,1)S(1)}, u32[]{:S(2)}, u32[]{:S(2)}) collective-permute-start(bf16[8,12,16,128]{3,2,1,0:T(8,128)(2,1)S(1)} %get-tuple-element.62), channel_id=1, source_target_pairs={{0,1},{1,0},{2,3},{3,2},{4,5},{5,4},{6,7},{7,6},{8,9},{9,8},{10,11... | collective-permute-start | bytes 1179656 | tf_op jit(solution)/shard_map/ppermute | solution.py:273
  24.6 47.3 %collective-permute-start.1 = (bf16[2,12,16,128]{3,2,1,0:T(8,128)(2,1)S(1)}, bf16[2,12,16,128]{3,2,1,0:T(8,128)(2,1)S(1)}, u32[]{:S(2)}, u32[]{:S(2)}) collective-permute-start(bf16[2,12,16,128]{3,2,1,0:T(8,128)(2,1)S(1)} %get-tuple-element.64), channel_id=1, source_target_pairs={{0,2},{1,3},{2,4},{3,5},{4,6},{5,7},{6,8},{7,9},{8,10},{9,11},{10,... | collective-permute-start | bytes 294920 | tf_op jit(solution)/shard_map/ppermute | solution.py:273
  26.0 48.6 %collective-permute-start.2 = (bf16[2,12,16,128]{3,2,1,0:T(8,128)(2,1)S(1)}, bf16[2,12,16,128]{3,2,1,0:T(8,128)(2,1)S(1)}, u32[]{:S(2)}, u32[]{:S(2)}) collective-permute-start(bf16[2,12,16,128]{3,2,1,0:T(8,128)(2,1)S(1)} %get-tuple-element.65), channel_id=1, source_target_pairs={{0,14},{1,15},{2,0},{3,1},{4,2},{5,3},{6,4},{7,5},{8,6},{9,7},{10,... | collective-permute-start | bytes 294920 | tf_op jit(solution)/shard_map/ppermute | solution.py:273
  27.2 62.5 %collective-permute-start.3 = (bf16[2,12,16,128]{3,2,1,0:T(8,128)(2,1)}, bf16[2,12,16,128]{3,2,1,0:T(8,128)(2,1)}, u32[]{:S(2)}, u32[]{:S(2)}) collective-permute-start(bf16[2,12,16,128]{3,2,1,0:T(8,128)(2,1)} %get-tuple-element.66), channel_id=1, source_target_pairs={{0,6},{1,7},{2,8},{3,9},{4,10},{5,11},{6,12},{7,13},{8,14},{9,15},... | collective-permute-start | bytes 294920 | tf_op jit(solution)/shard_map/ppermute | solution.py:273
  30.2 59.6 %collective-permute-start.4 = (bf16[2,12,16,128]{3,2,1,0:T(8,128)(2,1)}, bf16[2,12,16,128]{3,2,1,0:T(8,128)(2,1)}, u32[]{:S(2)}, u32[]{:S(2)}) collective-permute-start(bf16[2,12,16,128]{3,2,1,0:T(8,128)(2,1)} %get-tuple-element.67), channel_id=1, source_target_pairs={{0,10},{1,11},{2,12},{3,13},{4,14},{5,15},{6,0},{7,1},{8,2},{9,3},... | collective-permute-start | bytes 294920 | tf_op jit(solution)/shard_map/ppermute | solution.py:273
  31.7 58.1 %collective-permute-start.5 = (bf16[2,12,16,128]{3,2,1,0:T(8,128)(2,1)}, bf16[2,12,16,128]{3,2,1,0:T(8,128)(2,1)}, u32[]{:S(2)}, u32[]{:S(2)}) collective-permute-start(bf16[2,12,16,128]{3,2,1,0:T(8,128)(2,1)} %get-tuple-element.68), channel_id=1, source_target_pairs={{0,4},{1,5},{2,6},{3,7},{4,8},{5,9},{6,10},{7,11},{8,12},{9,13},{1... | collective-permute-start | bytes 294920 | tf_op jit(solution)/shard_map/ppermute | solution.py:273
  72.5 17.3 %collective-permute-start.6 = (bf16[2,12,16,128]{3,2,1,0:T(8,128)(2,1)}, bf16[2,12,16,128]{3,2,1,0:T(8,128)(2,1)}, u32[]{:S(2)}, u32[]{:S(2)}) collective-permute-start(bf16[2,12,16,128]{3,2,1,0:T(8,128)(2,1)} %get-tuple-element.69), channel_id=1, source_target_pairs={{0,12},{1,13},{2,14},{3,15},{4,0},{5,1},{6,2},{7,3},{8,4},{9,5},{1... | collective-permute-start | bytes 294920 | tf_op jit(solution)/shard_map/ppermute | solution.py:273
  75.2 14.6 %collective-permute-start.7 = (bf16[2,12,16,128]{3,2,1,0:T(8,128)(2,1)}, bf16[2,12,16,128]{3,2,1,0:T(8,128)(2,1)}, u32[]{:S(2)}, u32[]{:S(2)}) collective-permute-start(bf16[2,12,16,128]{3,2,1,0:T(8,128)(2,1)} %get-tuple-element.70), channel_id=1, source_target_pairs={{0,8},{1,9},{2,10},{3,11},{4,12},{5,13},{6,14},{7,15},{8,0},{9,1},... | collective-permute-start | bytes 294920 | tf_op jit(solution)/shard_map/ppermute | solution.py:273
  81.1 37.9 %all-to-all-start.2 = ((bf16[16,12,16,128]{3,2,1,0:T(8,128)(2,1)}), bf16[16,12,16,128]{3,2,1,0:T(8,128)(2,1)}, u32[]{:S(2)}, u32[]{:S(2)}) async-start(bf16[16,12,16,128]{3,2,1,0:T(8,128)(2,1)} %temporal_a.1), calls=%async_computation.2 | async-start | bytes 1572864 | tf_op jit(solution)/shard_map/all_to_all | solution.py:258
  100.0 29.6 %copy-start.3 = (bf16[1,256,1536]{2,1,0:T(8,128)(2,1)S(1)}, bf16[1,256,1536]{2,1,0:T(8,128)(2,1)}, u32[]{:S(2)}) copy-start(bf16[1,256,1536]{2,1,0:T(8,128)(2,1)} %k_ref.3) | copy-start | bytes 2359300
  100.0 1.9 %collective-permute-start.9 = (bf16[8,12,16,128]{3,2,1,0:T(8,128)(2,1)S(1)}, bf16[8,12,16,128]{3,2,1,0:T(8,128)(2,1)S(1)}, u32[]{:S(2)}, u32[]{:S(2)}) collective-permute-start(bf16[8,12,16,128]{3,2,1,0:T(8,128)(2,1)S(1)} %get-tuple-element.79), channel_id=1, source_target_pairs={{0,1},{1,0},{2,3},{3,2},{4,5},{5,4},{6,7},{7,6},{8,9},{9,8},{10,11... | collective-permute-start | bytes 1179656 | tf_op jit(solution)/shard_map/ppermute | solution.py:273
  100.6 1.2 collective-permute-start.8
  102.7 9.6 %collective-permute-start.10 = (bf16[25,16,128]{2,1,0:T(8,128)(2,1)S(1)}, bf16[25,16,128]{2,1,0:T(8,128)(2,1)S(1)}, u32[]{:S(2)}, u32[]{:S(2)}) collective-permute-start(bf16[25,16,128]{2,1,0:T(8,128)(2,1)S(1)} %get-tuple-element.81), channel_id=1, source_target_pairs={{0,2},{1,3},{2,4},{3,5},{4,6},{5,7},{6,8},{7,9},{8,10},{9,11},{10,... | collective-permute-start | bytes 307208 | tf_op jit(solution)/shard_map/ppermute | solution.py:273
  104.3 10.2 %collective-permute-start.11 = (bf16[25,16,128]{2,1,0:T(8,128)(2,1)S(1)}, bf16[25,16,128]{2,1,0:T(8,128)(2,1)S(1)}, u32[]{:S(2)}, u32[]{:S(2)}) collective-permute-start(bf16[25,16,128]{2,1,0:T(8,128)(2,1)S(1)} %get-tuple-element.82), channel_id=1, source_target_pairs={{0,14},{1,15},{2,0},{3,1},{4,2},{5,3},{6,4},{7,5},{8,6},{9,7},{10,... | collective-permute-start | bytes 307208 | tf_op jit(solution)/shard_map/ppermute | solution.py:273
  105.5 19.8 %collective-permute-start.12 = (bf16[25,16,128]{2,1,0:T(8,128)(2,1)}, bf16[25,16,128]{2,1,0:T(8,128)(2,1)}, u32[]{:S(2)}, u32[]{:S(2)}) collective-permute-start(bf16[25,16,128]{2,1,0:T(8,128)(2,1)} %get-tuple-element.83), channel_id=1, source_target_pairs={{0,6},{1,7},{2,8},{3,9},{4,10},{5,11},{6,12},{7,13},{8,14},{9,15},... | collective-permute-start | bytes 307208 | tf_op jit(solution)/shard_map/ppermute | solution.py:273
  108.5 16.8 %collective-permute-start.13 = (bf16[25,16,128]{2,1,0:T(8,128)(2,1)}, bf16[25,16,128]{2,1,0:T(8,128)(2,1)}, u32[]{:S(2)}, u32[]{:S(2)}) collective-permute-start(bf16[25,16,128]{2,1,0:T(8,128)(2,1)} %get-tuple-element.84), channel_id=1, source_target_pairs={{0,10},{1,11},{2,12},{3,13},{4,14},{5,15},{6,0},{7,1},{8,2},{9,3},... | collective-permute-start | bytes 307208 | tf_op jit(solution)/shard_map/ppermute | solution.py:273
  110.0 15.4 %collective-permute-start.14 = (bf16[25,16,128]{2,1,0:T(8,128)(2,1)}, bf16[25,16,128]{2,1,0:T(8,128)(2,1)}, u32[]{:S(2)}, u32[]{:S(2)}) collective-permute-start(bf16[25,16,128]{2,1,0:T(8,128)(2,1)} %get-tuple-element.85), channel_id=1, source_target_pairs={{0,4},{1,5},{2,6},{3,7},{4,8},{5,9},{6,10},{7,11},{8,12},{9,13},{1... | collective-permute-start | bytes 307208 | tf_op jit(solution)/shard_map/ppermute | solution.py:273
  112.3 13.1 %collective-permute-start.15 = (bf16[25,16,128]{2,1,0:T(8,128)(2,1)}, bf16[25,16,128]{2,1,0:T(8,128)(2,1)}, u32[]{:S(2)}, u32[]{:S(2)}) collective-permute-start(bf16[25,16,128]{2,1,0:T(8,128)(2,1)} %get-tuple-element.86), channel_id=1, source_target_pairs={{0,12},{1,13},{2,14},{3,15},{4,0},{5,1},{6,2},{7,3},{8,4},{9,5},{1... | collective-permute-start | bytes 307208 | tf_op jit(solution)/shard_map/ppermute | solution.py:273
  114.5 15.2 %collective-permute-start.16 = (bf16[25,16,128]{2,1,0:T(8,128)(2,1)}, bf16[25,16,128]{2,1,0:T(8,128)(2,1)}, u32[]{:S(2)}, u32[]{:S(2)}) collective-permute-start(bf16[25,16,128]{2,1,0:T(8,128)(2,1)} %get-tuple-element.87), channel_id=1, source_target_pairs={{0,8},{1,9},{2,10},{3,11},{4,12},{5,13},{6,14},{7,15},{8,0},{9,1},... | collective-permute-start | bytes 307208 | tf_op jit(solution)/shard_map/ppermute | solution.py:273
  118.9 44.7 %all-to-all-start.1 = ((bf16[16,2,16,1536]{3,2,1,0:T(8,128)(2,1)}), bf16[16,2,16,1536]{3,2,1,0:T(8,128)(2,1)S(1)}, u32[]{:S(2)}, u32[]{:S(2)}) async-start(bf16[16,2,16,1536]{3,2,1,0:T(8,128)(2,1)} %copy-done), calls=%async_computation.1 | async-start | bytes 3145728 | tf_op jit(solution)/shard_map/all_to_all | solution.py:258
  140.2 3.9 %collective-permute-start.17 = (f32[12,31]{1,0:T(8,128)S(1)}, f32[12,31]{1,0:T(8,128)S(1)}, u32[]{:S(2)}, u32[]{:S(2)}) collective-permute-start(f32[12,31]{1,0:T(8,128)S(1)} %get-tuple-element.102), channel_id=1, source_target_pairs={{0,16},{16,0},{32,48},{48,32},{64,80},{80,64},{96,112},{112,96},{1... | collective-permute-start | bytes 4472 | tf_op jit(solution)/shard_map/ppermute | solution.py:263
  141.5 4.3 %collective-permute-start.18 = (f32[12,31]{1,0:T(8,128)S(1)}, f32[12,31]{1,0:T(8,128)S(1)}, u32[]{:S(2)}, u32[]{:S(2)}) collective-permute-start(f32[12,31]{1,0:T(8,128)S(1)} %get-tuple-element.102), channel_id=1, source_target_pairs={{0,32},{16,48},{32,0},{48,16},{64,96},{80,112},{96,64},{112,80},{1... | collective-permute-start | bytes 4472 | tf_op jit(solution)/shard_map/ppermute | solution.py:263
  144.1 4.0 %collective-permute-start.19 = (f32[12,31]{1,0:T(8,128)S(1)}, f32[12,31]{1,0:T(8,128)S(1)}, u32[]{:S(2)}, u32[]{:S(2)}) collective-permute-start(f32[12,31]{1,0:T(8,128)S(1)} %get-tuple-element.102), channel_id=1, source_target_pairs={{0,48},{16,32},{32,16},{48,0},{64,112},{80,96},{96,80},{112,64},{1... | collective-permute-start | bytes 4472 | tf_op jit(solution)/shard_map/ppermute | solution.py:263
  148.1 3.9 %collective-permute-start.20 = (f32[12,31]{1,0:T(8,128)S(1)}, f32[12,31]{1,0:T(8,128)S(1)}, u32[]{:S(2)}, u32[]{:S(2)}) collective-permute-start(f32[12,31]{1,0:T(8,128)S(1)} %add_add_fusion.1), channel_id=1, source_target_pairs={{0,64},{16,80},{32,96},{48,112},{64,0},{80,16},{96,32},{112,48},{1... | collective-permute-start | bytes 4472 | tf_op jit(solution)/shard_map/ppermute | solution.py:263
  149.3 4.3 %collective-permute-start.21 = (f32[12,31]{1,0:T(8,128)S(1)}, f32[12,31]{1,0:T(8,128)S(1)}, u32[]{:S(2)}, u32[]{:S(2)}) collective-permute-start(f32[12,31]{1,0:T(8,128)S(1)} %add_add_fusion.1), channel_id=1, source_target_pairs={{0,128},{16,144},{32,160},{48,176},{64,192},{80,208},{96,224},{112... | collective-permute-start | bytes 4472 | tf_op jit(solution)/shard_map/ppermute | solution.py:263
  151.7 4.0 %collective-permute-start.22 = (f32[12,31]{1,0:T(8,128)S(1)}, f32[12,31]{1,0:T(8,128)S(1)}, u32[]{:S(2)}, u32[]{:S(2)}) collective-permute-start(f32[12,31]{1,0:T(8,128)S(1)} %add_add_fusion.1), channel_id=1, source_target_pairs={{0,192},{16,208},{32,224},{48,240},{64,128},{80,144},{96,160},{112... | collective-permute-start | bytes 4472 | tf_op jit(solution)/shard_map/ppermute | solution.py:263
  (9 other events, 14.8 us)

commit v10 on v9

--- a/solution.py
+++ b/solution.py
@@ -66,7 +66,7 @@
     return ref[:, tile].reshape(ROWS, DIM)
 
 
-SHIFTS = (1, -1, 3, -3, 2, -2, 4)
+SHIFTS = (1, -1, 4, 3, -3, 2, -2)
 SLOTS = tuple((d, x) for x in range(2) for d in range(CHIPS))
 
 

time: 166 us -> 165 us (level)
  waiting for transfers between devices: 62 us -> 56.6 us
  starting transfers between devices: 60.7 us -> 64.9 us
    ppermute x17, waiting for transfers between devices: 46.9 us -> 41.8 us  [move(): return lax.ppermute(message, 'seq', perm)]
    ppermute x17, starting transfers between devices: 27.7 us -> 32.9 us  [move(): return lax.ppermute(message, 'seq', perm)]
  transfers between devices with their start and end apart: 26 -> 26, of which waited for: 10 -> 11; matrix products, arithmetic and copies ran while one was open for 1% -> 1% of each run, Pallas kernels for 17% -> 17%
where the time goes in v10:
time: 165 us; the launch traced here: 164 us
  starting transfers between devices  64.9 us (39%)
  waiting for transfers between devices  56.6 us (34%)
  Pallas kernels  31.8 us (19%)
  local copies, waits for them, and re-layouts  7.81 us (5%)
    ppermute x17, waiting for transfers between devices, move(): return lax.ppermute(message, 'seq', perm)  41.8 us
    ppermute x17, starting transfers between devices, move(): return lax.ppermute(message, 'seq', perm)  32.9 us
    pallas_call x10, Pallas kernels, call(): pl.pallas_call(kernel, out_shape=tuple(outputs), in_specs=specs, out_spec...  31.8 us
    all_to_all x3, starting transfers between devices, exchange(): lax.all_to_all(packed, 'seq', split_axis=0, concat_axis=0, tiled=True)  24.3 us
    ppermute x6, waiting for transfers between devices, pair(): return lax.ppermute(terms, axis, [(i, i ^ mask) for i in range(size)])  7.81 us
    ppermute x6, starting transfers between devices, pair(): return lax.ppermute(terms, axis, [(i, i ^ mask) for i in range(size)])  7.78 us
    unnamed x30, local copies, waits for them, and re-layouts  7.65 us
    all_to_all x3, waiting for transfers between devices, exchange(): lax.all_to_all(packed, 'seq', split_axis=0, concat_axis=0, tiled=True)  7.06 us
  transfers between devices with their start and end apart: 26, of which 11 were waited for; matrix products, arithmetic and copies ran while one was open for 1% of the time, Pallas kernels for 17%

profile of v10, /device:TPU:1, one launch (start us, length us, event | category | flops | bytes accessed | tf_op | source)
XLA Modules:
  0.0 164.1 jit_solution(9002812690549129894)
XLA Ops:
  1.3 2.7 %pack.1 = bf16[16,37,16,128]{3,2,1,0:T(8,128)(2,1)} custom-call(s32[1,1]{1,0:T(1,128)S(6)} %copy.20.clip_ref, bf16[1,256,1536]{2,1,0:T(8,128)(2,1)} %q_ref.1, bf16[1,256,1536]{2,1,0:T(8,128)(2,1)} %k_ref.1, bf16[1,256,1536]{2,1,0:T(8,128)(2,1)} %up_ref.1), custom_call_target="tpu_custom_call" | custom-call | flops 1000 | bytes 1000 | tf_op jit(solution)/shard_map/pack/pallas_call | solution.py:245
  4.1 10.1 %all-to-all-start = ((bf16[16,37,16,128]{3,2,1,0:T(8,128)(2,1)}), bf16[16,37,16,128]{3,2,1,0:T(8,128)(2,1)S(1)}, u32[]{:S(2)}, u32[]{:S(2)}) async-start(bf16[16,37,16,128]{3,2,1,0:T(8,128)(2,1)} %pack.1), calls=%async_computation | async-start | bytes 4849664 | tf_op jit(solution)/shard_map/all_to_all | solution.py:258
  17.9 4.1 %spatial_fwd.1 = (bf16[8,12,16,128]{3,2,1,0:T(8,128)(2,1)S(1)}, bf16[8,12,16,128]{3,2,1,0:T(8,128)(2,1)S(1)}, f32[12,256,256]{2,1,0:T(8,128)}) custom-call(s32[2]{0:T(128)S(1)} %pad_add_fusion.pos_ref, bf16[1,256,1536]{2,1,0:T(8,128)(2,1)S(1)} %copy-done.1, bf16[1,256,1536]{2,1,0:T(8,128)(2,1)S(1)} %copy-done.2, bf16[1,256,1536]{2,1,0:T(8,128)(2,1)S(1)} %copy-done.4), custom_call_target="tpu_custom_call" | custom-call | flops 1000 | bytes 1000 | tf_op jit(solution)/shard_map/spatial_fwd/pallas_call | solution.py:245
  22.2 1.6 collective-permute-done.got_ref
  24.6 1.4 collective-permute-start.1
  26.0 1.3 collective-permute-start.2
  27.2 5.3 %collective-permute-start.3 = (bf16[2,12,16,128]{3,2,1,0:T(8,128)(2,1)}, bf16[2,12,16,128]{3,2,1,0:T(8,128)(2,1)}, u32[]{:S(2)}, u32[]{:S(2)}) collective-permute-start(bf16[2,12,16,128]{3,2,1,0:T(8,128)(2,1)} %get-tuple-element.66), channel_id=1, source_target_pairs={{0,8},{1,9},{2,10},{3,11},{4,12},{5,13},{6,14},{7,15},{8,0},{9,1},... | collective-permute-start | bytes 294920 | tf_op jit(solution)/shard_map/ppermute | solution.py:273
  32.5 4.5 %collective-permute-start.5 = (bf16[2,12,16,128]{3,2,1,0:T(8,128)(2,1)}, bf16[2,12,16,128]{3,2,1,0:T(8,128)(2,1)}, u32[]{:S(2)}, u32[]{:S(2)}) collective-permute-start(bf16[2,12,16,128]{3,2,1,0:T(8,128)(2,1)} %get-tuple-element.68), channel_id=1, source_target_pairs={{0,10},{1,11},{2,12},{3,13},{4,14},{5,15},{6,0},{7,1},{8,2},{9,3},... | collective-permute-start | bytes 294920 | tf_op jit(solution)/shard_map/ppermute | solution.py:273
  37.0 34.9 %collective-permute-done.1.refs_1_ = bf16[2,12,16,128]{3,2,1,0:T(8,128)(2,1)S(1)} collective-permute-done((bf16[2,12,16,128]{3,2,1,0:T(8,128)(2,1)S(1)}, bf16[2,12,16,128]{3,2,1,0:T(8,128)(2,1)S(1)}, u32[]{:S(2)}, u32[]{:S(2)}) %collective-permute-start.1) | collective-permute-done | bytes 98336 | tf_op jit(solution)/shard_map/ppermute | solution.py:273
  73.3 3.4 %collective-permute-start.7 = (bf16[2,12,16,128]{3,2,1,0:T(8,128)(2,1)}, bf16[2,12,16,128]{3,2,1,0:T(8,128)(2,1)}, u32[]{:S(2)}, u32[]{:S(2)}) collective-permute-start(bf16[2,12,16,128]{3,2,1,0:T(8,128)(2,1)} %get-tuple-element.70), channel_id=1, source_target_pairs={{0,12},{1,13},{2,14},{3,15},{4,0},{5,1},{6,2},{7,3},{8,4},{9,5},{1... | collective-permute-start | bytes 294920 | tf_op jit(solution)/shard_map/ppermute | solution.py:273
  76.7 4.2 %temporal_a.1 = bf16[16,12,16,128]{3,2,1,0:T(8,128)(2,1)} custom-call(s32[16]{0:T(128)S(1)} %fusion.11.frames_ref, bf16[16,37,16,128]{3,2,1,0:T(8,128)(2,1)S(1)} %all-to-all-done.in_ref, f32[12,16,256]{2,1,0:T(8,128)S(1)} %bias.1.bias_ref), custom_call_target="tpu_custom_call" | custom-call | flops 1000 | bytes 1000 | tf_op jit(solution)/shard_map/temporal_a/pallas_call | solution.py:245
  80.9 8.5 %all-to-all-start.2 = ((bf16[16,12,16,128]{3,2,1,0:T(8,128)(2,1)}), bf16[16,12,16,128]{3,2,1,0:T(8,128)(2,1)}, u32[]{:S(2)}, u32[]{:S(2)}) async-start(bf16[16,12,16,128]{3,2,1,0:T(8,128)(2,1)} %temporal_a.1), calls=%async_computation.2 | async-start | bytes 1572864 | tf_op jit(solution)/shard_map/all_to_all | solution.py:258
  91.3 7.2 %temporal_b.1 = (bf16[16,2,16,1536]{3,2,1,0:T(8,128)(2,1)S(1)}, bf16[8,12,16,128]{3,2,1,0:T(8,128)(2,1)S(1)}, bf16[8,12,16,128]{3,2,1,0:T(8,128)(2,1)S(1)}, f32[12,16,256]{2,1,0:T(8,128)S(1)}) custom-call(s32[16]{0:T(128)S(1)} %fusion.11.frames_ref, bf16[16,37,16,128]{3,2,1,0:T(8,128)(2,1)S(1)} %all-to-all-done.in_ref, f32[12,16,256]{2,1,0:T(8,128)S(1)} %bias.1.bias_ref, ...), custom_call_target="tpu_custom_call" | custom-call | flops 99999997952 | bytes 1000 | tf_op jit(solution)/shard_map/temporal_b/pallas_call | solution.py:245
  102.4 1.6 collective-permute-start.10
  104.0 1.2 collective-permute-start.11
  105.2 5.4 %collective-permute-start.12 = (bf16[25,16,128]{2,1,0:T(8,128)(2,1)}, bf16[25,16,128]{2,1,0:T(8,128)(2,1)}, u32[]{:S(2)}, u32[]{:S(2)}) collective-permute-start(bf16[25,16,128]{2,1,0:T(8,128)(2,1)} %get-tuple-element.83), channel_id=1, source_target_pairs={{0,8},{1,9},{2,10},{3,11},{4,12},{5,13},{6,14},{7,15},{8,0},{9,1},... | collective-permute-start | bytes 307208 | tf_op jit(solution)/shard_map/ppermute | solution.py:273
  110.6 4.5 %collective-permute-start.14 = (bf16[25,16,128]{2,1,0:T(8,128)(2,1)}, bf16[25,16,128]{2,1,0:T(8,128)(2,1)}, u32[]{:S(2)}, u32[]{:S(2)}) collective-permute-start(bf16[25,16,128]{2,1,0:T(8,128)(2,1)} %get-tuple-element.85), channel_id=1, source_target_pairs={{0,10},{1,11},{2,12},{3,13},{4,14},{5,15},{6,0},{7,1},{8,2},{9,3},... | collective-permute-start | bytes 307208 | tf_op jit(solution)/shard_map/ppermute | solution.py:273
  115.0 3.6 %collective-permute-start.16 = (bf16[25,16,128]{2,1,0:T(8,128)(2,1)}, bf16[25,16,128]{2,1,0:T(8,128)(2,1)}, u32[]{:S(2)}, u32[]{:S(2)}) collective-permute-start(bf16[25,16,128]{2,1,0:T(8,128)(2,1)} %get-tuple-element.87), channel_id=1, source_target_pairs={{0,12},{1,13},{2,14},{3,15},{4,0},{5,1},{6,2},{7,3},{8,4},{9,5},{1... | collective-permute-start | bytes 307208 | tf_op jit(solution)/shard_map/ppermute | solution.py:273
  118.6 5.6 %all-to-all-start.1 = ((bf16[16,2,16,1536]{3,2,1,0:T(8,128)(2,1)}), bf16[16,2,16,1536]{3,2,1,0:T(8,128)(2,1)S(1)}, u32[]{:S(2)}, u32[]{:S(2)}) async-start(bf16[16,2,16,1536]{3,2,1,0:T(8,128)(2,1)} %copy-done), calls=%async_computation.1 | async-start | bytes 3145728 | tf_op jit(solution)/shard_map/all_to_all | solution.py:258
  124.3 1.4 collective-permute-done.13.refs_4_
  126.7 2.0 %collective-permute-done.16.refs_7_ = bf16[25,16,128]{2,1,0:T(8,128)(2,1)} collective-permute-done((bf16[25,16,128]{2,1,0:T(8,128)(2,1)}, bf16[25,16,128]{2,1,0:T(8,128)(2,1)}, u32[]{:S(2)}, u32[]{:S(2)}) %collective-permute-start.16) | collective-permute-done | bytes 102432 | tf_op jit(solution)/shard_map/ppermute | solution.py:273
  129.8 7.2 %spatial_bwd.1 = (bf16[1,256,1536]{2,1,0:T(8,128)(2,1)}, bf16[1,256,1536]{2,1,0:T(8,128)(2,1)}, bf16[1,256,1536]{2,1,0:T(8,128)(2,1)}) custom-call(bf16[1,256,1536]{2,1,0:T(8,128)(2,1)S(1)} %copy-done.1, bf16[1,256,1536]{2,1,0:T(8,128)(2,1)S(1)} %copy-done.3, bf16[1,256,1536]{2,1,0:T(8,128)(2,1)S(1)} %copy-done.5, ...), custom_call_target="tpu_custom_call" | custom-call | flops 99999997952 | bytes 1000 | tf_op jit(solution)/shard_map/spatial_bwd/pallas_call | solution.py:245
  137.0 2.2 %finish.1 = (bf16[1,256,1536]{2,1,0:T(8,128)(2,1)}, f32[12,31]{1,0:T(8,128)S(1)}) custom-call(s32[2]{0:T(128)S(1)} %copy-done.8, bf16[25,16,128]{2,1,0:T(8,128)(2,1)S(1)} %get-tuple-element.93.refs_0_, bf16[25,16,128]{2,1,0:T(8,128)(2,1)S(1)} %collective-permute-done.10.refs_1_, bf16[25,16,128]{2,1,0:T(8,128)(2,1)S(1)} %collective-permute-done.11.refs_2_, ...), custom_call_target="tpu_custom_call" | custom-call | flops 1000 | bytes 1000 | tf_op jit(solution)/shard_map/finish/pallas_call | solution.py:245
  139.2 1.3 collective-permute-start.17
  140.5 2.6 %collective-permute-start.18 = (f32[12,31]{1,0:T(8,128)S(1)}, f32[12,31]{1,0:T(8,128)S(1)}, u32[]{:S(2)}, u32[]{:S(2)}) collective-permute-start(f32[12,31]{1,0:T(8,128)S(1)} %get-tuple-element.102), channel_id=1, source_target_pairs={{0,32},{16,48},{32,0},{48,16},{64,96},{80,112},{96,64},{112,80},{1... | collective-permute-start | bytes 4472 | tf_op jit(solution)/shard_map/ppermute | solution.py:263
  143.1 1.7 %collective-permute-done.18 = f32[12,31]{1,0:T(8,128)S(1)} collective-permute-done((f32[12,31]{1,0:T(8,128)S(1)}, f32[12,31]{1,0:T(8,128)S(1)}, u32[]{:S(2)}, u32[]{:S(2)}) %collective-permute-start.18) | collective-permute-done | bytes 1520 | tf_op jit(solution)/shard_map/ppermute | solution.py:263
  144.8 2.3 %collective-permute-done.19 = f32[12,31]{1,0:T(8,128)S(1)} collective-permute-done((f32[12,31]{1,0:T(8,128)S(1)}, f32[12,31]{1,0:T(8,128)S(1)}, u32[]{:S(2)}, u32[]{:S(2)}) %collective-permute-start.19) | collective-permute-done | bytes 1520 | tf_op jit(solution)/shard_map/ppermute | solution.py:263
  148.4 2.4 %collective-permute-start.21 = (f32[12,31]{1,0:T(8,128)S(1)}, f32[12,31]{1,0:T(8,128)S(1)}, u32[]{:S(2)}, u32[]{:S(2)}) collective-permute-start(f32[12,31]{1,0:T(8,128)S(1)} %add_add_fusion.1), channel_id=1, source_target_pairs={{0,128},{16,144},{32,160},{48,176},{64,192},{80,208},{96,224},{112... | collective-permute-start | bytes 4472 | tf_op jit(solution)/shard_map/ppermute | solution.py:263
  151.0 1.6 %collective-permute-done.21 = f32[12,31]{1,0:T(8,128)S(1)} collective-permute-done((f32[12,31]{1,0:T(8,128)S(1)}, f32[12,31]{1,0:T(8,128)S(1)}, u32[]{:S(2)}, u32[]{:S(2)}) %collective-permute-start.21) | collective-permute-done | bytes 1520 | tf_op jit(solution)/shard_map/ppermute | solution.py:263
  152.7 2.2 %collective-permute-done.22 = f32[12,31]{1,0:T(8,128)S(1)} collective-permute-done((f32[12,31]{1,0:T(8,128)S(1)}, f32[12,31]{1,0:T(8,128)S(1)}, u32[]{:S(2)}, u32[]{:S(2)}) %collective-permute-start.22) | collective-permute-done | bytes 1520 | tf_op jit(solution)/shard_map/ppermute | solution.py:263
  155.4 7.0 %all-to-all-done.1.in_ref = bf16[16,2,16,1536]{3,2,1,0:T(8,128)(2,1)S(1)} async-done(((bf16[16,2,16,1536]{3,2,1,0:T(8,128)(2,1)}), bf16[16,2,16,1536]{3,2,1,0:T(8,128)(2,1)S(1)}, u32[]{:S(2)}, u32[]{:S(2)}) %all-to-all-start.1) | async-done | bytes 1572896 | tf_op jit(solution)/shard_map/all_to_all | solution.py:258
  162.5 1.4 unpack.1
  (71 shorter events, 15.9 us)
Async XLA Ops:
  4.0 10.2 %copy-start.13 = (s32[16]{0:T(128)S(1)}, s32[16]{0:T(128)}, u32[]{:S(2)}) copy-start(s32[16]{0:T(128)} %constant.21.clone) | copy-start | bytes 196
  4.0 10.2 %copy-start.14 = (s32[16]{0:T(128)S(1)}, s32[16]{0:T(128)}, u32[]{:S(2)}) copy-start(s32[16]{0:T(128)} %constant.37) | copy-start | bytes 196
  4.0 10.4 %copy-start.6 = (f32[12,31]{1,0:T(8,128)S(1)}, f32[12,31]{1,0:T(8,128)}, u32[]{:S(2)}) copy-start(f32[12,31]{1,0:T(8,128)} %rel_ref) | copy-start | bytes 4468
  4.1 11.6 %copy-start.1 = (bf16[1,256,1536]{2,1,0:T(8,128)(2,1)S(1)}, bf16[1,256,1536]{2,1,0:T(8,128)(2,1)}, u32[]{:S(2)}) copy-start(bf16[1,256,1536]{2,1,0:T(8,128)(2,1)} %q_ref.3) | copy-start | bytes 2359300
  4.1 72.7 %all-to-all-start = ((bf16[16,37,16,128]{3,2,1,0:T(8,128)(2,1)}), bf16[16,37,16,128]{3,2,1,0:T(8,128)(2,1)S(1)}, u32[]{:S(2)}, u32[]{:S(2)}) async-start(bf16[16,37,16,128]{3,2,1,0:T(8,128)(2,1)} %pack.1), calls=%async_computation | async-start | bytes 4849664 | tf_op jit(solution)/shard_map/all_to_all | solution.py:258
  17.9 63.0 %copy-start.7 = (s32[2]{0:T(128)}, s32[2]{0:T(128)S(1)}, u32[]{:S(2)}) copy-start(s32[2]{0:T(128)S(1)} %pad_add_fusion.pos_ref) | copy-start | bytes 28
  22.0 1.7 %collective-permute-start = (bf16[8,12,16,128]{3,2,1,0:T(8,128)(2,1)S(1)}, bf16[8,12,16,128]{3,2,1,0:T(8,128)(2,1)S(1)}, u32[]{:S(2)}, u32[]{:S(2)}) collective-permute-start(bf16[8,12,16,128]{3,2,1,0:T(8,128)(2,1)S(1)} %get-tuple-element.62), channel_id=1, source_target_pairs={{0,1},{1,0},{2,3},{3,2},{4,5},{5,4},{6,7},{7,6},{8,9},{9,8},{10,11... | collective-permute-start | bytes 1179656 | tf_op jit(solution)/shard_map/ppermute | solution.py:273
  24.6 47.3 %collective-permute-start.1 = (bf16[2,12,16,128]{3,2,1,0:T(8,128)(2,1)S(1)}, bf16[2,12,16,128]{3,2,1,0:T(8,128)(2,1)S(1)}, u32[]{:S(2)}, u32[]{:S(2)}) collective-permute-start(bf16[2,12,16,128]{3,2,1,0:T(8,128)(2,1)S(1)} %get-tuple-element.64), channel_id=1, source_target_pairs={{0,2},{1,3},{2,4},{3,5},{4,6},{5,7},{6,8},{7,9},{8,10},{9,11},{10,... | collective-permute-start | bytes 294920 | tf_op jit(solution)/shard_map/ppermute | solution.py:273
  26.0 46.7 %collective-permute-start.2 = (bf16[2,12,16,128]{3,2,1,0:T(8,128)(2,1)S(1)}, bf16[2,12,16,128]{3,2,1,0:T(8,128)(2,1)S(1)}, u32[]{:S(2)}, u32[]{:S(2)}) collective-permute-start(bf16[2,12,16,128]{3,2,1,0:T(8,128)(2,1)S(1)} %get-tuple-element.65), channel_id=1, source_target_pairs={{0,14},{1,15},{2,0},{3,1},{4,2},{5,3},{6,4},{7,5},{8,6},{9,7},{10,... | collective-permute-start | bytes 294920 | tf_op jit(solution)/shard_map/ppermute | solution.py:273
  27.2 62.2 %collective-permute-start.3 = (bf16[2,12,16,128]{3,2,1,0:T(8,128)(2,1)}, bf16[2,12,16,128]{3,2,1,0:T(8,128)(2,1)}, u32[]{:S(2)}, u32[]{:S(2)}) collective-permute-start(bf16[2,12,16,128]{3,2,1,0:T(8,128)(2,1)} %get-tuple-element.66), channel_id=1, source_target_pairs={{0,8},{1,9},{2,10},{3,11},{4,12},{5,13},{6,14},{7,15},{8,0},{9,1},... | collective-permute-start | bytes 294920 | tf_op jit(solution)/shard_map/ppermute | solution.py:273
  32.5 56.9 %collective-permute-start.4 = (bf16[2,12,16,128]{3,2,1,0:T(8,128)(2,1)}, bf16[2,12,16,128]{3,2,1,0:T(8,128)(2,1)}, u32[]{:S(2)}, u32[]{:S(2)}) collective-permute-start(bf16[2,12,16,128]{3,2,1,0:T(8,128)(2,1)} %get-tuple-element.67), channel_id=1, source_target_pairs={{0,6},{1,7},{2,8},{3,9},{4,10},{5,11},{6,12},{7,13},{8,14},{9,15},... | collective-permute-start | bytes 294920 | tf_op jit(solution)/shard_map/ppermute | solution.py:273
  32.5 56.9 %collective-permute-start.5 = (bf16[2,12,16,128]{3,2,1,0:T(8,128)(2,1)}, bf16[2,12,16,128]{3,2,1,0:T(8,128)(2,1)}, u32[]{:S(2)}, u32[]{:S(2)}) collective-permute-start(bf16[2,12,16,128]{3,2,1,0:T(8,128)(2,1)} %get-tuple-element.68), channel_id=1, source_target_pairs={{0,10},{1,11},{2,12},{3,13},{4,14},{5,15},{6,0},{7,1},{8,2},{9,3},... | collective-permute-start | bytes 294920 | tf_op jit(solution)/shard_map/ppermute | solution.py:273
  72.5 17.0 %collective-permute-start.6 = (bf16[2,12,16,128]{3,2,1,0:T(8,128)(2,1)}, bf16[2,12,16,128]{3,2,1,0:T(8,128)(2,1)}, u32[]{:S(2)}, u32[]{:S(2)}) collective-permute-start(bf16[2,12,16,128]{3,2,1,0:T(8,128)(2,1)} %get-tuple-element.69), channel_id=1, source_target_pairs={{0,4},{1,5},{2,6},{3,7},{4,8},{5,9},{6,10},{7,11},{8,12},{9,13},{1... | collective-permute-start | bytes 294920 | tf_op jit(solution)/shard_map/ppermute | solution.py:273
  73.3 16.2 %collective-permute-start.7 = (bf16[2,12,16,128]{3,2,1,0:T(8,128)(2,1)}, bf16[2,12,16,128]{3,2,1,0:T(8,128)(2,1)}, u32[]{:S(2)}, u32[]{:S(2)}) collective-permute-start(bf16[2,12,16,128]{3,2,1,0:T(8,128)(2,1)} %get-tuple-element.70), channel_id=1, source_target_pairs={{0,12},{1,13},{2,14},{3,15},{4,0},{5,1},{6,2},{7,3},{8,4},{9,5},{1... | collective-permute-start | bytes 294920 | tf_op jit(solution)/shard_map/ppermute | solution.py:273
  80.9 37.7 %all-to-all-start.2 = ((bf16[16,12,16,128]{3,2,1,0:T(8,128)(2,1)}), bf16[16,12,16,128]{3,2,1,0:T(8,128)(2,1)}, u32[]{:S(2)}, u32[]{:S(2)}) async-start(bf16[16,12,16,128]{3,2,1,0:T(8,128)(2,1)} %temporal_a.1), calls=%async_computation.2 | async-start | bytes 1572864 | tf_op jit(solution)/shard_map/all_to_all | solution.py:258
  99.7 29.0 %copy-start.3 = (bf16[1,256,1536]{2,1,0:T(8,128)(2,1)S(1)}, bf16[1,256,1536]{2,1,0:T(8,128)(2,1)}, u32[]{:S(2)}) copy-start(bf16[1,256,1536]{2,1,0:T(8,128)(2,1)} %k_ref.3) | copy-start | bytes 2359300
  99.7 1.9 %collective-permute-start.9 = (bf16[8,12,16,128]{3,2,1,0:T(8,128)(2,1)S(1)}, bf16[8,12,16,128]{3,2,1,0:T(8,128)(2,1)S(1)}, u32[]{:S(2)}, u32[]{:S(2)}) collective-permute-start(bf16[8,12,16,128]{3,2,1,0:T(8,128)(2,1)S(1)} %get-tuple-element.79), channel_id=1, source_target_pairs={{0,1},{1,0},{2,3},{3,2},{4,5},{5,4},{6,7},{7,6},{8,9},{9,8},{10,11... | collective-permute-start | bytes 1179656 | tf_op jit(solution)/shard_map/ppermute | solution.py:273
  100.3 1.2 collective-permute-start.8
  102.4 12.6 %collective-permute-start.10 = (bf16[25,16,128]{2,1,0:T(8,128)(2,1)S(1)}, bf16[25,16,128]{2,1,0:T(8,128)(2,1)S(1)}, u32[]{:S(2)}, u32[]{:S(2)}) collective-permute-start(bf16[25,16,128]{2,1,0:T(8,128)(2,1)S(1)} %get-tuple-element.81), channel_id=1, source_target_pairs={{0,2},{1,3},{2,4},{3,5},{4,6},{5,7},{6,8},{7,9},{8,10},{9,11},{10,... | collective-permute-start | bytes 307208 | tf_op jit(solution)/shard_map/ppermute | solution.py:273
  104.0 11.1 %collective-permute-start.11 = (bf16[25,16,128]{2,1,0:T(8,128)(2,1)S(1)}, bf16[25,16,128]{2,1,0:T(8,128)(2,1)S(1)}, u32[]{:S(2)}, u32[]{:S(2)}) collective-permute-start(bf16[25,16,128]{2,1,0:T(8,128)(2,1)S(1)} %get-tuple-element.82), channel_id=1, source_target_pairs={{0,14},{1,15},{2,0},{3,1},{4,2},{5,3},{6,4},{7,5},{8,6},{9,7},{10,... | collective-permute-start | bytes 307208 | tf_op jit(solution)/shard_map/ppermute | solution.py:273
  105.2 19.1 %collective-permute-start.12 = (bf16[25,16,128]{2,1,0:T(8,128)(2,1)}, bf16[25,16,128]{2,1,0:T(8,128)(2,1)}, u32[]{:S(2)}, u32[]{:S(2)}) collective-permute-start(bf16[25,16,128]{2,1,0:T(8,128)(2,1)} %get-tuple-element.83), channel_id=1, source_target_pairs={{0,8},{1,9},{2,10},{3,11},{4,12},{5,13},{6,14},{7,15},{8,0},{9,1},... | collective-permute-start | bytes 307208 | tf_op jit(solution)/shard_map/ppermute | solution.py:273
  110.6 15.1 %collective-permute-start.13 = (bf16[25,16,128]{2,1,0:T(8,128)(2,1)}, bf16[25,16,128]{2,1,0:T(8,128)(2,1)}, u32[]{:S(2)}, u32[]{:S(2)}) collective-permute-start(bf16[25,16,128]{2,1,0:T(8,128)(2,1)} %get-tuple-element.84), channel_id=1, source_target_pairs={{0,6},{1,7},{2,8},{3,9},{4,10},{5,11},{6,12},{7,13},{8,14},{9,15},... | collective-permute-start | bytes 307208 | tf_op jit(solution)/shard_map/ppermute | solution.py:273
  110.6 15.1 %collective-permute-start.14 = (bf16[25,16,128]{2,1,0:T(8,128)(2,1)}, bf16[25,16,128]{2,1,0:T(8,128)(2,1)}, u32[]{:S(2)}, u32[]{:S(2)}) collective-permute-start(bf16[25,16,128]{2,1,0:T(8,128)(2,1)} %get-tuple-element.85), channel_id=1, source_target_pairs={{0,10},{1,11},{2,12},{3,13},{4,14},{5,15},{6,0},{7,1},{8,2},{9,3},... | collective-permute-start | bytes 307208 | tf_op jit(solution)/shard_map/ppermute | solution.py:273
  115.0 11.6 %collective-permute-start.15 = (bf16[25,16,128]{2,1,0:T(8,128)(2,1)}, bf16[25,16,128]{2,1,0:T(8,128)(2,1)}, u32[]{:S(2)}, u32[]{:S(2)}) collective-permute-start(bf16[25,16,128]{2,1,0:T(8,128)(2,1)} %get-tuple-element.86), channel_id=1, source_target_pairs={{0,4},{1,5},{2,6},{3,7},{4,8},{5,9},{6,10},{7,11},{8,12},{9,13},{1... | collective-permute-start | bytes 307208 | tf_op jit(solution)/shard_map/ppermute | solution.py:273
  115.0 13.6 %collective-permute-start.16 = (bf16[25,16,128]{2,1,0:T(8,128)(2,1)}, bf16[25,16,128]{2,1,0:T(8,128)(2,1)}, u32[]{:S(2)}, u32[]{:S(2)}) collective-permute-start(bf16[25,16,128]{2,1,0:T(8,128)(2,1)} %get-tuple-element.87), channel_id=1, source_target_pairs={{0,12},{1,13},{2,14},{3,15},{4,0},{5,1},{6,2},{7,3},{8,4},{9,5},{1... | collective-permute-start | bytes 307208 | tf_op jit(solution)/shard_map/ppermute | solution.py:273
  118.6 43.9 %all-to-all-start.1 = ((bf16[16,2,16,1536]{3,2,1,0:T(8,128)(2,1)}), bf16[16,2,16,1536]{3,2,1,0:T(8,128)(2,1)S(1)}, u32[]{:S(2)}, u32[]{:S(2)}) async-start(bf16[16,2,16,1536]{3,2,1,0:T(8,128)(2,1)} %copy-done), calls=%async_computation.1 | async-start | bytes 3145728 | tf_op jit(solution)/shard_map/all_to_all | solution.py:258
  139.2 3.9 %collective-permute-start.17 = (f32[12,31]{1,0:T(8,128)S(1)}, f32[12,31]{1,0:T(8,128)S(1)}, u32[]{:S(2)}, u32[]{:S(2)}) collective-permute-start(f32[12,31]{1,0:T(8,128)S(1)} %get-tuple-element.102), channel_id=1, source_target_pairs={{0,16},{16,0},{32,48},{48,32},{64,80},{80,64},{96,112},{112,96},{1... | collective-permute-start | bytes 4472 | tf_op jit(solution)/shard_map/ppermute | solution.py:263
  140.5 4.3 %collective-permute-start.18 = (f32[12,31]{1,0:T(8,128)S(1)}, f32[12,31]{1,0:T(8,128)S(1)}, u32[]{:S(2)}, u32[]{:S(2)}) collective-permute-start(f32[12,31]{1,0:T(8,128)S(1)} %get-tuple-element.102), channel_id=1, source_target_pairs={{0,32},{16,48},{32,0},{48,16},{64,96},{80,112},{96,64},{112,80},{1... | collective-permute-start | bytes 4472 | tf_op jit(solution)/shard_map/ppermute | solution.py:263
  143.1 4.0 %collective-permute-start.19 = (f32[12,31]{1,0:T(8,128)S(1)}, f32[12,31]{1,0:T(8,128)S(1)}, u32[]{:S(2)}, u32[]{:S(2)}) collective-permute-start(f32[12,31]{1,0:T(8,128)S(1)} %get-tuple-element.102), channel_id=1, source_target_pairs={{0,48},{16,32},{32,16},{48,0},{64,112},{80,96},{96,80},{112,64},{1... | collective-permute-start | bytes 4472 | tf_op jit(solution)/shard_map/ppermute | solution.py:263
  147.2 3.9 %collective-permute-start.20 = (f32[12,31]{1,0:T(8,128)S(1)}, f32[12,31]{1,0:T(8,128)S(1)}, u32[]{:S(2)}, u32[]{:S(2)}) collective-permute-start(f32[12,31]{1,0:T(8,128)S(1)} %add_add_fusion.1), channel_id=1, source_target_pairs={{0,64},{16,80},{32,96},{48,112},{64,0},{80,16},{96,32},{112,48},{1... | collective-permute-start | bytes 4472 | tf_op jit(solution)/shard_map/ppermute | solution.py:263
  148.4 4.3 %collective-permute-start.21 = (f32[12,31]{1,0:T(8,128)S(1)}, f32[12,31]{1,0:T(8,128)S(1)}, u32[]{:S(2)}, u32[]{:S(2)}) collective-permute-start(f32[12,31]{1,0:T(8,128)S(1)} %add_add_fusion.1), channel_id=1, source_target_pairs={{0,128},{16,144},{32,160},{48,176},{64,192},{80,208},{96,224},{112... | collective-permute-start | bytes 4472 | tf_op jit(solution)/shard_map/ppermute | solution.py:263
  150.8 4.0 %collective-permute-start.22 = (f32[12,31]{1,0:T(8,128)S(1)}, f32[12,31]{1,0:T(8,128)S(1)}, u32[]{:S(2)}, u32[]{:S(2)}) collective-permute-start(f32[12,31]{1,0:T(8,128)S(1)} %add_add_fusion.1), channel_id=1, source_target_pairs={{0,192},{16,208},{32,224},{48,240},{64,128},{80,144},{96,160},{112... | collective-permute-start | bytes 4472 | tf_op jit(solution)/shard_map/ppermute | solution.py:263
  (9 other events, 14.9 us)

commit v11 on v10

--- a/solution.py
+++ b/solution.py
@@ -66,7 +66,7 @@
     return ref[:, tile].reshape(ROWS, DIM)
 
 
-SHIFTS = (1, -1, 4, 3, -3, 2, -2)
+SHIFTS = (1, -1, 3, -3, 4, 2, -2)
 SLOTS = tuple((d, x) for x in range(2) for d in range(CHIPS))
 
 

time: 165 us -> 166 us (level)
  no operation moved by 1% of the time
where the time goes in v11:
time: 166 us; the launch traced here: 165 us
  starting transfers between devices  65.9 us (40%)
  waiting for transfers between devices  56.7 us (34%)
  Pallas kernels  31.8 us (19%)
  local copies, waits for them, and re-layouts  7.81 us (5%)
    ppermute x17, waiting for transfers between devices, move(): return lax.ppermute(message, 'seq', perm)  43.2 us
    ppermute x17, starting transfers between devices, move(): return lax.ppermute(message, 'seq', perm)  32.9 us
    pallas_call x10, Pallas kernels, call(): pl.pallas_call(kernel, out_shape=tuple(outputs), in_specs=specs, out_spec...  31.8 us
    all_to_all x3, starting transfers between devices, exchange(): lax.all_to_all(packed, 'seq', split_axis=0, concat_axis=0, tiled=True)  25.2 us
    ppermute x6, waiting for transfers between devices, pair(): return lax.ppermute(terms, axis, [(i, i ^ mask) for i in range(size)])  7.81 us
    ppermute x6, starting transfers between devices, pair(): return lax.ppermute(terms, axis, [(i, i ^ mask) for i in range(size)])  7.79 us
    unnamed x30, local copies, waits for them, and re-layouts  7.65 us
    all_to_all x3, waiting for transfers between devices, exchange(): lax.all_to_all(packed, 'seq', split_axis=0, concat_axis=0, tiled=True)  5.66 us
  transfers between devices with their start and end apart: 26, of which 11 were waited for; matrix products, arithmetic and copies ran while one was open for 1% of the time, Pallas kernels for 17%

profile of v11, /device:TPU:1, one launch (start us, length us, event | category | flops | bytes accessed | tf_op | source)
XLA Modules:
  0.0 165.1 jit_solution(15913595099147913350)
XLA Ops:
  1.3 2.7 %pack.1 = bf16[16,37,16,128]{3,2,1,0:T(8,128)(2,1)} custom-call(s32[1,1]{1,0:T(1,128)S(6)} %copy.20.clip_ref, bf16[1,256,1536]{2,1,0:T(8,128)(2,1)} %q_ref.1, bf16[1,256,1536]{2,1,0:T(8,128)(2,1)} %k_ref.1, bf16[1,256,1536]{2,1,0:T(8,128)(2,1)} %up_ref.1), custom_call_target="tpu_custom_call" | custom-call | flops 1000 | bytes 1000 | tf_op jit(solution)/shard_map/pack/pallas_call | solution.py:245
  4.1 10.1 %all-to-all-start = ((bf16[16,37,16,128]{3,2,1,0:T(8,128)(2,1)}), bf16[16,37,16,128]{3,2,1,0:T(8,128)(2,1)S(1)}, u32[]{:S(2)}, u32[]{:S(2)}) async-start(bf16[16,37,16,128]{3,2,1,0:T(8,128)(2,1)} %pack.1), calls=%async_computation | async-start | bytes 4849664 | tf_op jit(solution)/shard_map/all_to_all | solution.py:258
  17.9 4.1 %spatial_fwd.1 = (bf16[8,12,16,128]{3,2,1,0:T(8,128)(2,1)S(1)}, bf16[8,12,16,128]{3,2,1,0:T(8,128)(2,1)S(1)}, f32[12,256,256]{2,1,0:T(8,128)}) custom-call(s32[2]{0:T(128)S(1)} %pad_add_fusion.pos_ref, bf16[1,256,1536]{2,1,0:T(8,128)(2,1)S(1)} %copy-done.1, bf16[1,256,1536]{2,1,0:T(8,128)(2,1)S(1)} %copy-done.2, bf16[1,256,1536]{2,1,0:T(8,128)(2,1)S(1)} %copy-done.4), custom_call_target="tpu_custom_call" | custom-call | flops 1000 | bytes 1000 | tf_op jit(solution)/shard_map/spatial_fwd/pallas_call | solution.py:245
  22.2 1.6 collective-permute-done.got_ref
  24.6 1.4 collective-permute-start.1
  27.2 2.9 %collective-permute-start.3 = (bf16[2,12,16,128]{3,2,1,0:T(8,128)(2,1)}, bf16[2,12,16,128]{3,2,1,0:T(8,128)(2,1)}, u32[]{:S(2)}, u32[]{:S(2)}) collective-permute-start(bf16[2,12,16,128]{3,2,1,0:T(8,128)(2,1)} %get-tuple-element.66), channel_id=1, source_target_pairs={{0,6},{1,7},{2,8},{3,9},{4,10},{5,11},{6,12},{7,13},{8,14},{9,15},... | collective-permute-start | bytes 294920 | tf_op jit(solution)/shard_map/ppermute | solution.py:273
  30.2 1.6 collective-permute-start.4
  31.7 5.3 %collective-permute-start.5 = (bf16[2,12,16,128]{3,2,1,0:T(8,128)(2,1)}, bf16[2,12,16,128]{3,2,1,0:T(8,128)(2,1)}, u32[]{:S(2)}, u32[]{:S(2)}) collective-permute-start(bf16[2,12,16,128]{3,2,1,0:T(8,128)(2,1)} %get-tuple-element.68), channel_id=1, source_target_pairs={{0,8},{1,9},{2,10},{3,11},{4,12},{5,13},{6,14},{7,15},{8,0},{9,1},... | collective-permute-start | bytes 294920 | tf_op jit(solution)/shard_map/ppermute | solution.py:273
  37.0 34.9 %collective-permute-done.1.refs_1_ = bf16[2,12,16,128]{3,2,1,0:T(8,128)(2,1)S(1)} collective-permute-done((bf16[2,12,16,128]{3,2,1,0:T(8,128)(2,1)S(1)}, bf16[2,12,16,128]{3,2,1,0:T(8,128)(2,1)S(1)}, u32[]{:S(2)}, u32[]{:S(2)}) %collective-permute-start.1) | collective-permute-done | bytes 98336 | tf_op jit(solution)/shard_map/ppermute | solution.py:273
  73.3 3.4 %collective-permute-start.7 = (bf16[2,12,16,128]{3,2,1,0:T(8,128)(2,1)}, bf16[2,12,16,128]{3,2,1,0:T(8,128)(2,1)}, u32[]{:S(2)}, u32[]{:S(2)}) collective-permute-start(bf16[2,12,16,128]{3,2,1,0:T(8,128)(2,1)} %get-tuple-element.70), channel_id=1, source_target_pairs={{0,12},{1,13},{2,14},{3,15},{4,0},{5,1},{6,2},{7,3},{8,4},{9,5},{1... | collective-permute-start | bytes 294920 | tf_op jit(solution)/shard_map/ppermute | solution.py:273
  76.7 4.2 %temporal_a.1 = bf16[16,12,16,128]{3,2,1,0:T(8,128)(2,1)} custom-call(s32[16]{0:T(128)S(1)} %fusion.11.frames_ref, bf16[16,37,16,128]{3,2,1,0:T(8,128)(2,1)S(1)} %all-to-all-done.in_ref, f32[12,16,256]{2,1,0:T(8,128)S(1)} %bias.1.bias_ref), custom_call_target="tpu_custom_call" | custom-call | flops 1000 | bytes 1000 | tf_op jit(solution)/shard_map/temporal_a/pallas_call | solution.py:245
  80.9 8.8 %all-to-all-start.2 = ((bf16[16,12,16,128]{3,2,1,0:T(8,128)(2,1)}), bf16[16,12,16,128]{3,2,1,0:T(8,128)(2,1)}, u32[]{:S(2)}, u32[]{:S(2)}) async-start(bf16[16,12,16,128]{3,2,1,0:T(8,128)(2,1)} %temporal_a.1), calls=%async_computation.2 | async-start | bytes 1572864 | tf_op jit(solution)/shard_map/all_to_all | solution.py:258
  91.5 7.2 %temporal_b.1 = (bf16[16,2,16,1536]{3,2,1,0:T(8,128)(2,1)S(1)}, bf16[8,12,16,128]{3,2,1,0:T(8,128)(2,1)S(1)}, bf16[8,12,16,128]{3,2,1,0:T(8,128)(2,1)S(1)}, f32[12,16,256]{2,1,0:T(8,128)S(1)}) custom-call(s32[16]{0:T(128)S(1)} %fusion.11.frames_ref, bf16[16,37,16,128]{3,2,1,0:T(8,128)(2,1)S(1)} %all-to-all-done.in_ref, f32[12,16,256]{2,1,0:T(8,128)S(1)} %bias.1.bias_ref, ...), custom_call_target="tpu_custom_call" | custom-call | flops 99999997952 | bytes 1000 | tf_op jit(solution)/shard_map/temporal_b/pallas_call | solution.py:245
  102.6 1.6 collective-permute-start.10
  105.4 3.0 %collective-permute-start.12 = (bf16[25,16,128]{2,1,0:T(8,128)(2,1)}, bf16[25,16,128]{2,1,0:T(8,128)(2,1)}, u32[]{:S(2)}, u32[]{:S(2)}) collective-permute-start(bf16[25,16,128]{2,1,0:T(8,128)(2,1)} %get-tuple-element.83), channel_id=1, source_target_pairs={{0,6},{1,7},{2,8},{3,9},{4,10},{5,11},{6,12},{7,13},{8,14},{9,15},... | collective-permute-start | bytes 307208 | tf_op jit(solution)/shard_map/ppermute | solution.py:273
  108.4 1.5 collective-permute-start.13
  109.9 5.4 %collective-permute-start.14 = (bf16[25,16,128]{2,1,0:T(8,128)(2,1)}, bf16[25,16,128]{2,1,0:T(8,128)(2,1)}, u32[]{:S(2)}, u32[]{:S(2)}) collective-permute-start(bf16[25,16,128]{2,1,0:T(8,128)(2,1)} %get-tuple-element.85), channel_id=1, source_target_pairs={{0,8},{1,9},{2,10},{3,11},{4,12},{5,13},{6,14},{7,15},{8,0},{9,1},... | collective-permute-start | bytes 307208 | tf_op jit(solution)/shard_map/ppermute | solution.py:273
  115.3 3.6 %collective-permute-start.16 = (bf16[25,16,128]{2,1,0:T(8,128)(2,1)}, bf16[25,16,128]{2,1,0:T(8,128)(2,1)}, u32[]{:S(2)}, u32[]{:S(2)}) collective-permute-start(bf16[25,16,128]{2,1,0:T(8,128)(2,1)} %get-tuple-element.87), channel_id=1, source_target_pairs={{0,12},{1,13},{2,14},{3,15},{4,0},{5,1},{6,2},{7,3},{8,4},{9,5},{1... | collective-permute-start | bytes 307208 | tf_op jit(solution)/shard_map/ppermute | solution.py:273
  118.9 6.3 %all-to-all-start.1 = ((bf16[16,2,16,1536]{3,2,1,0:T(8,128)(2,1)}), bf16[16,2,16,1536]{3,2,1,0:T(8,128)(2,1)S(1)}, u32[]{:S(2)}, u32[]{:S(2)}) async-start(bf16[16,2,16,1536]{3,2,1,0:T(8,128)(2,1)} %copy-done), calls=%async_computation.1 | async-start | bytes 3145728 | tf_op jit(solution)/shard_map/all_to_all | solution.py:258
  125.2 2.6 %collective-permute-done.14.refs_5_ = bf16[25,16,128]{2,1,0:T(8,128)(2,1)} collective-permute-done((bf16[25,16,128]{2,1,0:T(8,128)(2,1)}, bf16[25,16,128]{2,1,0:T(8,128)(2,1)}, u32[]{:S(2)}, u32[]{:S(2)}) %collective-permute-start.14) | collective-permute-done | bytes 102432 | tf_op jit(solution)/shard_map/ppermute | solution.py:273
  128.5 2.6 %collective-permute-done.16.refs_7_ = bf16[25,16,128]{2,1,0:T(8,128)(2,1)} collective-permute-done((bf16[25,16,128]{2,1,0:T(8,128)(2,1)}, bf16[25,16,128]{2,1,0:T(8,128)(2,1)}, u32[]{:S(2)}, u32[]{:S(2)}) %collective-permute-start.16) | collective-permute-done | bytes 102432 | tf_op jit(solution)/shard_map/ppermute | solution.py:273
  132.2 7.2 %spatial_bwd.1 = (bf16[1,256,1536]{2,1,0:T(8,128)(2,1)}, bf16[1,256,1536]{2,1,0:T(8,128)(2,1)}, bf16[1,256,1536]{2,1,0:T(8,128)(2,1)}) custom-call(bf16[1,256,1536]{2,1,0:T(8,128)(2,1)S(1)} %copy-done.1, bf16[1,256,1536]{2,1,0:T(8,128)(2,1)S(1)} %copy-done.3, bf16[1,256,1536]{2,1,0:T(8,128)(2,1)S(1)} %copy-done.5, ...), custom_call_target="tpu_custom_call" | custom-call | flops 99999997952 | bytes 1000 | tf_op jit(solution)/shard_map/spatial_bwd/pallas_call | solution.py:245
  139.4 2.2 %finish.1 = (bf16[1,256,1536]{2,1,0:T(8,128)(2,1)}, f32[12,31]{1,0:T(8,128)S(1)}) custom-call(s32[2]{0:T(128)S(1)} %copy-done.8, bf16[25,16,128]{2,1,0:T(8,128)(2,1)S(1)} %get-tuple-element.93.refs_0_, bf16[25,16,128]{2,1,0:T(8,128)(2,1)S(1)} %collective-permute-done.10.refs_1_, bf16[25,16,128]{2,1,0:T(8,128)(2,1)S(1)} %collective-permute-done.11.refs_2_, ...), custom_call_target="tpu_custom_call" | custom-call | flops 1000 | bytes 1000 | tf_op jit(solution)/shard_map/finish/pallas_call | solution.py:245
  141.6 1.3 collective-permute-start.17
  142.9 2.6 %collective-permute-start.18 = (f32[12,31]{1,0:T(8,128)S(1)}, f32[12,31]{1,0:T(8,128)S(1)}, u32[]{:S(2)}, u32[]{:S(2)}) collective-permute-start(f32[12,31]{1,0:T(8,128)S(1)} %get-tuple-element.102), channel_id=1, source_target_pairs={{0,32},{16,48},{32,0},{48,16},{64,96},{80,112},{96,64},{112,80},{1... | collective-permute-start | bytes 4472 | tf_op jit(solution)/shard_map/ppermute | solution.py:263
  145.5 1.7 %collective-permute-done.18 = f32[12,31]{1,0:T(8,128)S(1)} collective-permute-done((f32[12,31]{1,0:T(8,128)S(1)}, f32[12,31]{1,0:T(8,128)S(1)}, u32[]{:S(2)}, u32[]{:S(2)}) %collective-permute-start.18) | collective-permute-done | bytes 1520 | tf_op jit(solution)/shard_map/ppermute | solution.py:263
  147.2 2.3 %collective-permute-done.19 = f32[12,31]{1,0:T(8,128)S(1)} collective-permute-done((f32[12,31]{1,0:T(8,128)S(1)}, f32[12,31]{1,0:T(8,128)S(1)}, u32[]{:S(2)}, u32[]{:S(2)}) %collective-permute-start.19) | collective-permute-done | bytes 1520 | tf_op jit(solution)/shard_map/ppermute | solution.py:263
  150.8 2.5 %collective-permute-start.21 = (f32[12,31]{1,0:T(8,128)S(1)}, f32[12,31]{1,0:T(8,128)S(1)}, u32[]{:S(2)}, u32[]{:S(2)}) collective-permute-start(f32[12,31]{1,0:T(8,128)S(1)} %add_add_fusion.1), channel_id=1, source_target_pairs={{0,128},{16,144},{32,160},{48,176},{64,192},{80,208},{96,224},{112... | collective-permute-start | bytes 4472 | tf_op jit(solution)/shard_map/ppermute | solution.py:263
  153.4 1.6 collective-permute-done.21
  155.1 2.2 %collective-permute-done.22 = f32[12,31]{1,0:T(8,128)S(1)} collective-permute-done((f32[12,31]{1,0:T(8,128)S(1)}, f32[12,31]{1,0:T(8,128)S(1)}, u32[]{:S(2)}, u32[]{:S(2)}) %collective-permute-start.22) | collective-permute-done | bytes 1520 | tf_op jit(solution)/shard_map/ppermute | solution.py:263
  157.8 5.7 %all-to-all-done.1.in_ref = bf16[16,2,16,1536]{3,2,1,0:T(8,128)(2,1)S(1)} async-done(((bf16[16,2,16,1536]{3,2,1,0:T(8,128)(2,1)}), bf16[16,2,16,1536]{3,2,1,0:T(8,128)(2,1)S(1)}, u32[]{:S(2)}, u32[]{:S(2)}) %all-to-all-start.1) | async-done | bytes 1572896 | tf_op jit(solution)/shard_map/all_to_all | solution.py:258
  163.5 1.4 unpack.1
  (71 shorter events, 18.1 us)
Async XLA Ops:
  4.0 10.2 %copy-start.13 = (s32[16]{0:T(128)S(1)}, s32[16]{0:T(128)}, u32[]{:S(2)}) copy-start(s32[16]{0:T(128)} %constant.21.clone) | copy-start | bytes 196
  4.0 10.2 %copy-start.14 = (s32[16]{0:T(128)S(1)}, s32[16]{0:T(128)}, u32[]{:S(2)}) copy-start(s32[16]{0:T(128)} %constant.37) | copy-start | bytes 196
  4.0 10.4 %copy-start.6 = (f32[12,31]{1,0:T(8,128)S(1)}, f32[12,31]{1,0:T(8,128)}, u32[]{:S(2)}) copy-start(f32[12,31]{1,0:T(8,128)} %rel_ref) | copy-start | bytes 4468
  4.1 11.6 %copy-start.1 = (bf16[1,256,1536]{2,1,0:T(8,128)(2,1)S(1)}, bf16[1,256,1536]{2,1,0:T(8,128)(2,1)}, u32[]{:S(2)}) copy-start(bf16[1,256,1536]{2,1,0:T(8,128)(2,1)} %q_ref.3) | copy-start | bytes 2359300
  4.1 72.7 %all-to-all-start = ((bf16[16,37,16,128]{3,2,1,0:T(8,128)(2,1)}), bf16[16,37,16,128]{3,2,1,0:T(8,128)(2,1)S(1)}, u32[]{:S(2)}, u32[]{:S(2)}) async-start(bf16[16,37,16,128]{3,2,1,0:T(8,128)(2,1)} %pack.1), calls=%async_computation | async-start | bytes 4849664 | tf_op jit(solution)/shard_map/all_to_all | solution.py:258
  17.9 63.0 %copy-start.7 = (s32[2]{0:T(128)}, s32[2]{0:T(128)S(1)}, u32[]{:S(2)}) copy-start(s32[2]{0:T(128)S(1)} %pad_add_fusion.pos_ref) | copy-start | bytes 28
  22.0 1.7 %collective-permute-start = (bf16[8,12,16,128]{3,2,1,0:T(8,128)(2,1)S(1)}, bf16[8,12,16,128]{3,2,1,0:T(8,128)(2,1)S(1)}, u32[]{:S(2)}, u32[]{:S(2)}) collective-permute-start(bf16[8,12,16,128]{3,2,1,0:T(8,128)(2,1)S(1)} %get-tuple-element.62), channel_id=1, source_target_pairs={{0,1},{1,0},{2,3},{3,2},{4,5},{5,4},{6,7},{7,6},{8,9},{9,8},{10,11... | collective-permute-start | bytes 1179656 | tf_op jit(solution)/shard_map/ppermute | solution.py:273
  24.6 47.3 %collective-permute-start.1 = (bf16[2,12,16,128]{3,2,1,0:T(8,128)(2,1)S(1)}, bf16[2,12,16,128]{3,2,1,0:T(8,128)(2,1)S(1)}, u32[]{:S(2)}, u32[]{:S(2)}) collective-permute-start(bf16[2,12,16,128]{3,2,1,0:T(8,128)(2,1)S(1)} %get-tuple-element.64), channel_id=1, source_target_pairs={{0,2},{1,3},{2,4},{3,5},{4,6},{5,7},{6,8},{7,9},{8,10},{9,11},{10,... | collective-permute-start | bytes 294920 | tf_op jit(solution)/shard_map/ppermute | solution.py:273
  26.0 46.7 %collective-permute-start.2 = (bf16[2,12,16,128]{3,2,1,0:T(8,128)(2,1)S(1)}, bf16[2,12,16,128]{3,2,1,0:T(8,128)(2,1)S(1)}, u32[]{:S(2)}, u32[]{:S(2)}) collective-permute-start(bf16[2,12,16,128]{3,2,1,0:T(8,128)(2,1)S(1)} %get-tuple-element.65), channel_id=1, source_target_pairs={{0,14},{1,15},{2,0},{3,1},{4,2},{5,3},{6,4},{7,5},{8,6},{9,7},{10,... | collective-permute-start | bytes 294920 | tf_op jit(solution)/shard_map/ppermute | solution.py:273
  27.2 62.4 %collective-permute-start.3 = (bf16[2,12,16,128]{3,2,1,0:T(8,128)(2,1)}, bf16[2,12,16,128]{3,2,1,0:T(8,128)(2,1)}, u32[]{:S(2)}, u32[]{:S(2)}) collective-permute-start(bf16[2,12,16,128]{3,2,1,0:T(8,128)(2,1)} %get-tuple-element.66), channel_id=1, source_target_pairs={{0,6},{1,7},{2,8},{3,9},{4,10},{5,11},{6,12},{7,13},{8,14},{9,15},... | collective-permute-start | bytes 294920 | tf_op jit(solution)/shard_map/ppermute | solution.py:273
  30.2 59.5 %collective-permute-start.4 = (bf16[2,12,16,128]{3,2,1,0:T(8,128)(2,1)}, bf16[2,12,16,128]{3,2,1,0:T(8,128)(2,1)}, u32[]{:S(2)}, u32[]{:S(2)}) collective-permute-start(bf16[2,12,16,128]{3,2,1,0:T(8,128)(2,1)} %get-tuple-element.67), channel_id=1, source_target_pairs={{0,10},{1,11},{2,12},{3,13},{4,14},{5,15},{6,0},{7,1},{8,2},{9,3},... | collective-permute-start | bytes 294920 | tf_op jit(solution)/shard_map/ppermute | solution.py:273
  31.7 58.0 %collective-permute-start.5 = (bf16[2,12,16,128]{3,2,1,0:T(8,128)(2,1)}, bf16[2,12,16,128]{3,2,1,0:T(8,128)(2,1)}, u32[]{:S(2)}, u32[]{:S(2)}) collective-permute-start(bf16[2,12,16,128]{3,2,1,0:T(8,128)(2,1)} %get-tuple-element.68), channel_id=1, source_target_pairs={{0,8},{1,9},{2,10},{3,11},{4,12},{5,13},{6,14},{7,15},{8,0},{9,1},... | collective-permute-start | bytes 294920 | tf_op jit(solution)/shard_map/ppermute | solution.py:273
  72.5 17.2 %collective-permute-start.6 = (bf16[2,12,16,128]{3,2,1,0:T(8,128)(2,1)}, bf16[2,12,16,128]{3,2,1,0:T(8,128)(2,1)}, u32[]{:S(2)}, u32[]{:S(2)}) collective-permute-start(bf16[2,12,16,128]{3,2,1,0:T(8,128)(2,1)} %get-tuple-element.69), channel_id=1, source_target_pairs={{0,4},{1,5},{2,6},{3,7},{4,8},{5,9},{6,10},{7,11},{8,12},{9,13},{1... | collective-permute-start | bytes 294920 | tf_op jit(solution)/shard_map/ppermute | solution.py:273
  73.3 16.4 %collective-permute-start.7 = (bf16[2,12,16,128]{3,2,1,0:T(8,128)(2,1)}, bf16[2,12,16,128]{3,2,1,0:T(8,128)(2,1)}, u32[]{:S(2)}, u32[]{:S(2)}) collective-permute-start(bf16[2,12,16,128]{3,2,1,0:T(8,128)(2,1)} %get-tuple-element.70), channel_id=1, source_target_pairs={{0,12},{1,13},{2,14},{3,15},{4,0},{5,1},{6,2},{7,3},{8,4},{9,5},{1... | collective-permute-start | bytes 294920 | tf_op jit(solution)/shard_map/ppermute | solution.py:273
  80.9 37.9 %all-to-all-start.2 = ((bf16[16,12,16,128]{3,2,1,0:T(8,128)(2,1)}), bf16[16,12,16,128]{3,2,1,0:T(8,128)(2,1)}, u32[]{:S(2)}, u32[]{:S(2)}) async-start(bf16[16,12,16,128]{3,2,1,0:T(8,128)(2,1)} %temporal_a.1), calls=%async_computation.2 | async-start | bytes 1572864 | tf_op jit(solution)/shard_map/all_to_all | solution.py:258
  99.9 31.2 %copy-start.3 = (bf16[1,256,1536]{2,1,0:T(8,128)(2,1)S(1)}, bf16[1,256,1536]{2,1,0:T(8,128)(2,1)}, u32[]{:S(2)}) copy-start(bf16[1,256,1536]{2,1,0:T(8,128)(2,1)} %k_ref.3) | copy-start | bytes 2359300
  99.9 1.9 %collective-permute-start.9 = (bf16[8,12,16,128]{3,2,1,0:T(8,128)(2,1)S(1)}, bf16[8,12,16,128]{3,2,1,0:T(8,128)(2,1)S(1)}, u32[]{:S(2)}, u32[]{:S(2)}) collective-permute-start(bf16[8,12,16,128]{3,2,1,0:T(8,128)(2,1)S(1)} %get-tuple-element.79), channel_id=1, source_target_pairs={{0,1},{1,0},{2,3},{3,2},{4,5},{5,4},{6,7},{7,6},{8,9},{9,8},{10,11... | collective-permute-start | bytes 1179656 | tf_op jit(solution)/shard_map/ppermute | solution.py:273
  100.5 1.2 collective-permute-start.8
  102.6 12.7 %collective-permute-start.10 = (bf16[25,16,128]{2,1,0:T(8,128)(2,1)S(1)}, bf16[25,16,128]{2,1,0:T(8,128)(2,1)S(1)}, u32[]{:S(2)}, u32[]{:S(2)}) collective-permute-start(bf16[25,16,128]{2,1,0:T(8,128)(2,1)S(1)} %get-tuple-element.81), channel_id=1, source_target_pairs={{0,2},{1,3},{2,4},{3,5},{4,6},{5,7},{6,8},{7,9},{8,10},{9,11},{10,... | collective-permute-start | bytes 307208 | tf_op jit(solution)/shard_map/ppermute | solution.py:273
  104.2 11.1 %collective-permute-start.11 = (bf16[25,16,128]{2,1,0:T(8,128)(2,1)S(1)}, bf16[25,16,128]{2,1,0:T(8,128)(2,1)S(1)}, u32[]{:S(2)}, u32[]{:S(2)}) collective-permute-start(bf16[25,16,128]{2,1,0:T(8,128)(2,1)S(1)} %get-tuple-element.82), channel_id=1, source_target_pairs={{0,14},{1,15},{2,0},{3,1},{4,2},{5,3},{6,4},{7,5},{8,6},{9,7},{10,... | collective-permute-start | bytes 307208 | tf_op jit(solution)/shard_map/ppermute | solution.py:273
  105.4 19.8 %collective-permute-start.12 = (bf16[25,16,128]{2,1,0:T(8,128)(2,1)}, bf16[25,16,128]{2,1,0:T(8,128)(2,1)}, u32[]{:S(2)}, u32[]{:S(2)}) collective-permute-start(bf16[25,16,128]{2,1,0:T(8,128)(2,1)} %get-tuple-element.83), channel_id=1, source_target_pairs={{0,6},{1,7},{2,8},{3,9},{4,10},{5,11},{6,12},{7,13},{8,14},{9,15},... | collective-permute-start | bytes 307208 | tf_op jit(solution)/shard_map/ppermute | solution.py:273
  108.4 16.8 %collective-permute-start.13 = (bf16[25,16,128]{2,1,0:T(8,128)(2,1)}, bf16[25,16,128]{2,1,0:T(8,128)(2,1)}, u32[]{:S(2)}, u32[]{:S(2)}) collective-permute-start(bf16[25,16,128]{2,1,0:T(8,128)(2,1)} %get-tuple-element.84), channel_id=1, source_target_pairs={{0,10},{1,11},{2,12},{3,13},{4,14},{5,15},{6,0},{7,1},{8,2},{9,3},... | collective-permute-start | bytes 307208 | tf_op jit(solution)/shard_map/ppermute | solution.py:273
  109.9 17.9 %collective-permute-start.14 = (bf16[25,16,128]{2,1,0:T(8,128)(2,1)}, bf16[25,16,128]{2,1,0:T(8,128)(2,1)}, u32[]{:S(2)}, u32[]{:S(2)}) collective-permute-start(bf16[25,16,128]{2,1,0:T(8,128)(2,1)} %get-tuple-element.85), channel_id=1, source_target_pairs={{0,8},{1,9},{2,10},{3,11},{4,12},{5,13},{6,14},{7,15},{8,0},{9,1},... | collective-permute-start | bytes 307208 | tf_op jit(solution)/shard_map/ppermute | solution.py:273
  115.3 13.2 %collective-permute-start.15 = (bf16[25,16,128]{2,1,0:T(8,128)(2,1)}, bf16[25,16,128]{2,1,0:T(8,128)(2,1)}, u32[]{:S(2)}, u32[]{:S(2)}) collective-permute-start(bf16[25,16,128]{2,1,0:T(8,128)(2,1)} %get-tuple-element.86), channel_id=1, source_target_pairs={{0,4},{1,5},{2,6},{3,7},{4,8},{5,9},{6,10},{7,11},{8,12},{9,13},{1... | collective-permute-start | bytes 307208 | tf_op jit(solution)/shard_map/ppermute | solution.py:273
  115.3 15.8 %collective-permute-start.16 = (bf16[25,16,128]{2,1,0:T(8,128)(2,1)}, bf16[25,16,128]{2,1,0:T(8,128)(2,1)}, u32[]{:S(2)}, u32[]{:S(2)}) collective-permute-start(bf16[25,16,128]{2,1,0:T(8,128)(2,1)} %get-tuple-element.87), channel_id=1, source_target_pairs={{0,12},{1,13},{2,14},{3,15},{4,0},{5,1},{6,2},{7,3},{8,4},{9,5},{1... | collective-permute-start | bytes 307208 | tf_op jit(solution)/shard_map/ppermute | solution.py:273
  118.9 44.6 %all-to-all-start.1 = ((bf16[16,2,16,1536]{3,2,1,0:T(8,128)(2,1)}), bf16[16,2,16,1536]{3,2,1,0:T(8,128)(2,1)S(1)}, u32[]{:S(2)}, u32[]{:S(2)}) async-start(bf16[16,2,16,1536]{3,2,1,0:T(8,128)(2,1)} %copy-done), calls=%async_computation.1 | async-start | bytes 3145728 | tf_op jit(solution)/shard_map/all_to_all | solution.py:258
  141.6 3.9 %collective-permute-start.17 = (f32[12,31]{1,0:T(8,128)S(1)}, f32[12,31]{1,0:T(8,128)S(1)}, u32[]{:S(2)}, u32[]{:S(2)}) collective-permute-start(f32[12,31]{1,0:T(8,128)S(1)} %get-tuple-element.102), channel_id=1, source_target_pairs={{0,16},{16,0},{32,48},{48,32},{64,80},{80,64},{96,112},{112,96},{1... | collective-permute-start | bytes 4472 | tf_op jit(solution)/shard_map/ppermute | solution.py:263
  142.9 4.3 %collective-permute-start.18 = (f32[12,31]{1,0:T(8,128)S(1)}, f32[12,31]{1,0:T(8,128)S(1)}, u32[]{:S(2)}, u32[]{:S(2)}) collective-permute-start(f32[12,31]{1,0:T(8,128)S(1)} %get-tuple-element.102), channel_id=1, source_target_pairs={{0,32},{16,48},{32,0},{48,16},{64,96},{80,112},{96,64},{112,80},{1... | collective-permute-start | bytes 4472 | tf_op jit(solution)/shard_map/ppermute | solution.py:263
  145.5 4.0 %collective-permute-start.19 = (f32[12,31]{1,0:T(8,128)S(1)}, f32[12,31]{1,0:T(8,128)S(1)}, u32[]{:S(2)}, u32[]{:S(2)}) collective-permute-start(f32[12,31]{1,0:T(8,128)S(1)} %get-tuple-element.102), channel_id=1, source_target_pairs={{0,48},{16,32},{32,16},{48,0},{64,112},{80,96},{96,80},{112,64},{1... | collective-permute-start | bytes 4472 | tf_op jit(solution)/shard_map/ppermute | solution.py:263
  149.6 3.9 %collective-permute-start.20 = (f32[12,31]{1,0:T(8,128)S(1)}, f32[12,31]{1,0:T(8,128)S(1)}, u32[]{:S(2)}, u32[]{:S(2)}) collective-permute-start(f32[12,31]{1,0:T(8,128)S(1)} %add_add_fusion.1), channel_id=1, source_target_pairs={{0,64},{16,80},{32,96},{48,112},{64,0},{80,16},{96,32},{112,48},{1... | collective-permute-start | bytes 4472 | tf_op jit(solution)/shard_map/ppermute | solution.py:263
  150.8 4.3 %collective-permute-start.21 = (f32[12,31]{1,0:T(8,128)S(1)}, f32[12,31]{1,0:T(8,128)S(1)}, u32[]{:S(2)}, u32[]{:S(2)}) collective-permute-start(f32[12,31]{1,0:T(8,128)S(1)} %add_add_fusion.1), channel_id=1, source_target_pairs={{0,128},{16,144},{32,160},{48,176},{64,192},{80,208},{96,224},{112... | collective-permute-start | bytes 4472 | tf_op jit(solution)/shard_map/ppermute | solution.py:263
  153.2 4.0 %collective-permute-start.22 = (f32[12,31]{1,0:T(8,128)S(1)}, f32[12,31]{1,0:T(8,128)S(1)}, u32[]{:S(2)}, u32[]{:S(2)}) collective-permute-start(f32[12,31]{1,0:T(8,128)S(1)} %add_add_fusion.1), channel_id=1, source_target_pairs={{0,192},{16,208},{32,224},{48,240},{64,128},{80,144},{96,160},{112... | collective-permute-start | bytes 4472 | tf_op jit(solution)/shard_map/ppermute | solution.py:263
  (9 other events, 14.8 us)
